TPU v7x, 512 devices: a whole 4x4x16 slice. The times are simulated.
512 devices in a mesh: gx: 8 (over x, core), gy: 16 (over z), gz: 4 (over y).
Axes of the slice: x: 4, y: 4, z: 16, core: 2. Of those that a mesh axis runs over, the one named last changes fastest.
Arguments:
- positions: float32 [3, 8, 16, 4, 1024], P(None, 'gx', 'gy', 'gz'), may hold values from 0 to 1
- velocities: float32 [3, 8, 16, 4, 1024], P(None, 'gx', 'gy', 'gz'), may hold values from -2.5 to 2.5
- forces: float32 [3, 8, 16, 4, 1024], P(None, 'gx', 'gy', 'gz'), may hold values from -6 to 6
- counts: int32 [8, 16, 4], P('gx', 'gy', 'gz'), may hold values from 512 to 1024, as said below
- pair_tiles: int32 [2, 8, 16, 4, 128], P(None, 'gx', 'gy', 'gz'), may hold values from 0 to 287, as said below
- pair_count: int32 [8, 16, 4], P('gx', 'gy', 'gz'), may hold values from 16 to 128, as said below
- mig_slots: int32 [2, 4, 8, 16, 4, 128], P(None, None, 'gx', 'gy', 'gz'), may hold values from 0 to 511, as said below
Outputs:
- final_positions: float32 [3, 8, 16, 4, 1024], P(None, 'gx', 'gy', 'gz')
- final_velocities: float32 [3, 8, 16, 4, 1024], P(None, 'gx', 'gy', 'gz')
Inputs may be any that keep to these rules, and one draw needn't show every extreme that they name: `counts`: a brick's live atoms fill its first slots. `pair_count`: a brick's live list entries are its first ones. `pair_tiles`: row 0 holds a tile below 8, row 1 a ghost tile of the brick's neighbourhood. `mig_slots`: in each step and brick the 512 slots are distinct and below 512.
All inputs are finite; a program needn't handle non-finite values.
Results may differ from a plain program's by a relative error of at most 0.0003.
Values sent between devices are 32-bit elements; how exact they have to be, the bound alone decides.
No kernel may reach another device: no remote copies, remote signals or barrier semaphores. Data moves between devices by JAX's collectives and lax.ppermute only.
A program may use at most 64 MiB of HBM per device.

v0:
```python
import jax
import jax.numpy as jnp
from jax import lax
from jax.sharding import PartitionSpec as P

box_edge = 1.0
cutoff_sq = 0.81
height_ratio = 0.25
density_scale = 1.0 / 256.0
repulsion = 1.0 / 512.0
embed_scale = 1.0
time_step = 0.25
pair_block = 16


def padded(cells, sides, width):
    for axis, dim in sides:
        count = lax.axis_size(axis)
        head = lax.slice_in_dim(cells, 0, width, axis=dim)
        tail = lax.slice_in_dim(cells, cells.shape[dim] - width, cells.shape[dim], axis=dim)
        cells = jnp.concatenate(
            [
                lax.ppermute(tail, axis, [(i, (i + 1) % count) for i in range(count)]),
                cells,
                lax.ppermute(head, axis, [((i + 1) % count, i) for i in range(count)]),
            ],
            axis=dim,
        )
    return cells


def geometry(own_rows, ghost_rows, local_tile, ghost_tile, in_list, selfbase):
    near_tiles = jnp.take(own_rows.reshape(4, -1, 128), local_tile, axis=1)
    far_tiles = jnp.take(ghost_rows.reshape(4, -1, 128), ghost_tile, axis=1)
    raw_offset = near_tiles[:3, :, :, None] - far_tiles[:3, :, None, :]
    offset_vec = jnp.stack([raw_offset[0], raw_offset[1], height_ratio * raw_offset[2]])
    dist_sq = (
        offset_vec[0] * offset_vec[0]
        + offset_vec[1] * offset_vec[1]
        + offset_vec[2] * offset_vec[2]
    )
    shrink = jnp.maximum(1.0 - dist_sq / cutoff_sq, 0.0)
    lane_ids = jnp.arange(128, dtype=jnp.int32)
    same_atom = (ghost_tile == local_tile + selfbase)[:, None, None] & (
        lane_ids[:, None] == lane_ids[None, :]
    )[None]
    weight = (
        near_tiles[3][:, :, None]
        * far_tiles[3][:, None, :]
        * in_list.astype(jnp.float32)[:, None, None]
    )
    weight = jnp.where(same_atom, 0.0, weight)
    return (offset_vec, shrink, weight)


def tile_sum(row_terms, local_tile, tile_count):
    onehot = (local_tile[:, None] == jnp.arange(tile_count, dtype=jnp.int32)[None, :]).astype(
        jnp.float32
    )
    return jnp.einsum("pt,...pr->...tr", onehot, row_terms, precision=lax.Precision.HIGHEST)


def density_rows(shrink, weight):
    return jnp.sum(weight * shrink**3, axis=2) * density_scale


def force_rows(offset_vec, shrink, weight, near_fp, far_fp):
    slope_sum = -4.0 * repulsion * shrink**3 / cutoff_sq + (
        near_fp[:, :, None] + far_fp[:, None, :]
    ) * (-3.0 * density_scale * shrink**2 / cutoff_sq)
    coefficient = 2.0 * weight * slope_sum
    return -jnp.sum(coefficient[None] * offset_vec, axis=3)


def ghost_offsets(zbrick, tower_size):
    side_shift = (jnp.arange(3, dtype=jnp.int32) - 1).astype(jnp.float32) * box_edge
    depth_shift = (jnp.arange(tower_size, dtype=jnp.int32) - zbrick).astype(jnp.float32) * box_edge
    extent = (3, 3, tower_size, 1)
    return jnp.stack(
        [
            jnp.broadcast_to(side_shift[:, None, None, None], extent),
            jnp.broadcast_to(side_shift[None, :, None, None], extent),
            jnp.broadcast_to(depth_shift[None, None, :, None], extent),
        ]
    )


def advance(place_now, speed_now):
    return jnp.concatenate(
        [
            place_now[:2] + time_step * speed_now[:2],
            place_now[2:] + time_step / height_ratio * speed_now[2:],
        ],
        axis=0,
    )


def plate_cells(values_in):
    return padded(values_in, (("gx", 1), ("gy", 2)), 1)


def spread(values_in):
    tower_cells = lax.all_gather(values_in, "gz", axis=3, tiled=True)
    return plate_cells(tower_cells)


def evaluate(place_now, live, local_all, ghost_all, pair_total, zbrick, tower_size):
    row_total = place_now.shape[1]
    tile_count = row_total // 128
    own_rows = jnp.concatenate([place_now, live[None]], axis=0)
    cells = spread(own_rows.reshape(4, 1, 1, 1, row_total))
    ghost_rows = jnp.concatenate(
        [cells[:3] + ghost_offsets(zbrick, tower_size), cells[3:]], axis=0
    ).reshape(4, -1)
    selfbase = (4 * tower_size + zbrick) * tile_count
    blocks = (pair_total + pair_block - 1) // pair_block

    def block_geometry(number):
        first_pair = number * pair_block
        local_tile = lax.dynamic_slice_in_dim(local_all, first_pair, pair_block)
        ghost_tile = lax.dynamic_slice_in_dim(ghost_all, first_pair, pair_block)
        in_list = first_pair + jnp.arange(pair_block, dtype=jnp.int32) < pair_total
        return (
            geometry(own_rows, ghost_rows, local_tile, ghost_tile, in_list, selfbase),
            local_tile,
            ghost_tile,
        )

    def add_density(number, running):
        pair_parts, local_tile, ghost_tile = block_geometry(number)
        return running + tile_sum(
            density_rows(pair_parts[1], pair_parts[2]), local_tile, tile_count
        )

    density = lax.fori_loop(
        0, blocks, add_density, jnp.zeros((tile_count, 128), jnp.float32)
    ).reshape(row_total)
    slope_fp = -0.5 * embed_scale / jnp.sqrt(1.0 + density)
    far_all = spread(slope_fp.reshape(1, 1, 1, 1, row_total)).reshape(-1, 128)
    own_fp = slope_fp.reshape(tile_count, 128)

    def add_force(number, running):
        pair_parts, local_tile, ghost_tile = block_geometry(number)
        near_fp = jnp.take(own_fp, local_tile, axis=0)
        far_fp = jnp.take(far_all, ghost_tile, axis=0)
        terms = force_rows(pair_parts[0], pair_parts[1], pair_parts[2], near_fp, far_fp)
        return running + tile_sum(terms, local_tile, tile_count)

    pushes = lax.fori_loop(0, blocks, add_force, jnp.zeros((3, tile_count, 128), jnp.float32))
    return pushes.reshape(3, row_total)


def migrate(place_now, speed_now, slots):
    state_rows = jnp.concatenate([place_now, speed_now], axis=0)
    count_mig = slots.shape[1]
    packed = jnp.take(state_rows, slots.reshape(-1), axis=1).reshape(6, 1, 1, 4, count_mig)
    beside_all = padded(packed, (("gx", 1), ("gy", 2)), 1)
    arrivals = (
        (beside_all[:, 2, 1, 1], 0, 1.0),
        (beside_all[:, 0, 1, 0], 0, -1.0),
        (beside_all[:, 1, 2, 3], 1, 1.0),
        (beside_all[:, 1, 0, 2], 1, -1.0),
    )
    for direction, (arrived, component, direction_sign) in enumerate(arrivals):
        arrived = arrived.at[component].add(direction_sign * box_edge)
        state_rows = state_rows.at[:, slots[direction]].set(arrived)
    return (state_rows[:3], state_rows[3:])


def per_device(positions, velocities, forces, counts, pair_tiles, pair_count, mig_slots):
    row_total = positions.shape[4]
    zbrick = lax.axis_index("gz")
    tower_size = lax.axis_size("gz")
    live = (jnp.arange(row_total, dtype=jnp.int32) < counts.reshape(())).astype(jnp.float32)
    local_all = pair_tiles[0].reshape(-1)
    ghost_all = pair_tiles[1].reshape(-1)
    pair_total = pair_count.reshape(())
    place_now = positions.reshape(3, row_total)
    speed_now = velocities.reshape(3, row_total)
    push_now = forces.reshape(3, row_total)
    for step_index in range(mig_slots.shape[0]):
        speed_now = speed_now + 0.5 * time_step * push_now
        place_now = advance(place_now, speed_now)
        place_now, speed_now = migrate(place_now, speed_now, mig_slots[step_index].reshape(4, -1))
        push_now = evaluate(place_now, live, local_all, ghost_all, pair_total, zbrick, tower_size)
        speed_now = speed_now + 0.5 * time_step * push_now
    return (place_now.reshape(positions.shape), speed_now.reshape(velocities.shape))


def solution(mesh):
    placed = (
        P(None, "gx", "gy", "gz", None),
        P(None, "gx", "gy", "gz", None),
        P(None, "gx", "gy", "gz", None),
        P("gx", "gy", "gz"),
        P(None, "gx", "gy", "gz", None),
        P("gx", "gy", "gz"),
        P(None, None, "gx", "gy", "gz", None),
    )
    return jax.shard_map(
        per_device,
        mesh=mesh,
        in_specs=placed,
        out_specs=(P(None, "gx", "gy", "gz", None), P(None, "gx", "gy", "gz", None)),
        check_vma=False,
    )
```

profile of v0, /device:TPU:1, one launch (start us, length us, event | category | flops | bytes accessed | tf_op | source)
XLA Modules:
  0.0 345.9 jit_solution(15035875307815251270)
XLA Ops:
  5.1 6.9 %collective-permute-start = (f32[6,1,1,4,128]{4,3,2,1,0:T(4,128)S(1)}, f32[6,1,1,4,128]{4,3,2,1,0:T(4,128)S(1)}, u32[]{:S(2)}, u32[]{:S(2)}) collective-permute-start(f32[6,1,1,4,128]{4,3,2,1,0:T(4,128)S(1)} %copy.251), channel_id=1, source_target_pairs={{64,0},{128,64},{192,128},{256,192},{320,256},{384,320},{448,384},... | collective-permute-start | bytes 36872 | tf_op jit(solution)/shard_map/ppermute | solution.py:25
  14.1 6.8 %collective-permute-start.2 = (f32[6,3,1,4,128]{4,3,2,1,0:T(4,128)S(1)}, f32[6,3,1,4,128]{4,3,2,1,0:T(4,128)S(1)}, u32[]{:S(2)}, u32[]{:S(2)}) collective-permute-start(f32[6,3,1,4,128]{4,3,2,1,0:T(4,128)S(1)} %pad_maximum_fusion.13), channel_id=1, source_target_pairs={{4,0},{8,4},{12,8},{16,12},{20,16},{24,20},{28,24},{32,28},{36,32}... | collective-permute-start | bytes 110600 | tf_op jit(solution)/shard_map/ppermute | solution.py:25
  21.0 1.9 collective-permute-start.3
  29.5 9.5 %all-gather = f32[4,4096]{1,0:T(4,128)S(1)} all-gather(f32[4,1024]{1,0:T(4,128)S(1)} %pad_maximum_fusion.17), channel_id=2, replica_groups=mesh['gx'=8,'gy'=16,'gz'=4] {'gz'}, dimensions={1}, use_global_device_ids=true | all-gather | bytes 81920 | tf_op jit(solution)/shard_map/all_gather | solution.py:103
  39.1 5.3 %collective-permute-start.4 = (f32[4,1,1,4,1024]{4,3,2,1,0:T(4,128)S(1)}, f32[4,1,1,4,1024]{4,3,2,1,0:T(4,128)S(1)}, u32[]{:S(2)}, u32[]{:S(2)}) collective-permute-start(f32[4,1,1,4,1024]{4,3,2,1,0:T(4,128)S(1)} %bitcast.311), channel_id=1, source_target_pairs={{0,64},{64,128},{128,192},{192,256},{256,320},{320,384},{384,448},... | collective-permute-start | bytes 196616 | tf_op jit(solution)/shard_map/ppermute | solution.py:23
  44.4 2.3 collective-permute-start.5
  48.1 1.9 collective-permute-start.6
  50.1 4.6 %collective-permute-start.7 = (f32[4,3,1,4,1024]{4,3,2,1,0:T(4,128)S(1)}, f32[4,3,1,4,1024]{4,3,2,1,0:T(4,128)S(1)}, u32[]{:S(2)}, u32[]{:S(2)}) collective-permute-start(f32[4,3,1,4,1024]{4,3,2,1,0:T(4,128)S(1)} %pad_maximum_fusion.9), channel_id=1, source_target_pairs={{4,0},{8,4},{12,8},{16,12},{20,16},{24,20},{28,24},{32,28},{36,32}... | collective-permute-start | bytes 589832 | tf_op jit(solution)/shard_map/ppermute | solution.py:25
  55.7 1.5 collective-permute-done.7
  58.6 36.8 %while.56 = (s32[]{:T(128)}, f32[8,128]{1,0:T(8,128)S(1)}, s32[]{:T(128)}, s32[128]{0:T(128)S(1)}, s32[128]{0:T(128)S(1)}, /*index=5*/s32[]{:T(128)}, f32[4,1024...) while((s32[]{:T(128)}, f32[8,128]{1,0:T(8,128)S(1)}, ...), condition=%wide.wide.region_6.10_spmd, body=%wide.wide.region_4.9_spmd.sunk | while | flops 5475782 | bytes 7996579 | solution.py:135
  95.3 9.0 %all_gather.13 = f32[1,1,1,4,1024]{4,2,1,0,3:T(1,128)S(1)} all-gather(f32[1,1,1,1,1024]{4,2,1,0,3:T(1,128)S(1)} %bitcast.294), channel_id=1, replica_groups=mesh['gx'=8,'gy'=16,'gz'=4] {'gz'}, dimensions={3}, use_global_device_ids=true | all-gather | bytes 20480 | tf_op jit(solution)/shard_map/all_gather | solution.py:103
  104.4 5.1 %collective-permute-start.8 = (f32[1,1,1,4,1024]{4,2,1,0,3:T(1,128)S(1)}, f32[1,1,1,4,1024]{4,2,1,0,3:T(1,128)S(1)}, u32[]{:S(2)}, u32[]{:S(2)}) collective-permute-start(f32[1,1,1,4,1024]{4,2,1,0,3:T(1,128)S(1)} %all_gather.13), channel_id=1, source_target_pairs={{0,64},{64,128},{128,192},{192,256},{256,320},{320,384},{384,448},... | collective-permute-start | bytes 49160 | tf_op jit(solution)/shard_map/ppermute | solution.py:23
  110.3 2.3 collective-permute-done.9
  112.6 1.9 collective-permute-start.10
  114.5 4.6 %collective-permute-start.11 = (f32[1,3,1,4,1024]{4,2,1,0,3:T(1,128)S(1)}, f32[1,3,1,4,1024]{4,2,1,0,3:T(1,128)S(1)}, u32[]{:S(2)}, u32[]{:S(2)}) collective-permute-start(f32[1,3,1,4,1024]{4,2,1,0,3:T(1,128)S(1)} %constant_dynamic-update-slice_fusion), channel_id=1, source_target_pairs={{4,0},{8,4},{12,8},{16,12},{20,16},{24,20},{28,24},{32,28},{36,32}... | collective-permute-start | bytes 147464 | tf_op jit(solution)/shard_map/ppermute | solution.py:25
  120.8 56.1 %while.57 = (s32[]{:T(128)}, f32[3,8,128]{2,1,0:T(8,128)S(1)}, s32[]{:T(128)}, s32[128]{0:T(128)S(1)}, s32[128]{0:T(128)S(1)}, /*index=5*/s32[]{:T(128)}, f32[4,...) while((s32[]{:T(128)}, f32[3,8,128]{2,1,0:T(8,128)S(1)}, ...), condition=%wide.wide.region_9.15_spmd, body=%wide.wide.region_7.14_spmd.sunk | while | flops 9545158 | bytes 23332236 | solution.py:149
  181.5 1.8 collective-permute-start.13
  184.7 1.9 collective-permute-start.15
  186.6 4.6 %collective-permute-start.14 = (f32[6,3,1,4,128]{4,3,2,1,0:T(4,128)S(1)}, f32[6,3,1,4,128]{4,3,2,1,0:T(4,128)S(1)}, u32[]{:S(2)}, u32[]{:S(2)}) collective-permute-start(f32[6,3,1,4,128]{4,3,2,1,0:T(4,128)S(1)} %pad_maximum_fusion.14), channel_id=1, source_target_pairs={{4,0},{8,4},{12,8},{16,12},{20,16},{24,20},{28,24},{32,28},{36,32}... | collective-permute-start | bytes 110600 | tf_op jit(solution)/shard_map/ppermute | solution.py:25
  196.6 9.2 %all-gather.1 = f32[4,4096]{1,0:T(4,128)S(1)} all-gather(f32[4,1024]{1,0:T(4,128)S(1)} %pad_maximum_fusion.16), channel_id=3, replica_groups=mesh['gx'=8,'gy'=16,'gz'=4] {'gz'}, dimensions={1}, use_global_device_ids=true | all-gather | bytes 81920 | tf_op jit(solution)/shard_map/all_gather | solution.py:103
  205.9 4.9 %collective-permute-start.16 = (f32[4,1,1,4,1024]{4,3,2,1,0:T(4,128)S(1)}, f32[4,1,1,4,1024]{4,3,2,1,0:T(4,128)S(1)}, u32[]{:S(2)}, u32[]{:S(2)}) collective-permute-start(f32[4,1,1,4,1024]{4,3,2,1,0:T(4,128)S(1)} %bitcast.316), channel_id=1, source_target_pairs={{0,64},{64,128},{128,192},{192,256},{256,320},{320,384},{384,448},... | collective-permute-start | bytes 196616 | tf_op jit(solution)/shard_map/ppermute | solution.py:23
  210.8 1.8 collective-permute-start.17
  214.6 1.9 collective-permute-start.18
  216.5 4.6 %collective-permute-start.19 = (f32[4,3,1,4,1024]{4,3,2,1,0:T(4,128)S(1)}, f32[4,3,1,4,1024]{4,3,2,1,0:T(4,128)S(1)}, u32[]{:S(2)}, u32[]{:S(2)}) collective-permute-start(f32[4,3,1,4,1024]{4,3,2,1,0:T(4,128)S(1)} %pad_maximum_fusion.11), channel_id=1, source_target_pairs={{4,0},{8,4},{12,8},{16,12},{20,16},{24,20},{28,24},{32,28},{36,32}... | collective-permute-start | bytes 589832 | tf_op jit(solution)/shard_map/ppermute | solution.py:25
  222.2 1.5 collective-permute-done.19
  225.0 36.8 %while.58 = (s32[]{:T(128)}, f32[8,128]{1,0:T(8,128)S(1)}, s32[]{:T(128)}, s32[128]{0:T(128)S(1)}, s32[128]{0:T(128)S(1)}, /*index=5*/s32[]{:T(128)}, f32[4,1024...) while((s32[]{:T(128)}, f32[8,128]{1,0:T(8,128)S(1)}, ...), condition=%wide.wide.region_16.22_spmd, body=%wide.wide.region_14.21_spmd.sunk | while | flops 5475782 | bytes 7996579 | solution.py:135
  261.8 9.0 %all_gather.15 = f32[1,1,1,4,1024]{4,2,1,0,3:T(1,128)S(1)} all-gather(f32[1,1,1,1,1024]{4,2,1,0,3:T(1,128)S(1)} %bitcast.293), channel_id=1, replica_groups=mesh['gx'=8,'gy'=16,'gz'=4] {'gz'}, dimensions={3}, use_global_device_ids=true | all-gather | bytes 20480 | tf_op jit(solution)/shard_map/all_gather | solution.py:103
  270.8 4.6 %collective-permute-start.20 = (f32[1,1,1,4,1024]{4,2,1,0,3:T(1,128)S(1)}, f32[1,1,1,4,1024]{4,2,1,0,3:T(1,128)S(1)}, u32[]{:S(2)}, u32[]{:S(2)}) collective-permute-start(f32[1,1,1,4,1024]{4,2,1,0,3:T(1,128)S(1)} %all_gather.15), channel_id=1, source_target_pairs={{0,64},{64,128},{128,192},{192,256},{256,320},{320,384},{384,448},... | collective-permute-start | bytes 49160 | tf_op jit(solution)/shard_map/ppermute | solution.py:23
  276.3 2.3 collective-permute-done.21
  278.6 1.9 collective-permute-start.22
  280.5 4.6 %collective-permute-start.23 = (f32[1,3,1,4,1024]{4,2,1,0,3:T(1,128)S(1)}, f32[1,3,1,4,1024]{4,2,1,0,3:T(1,128)S(1)}, u32[]{:S(2)}, u32[]{:S(2)}) collective-permute-start(f32[1,3,1,4,1024]{4,2,1,0,3:T(1,128)S(1)} %constant_dynamic-update-slice_fusion.3), channel_id=1, source_target_pairs={{4,0},{8,4},{12,8},{16,12},{20,16},{24,20},{28,24},{32,28},{36,32}... | collective-permute-start | bytes 147464 | tf_op jit(solution)/shard_map/ppermute | solution.py:25
  286.7 56.0 %while.59 = (s32[]{:T(128)}, f32[3,8,128]{2,1,0:T(8,128)S(1)}, s32[]{:T(128)}, s32[128]{0:T(128)S(1)}, s32[128]{0:T(128)S(1)}, /*index=5*/s32[]{:T(128)}, f32[4,...) while((s32[]{:T(128)}, f32[3,8,128]{2,1,0:T(8,128)S(1)}, ...), condition=%wide.wide.region_19.25_spmd, body=%wide.wide.region_17.24_spmd.sunk | while | flops 9545158 | bytes 23332236 | solution.py:149
  (896 shorter events, 221.4 us)
Async XLA Ops:
  0.6 54.0 %copy-start.9 = (s32[2,1,1,1,128]{4,3,2,1,0:T(1,128)S(1)}, s32[2,1,1,1,128]{4,3,2,1,0:T(1,128)}, u32[]{:S(2)}) copy-start(s32[2,1,1,1,128]{4,3,2,1,0:T(1,128)} %param.45) | copy-start | bytes 3076
  5.1 9.0 %collective-permute-start = (f32[6,1,1,4,128]{4,3,2,1,0:T(4,128)S(1)}, f32[6,1,1,4,128]{4,3,2,1,0:T(4,128)S(1)}, u32[]{:S(2)}, u32[]{:S(2)}) collective-permute-start(f32[6,1,1,4,128]{4,3,2,1,0:T(4,128)S(1)} %copy.251), channel_id=1, source_target_pairs={{64,0},{128,64},{192,128},{256,192},{320,256},{384,320},{448,384},... | collective-permute-start | bytes 36872 | tf_op jit(solution)/shard_map/ppermute | solution.py:25
  12.0 2.1 collective-permute-start.1
  14.1 11.4 %collective-permute-start.2 = (f32[6,3,1,4,128]{4,3,2,1,0:T(4,128)S(1)}, f32[6,3,1,4,128]{4,3,2,1,0:T(4,128)S(1)}, u32[]{:S(2)}, u32[]{:S(2)}) collective-permute-start(f32[6,3,1,4,128]{4,3,2,1,0:T(4,128)S(1)} %pad_maximum_fusion.13), channel_id=1, source_target_pairs={{4,0},{8,4},{12,8},{16,12},{20,16},{24,20},{28,24},{32,28},{36,32}... | collective-permute-start | bytes 110600 | tf_op jit(solution)/shard_map/ppermute | solution.py:25
  21.0 5.9 %collective-permute-start.3 = (f32[6,3,1,4,128]{4,3,2,1,0:T(4,128)S(1)}, f32[6,3,1,4,128]{4,3,2,1,0:T(4,128)S(1)}, u32[]{:S(2)}, u32[]{:S(2)}) collective-permute-start(f32[6,3,1,4,128]{4,3,2,1,0:T(4,128)S(1)} %pad_maximum_fusion.13), channel_id=1, source_target_pairs={{0,4},{4,8},{8,12},{12,16},{16,20},{20,24},{24,28},{28,32},{32,36}... | collective-permute-start | bytes 110600 | tf_op jit(solution)/shard_map/ppermute | solution.py:23
  29.3 28.3 %copy-start.4 = (f32[6,1024]{0,1:T(8,128)}, f32[6,1024]{0,1:T(8,128)S(1)}, u32[]{:S(2)}) copy-start(f32[6,1024]{0,1:T(8,128)S(1)} %scatter_fusion.3) | copy-start | bytes 73732
  39.1 8.4 %collective-permute-start.4 = (f32[4,1,1,4,1024]{4,3,2,1,0:T(4,128)S(1)}, f32[4,1,1,4,1024]{4,3,2,1,0:T(4,128)S(1)}, u32[]{:S(2)}, u32[]{:S(2)}) collective-permute-start(f32[4,1,1,4,1024]{4,3,2,1,0:T(4,128)S(1)} %bitcast.311), channel_id=1, source_target_pairs={{0,64},{64,128},{128,192},{192,256},{256,320},{320,384},{384,448},... | collective-permute-start | bytes 196616 | tf_op jit(solution)/shard_map/ppermute | solution.py:23
  44.4 3.7 %collective-permute-start.5 = (f32[4,1,1,4,1024]{4,3,2,1,0:T(4,128)S(1)}, f32[4,1,1,4,1024]{4,3,2,1,0:T(4,128)S(1)}, u32[]{:S(2)}, u32[]{:S(2)}) collective-permute-start(f32[4,1,1,4,1024]{4,3,2,1,0:T(4,128)S(1)} %bitcast.312), channel_id=1, source_target_pairs={{64,0},{128,64},{192,128},{256,192},{320,256},{384,320},{448,384},... | collective-permute-start | bytes 196616 | tf_op jit(solution)/shard_map/ppermute | solution.py:25
  48.1 7.6 %collective-permute-start.6 = (f32[4,3,1,4,1024]{4,3,2,1,0:T(4,128)S(1)}, f32[4,3,1,4,1024]{4,3,2,1,0:T(4,128)S(1)}, u32[]{:S(2)}, u32[]{:S(2)}) collective-permute-start(f32[4,3,1,4,1024]{4,3,2,1,0:T(4,128)S(1)} %pad_maximum_fusion.9), channel_id=1, source_target_pairs={{0,4},{4,8},{8,12},{12,16},{16,20},{20,24},{24,28},{28,32},{32,36}... | collective-permute-start | bytes 589832 | tf_op jit(solution)/shard_map/ppermute | solution.py:23
  50.1 7.2 %collective-permute-start.7 = (f32[4,3,1,4,1024]{4,3,2,1,0:T(4,128)S(1)}, f32[4,3,1,4,1024]{4,3,2,1,0:T(4,128)S(1)}, u32[]{:S(2)}, u32[]{:S(2)}) collective-permute-start(f32[4,3,1,4,1024]{4,3,2,1,0:T(4,128)S(1)} %pad_maximum_fusion.9), channel_id=1, source_target_pairs={{4,0},{8,4},{12,8},{16,12},{20,16},{24,20},{28,24},{32,28},{36,32}... | collective-permute-start | bytes 589832 | tf_op jit(solution)/shard_map/ppermute | solution.py:25
  104.4 5.9 %collective-permute-start.8 = (f32[1,1,1,4,1024]{4,2,1,0,3:T(1,128)S(1)}, f32[1,1,1,4,1024]{4,2,1,0,3:T(1,128)S(1)}, u32[]{:S(2)}, u32[]{:S(2)}) collective-permute-start(f32[1,1,1,4,1024]{4,2,1,0,3:T(1,128)S(1)} %all_gather.13), channel_id=1, source_target_pairs={{0,64},{64,128},{128,192},{192,256},{256,320},{320,384},{384,448},... | collective-permute-start | bytes 49160 | tf_op jit(solution)/shard_map/ppermute | solution.py:23
  109.4 3.2 collective-permute-start.9
  112.6 7.8 %collective-permute-start.10 = (f32[1,3,1,4,1024]{4,2,1,0,3:T(1,128)S(1)}, f32[1,3,1,4,1024]{4,2,1,0,3:T(1,128)S(1)}, u32[]{:S(2)}, u32[]{:S(2)}) collective-permute-start(f32[1,3,1,4,1024]{4,2,1,0,3:T(1,128)S(1)} %constant_dynamic-update-slice_fusion), channel_id=1, source_target_pairs={{0,4},{4,8},{8,12},{12,16},{16,20},{20,24},{24,28},{28,32},{32,36}... | collective-permute-start | bytes 147464 | tf_op jit(solution)/shard_map/ppermute | solution.py:23
  114.5 6.0 %collective-permute-start.11 = (f32[1,3,1,4,1024]{4,2,1,0,3:T(1,128)S(1)}, f32[1,3,1,4,1024]{4,2,1,0,3:T(1,128)S(1)}, u32[]{:S(2)}, u32[]{:S(2)}) collective-permute-start(f32[1,3,1,4,1024]{4,2,1,0,3:T(1,128)S(1)} %constant_dynamic-update-slice_fusion), channel_id=1, source_target_pairs={{4,0},{8,4},{12,8},{16,12},{20,16},{24,20},{28,24},{32,28},{36,32}... | collective-permute-start | bytes 147464 | tf_op jit(solution)/shard_map/ppermute | solution.py:25
  120.8 2.6 copy-start.2
  148.9 2.5 copy-start.2
  176.9 2.6 copy-start.5
  181.5 3.1 collective-permute-start.12
  181.5 3.1 collective-permute-start.13
  184.7 9.1 %collective-permute-start.15 = (f32[6,3,1,4,128]{4,3,2,1,0:T(4,128)S(1)}, f32[6,3,1,4,128]{4,3,2,1,0:T(4,128)S(1)}, u32[]{:S(2)}, u32[]{:S(2)}) collective-permute-start(f32[6,3,1,4,128]{4,3,2,1,0:T(4,128)S(1)} %pad_maximum_fusion.14), channel_id=1, source_target_pairs={{0,4},{4,8},{8,12},{12,16},{16,20},{20,24},{24,28},{28,32},{32,36}... | collective-permute-start | bytes 110600 | tf_op jit(solution)/shard_map/ppermute | solution.py:23
  186.6 7.3 %collective-permute-start.14 = (f32[6,3,1,4,128]{4,3,2,1,0:T(4,128)S(1)}, f32[6,3,1,4,128]{4,3,2,1,0:T(4,128)S(1)}, u32[]{:S(2)}, u32[]{:S(2)}) collective-permute-start(f32[6,3,1,4,128]{4,3,2,1,0:T(4,128)S(1)} %pad_maximum_fusion.14), channel_id=1, source_target_pairs={{4,0},{8,4},{12,8},{16,12},{20,16},{24,20},{28,24},{32,28},{36,32}... | collective-permute-start | bytes 110600 | tf_op jit(solution)/shard_map/ppermute | solution.py:25
  196.3 27.6 %copy-start.6 = (f32[6,1024]{0,1:T(8,128)}, f32[6,1024]{0,1:T(8,128)S(1)}, u32[]{:S(2)}) copy-start(f32[6,1024]{0,1:T(8,128)S(1)} %scatter_fusion.7) | copy-start | bytes 73732
  205.9 7.4 %collective-permute-start.16 = (f32[4,1,1,4,1024]{4,3,2,1,0:T(4,128)S(1)}, f32[4,1,1,4,1024]{4,3,2,1,0:T(4,128)S(1)}, u32[]{:S(2)}, u32[]{:S(2)}) collective-permute-start(f32[4,1,1,4,1024]{4,3,2,1,0:T(4,128)S(1)} %bitcast.316), channel_id=1, source_target_pairs={{0,64},{64,128},{128,192},{192,256},{256,320},{320,384},{384,448},... | collective-permute-start | bytes 196616 | tf_op jit(solution)/shard_map/ppermute | solution.py:23
  210.8 3.7 %collective-permute-start.17 = (f32[4,1,1,4,1024]{4,3,2,1,0:T(4,128)S(1)}, f32[4,1,1,4,1024]{4,3,2,1,0:T(4,128)S(1)}, u32[]{:S(2)}, u32[]{:S(2)}) collective-permute-start(f32[4,1,1,4,1024]{4,3,2,1,0:T(4,128)S(1)} %bitcast.317), channel_id=1, source_target_pairs={{64,0},{128,64},{192,128},{256,192},{320,256},{384,320},{448,384},... | collective-permute-start | bytes 196616 | tf_op jit(solution)/shard_map/ppermute | solution.py:25
  214.6 7.6 %collective-permute-start.18 = (f32[4,3,1,4,1024]{4,3,2,1,0:T(4,128)S(1)}, f32[4,3,1,4,1024]{4,3,2,1,0:T(4,128)S(1)}, u32[]{:S(2)}, u32[]{:S(2)}) collective-permute-start(f32[4,3,1,4,1024]{4,3,2,1,0:T(4,128)S(1)} %pad_maximum_fusion.11), channel_id=1, source_target_pairs={{0,4},{4,8},{8,12},{12,16},{16,20},{20,24},{24,28},{28,32},{32,36}... | collective-permute-start | bytes 589832 | tf_op jit(solution)/shard_map/ppermute | solution.py:23
  216.5 7.2 %collective-permute-start.19 = (f32[4,3,1,4,1024]{4,3,2,1,0:T(4,128)S(1)}, f32[4,3,1,4,1024]{4,3,2,1,0:T(4,128)S(1)}, u32[]{:S(2)}, u32[]{:S(2)}) collective-permute-start(f32[4,3,1,4,1024]{4,3,2,1,0:T(4,128)S(1)} %pad_maximum_fusion.11), channel_id=1, source_target_pairs={{4,0},{8,4},{12,8},{16,12},{20,16},{24,20},{28,24},{32,28},{36,32}... | collective-permute-start | bytes 589832 | tf_op jit(solution)/shard_map/ppermute | solution.py:25
  270.8 5.4 %collective-permute-start.20 = (f32[1,1,1,4,1024]{4,2,1,0,3:T(1,128)S(1)}, f32[1,1,1,4,1024]{4,2,1,0,3:T(1,128)S(1)}, u32[]{:S(2)}, u32[]{:S(2)}) collective-permute-start(f32[1,1,1,4,1024]{4,2,1,0,3:T(1,128)S(1)} %all_gather.15), channel_id=1, source_target_pairs={{0,64},{64,128},{128,192},{192,256},{256,320},{320,384},{384,448},... | collective-permute-start | bytes 49160 | tf_op jit(solution)/shard_map/ppermute | solution.py:23
  275.4 3.2 collective-permute-start.21
  278.6 7.8 %collective-permute-start.22 = (f32[1,3,1,4,1024]{4,2,1,0,3:T(1,128)S(1)}, f32[1,3,1,4,1024]{4,2,1,0,3:T(1,128)S(1)}, u32[]{:S(2)}, u32[]{:S(2)}) collective-permute-start(f32[1,3,1,4,1024]{4,2,1,0,3:T(1,128)S(1)} %constant_dynamic-update-slice_fusion.3), channel_id=1, source_target_pairs={{0,4},{4,8},{8,12},{12,16},{16,20},{20,24},{24,28},{28,32},{32,36}... | collective-permute-start | bytes 147464 | tf_op jit(solution)/shard_map/ppermute | solution.py:23
  280.5 5.9 %collective-permute-start.23 = (f32[1,3,1,4,1024]{4,2,1,0,3:T(1,128)S(1)}, f32[1,3,1,4,1024]{4,2,1,0,3:T(1,128)S(1)}, u32[]{:S(2)}, u32[]{:S(2)}) collective-permute-start(f32[1,3,1,4,1024]{4,2,1,0,3:T(1,128)S(1)} %constant_dynamic-update-slice_fusion.3), channel_id=1, source_target_pairs={{4,0},{8,4},{12,8},{16,12},{20,16},{24,20},{28,24},{32,28},{36,32}... | collective-permute-start | bytes 147464 | tf_op jit(solution)/shard_map/ppermute | solution.py:25
  286.7 2.6 copy-start
  314.8 2.5 copy-start
  (30 other events, 49.0 us)
where the time goes:
time: 351 us; the launch traced here: 346 us
  other arithmetic  113 us (32%)
  local copies, waits for them, and re-layouts  92.8 us (26%)
  starting transfers between devices  73.8 us (21%)
  blocking collectives  36.8 us (10%)
  waiting for transfers between devices  17.3 us (5%)
  matrix products  6.21 us (2%)
  loops' own time  3.57 us (1%)
    ppermute x12, starting transfers between devices, padded(): lax.ppermute(head, axis, [((i + 1) % count, i) for i in range(count)])  40.7 us
    all_gather x4, blocking collectives, spread(): tower_cells = lax.all_gather(values_in, 'gz', axis=3, tiled=True)  36.8 us
    ppermute x12, starting transfers between devices, padded(): lax.ppermute(tail, axis, [(i, (i + 1) % count) for i in range(count)])  33.1 us
    sub x32, other arithmetic, geometry(): raw_offset = near_tiles[:3, :, :, None] - far_tiles[:3, :, None, :]  28 us
    eq x32, other arithmetic, geometry(): ghost_tile == local_tile + selfbase  23.4 us
    gather x32, local copies, waits for them, and re-layouts, geometry(): far_tiles = jnp.take(ghost_rows.reshape(4, -1, 128), ghost_tile, axis=1)  18.8 us
    gather x32, local copies, waits for them, and re-layouts, geometry(): near_tiles = jnp.take(own_rows.reshape(4, -1, 128), local_tile, axis=1)  18.8 us
    mul x16, other arithmetic, force_rows(): return -jnp.sum(coefficient[None] * offset_vec, axis=3)  16.2 us
  transfers between devices with their start and end apart: 24, of which 15 were waited for; matrix products, arithmetic and copies ran while one was open for 3% of the time, Pallas kernels for 0%

commit v1 on v0

v1 whole, which is shorter than its diff:
```python
import functools

import jax
import jax.numpy as jnp
from jax import lax
from jax.experimental import pallas as pl
from jax.experimental.pallas import tpu as pltpu
from jax.sharding import PartitionSpec as P

cutoff_sq = 0.81
cutoff = 0.9
height_ratio = 0.25
density_scale = 1.0 / 256.0
repulsion = 1.0 / 512.0
time_step = 0.25
kick = 0.5 * time_step
flat_scale = 1.0 / cutoff
tall_scale = height_ratio / cutoff
cube_factor = -8.0 * repulsion / cutoff_sq
slope_factor = -6.0 * density_scale / cutoff_sq
far_away = 1e15

VMEM = pl.BlockSpec(memory_space=pltpu.VMEM)
ANY = pl.BlockSpec(memory_space=pl.ANY)
SMEM = pl.BlockSpec(memory_space=pltpu.SMEM)
params = pltpu.CompilerParams(vmem_limit_bytes=24 * 1024 * 1024)
unrolled = 4
nt_dims = (((1,), (1,)), ((), ()))
nn_dims = (((1,), (0,)), ((), ()))


def dot(left, right, dims):
    return lax.dot_general(left, right, dims, preferred_element_type=jnp.float32)


def pieces(values, count):
    out = []
    for _ in range(count):
        part = values.astype(jnp.bfloat16)
        out.append(part)
        values = values - part.astype(jnp.float32)
    return out


def slot_masks(slots_ref, direction):
    slots = slots_ref[direction : direction + 1, :]
    lane_hit = lax.broadcasted_iota(jnp.int32, (128, 128), 0) == (slots & 127)
    tile_hit = lax.broadcasted_iota(jnp.int32, (8, 128), 0) == (slots >> 7)
    return jnp.where(lane_hit, 1.0, 0.0).astype(jnp.bfloat16), tile_hit


def drift_and_pack(place, speed, push, slots_ref, place_ref, speed_ref, packed_refs):
    speed = [speed[c] + kick * push[c] for c in range(3)]
    rates = (time_step, time_step, time_step / height_ratio)
    place = [place[c] + rates[c] * speed[c] for c in range(3)]
    for c in range(3):
        place_ref[c] = place[c]
        speed_ref[c] = speed[c]
    rows = jnp.concatenate(place + speed, axis=0)
    split = jnp.concatenate(pieces(rows, 3), axis=0)
    for direction in range(4):
        lane_hit, tile_hit = slot_masks(slots_ref, direction)
        found = dot(split, lane_hit, nn_dims)
        found = found[0:48] + found[48:96] + found[96:144]
        for c in range(6):
            chosen = jnp.where(tile_hit, found[8 * c : 8 * c + 8], 0.0)
            packed_refs[direction][c : c + 1, :] = jnp.sum(chosen, axis=0, keepdims=True)
        packed_refs[direction][6:8, :] = jnp.zeros((2, 128), jnp.float32)


def pack_kernel(
    place_in,
    speed_in,
    push_in,
    slots_in,
    place_ref,
    speed_ref,
    p0,
    p1,
    p2,
    p3,
    slots_out,
    place_at,
    speed_at,
    push_at,
    sems,
):
    pairs = (
        (place_in, place_at),
        (speed_in, speed_at),
        (push_in, push_at),
        (slots_in, slots_out),
    )
    copies = [
        pltpu.make_async_copy(here, there, sems.at[i]) for i, (here, there) in enumerate(pairs)
    ]
    for copy in copies:
        copy.start()
    for copy in copies:
        copy.wait()
    drift_and_pack(
        [place_at[c] for c in range(3)],
        [speed_at[c] for c in range(3)],
        [push_at[c] for c in range(3)],
        slots_out.at[0],
        place_ref,
        speed_ref,
        (p0, p1, p2, p3),
    )


def unpack_kernel(
    step, count_ref, place_in, speed_in, slots_in, a0, a1, a2, a3, place_ref, speed_ref, sent_ref
):
    slots_ref = slots_in.at[step]
    total = jnp.zeros((160, 128), jnp.float32)
    plan = ((a0, 0, 1.0), (a1, 0, -1.0), (a2, 1, 1.0), (a3, 1, -1.0))
    for direction, (arrived, component, shift) in enumerate(plan):
        lane_hit, tile_hit = slot_masks(slots_ref, direction)
        rows = []
        for c in range(6):
            row = arrived[c : c + 1, :]
            if c == component:
                row = row + shift
            rows.append(jnp.where(tile_hit, row, 0.0))
        marks = jnp.where(tile_hit, 1.0, 0.0)
        split = pieces(jnp.concatenate(rows, axis=0), 3)
        split.append(jnp.concatenate([marks, jnp.zeros_like(marks)], axis=0).astype(jnp.bfloat16))
        total = total + dot(jnp.concatenate(split, axis=0), lane_hit, nt_dims)
    put = total[0:48] + total[48:96] + total[96:144]
    taken = total[144:152] > 0.5
    slot_ids = lax.broadcasted_iota(jnp.int32, (8, 128), 0) * 128 + lax.broadcasted_iota(
        jnp.int32, (8, 128), 1
    )
    live = slot_ids < count_ref[0]
    scales = (flat_scale, flat_scale, tall_scale)
    for c in range(3):
        place = jnp.where(taken, put[8 * c : 8 * c + 8], place_in[c])
        place_ref[c] = place
        speed_ref[c] = jnp.where(taken, put[24 + 8 * c : 32 + 8 * c], speed_in[c])
        sent_ref[c] = jnp.where(live, place * scales[c], far_away)


def put_ghosts(cells, ghost_ref):
    zbrick = lax.axis_index("gz")
    for level in range(4):
        rise = ((level - zbrick).astype(jnp.float32) - 0.5) * tall_scale
        for dx, cell in enumerate(cells):
            for dy in range(3):
                brick = dx * 12 + dy * 4 + level
                ghost_ref[brick, 0] = cell[level, dy, 0] + (dx - 1.5) * flat_scale
                ghost_ref[brick, 1] = cell[level, dy, 1] + (dy - 1.5) * flat_scale
                ghost_ref[brick, 2] = cell[level, dy, 2] + rise
    ghost_ref[36] = jnp.full(ghost_ref.shape[1:], far_away, jnp.float32)


def own_places(middle):
    zbrick = lax.axis_index("gz")
    own = [middle[zbrick, 1, c] for c in range(3)]
    live = own[0] < 0.5 * far_away
    shifts = (0.5 * flat_scale, 0.5 * flat_scale, 0.5 * tall_scale)
    return [jnp.where(live, row - shift, -far_away) for row, shift in zip(own, shifts)], live


def eight(row):
    return jnp.broadcast_to(row, (8, 128))


def in_three(values):
    first = values.astype(jnp.bfloat16).astype(jnp.float32)
    values = values - first
    second = values.astype(jnp.bfloat16).astype(jnp.float32)
    third = (values - second).astype(jnp.bfloat16).astype(jnp.float32)
    return first, second, third


def sublanes():
    return lax.broadcasted_iota(jnp.int32, (8, 128), 0)


def by_rows(at, rows):
    out = jnp.zeros((8, 128), jnp.float32)
    for i, row in enumerate(rows):
        if row is not None:
            out = jnp.where(at == i, row, out)
    return out


def near_factors(places, slopes):
    at = sublanes()
    x, y, z = (eight(row) for row in places)
    rest = 0.5 - (x * x + y * y + z * z)
    at_flat = jnp.where(at >= 4, at - 4, at)
    mixed = jnp.where(at_flat == 0, x, jnp.where(at_flat == 1, y, z))
    first, second, third = in_three(mixed)
    ends = in_three(rest)
    blocks = []
    for later, end in zip((second, second, third), ends):
        block = 2.0 * jnp.where(at < 4, first, later)
        block = jnp.where(at == 3, 1.0, jnp.where(at == 7, end, block))
        blocks.append(block)
    none = jnp.zeros((8, 128), jnp.float32)
    plain = jnp.concatenate(blocks + [none], axis=0).T
    if slopes is None:
        return plain.astype(jnp.bfloat16)
    one, two, three = in_three(eight(slopes))
    sloped = by_rows(at, (one, two, three, 1.0, 1.0, 1.0))
    sloped = jnp.concatenate(blocks + [sloped], axis=0).T
    return jnp.concatenate([plain, sloped], axis=0).astype(jnp.bfloat16)


def far_factors(places, slopes):
    at = sublanes()
    x, y, z = (eight(row) for row in places)
    rest = 0.5 - (x * x + y * y + z * z)
    at_flat = jnp.where(at >= 4, at - 4, at)
    mixed = jnp.where(at_flat == 0, x, jnp.where(at_flat == 1, y, jnp.where(at == 3, rest, z)))
    first, second, third = in_three(mixed)
    last = at == 7
    blocks = [
        jnp.where(last, 1.0, first),
        jnp.where(last, 1.0, second),
        jnp.where(last, 1.0, jnp.where(at < 4, third, first)),
    ]
    if slopes is None:
        blocks.append(jnp.zeros((8, 128), jnp.float32))
    else:
        one, two, three = in_three(eight(slopes))
        blocks.append(by_rows(at, (1.0, 1.0, 1.0, one, two, three)))
    summed = jnp.where(at == 3, 1.0, jnp.where(at < 4, first, second))
    summed = jnp.concatenate([summed, third], axis=0).astype(jnp.bfloat16)
    return jnp.concatenate(blocks, axis=0).astype(jnp.bfloat16), summed


def entry(tiles_ref, number, total):
    listed = number < total
    near = jnp.where(listed, tiles_ref[0, number], 0)
    far = tiles_ref[1, number]
    return near, far, jnp.where(listed, far >> 3, 36), far & 7, listed


def halves(block):
    first = block.astype(jnp.bfloat16)
    second = (block - first.astype(jnp.float32)).astype(jnp.bfloat16)
    return jnp.concatenate([first, second], axis=1)


def density_kernel(
    total_ref,
    tiles_in,
    behind,
    middle,
    ahead,
    slope_ref,
    tiles_ref,
    ghost_ref,
    near_ref,
    sum_ref,
    row_ref,
    sem,
):
    copy = pltpu.make_async_copy(tiles_in, tiles_ref, sem)
    copy.start()
    zbrick = lax.axis_index("gz")
    put_ghosts((behind, middle, ahead), ghost_ref)
    own, live = own_places(middle)
    for t in range(8):
        near_ref[t] = near_factors([row[t : t + 1] for row in own], None)
    sum_ref[...] = jnp.zeros_like(sum_ref)
    tile_ids = sublanes()
    total = total_ref[0]
    copy.wait()

    def add(group, selves):
        for part in range(unrolled):
            near, far, brick, tile, listed = entry(tiles_ref, group * unrolled + part, total)
            places = [ghost_ref[brick, c, pl.ds(tile, 1), :] for c in range(3)]
            factors, _ = far_factors(places, None)
            shrink = jnp.maximum(dot(near_ref[near], factors, nn_dims), 0.0)
            sum_ref[near] += shrink * shrink * shrink
            same = jnp.logical_and(listed, far == (16 + zbrick) * 8 + near)
            selves = selves + jnp.where(tile_ids == jnp.where(same, near, -1), 1.0, 0.0)
        return selves

    selves = lax.fori_loop(
        0, (total + unrolled - 1) // unrolled, add, jnp.zeros((8, 128), jnp.float32)
    )
    ones = jnp.ones((16, 256), jnp.bfloat16)
    for t in range(8):
        row_ref[t : t + 1, :] = dot(ones, halves(sum_ref[t]), nt_dims)[0:1]
    density = (row_ref[...] - jnp.where(live, selves, 0.0)) * density_scale
    slope_ref[...] = (-0.5 * slope_factor / cube_factor) / jnp.sqrt(1.0 + density)


def force_sums(
    total_ref,
    tiles_in,
    cells,
    slope_cells,
    own_slope,
    tiles_ref,
    ghost_ref,
    near_ref,
    sum_ref,
    push_ref,
    sem,
):
    copy = pltpu.make_async_copy(tiles_in, tiles_ref, sem)
    copy.start()
    put_ghosts(cells, ghost_ref)
    for dy, cell in enumerate(slope_cells):
        for dx in range(3):
            for level in range(4):
                ghost_ref[dx * 12 + dy * 4 + level, 3] = cell[dx * 4 + level]
    own, _ = own_places(cells[1])
    for t in range(8):
        near_ref[t] = near_factors([row[t : t + 1] for row in own], own_slope[t : t + 1, :])
    sum_ref[...] = jnp.zeros_like(sum_ref)
    total = total_ref[0]
    copy.wait()

    def add(group, carry):
        for part in range(unrolled):
            near, _, brick, tile, _ = entry(tiles_ref, group * unrolled + part, total)
            places = [ghost_ref[brick, c, pl.ds(tile, 1), :] for c in range(3)]
            factors, summed = far_factors(places, ghost_ref[brick, 3, pl.ds(tile, 1), :])
            both = dot(near_ref[near], factors, nn_dims)
            shrink = jnp.maximum(both[0:128], 0.0)
            weight = shrink * shrink * both[128:256]
            twice = jnp.concatenate([summed, summed], axis=1)
            sum_ref[near] += dot(twice, halves(weight), nt_dims)
        return carry

    lax.fori_loop(0, (total + unrolled - 1) // unrolled, add, 0)
    for c in range(3):
        for t in range(8):
            found = sum_ref[t]
            there = found[c : c + 1] + found[c + 4 : c + 5] + found[c + 8 : c + 9]
            here = own[c][t : t + 1] * found[3:4]
            push_ref[c, t : t + 1, :] = (-cutoff * cube_factor) * (here - there)


def force_pack_kernel(
    step,
    total_ref,
    tiles_in,
    c0,
    c1,
    c2,
    s0,
    s1,
    s2,
    own_slope,
    place_in,
    speed_in,
    slots_ref,
    place_ref,
    speed_ref,
    p0,
    p1,
    p2,
    p3,
    tiles_ref,
    ghost_ref,
    near_ref,
    sum_ref,
    push_ref,
    sem,
):
    force_sums(
        total_ref,
        tiles_in,
        (c0, c1, c2),
        (s0, s1, s2),
        own_slope,
        tiles_ref,
        ghost_ref,
        near_ref,
        sum_ref,
        push_ref,
        sem,
    )
    push = [push_ref[c] for c in range(3)]
    speed = [speed_in[c] + kick * push[c] for c in range(3)]
    drift_and_pack(
        [place_in[c] for c in range(3)],
        speed,
        push,
        slots_ref.at[step],
        place_ref,
        speed_ref,
        (p0, p1, p2, p3),
    )


def force_last_kernel(
    total_ref,
    tiles_in,
    c0,
    c1,
    c2,
    s0,
    s1,
    s2,
    own_slope,
    speed_in,
    speed_ref,
    tiles_ref,
    ghost_ref,
    near_ref,
    sum_ref,
    push_ref,
    sem,
):
    force_sums(
        total_ref,
        tiles_in,
        (c0, c1, c2),
        (s0, s1, s2),
        own_slope,
        tiles_ref,
        ghost_ref,
        near_ref,
        sum_ref,
        push_ref,
        sem,
    )
    for c in range(3):
        speed_ref[c] = speed_in[c] + kick * push_ref[c]


def pick_kernel(plane_ref, column_ref):
    count = lax.axis_size("gx")
    xbrick = lax.axis_index("gx")
    for dx in range(3):
        at = lax.rem(xbrick + (dx - 1 + count), count)
        for level in range(4):
            column_ref[dx * 4 + level] = plane_ref[at * 4 + level]


def shaped(*extent):
    return jax.ShapeDtypeStruct(extent, jnp.float32)


def call(kernel, outs, specs, scratch=()):
    return pl.pallas_call(
        kernel,
        out_shape=outs,
        in_specs=specs,
        out_specs=[VMEM] * len(outs),
        scratch_shapes=list(scratch),
        compiler_params=params,
    )


def moved(values, axis, shift):
    count = lax.axis_size(axis)
    return lax.ppermute(values, axis, [((i + shift) % count, i) for i in range(count)])


def migrants(packed):
    return (
        moved(packed[1], "gx", 1),
        moved(packed[0], "gx", -1),
        moved(packed[3], "gy", 1),
        moved(packed[2], "gy", -1),
    )


def around(values):
    rows = jnp.stack([moved(values, "gy", -1), values, moved(values, "gy", 1)])
    copies = jnp.broadcast_to(rows[None], (4,) + rows.shape)
    tower = lax.all_to_all(copies, "gz", 0, 0, tiled=True)
    return moved(tower, "gx", -1), tower, moved(tower, "gx", 1)


def slopes_around(values):
    count = lax.axis_size("gx") * lax.axis_size("gz")
    copies = jnp.broadcast_to(values[None], (count,) + values.shape)
    plane = lax.all_to_all(copies, ("gx", "gz"), 0, 0, tiled=True)
    (column,) = call(pick_kernel, [shaped(12, 8, 128)], [VMEM])(plane)
    return moved(column, "gy", -1), column, moved(column, "gy", 1)


def per_device(positions, velocities, forces, counts, pair_tiles, pair_count, mig_slots):
    live_count = counts.reshape(1)
    total = pair_count.reshape(1)
    tiles = pair_tiles.reshape(2, 128)
    steps = mig_slots.shape[0]
    slots = mig_slots.reshape(steps, 4, 128)
    atoms = shaped(3, 8, 128)
    block = shaped(8, 128)
    atoms_scratch = pltpu.VMEM((3, 8, 128), jnp.float32)

    def pair_scratch(comps, near_rows, sum_rows, found):
        return (
            pltpu.SMEM((2, 128), jnp.int32),
            pltpu.VMEM((37, comps, 8, 128), jnp.float32),
            pltpu.VMEM((8, near_rows, 32), jnp.bfloat16),
            pltpu.VMEM((8, sum_rows, 128), jnp.float32),
            found,
            pltpu.SemaphoreType.DMA,
        )

    place, speed, *packed, slots = call(
        pack_kernel,
        [atoms, atoms] + [block] * 4 + [jax.ShapeDtypeStruct(slots.shape, jnp.int32)],
        [ANY] * 4,
        (atoms_scratch, atoms_scratch, atoms_scratch, pltpu.SemaphoreType.DMA((4,))),
    )(
        positions.reshape(3, 8, 128),
        velocities.reshape(3, 8, 128),
        forces.reshape(3, 8, 128),
        slots,
    )
    for n in range(steps):
        place, speed, sent = call(
            functools.partial(unpack_kernel, n), [atoms, atoms, atoms], [SMEM] + [VMEM] * 7
        )(live_count, place, speed, slots, *migrants(packed))
        cells = around(sent)
        (slope,) = call(
            density_kernel,
            [block],
            [SMEM, ANY] + [VMEM] * 3,
            pair_scratch(3, 128, 128, pltpu.VMEM((8, 128), jnp.float32)),
        )(total, tiles, *cells)
        slope_cells = slopes_around(slope)
        scratch = pair_scratch(4, 256, 16, atoms_scratch)
        if n + 1 < steps:
            place, speed, *packed = call(
                functools.partial(force_pack_kernel, n + 1),
                [atoms, atoms] + [block] * 4,
                [SMEM, ANY] + [VMEM] * 10,
                scratch,
            )(total, tiles, *cells, *slope_cells, slope, place, speed, slots)
        else:
            (speed,) = call(
                force_last_kernel, [atoms], [SMEM, ANY] + [VMEM] * 8, scratch
            )(total, tiles, *cells, *slope_cells, slope, speed)
    return (place.reshape(positions.shape), speed.reshape(velocities.shape))


def solution(mesh):
    placed = (
        P(None, "gx", "gy", "gz", None),
        P(None, "gx", "gy", "gz", None),
        P(None, "gx", "gy", "gz", None),
        P("gx", "gy", "gz"),
        P(None, "gx", "gy", "gz", None),
        P("gx", "gy", "gz"),
        P(None, None, "gx", "gy", "gz", None),
    )
    return jax.shard_map(
        per_device,
        mesh=mesh,
        in_specs=placed,
        out_specs=(P(None, "gx", "gy", "gz", None), P(None, "gx", "gy", "gz", None)),
        check_vma=False,
    )
```

time: 351 us -> 166 us (0.47)
  the two profiles are of different devices: /device:TPU:1 before, /device:TPU:2 now
where the time goes in v1:
time: 166 us; the launch traced here: 165 us
  starting transfers between devices  44.5 us (27%)
  Pallas kernels  43.8 us (26%)
  blocking collectives  43 us (26%)
  waiting for transfers between devices  27.9 us (17%)
  local copies, waits for them, and re-layouts  3.53 us (2%)
  between operations  2.19 us (1%)
    ppermute x20, starting transfers between devices, moved(): lax.ppermute(values, axis, [((i + shift) % count, i) for i in range(count)])  44.5 us
    ppermute x20, waiting for transfers between devices, moved(): lax.ppermute(values, axis, [((i + shift) % count, i) for i in range(count)])  27.9 us
    all_to_all x2, blocking collectives, slopes_around(): plane = lax.all_to_all(copies, ('gx', 'gz'), 0, 0, tiled=True)  23.5 us
    all_to_all x2, blocking collectives, around(): tower = lax.all_to_all(copies, 'gz', 0, 0, tiled=True)  19.5 us
    pallas_call x1, Pallas kernels, per_device(): call(force_last_kernel, [atoms], [SMEM, ANY] + [VMEM] * 8, scratch)  14.3 us
    pallas_call x2, Pallas kernels, per_device(): call(density_kernel, [block], [SMEM, ANY] + [VMEM] * 3, pair_scratch(3, 1...  14.2 us
    pallas_call x1, Pallas kernels, per_device(): call(functools.partial(force_pack_kernel, n + 1), [atoms, atoms] + [block...  14 us
    unnamed x10, local copies, waits for them, and re-layouts  3.48 us
  transfers between devices with their start and end apart: 20, of which 12 were waited for; matrix products, arithmetic and copies ran while one was open for 0% of the time, Pallas kernels for 0%

profile of v1, /device:TPU:2, one launch (start us, length us, event | category | flops | bytes accessed | tf_op | source)
XLA Modules:
  0.0 165.0 jit_solution(496306394313423364)
XLA Ops:
  1.3 0.7 copy-done.1
  4.3 11.4 %collective-permute-start.2 = (f32[8,128]{1,0:T(8,128)S(1)}, f32[8,128]{1,0:T(8,128)S(1)}, u32[]{:S(2)}, u32[]{:S(2)}) collective-permute-start(f32[8,128]{1,0:T(8,128)S(1)} %get-tuple-element.26), channel_id=1, source_target_pairs={{4,0},{8,4},{12,8},{16,12},{20,16},{24,20},{28,24},{32,28},{36,32}... | collective-permute-start | bytes 12296 | tf_op jit(solution)/shard_map/ppermute | solution.py:458
  15.7 1.9 %collective-permute-start.3 = (f32[8,128]{1,0:T(8,128)S(1)}, f32[8,128]{1,0:T(8,128)S(1)}, u32[]{:S(2)}, u32[]{:S(2)}) collective-permute-start(f32[8,128]{1,0:T(8,128)S(1)} %get-tuple-element.27), channel_id=1, source_target_pairs={{60,0},{0,4},{4,8},{8,12},{12,16},{16,20},{20,24},{24,28},{28,32},... | collective-permute-start | bytes 12296 | tf_op jit(solution)/shard_map/ppermute | solution.py:458
  18.3 4.1 %collective-permute-done.3.a3 = f32[8,128]{1,0:T(8,128)S(1)} collective-permute-done((f32[8,128]{1,0:T(8,128)S(1)}, f32[8,128]{1,0:T(8,128)S(1)}, u32[]{:S(2)}, u32[]{:S(2)}) %collective-permute-start.3) | collective-permute-done | bytes 4128 | tf_op jit(solution)/shard_map/ppermute | solution.py:458
  22.6 1.9 %collective-permute-start.5 = (f32[3,8,128]{2,1,0:T(8,128)S(1)}, f32[3,8,128]{2,1,0:T(8,128)S(1)}, u32[]{:S(2)}, u32[]{:S(2)}) collective-permute-start(f32[3,8,128]{2,1,0:T(8,128)S(1)} %get-tuple-element.28), channel_id=1, source_target_pairs={{4,0},{8,4},{12,8},{16,12},{20,16},{24,20},{28,24},{32,28},{36,32}... | collective-permute-start | bytes 36872 | tf_op jit(solution)/shard_map/ppermute | solution.py:458
  24.5 3.9 %collective-permute-start.4 = (f32[3,8,128]{2,1,0:T(8,128)S(1)}, f32[3,8,128]{2,1,0:T(8,128)S(1)}, u32[]{:S(2)}, u32[]{:S(2)}) collective-permute-start(f32[3,8,128]{2,1,0:T(8,128)S(1)} %get-tuple-element.28), channel_id=1, source_target_pairs={{60,0},{0,4},{4,8},{8,12},{12,16},{16,20},{20,24},{24,28},{28,32},... | collective-permute-start | bytes 36872 | tf_op jit(solution)/shard_map/ppermute | solution.py:458
  28.5 2.9 %collective-permute-done.4 = f32[3,8,128]{2,1,0:T(8,128)S(1)} collective-permute-done((f32[3,8,128]{2,1,0:T(8,128)S(1)}, f32[3,8,128]{2,1,0:T(8,128)S(1)}, u32[]{:S(2)}, u32[]{:S(2)}) %collective-permute-start.4) | collective-permute-done | bytes 12320 | tf_op jit(solution)/shard_map/ppermute | solution.py:458
  31.4 10.3 %all_to_all.20.middle.c1 = f32[4,3,3,8,128]{4,3,2,1,0:T(8,128)S(1)} all-to-all(f32[4,3,3,8,128]{4,3,2,1,0:T(8,128)S(1)} %broadcast_in_dim.8), channel_id=1, replica_groups=mesh['gx'=8,'gy'=16,'gz'=4] {'gz'}, dimensions={0} | all-to-all | bytes 294912 | tf_op jit(solution)/shard_map/all_to_all | solution.py:473
  42.8 1.5 collective-permute-done.7.ahead.c2
  44.4 2.5 %collective-permute-done.6.behind.c0 = f32[4,3,3,8,128]{4,3,2,1,0:T(8,128)S(1)} collective-permute-done((f32[4,3,3,8,128]{4,3,2,1,0:T(8,128)S(1)}, f32[4,3,3,8,128]{4,3,2,1,0:T(8,128)S(1)}, u32[]{:S(2)}, u32[]{:S(2)}) %collective-permute-start.6) | collective-permute-done | bytes 147488 | tf_op jit(solution)/shard_map/ppermute | solution.py:458
  47.5 7.1 %shard_map.88.own_slope = f32[8,128]{1,0:T(8,128)S(1)} custom-call(s32[1]{0:T(128)} %bitcast.17.total_ref, s32[2,128]{1,0:T(2,128)S(1)} %bitcast.21, f32[4,3,3,8,128]{4,3,2,1,0:T(8,128)S(1)} %collective-permute-done.6.behind.c0, f32[4,3,3,8,128]{4,3,2,1,0:T(8,128)S(1)} %all_to_all.20.middle.c1, f32[4,3,3,8,128]{4,3,2,1,0:T(8,128)S(1)} %collective-permute-done.7.ahead.c2), custom_call_target="tpu_custom_call" | custom-call | tf_op jit(solution)/shard_map/pallas_call | solution.py:521
  54.6 12.2 %all_to_all.21.plane_ref = f32[32,8,128]{2,1,0:T(8,128)S(1)} all-to-all(f32[32,8,128]{2,1,0:T(8,128)S(1)} %broadcast_in_dim.9), channel_id=1, replica_groups=mesh['gx'=8,'gy'=16,'gz'=4] {'gx','gz'}, dimensions={0} | all-to-all | bytes 262144 | tf_op jit(solution)/shard_map/all_to_all | solution.py:480
  66.8 1.9 %collective-permute-start.9 = (f32[12,8,128]{2,1,0:T(8,128)S(1)}, f32[12,8,128]{2,1,0:T(8,128)S(1)}, u32[]{:S(2)}, u32[]{:S(2)}) collective-permute-start(f32[12,8,128]{2,1,0:T(8,128)S(1)} %shard_map.89.s1), channel_id=1, source_target_pairs={{4,0},{8,4},{12,8},{16,12},{20,16},{24,20},{28,24},{32,28},{36,32}... | collective-permute-start | bytes 147464 | tf_op jit(solution)/shard_map/ppermute | solution.py:458
  68.8 3.9 %collective-permute-start.8 = (f32[12,8,128]{2,1,0:T(8,128)S(1)}, f32[12,8,128]{2,1,0:T(8,128)S(1)}, u32[]{:S(2)}, u32[]{:S(2)}) collective-permute-start(f32[12,8,128]{2,1,0:T(8,128)S(1)} %shard_map.89.s1), channel_id=1, source_target_pairs={{60,0},{0,4},{4,8},{8,12},{12,16},{16,20},{20,24},{24,28},{28,32},... | collective-permute-start | bytes 147464 | tf_op jit(solution)/shard_map/ppermute | solution.py:458
  72.8 3.1 %collective-permute-done.8.s0 = f32[12,8,128]{2,1,0:T(8,128)S(1)} collective-permute-done((f32[12,8,128]{2,1,0:T(8,128)S(1)}, f32[12,8,128]{2,1,0:T(8,128)S(1)}, u32[]{:S(2)}, u32[]{:S(2)}) %collective-permute-start.8) | collective-permute-done | bytes 49184 | tf_op jit(solution)/shard_map/ppermute | solution.py:458
  76.0 14.0 %shard_map.90 = (f32[3,8,128]{2,1,0:T(8,128)S(1)}, f32[3,8,128]{2,1,0:T(8,128)S(1)}, f32[8,128]{1,0:T(8,128)S(1)}, f32[8,128]{1,0:T(8,128)S(1)}, f32[8,128]{1,0:T(8,128)S(1)}, /*index=5*/f32[8,128]{1,0:T(8,128)S(1)}) custom-call(s32[1]{0:T(128)} %bitcast.18.total_ref, s32[2,128]{1,0:T(2,128)S(1)} %bitcast.22, ...), custom_call_target="tpu_custom_call" | custom-call | tf_op jit(solution)/shard_map/pallas_call | solution.py:530
  90.5 1.9 %collective-permute-start.12 = (f32[8,128]{1,0:T(8,128)S(1)}, f32[8,128]{1,0:T(8,128)S(1)}, u32[]{:S(2)}, u32[]{:S(2)}) collective-permute-start(f32[8,128]{1,0:T(8,128)S(1)} %get-tuple-element.35), channel_id=1, source_target_pairs={{4,0},{8,4},{12,8},{16,12},{20,16},{24,20},{28,24},{32,28},{36,32}... | collective-permute-start | bytes 12296 | tf_op jit(solution)/shard_map/ppermute | solution.py:458
  92.4 3.9 %collective-permute-start.13 = (f32[8,128]{1,0:T(8,128)S(1)}, f32[8,128]{1,0:T(8,128)S(1)}, u32[]{:S(2)}, u32[]{:S(2)}) collective-permute-start(f32[8,128]{1,0:T(8,128)S(1)} %get-tuple-element.36), channel_id=1, source_target_pairs={{60,0},{0,4},{4,8},{8,12},{12,16},{16,20},{20,24},{24,28},{28,32},... | collective-permute-start | bytes 12296 | tf_op jit(solution)/shard_map/ppermute | solution.py:458
  96.3 2.8 %collective-permute-done.13.a3 = f32[8,128]{1,0:T(8,128)S(1)} collective-permute-done((f32[8,128]{1,0:T(8,128)S(1)}, f32[8,128]{1,0:T(8,128)S(1)}, u32[]{:S(2)}, u32[]{:S(2)}) %collective-permute-start.13) | collective-permute-done | bytes 4128 | tf_op jit(solution)/shard_map/ppermute | solution.py:458
  99.1 0.8 shard_map.91
  99.9 1.9 %collective-permute-start.15 = (f32[3,8,128]{2,1,0:T(8,128)S(1)}, f32[3,8,128]{2,1,0:T(8,128)S(1)}, u32[]{:S(2)}, u32[]{:S(2)}) collective-permute-start(f32[3,8,128]{2,1,0:T(8,128)S(1)} %get-tuple-element.38), channel_id=1, source_target_pairs={{4,0},{8,4},{12,8},{16,12},{20,16},{24,20},{28,24},{32,28},{36,32}... | collective-permute-start | bytes 36872 | tf_op jit(solution)/shard_map/ppermute | solution.py:458
  101.8 3.9 %collective-permute-start.14 = (f32[3,8,128]{2,1,0:T(8,128)S(1)}, f32[3,8,128]{2,1,0:T(8,128)S(1)}, u32[]{:S(2)}, u32[]{:S(2)}) collective-permute-start(f32[3,8,128]{2,1,0:T(8,128)S(1)} %get-tuple-element.38), channel_id=1, source_target_pairs={{60,0},{0,4},{4,8},{8,12},{12,16},{16,20},{20,24},{24,28},{28,32},... | collective-permute-start | bytes 36872 | tf_op jit(solution)/shard_map/ppermute | solution.py:458
  105.8 2.9 %collective-permute-done.14 = f32[3,8,128]{2,1,0:T(8,128)S(1)} collective-permute-done((f32[3,8,128]{2,1,0:T(8,128)S(1)}, f32[3,8,128]{2,1,0:T(8,128)S(1)}, u32[]{:S(2)}, u32[]{:S(2)}) %collective-permute-start.14) | collective-permute-done | bytes 12320 | tf_op jit(solution)/shard_map/ppermute | solution.py:458
  108.6 9.2 %all_to_all.22.middle.c1 = f32[4,3,3,8,128]{4,3,2,1,0:T(8,128)S(1)} all-to-all(f32[4,3,3,8,128]{4,3,2,1,0:T(8,128)S(1)} %broadcast_in_dim.10), channel_id=1, replica_groups=mesh['gx'=8,'gy'=16,'gz'=4] {'gz'}, dimensions={0} | all-to-all | bytes 294912 | tf_op jit(solution)/shard_map/all_to_all | solution.py:473
  118.3 2.2 %collective-permute-done.17.ahead.c2 = f32[4,3,3,8,128]{4,3,2,1,0:T(8,128)S(1)} collective-permute-done((f32[4,3,3,8,128]{4,3,2,1,0:T(8,128)S(1)}, f32[4,3,3,8,128]{4,3,2,1,0:T(8,128)S(1)}, u32[]{:S(2)}, u32[]{:S(2)}) %collective-permute-start.17) | collective-permute-done | bytes 147488 | tf_op jit(solution)/shard_map/ppermute | solution.py:458
  120.5 1.9 %collective-permute-done.16.behind.c0 = f32[4,3,3,8,128]{4,3,2,1,0:T(8,128)S(1)} collective-permute-done((f32[4,3,3,8,128]{4,3,2,1,0:T(8,128)S(1)}, f32[4,3,3,8,128]{4,3,2,1,0:T(8,128)S(1)}, u32[]{:S(2)}, u32[]{:S(2)}) %collective-permute-start.16) | collective-permute-done | bytes 147488 | tf_op jit(solution)/shard_map/ppermute | solution.py:458
  122.4 7.1 %shard_map.92.own_slope = f32[8,128]{1,0:T(8,128)S(1)} custom-call(s32[1]{0:T(128)} %bitcast.19.total_ref, s32[2,128]{1,0:T(2,128)S(1)} %bitcast.23, f32[4,3,3,8,128]{4,3,2,1,0:T(8,128)S(1)} %collective-permute-done.16.behind.c0, f32[4,3,3,8,128]{4,3,2,1,0:T(8,128)S(1)} %all_to_all.22.middle.c1, f32[4,3,3,8,128]{4,3,2,1,0:T(8,128)S(1)} %collective-permute-done.17.ahead.c2), custom_call_target="tpu_custom_call" | custom-call | tf_op jit(solution)/shard_map/pallas_call | solution.py:521
  129.5 11.3 %all_to_all.23.plane_ref = f32[32,8,128]{2,1,0:T(8,128)S(1)} all-to-all(f32[32,8,128]{2,1,0:T(8,128)S(1)} %broadcast_in_dim.11), channel_id=1, replica_groups=mesh['gx'=8,'gy'=16,'gz'=4] {'gx','gz'}, dimensions={0} | all-to-all | bytes 262144 | tf_op jit(solution)/shard_map/all_to_all | solution.py:480
  140.8 2.6 %collective-permute-start.19 = (f32[12,8,128]{2,1,0:T(8,128)S(1)}, f32[12,8,128]{2,1,0:T(8,128)S(1)}, u32[]{:S(2)}, u32[]{:S(2)}) collective-permute-start(f32[12,8,128]{2,1,0:T(8,128)S(1)} %shard_map.93.s1), channel_id=1, source_target_pairs={{4,0},{8,4},{12,8},{16,12},{20,16},{24,20},{28,24},{32,28},{36,32}... | collective-permute-start | bytes 147464 | tf_op jit(solution)/shard_map/ppermute | solution.py:458
  143.4 3.2 %collective-permute-start.18 = (f32[12,8,128]{2,1,0:T(8,128)S(1)}, f32[12,8,128]{2,1,0:T(8,128)S(1)}, u32[]{:S(2)}, u32[]{:S(2)}) collective-permute-start(f32[12,8,128]{2,1,0:T(8,128)S(1)} %shard_map.93.s1), channel_id=1, source_target_pairs={{60,0},{0,4},{4,8},{8,12},{12,16},{16,20},{20,24},{24,28},{28,32},... | collective-permute-start | bytes 147464 | tf_op jit(solution)/shard_map/ppermute | solution.py:458
  146.8 3.8 %collective-permute-done.18.s0 = f32[12,8,128]{2,1,0:T(8,128)S(1)} collective-permute-done((f32[12,8,128]{2,1,0:T(8,128)S(1)}, f32[12,8,128]{2,1,0:T(8,128)S(1)}, u32[]{:S(2)}, u32[]{:S(2)}) %collective-permute-start.18) | collective-permute-done | bytes 49184 | tf_op jit(solution)/shard_map/ppermute | solution.py:458
  150.6 14.3 %shard_map.94 = f32[3,8,128]{2,1,0:T(8,128)} custom-call(s32[1]{0:T(128)} %bitcast.20.total_ref, s32[2,128]{1,0:T(2,128)S(1)} %bitcast.24, f32[4,3,3,8,128]{4,3,2,1,0:T(8,128)S(1)} %collective-permute-done.16.behind.c0, f32[4,3,3,8,128]{4,3,2,1,0:T(8,128)S(1)} %all_to_all.22.middle.c1, f32[4,3,3,8,128]{4,3,2,1,0:T(8,128)S(1)} %collective-permute-done.17.ahead.c2, ...), custom_call_target="tpu_custom_call" | custom-call | tf_op jit(solution)/shard_map/pallas_call | solution.py:537
  (37 shorter events, 5.7 us)
Async XLA Ops:
  0.6 0.7 copy-start.4
  1.3 0.7 copy-start.1
  2.0 0.7 copy-start.2
  2.7 0.7 copy-start.3
  3.7 14.5 %collective-permute-start = (f32[8,128]{1,0:T(8,128)S(1)}, f32[8,128]{1,0:T(8,128)S(1)}, u32[]{:S(2)}, u32[]{:S(2)}) collective-permute-start(f32[8,128]{1,0:T(8,128)S(1)} %get-tuple-element.24), channel_id=1, source_target_pairs={{64,0},{128,64},{192,128},{256,192},{320,256},{384,320},{448,384},... | collective-permute-start | bytes 12296 | tf_op jit(solution)/shard_map/ppermute | solution.py:458
  3.8 14.5 %collective-permute-start.1 = (f32[8,128]{1,0:T(8,128)S(1)}, f32[8,128]{1,0:T(8,128)S(1)}, u32[]{:S(2)}, u32[]{:S(2)}) collective-permute-start(f32[8,128]{1,0:T(8,128)S(1)} %get-tuple-element.25), channel_id=1, source_target_pairs={{448,0},{0,64},{64,128},{128,192},{192,256},{256,320},{320,384},{3... | collective-permute-start | bytes 12296 | tf_op jit(solution)/shard_map/ppermute | solution.py:458
  4.3 14.0 %collective-permute-start.2 = (f32[8,128]{1,0:T(8,128)S(1)}, f32[8,128]{1,0:T(8,128)S(1)}, u32[]{:S(2)}, u32[]{:S(2)}) collective-permute-start(f32[8,128]{1,0:T(8,128)S(1)} %get-tuple-element.26), channel_id=1, source_target_pairs={{4,0},{8,4},{12,8},{16,12},{20,16},{24,20},{28,24},{32,28},{36,32}... | collective-permute-start | bytes 12296 | tf_op jit(solution)/shard_map/ppermute | solution.py:458
  15.7 6.7 %collective-permute-start.3 = (f32[8,128]{1,0:T(8,128)S(1)}, f32[8,128]{1,0:T(8,128)S(1)}, u32[]{:S(2)}, u32[]{:S(2)}) collective-permute-start(f32[8,128]{1,0:T(8,128)S(1)} %get-tuple-element.27), channel_id=1, source_target_pairs={{60,0},{0,4},{4,8},{8,12},{12,16},{16,20},{20,24},{24,28},{28,32},... | collective-permute-start | bytes 12296 | tf_op jit(solution)/shard_map/ppermute | solution.py:458
  22.6 5.9 %collective-permute-start.5 = (f32[3,8,128]{2,1,0:T(8,128)S(1)}, f32[3,8,128]{2,1,0:T(8,128)S(1)}, u32[]{:S(2)}, u32[]{:S(2)}) collective-permute-start(f32[3,8,128]{2,1,0:T(8,128)S(1)} %get-tuple-element.28), channel_id=1, source_target_pairs={{4,0},{8,4},{12,8},{16,12},{20,16},{24,20},{28,24},{32,28},{36,32}... | collective-permute-start | bytes 36872 | tf_op jit(solution)/shard_map/ppermute | solution.py:458
  24.5 6.8 %collective-permute-start.4 = (f32[3,8,128]{2,1,0:T(8,128)S(1)}, f32[3,8,128]{2,1,0:T(8,128)S(1)}, u32[]{:S(2)}, u32[]{:S(2)}) collective-permute-start(f32[3,8,128]{2,1,0:T(8,128)S(1)} %get-tuple-element.28), channel_id=1, source_target_pairs={{60,0},{0,4},{4,8},{8,12},{12,16},{16,20},{20,24},{24,28},{28,32},... | collective-permute-start | bytes 36872 | tf_op jit(solution)/shard_map/ppermute | solution.py:458
  41.7 2.7 %collective-permute-start.7 = (f32[4,3,3,8,128]{4,3,2,1,0:T(8,128)S(1)}, f32[4,3,3,8,128]{4,3,2,1,0:T(8,128)S(1)}, u32[]{:S(2)}, u32[]{:S(2)}) collective-permute-start(f32[4,3,3,8,128]{4,3,2,1,0:T(8,128)S(1)} %all_to_all.20.middle.c1), channel_id=1, source_target_pairs={{64,0},{128,64},{192,128},{256,192},{320,256},{384,320},{448,384},... | collective-permute-start | bytes 442376 | tf_op jit(solution)/shard_map/ppermute | solution.py:458
  41.7 5.2 %collective-permute-start.6 = (f32[4,3,3,8,128]{4,3,2,1,0:T(8,128)S(1)}, f32[4,3,3,8,128]{4,3,2,1,0:T(8,128)S(1)}, u32[]{:S(2)}, u32[]{:S(2)}) collective-permute-start(f32[4,3,3,8,128]{4,3,2,1,0:T(8,128)S(1)} %all_to_all.20.middle.c1), channel_id=1, source_target_pairs={{448,0},{0,64},{64,128},{128,192},{192,256},{256,320},{320,384},{3... | collective-permute-start | bytes 442376 | tf_op jit(solution)/shard_map/ppermute | solution.py:458
  46.9 0.7 copy-start
  66.8 6.0 %collective-permute-start.9 = (f32[12,8,128]{2,1,0:T(8,128)S(1)}, f32[12,8,128]{2,1,0:T(8,128)S(1)}, u32[]{:S(2)}, u32[]{:S(2)}) collective-permute-start(f32[12,8,128]{2,1,0:T(8,128)S(1)} %shard_map.89.s1), channel_id=1, source_target_pairs={{4,0},{8,4},{12,8},{16,12},{20,16},{24,20},{28,24},{32,28},{36,32}... | collective-permute-start | bytes 147464 | tf_op jit(solution)/shard_map/ppermute | solution.py:458
  68.8 7.2 %collective-permute-start.8 = (f32[12,8,128]{2,1,0:T(8,128)S(1)}, f32[12,8,128]{2,1,0:T(8,128)S(1)}, u32[]{:S(2)}, u32[]{:S(2)}) collective-permute-start(f32[12,8,128]{2,1,0:T(8,128)S(1)} %shard_map.89.s1), channel_id=1, source_target_pairs={{60,0},{0,4},{4,8},{8,12},{12,16},{16,20},{20,24},{24,28},{28,32},... | collective-permute-start | bytes 147464 | tf_op jit(solution)/shard_map/ppermute | solution.py:458
  89.9 6.4 %collective-permute-start.10 = (f32[8,128]{1,0:T(8,128)S(1)}, f32[8,128]{1,0:T(8,128)S(1)}, u32[]{:S(2)}, u32[]{:S(2)}) collective-permute-start(f32[8,128]{1,0:T(8,128)S(1)} %get-tuple-element.33), channel_id=1, source_target_pairs={{64,0},{128,64},{192,128},{256,192},{320,256},{384,320},{448,384},... | collective-permute-start | bytes 12296 | tf_op jit(solution)/shard_map/ppermute | solution.py:458
  90.0 6.4 %collective-permute-start.11 = (f32[8,128]{1,0:T(8,128)S(1)}, f32[8,128]{1,0:T(8,128)S(1)}, u32[]{:S(2)}, u32[]{:S(2)}) collective-permute-start(f32[8,128]{1,0:T(8,128)S(1)} %get-tuple-element.34), channel_id=1, source_target_pairs={{448,0},{0,64},{64,128},{128,192},{192,256},{256,320},{320,384},{3... | collective-permute-start | bytes 12296 | tf_op jit(solution)/shard_map/ppermute | solution.py:458
  90.5 5.9 %collective-permute-start.12 = (f32[8,128]{1,0:T(8,128)S(1)}, f32[8,128]{1,0:T(8,128)S(1)}, u32[]{:S(2)}, u32[]{:S(2)}) collective-permute-start(f32[8,128]{1,0:T(8,128)S(1)} %get-tuple-element.35), channel_id=1, source_target_pairs={{4,0},{8,4},{12,8},{16,12},{20,16},{24,20},{28,24},{32,28},{36,32}... | collective-permute-start | bytes 12296 | tf_op jit(solution)/shard_map/ppermute | solution.py:458
  92.4 6.7 %collective-permute-start.13 = (f32[8,128]{1,0:T(8,128)S(1)}, f32[8,128]{1,0:T(8,128)S(1)}, u32[]{:S(2)}, u32[]{:S(2)}) collective-permute-start(f32[8,128]{1,0:T(8,128)S(1)} %get-tuple-element.36), channel_id=1, source_target_pairs={{60,0},{0,4},{4,8},{8,12},{12,16},{16,20},{20,24},{24,28},{28,32},... | collective-permute-start | bytes 12296 | tf_op jit(solution)/shard_map/ppermute | solution.py:458
  99.9 5.8 %collective-permute-start.15 = (f32[3,8,128]{2,1,0:T(8,128)S(1)}, f32[3,8,128]{2,1,0:T(8,128)S(1)}, u32[]{:S(2)}, u32[]{:S(2)}) collective-permute-start(f32[3,8,128]{2,1,0:T(8,128)S(1)} %get-tuple-element.38), channel_id=1, source_target_pairs={{4,0},{8,4},{12,8},{16,12},{20,16},{24,20},{28,24},{32,28},{36,32}... | collective-permute-start | bytes 36872 | tf_op jit(solution)/shard_map/ppermute | solution.py:458
  101.8 6.8 %collective-permute-start.14 = (f32[3,8,128]{2,1,0:T(8,128)S(1)}, f32[3,8,128]{2,1,0:T(8,128)S(1)}, u32[]{:S(2)}, u32[]{:S(2)}) collective-permute-start(f32[3,8,128]{2,1,0:T(8,128)S(1)} %get-tuple-element.38), channel_id=1, source_target_pairs={{60,0},{0,4},{4,8},{8,12},{12,16},{16,20},{20,24},{24,28},{28,32},... | collective-permute-start | bytes 36872 | tf_op jit(solution)/shard_map/ppermute | solution.py:458
  117.8 2.7 %collective-permute-start.17 = (f32[4,3,3,8,128]{4,3,2,1,0:T(8,128)S(1)}, f32[4,3,3,8,128]{4,3,2,1,0:T(8,128)S(1)}, u32[]{:S(2)}, u32[]{:S(2)}) collective-permute-start(f32[4,3,3,8,128]{4,3,2,1,0:T(8,128)S(1)} %all_to_all.22.middle.c1), channel_id=1, source_target_pairs={{64,0},{128,64},{192,128},{256,192},{320,256},{384,320},{448,384},... | collective-permute-start | bytes 442376 | tf_op jit(solution)/shard_map/ppermute | solution.py:458
  117.8 4.6 %collective-permute-start.16 = (f32[4,3,3,8,128]{4,3,2,1,0:T(8,128)S(1)}, f32[4,3,3,8,128]{4,3,2,1,0:T(8,128)S(1)}, u32[]{:S(2)}, u32[]{:S(2)}) collective-permute-start(f32[4,3,3,8,128]{4,3,2,1,0:T(8,128)S(1)} %all_to_all.22.middle.c1), channel_id=1, source_target_pairs={{448,0},{0,64},{64,128},{128,192},{192,256},{256,320},{320,384},{3... | collective-permute-start | bytes 442376 | tf_op jit(solution)/shard_map/ppermute | solution.py:458
  140.8 6.0 %collective-permute-start.19 = (f32[12,8,128]{2,1,0:T(8,128)S(1)}, f32[12,8,128]{2,1,0:T(8,128)S(1)}, u32[]{:S(2)}, u32[]{:S(2)}) collective-permute-start(f32[12,8,128]{2,1,0:T(8,128)S(1)} %shard_map.93.s1), channel_id=1, source_target_pairs={{4,0},{8,4},{12,8},{16,12},{20,16},{24,20},{28,24},{32,28},{36,32}... | collective-permute-start | bytes 147464 | tf_op jit(solution)/shard_map/ppermute | solution.py:458
  143.4 7.2 %collective-permute-start.18 = (f32[12,8,128]{2,1,0:T(8,128)S(1)}, f32[12,8,128]{2,1,0:T(8,128)S(1)}, u32[]{:S(2)}, u32[]{:S(2)}) collective-permute-start(f32[12,8,128]{2,1,0:T(8,128)S(1)} %shard_map.93.s1), channel_id=1, source_target_pairs={{60,0},{0,4},{4,8},{8,12},{12,16},{16,20},{20,24},{24,28},{28,32},... | collective-permute-start | bytes 147464 | tf_op jit(solution)/shard_map/ppermute | solution.py:458

commit v2 on v1

v2 whole, which is shorter than its diff:
```python
import functools

import jax
import jax.numpy as jnp
from jax import lax
from jax.experimental import pallas as pl
from jax.experimental.pallas import tpu as pltpu
from jax.sharding import PartitionSpec as P

cutoff_sq = 0.81
cutoff = 0.9
height_ratio = 0.25
density_scale = 1.0 / 256.0
repulsion = 1.0 / 512.0
time_step = 0.25
kick = 0.5 * time_step
flat_scale = 1.0 / cutoff
tall_scale = height_ratio / cutoff
cube_factor = -8.0 * repulsion / cutoff_sq
slope_factor = -6.0 * density_scale / cutoff_sq
far_away = 1e15

VMEM = pl.BlockSpec(memory_space=pltpu.VMEM)
ANY = pl.BlockSpec(memory_space=pl.ANY)
SMEM = pl.BlockSpec(memory_space=pltpu.SMEM)
unrolled = 4
nt_dims = (((1,), (1,)), ((), ()))
nn_dims = (((1,), (0,)), ((), ()))


def dot(left, right, dims):
    return lax.dot_general(left, right, dims, preferred_element_type=jnp.float32)


def pieces(values, count):
    out = []
    for _ in range(count):
        part = values.astype(jnp.bfloat16)
        out.append(part)
        values = values - part.astype(jnp.float32)
    return out


def slot_masks(slots_ref, direction):
    slots = slots_ref[direction : direction + 1, :]
    lane_hit = lax.broadcasted_iota(jnp.int32, (128, 128), 0) == (slots & 127)
    tile_hit = lax.broadcasted_iota(jnp.int32, (8, 128), 0) == (slots >> 7)
    return jnp.where(lane_hit, 1.0, 0.0).astype(jnp.bfloat16), tile_hit


def drift_and_pack(place, speed, push, slots_ref, place_ref, speed_ref, packed_refs):
    speed = [speed[c] + kick * push[c] for c in range(3)]
    rates = (time_step, time_step, time_step / height_ratio)
    place = [place[c] + rates[c] * speed[c] for c in range(3)]
    for c in range(3):
        place_ref[c] = place[c]
        speed_ref[c] = speed[c]
    rows = jnp.concatenate(place + speed, axis=0)
    split = jnp.concatenate(pieces(rows, 3), axis=0)
    for direction in range(4):
        lane_hit, tile_hit = slot_masks(slots_ref, direction)
        found = dot(split, lane_hit, nn_dims)
        found = found[0:48] + found[48:96] + found[96:144]
        for c in range(6):
            chosen = jnp.where(tile_hit, found[8 * c : 8 * c + 8], 0.0)
            packed_refs[direction][c : c + 1, :] = jnp.sum(chosen, axis=0, keepdims=True)
        packed_refs[direction][6:8, :] = jnp.zeros((2, 128), jnp.float32)


def put_plan(total, tiles, plan_ref, selves_ref):
    zbrick = lax.axis_index("gz")
    near = tiles[0:1]
    far = tiles[1:2]
    lanes = lax.broadcasted_iota(jnp.int32, (1, 128), 1)
    near = jnp.where(lanes < total, near, -1)
    rows = lax.broadcasted_iota(jnp.int32, (16, 128), 0)
    mine = jnp.where(rows == near, 1.0, 0.0)
    before = lax.broadcasted_iota(jnp.int32, (128, 128), 0) < lax.broadcasted_iota(
        jnp.int32, (128, 128), 1
    )
    ones = jnp.ones((128, 128), jnp.bfloat16)
    rank = dot(mine.astype(jnp.bfloat16), jnp.where(before, 1.0, 0.0).astype(jnp.bfloat16), nn_dims)
    count = dot(mine.astype(jnp.bfloat16), ones, nn_dims)
    itself = jnp.where(far == (16 + zbrick) * 8 + near, mine, 0.0)
    selves_ref[...] = dot(itself.astype(jnp.bfloat16), ones, nn_dims)[0:8]
    groups = (count.astype(jnp.int32) + (unrolled - 1)) // unrolled
    place = jnp.full((1, 128), -1, jnp.int32)
    start = jnp.zeros((1, 128), jnp.int32)
    starts = jnp.zeros((1, 128), jnp.int32)
    for t in range(8):
        at = start * unrolled + rank[t : t + 1].astype(jnp.int32)
        place = jnp.where(near == t, at, place)
        starts = jnp.where(lanes == t, start, starts)
        start = start + groups[t : t + 1]
    starts = jnp.where(lanes == 8, start, starts)
    values = jnp.where(
        rows == 0,
        (far >> 3).astype(jnp.float32),
        jnp.where(rows == 1, (far & 7).astype(jnp.float32), 1.0),
    ).astype(jnp.bfloat16)
    for half in range(2):
        spot = lax.broadcasted_iota(jnp.int32, (128, 128), 0) + 128 * half
        sent = jnp.where(spot == place, 1.0, 0.0).astype(jnp.bfloat16)
        sorted_rows = dot(values, sent, nt_dims).astype(jnp.int32)
        brick = jnp.where(sorted_rows[2:3] > 0, sorted_rows[0:1], 36)
        plan_ref[half : half + 1, :] = brick * 8 + sorted_rows[1:2]
    plan_ref[2:3, :] = starts
    plan_ref[3:8, :] = jnp.zeros((5, 128), jnp.int32)


def pack_kernel(
    total_ref,
    place_in,
    speed_in,
    push_in,
    slots_in,
    tiles_in,
    place_ref,
    speed_ref,
    p0,
    p1,
    p2,
    p3,
    slots_out,
    plan_ref,
    selves_ref,
    place_at,
    speed_at,
    push_at,
    tiles_at,
    sems,
):
    pairs = (
        (place_in, place_at),
        (speed_in, speed_at),
        (push_in, push_at),
        (slots_in, slots_out),
        (tiles_in, tiles_at),
    )
    copies = [
        pltpu.make_async_copy(here, there, sems.at[i]) for i, (here, there) in enumerate(pairs)
    ]
    for copy in copies:
        copy.start()
    for copy in copies:
        copy.wait()
    drift_and_pack(
        [place_at[c] for c in range(3)],
        [speed_at[c] for c in range(3)],
        [push_at[c] for c in range(3)],
        slots_out.at[0],
        place_ref,
        speed_ref,
        (p0, p1, p2, p3),
    )
    put_plan(total_ref[0], tiles_at[...], plan_ref, selves_ref)


def unpack_kernel(
    step, count_ref, place_in, speed_in, slots_in, a0, a1, a2, a3, place_ref, speed_ref, sent_ref
):
    slots_ref = slots_in.at[step]
    total = jnp.zeros((160, 128), jnp.float32)
    plan = ((a0, 0, 1.0), (a1, 0, -1.0), (a2, 1, 1.0), (a3, 1, -1.0))
    for direction, (arrived, component, shift) in enumerate(plan):
        lane_hit, tile_hit = slot_masks(slots_ref, direction)
        rows = []
        for c in range(6):
            row = arrived[c : c + 1, :]
            if c == component:
                row = row + shift
            rows.append(jnp.where(tile_hit, row, 0.0))
        marks = jnp.where(tile_hit, 1.0, 0.0)
        split = pieces(jnp.concatenate(rows, axis=0), 3)
        split.append(jnp.concatenate([marks, jnp.zeros_like(marks)], axis=0).astype(jnp.bfloat16))
        total = total + dot(jnp.concatenate(split, axis=0), lane_hit, nt_dims)
    put = total[0:48] + total[48:96] + total[96:144]
    taken = total[144:152] > 0.5
    slot_ids = lax.broadcasted_iota(jnp.int32, (8, 128), 0) * 128 + lax.broadcasted_iota(
        jnp.int32, (8, 128), 1
    )
    live = slot_ids < count_ref[0]
    scales = (flat_scale, flat_scale, tall_scale)
    for c in range(3):
        place = jnp.where(taken, put[8 * c : 8 * c + 8], place_in[c])
        place_ref[c] = place
        speed_ref[c] = jnp.where(taken, put[24 + 8 * c : 32 + 8 * c], speed_in[c])
        sent_ref[c] = jnp.where(live, place * scales[c], far_away)


def put_ghosts(cells, ghost_ref):
    zbrick = lax.axis_index("gz")
    for level in range(4):
        rise = ((level - zbrick).astype(jnp.float32) - 0.5) * tall_scale
        for dx, cell in enumerate(cells):
            for dy in range(3):
                brick = dx * 12 + dy * 4 + level
                ghost_ref[brick, 0] = cell[level, dy, 0] + (dx - 1.5) * flat_scale
                ghost_ref[brick, 1] = cell[level, dy, 1] + (dy - 1.5) * flat_scale
                ghost_ref[brick, 2] = cell[level, dy, 2] + rise
    ghost_ref[36] = jnp.full(ghost_ref.shape[1:], far_away, jnp.float32)


def own_places(middle):
    zbrick = lax.axis_index("gz")
    own = [middle[zbrick, 1, c] for c in range(3)]
    live = own[0] < 0.5 * far_away
    shifts = (0.5 * flat_scale, 0.5 * flat_scale, 0.5 * tall_scale)
    return [jnp.where(live, row - shift, -far_away) for row, shift in zip(own, shifts)], live


def put_columns(rows, column_ref):
    turned = jnp.concatenate(rows, axis=0).T
    for at in range(8 * len(rows)):
        column_ref[at] = jnp.broadcast_to(turned[:, at : at + 1], (128, 128))


def row_sums(block):
    first = block.astype(jnp.bfloat16)
    second = (block - first.astype(jnp.float32)).astype(jnp.bfloat16)
    split = jnp.concatenate([first, second], axis=1)
    sums = dot(split, jnp.ones((256, 128), jnp.bfloat16), nn_dims)
    on_line = lax.broadcasted_iota(jnp.int32, (128, 128), 0) == lax.broadcasted_iota(
        jnp.int32, (128, 128), 1
    )
    return jnp.sum(jnp.where(on_line, sums, 0.0), axis=0, keepdims=True)


def over_entries(plan_ref, body):
    def over_tile(near, carry):
        def over_group(group, carry):
            first = group * unrolled
            codes = [plan_ref[(first + i) >> 7, (first + i) & 127] for i in range(unrolled)]
            body(near, [(code >> 3, code & 7) for code in codes])
            return carry

        return lax.fori_loop(plan_ref[2, near], plan_ref[2, near + 1], over_group, carry)

    lax.fori_loop(0, 8, over_tile, 0)


def density_kernel(
    plan_in,
    selves_ref,
    behind,
    middle,
    ahead,
    slope_ref,
    plan_ref,
    ghost_ref,
    column_ref,
    sum_ref,
    row_ref,
    sem,
):
    copy = pltpu.make_async_copy(plan_in, plan_ref, sem)
    copy.start()
    put_ghosts((behind, middle, ahead), ghost_ref)
    own, live = own_places(middle)
    rest = 0.5 - (own[0] * own[0] + own[1] * own[1] + own[2] * own[2])
    put_columns([2.0 * row for row in own] + [rest], column_ref)
    sum_ref[...] = jnp.zeros_like(sum_ref)
    copy.wait()

    def add(near, ghosts):
        far = []
        for brick, tile in ghosts:
            x, y, z = (ghost_ref[brick, c, pl.ds(tile, 1), :] for c in range(3))
            rows = (x, y, z, 0.5 - (x * x + y * y + z * z))
            far.append([jnp.broadcast_to(row, (8, 128)) for row in rows])
        for r in range(16):
            part = pl.ds(8 * r, 8)
            ax, ay, az, rest = (column_ref[8 * c + near, part, :] for c in range(4))
            total = sum_ref[near, part, :]
            for cx, cy, cz, cn in far:
                shrink = jnp.maximum((ax * cx + ay * cy) + (az * cz + (rest + cn)), 0.0)
                total = total + shrink * shrink * shrink
            sum_ref[near, part, :] = total

    over_entries(plan_ref, add)
    for t in range(8):
        row_ref[t : t + 1, :] = row_sums(sum_ref[t])
    density = (row_ref[...] - jnp.where(live, selves_ref[...], 0.0)) * density_scale
    slope_ref[...] = (-0.5 * slope_factor / cube_factor) / jnp.sqrt(1.0 + density)


def force_sums(
    plan_in,
    cells,
    slope_cells,
    own_slope,
    plan_ref,
    ghost_ref,
    column_ref,
    sum_ref,
    push_ref,
    sem,
):
    copy = pltpu.make_async_copy(plan_in, plan_ref, sem)
    copy.start()
    put_ghosts(cells, ghost_ref)
    for dy, cell in enumerate(slope_cells):
        for dx in range(3):
            for level in range(4):
                ghost_ref[dx * 12 + dy * 4 + level, 3] = cell[dx * 4 + level]
    own, _ = own_places(cells[1])
    put_columns(own + [own_slope[...]], column_ref)
    sum_ref[...] = jnp.zeros_like(sum_ref)
    copy.wait()

    def add(near, ghosts):
        far = []
        for brick, tile in ghosts:
            rows = [ghost_ref[brick, c, pl.ds(tile, 1), :] for c in range(4)]
            far.append([jnp.broadcast_to(row, (8, 128)) for row in rows])
        for r in range(16):
            part = pl.ds(8 * r, 8)
            ax, ay, az, slope = (column_ref[8 * c + near, part, :] for c in range(4))
            sums = [sum_ref[8 * c + near, part, :] for c in range(3)]
            for cx, cy, cz, far_slope in far:
                dx = ax - cx
                dy = ay - cy
                dz = az - cz
                shrink = jnp.maximum(1.0 - (dx * dx + dy * dy + dz * dz), 0.0)
                weight = shrink * shrink * (shrink + (slope + far_slope))
                sums = [sums[0] + weight * dx, sums[1] + weight * dy, sums[2] + weight * dz]
            for c in range(3):
                sum_ref[8 * c + near, part, :] = sums[c]

    over_entries(plan_ref, add)
    for c in range(3):
        for t in range(8):
            push_ref[c, t : t + 1, :] = (-cutoff * cube_factor) * row_sums(sum_ref[8 * c + t])


def force_pack_kernel(
    step,
    plan_in,
    c0,
    c1,
    c2,
    s0,
    s1,
    s2,
    own_slope,
    place_in,
    speed_in,
    slots_ref,
    place_ref,
    speed_ref,
    p0,
    p1,
    p2,
    p3,
    plan_ref,
    ghost_ref,
    column_ref,
    sum_ref,
    push_ref,
    sem,
):
    force_sums(
        plan_in,
        (c0, c1, c2),
        (s0, s1, s2),
        own_slope,
        plan_ref,
        ghost_ref,
        column_ref,
        sum_ref,
        push_ref,
        sem,
    )
    push = [push_ref[c] for c in range(3)]
    speed = [speed_in[c] + kick * push[c] for c in range(3)]
    drift_and_pack(
        [place_in[c] for c in range(3)],
        speed,
        push,
        slots_ref.at[step],
        place_ref,
        speed_ref,
        (p0, p1, p2, p3),
    )


def force_last_kernel(
    plan_in,
    c0,
    c1,
    c2,
    s0,
    s1,
    s2,
    own_slope,
    speed_in,
    speed_ref,
    plan_ref,
    ghost_ref,
    column_ref,
    sum_ref,
    push_ref,
    sem,
):
    force_sums(
        plan_in,
        (c0, c1, c2),
        (s0, s1, s2),
        own_slope,
        plan_ref,
        ghost_ref,
        column_ref,
        sum_ref,
        push_ref,
        sem,
    )
    for c in range(3):
        speed_ref[c] = speed_in[c] + kick * push_ref[c]


def pick_kernel(plane_ref, column_ref):
    count = lax.axis_size("gx")
    xbrick = lax.axis_index("gx")
    for dx in range(3):
        at = lax.rem(xbrick + (dx - 1 + count), count)
        for level in range(4):
            column_ref[dx * 4 + level] = plane_ref[at * 4 + level]


def shaped(*extent):
    return jax.ShapeDtypeStruct(extent, jnp.float32)


def call(kernel, outs, specs, scratch=(), mebibytes=24):
    return pl.pallas_call(
        kernel,
        out_shape=outs,
        in_specs=specs,
        out_specs=[VMEM] * len(outs),
        scratch_shapes=list(scratch),
        compiler_params=pltpu.CompilerParams(vmem_limit_bytes=mebibytes * 2**20),
    )


def moved(values, axis, shift):
    count = lax.axis_size(axis)
    return lax.ppermute(values, axis, [((i + shift) % count, i) for i in range(count)])


def migrants(packed):
    return (
        moved(packed[1], "gx", 1),
        moved(packed[0], "gx", -1),
        moved(packed[3], "gy", 1),
        moved(packed[2], "gy", -1),
    )


def around(values):
    rows = jnp.stack([moved(values, "gy", -1), values, moved(values, "gy", 1)])
    copies = jnp.broadcast_to(rows[None], (4,) + rows.shape)
    tower = lax.all_to_all(copies, "gz", 0, 0, tiled=True)
    return moved(tower, "gx", -1), tower, moved(tower, "gx", 1)


def slopes_around(values):
    count = lax.axis_size("gx") * lax.axis_size("gz")
    copies = jnp.broadcast_to(values[None], (count,) + values.shape)
    plane = lax.all_to_all(copies, ("gx", "gz"), 0, 0, tiled=True)
    (column,) = call(pick_kernel, [shaped(12, 8, 128)], [VMEM])(plane)
    return moved(column, "gy", -1), column, moved(column, "gy", 1)


def per_device(positions, velocities, forces, counts, pair_tiles, pair_count, mig_slots):
    live_count = counts.reshape(1)
    total = pair_count.reshape(1)
    tiles = pair_tiles.reshape(2, 128)
    steps = mig_slots.shape[0]
    slots = mig_slots.reshape(steps, 4, 128)
    atoms = shaped(3, 8, 128)
    block = shaped(8, 128)
    atoms_scratch = pltpu.VMEM((3, 8, 128), jnp.float32)

    plan_shape = jax.ShapeDtypeStruct((8, 128), jnp.int32)

    def pair_scratch(columns, sums, found):
        return (
            pltpu.SMEM((8, 128), jnp.int32),
            pltpu.VMEM((37, columns, 8, 128), jnp.float32),
            pltpu.VMEM((8 * columns, 128, 128), jnp.float32),
            pltpu.VMEM((8 * sums, 128, 128), jnp.float32),
            found,
            pltpu.SemaphoreType.DMA,
        )

    place, speed, p0, p1, p2, p3, slots, plan, selves = call(
        pack_kernel,
        [atoms, atoms]
        + [block] * 4
        + [jax.ShapeDtypeStruct(slots.shape, jnp.int32), plan_shape, block],
        [SMEM] + [ANY] * 5,
        (atoms_scratch,) * 3
        + (pltpu.VMEM((2, 128), jnp.int32), pltpu.SemaphoreType.DMA((5,))),
        56,
    )(
        total,
        positions.reshape(3, 8, 128),
        velocities.reshape(3, 8, 128),
        forces.reshape(3, 8, 128),
        slots,
        tiles,
    )
    packed = p0, p1, p2, p3
    for n in range(steps):
        place, speed, sent = call(
            functools.partial(unpack_kernel, n), [atoms, atoms, atoms], [SMEM] + [VMEM] * 7
        )(live_count, place, speed, slots, *migrants(packed))
        cells = around(sent)
        (slope,) = call(
            density_kernel,
            [block],
            [ANY] + [VMEM] * 4,
            pair_scratch(4, 1, pltpu.VMEM((8, 128), jnp.float32)),
        )(plan, selves, *cells)
        slope_cells = slopes_around(slope)
        scratch = pair_scratch(4, 3, atoms_scratch)
        if n + 1 < steps:
            place, speed, *packed = call(
                functools.partial(force_pack_kernel, n + 1),
                [atoms, atoms] + [block] * 4,
                [ANY] + [VMEM] * 10,
                scratch,
            )(plan, *cells, *slope_cells, slope, place, speed, slots)
        else:
            (speed,) = call(force_last_kernel, [atoms], [ANY] + [VMEM] * 8, scratch)(
                plan, *cells, *slope_cells, slope, speed
            )
    return (place.reshape(positions.shape), speed.reshape(velocities.shape))


def solution(mesh):
    placed = (
        P(None, "gx", "gy", "gz", None),
        P(None, "gx", "gy", "gz", None),
        P(None, "gx", "gy", "gz", None),
        P("gx", "gy", "gz"),
        P(None, "gx", "gy", "gz", None),
        P("gx", "gy", "gz"),
        P(None, None, "gx", "gy", "gz", None),
    )
    return jax.shard_map(
        per_device,
        mesh=mesh,
        in_specs=placed,
        out_specs=(P(None, "gx", "gy", "gz", None), P(None, "gx", "gy", "gz", None)),
        check_vma=False,
    )
```

time: 166 us -> 150 us (0.904)
  the two profiles are of different devices: /device:TPU:2 before, /device:TPU:4 now
where the time goes in v2:
time: 150 us; the launch traced here: 149 us
  starting transfers between devices  44.5 us (30%)
  blocking collectives  42.6 us (28%)
  Pallas kernels  31.1 us (21%)
  waiting for transfers between devices  28.1 us (19%)
  between operations  2.21 us (1%)
    ppermute x20, starting transfers between devices, moved(): lax.ppermute(values, axis, [((i + shift) % count, i) for i in range(count)])  44.5 us
    ppermute x20, waiting for transfers between devices, moved(): lax.ppermute(values, axis, [((i + shift) % count, i) for i in range(count)])  28.1 us
    all_to_all x2, blocking collectives, slopes_around(): plane = lax.all_to_all(copies, ('gx', 'gz'), 0, 0, tiled=True)  23.4 us
    all_to_all x2, blocking collectives, around(): tower = lax.all_to_all(copies, 'gz', 0, 0, tiled=True)  19.2 us
    pallas_call x2, Pallas kernels, per_device(): call(density_kernel, [block], [ANY] + [VMEM] * 4, pair_scratch(4, 1, pltp...  10.8 us
    pallas_call x1, Pallas kernels, per_device(): call(force_last_kernel, [atoms], [ANY] + [VMEM] * 8, scratch)  8.9 us
    pallas_call x1, Pallas kernels, per_device(): call(functools.partial(force_pack_kernel, n + 1), [atoms, atoms] + [block...  8.54 us
  transfers between devices with their start and end apart: 20, of which 12 were waited for; matrix products, arithmetic and copies ran while one was open for 0% of the time, Pallas kernels for 0%

profile of v2, /device:TPU:4, one launch (start us, length us, event | category | flops | bytes accessed | tf_op | source)
XLA Modules:
  0.0 149.3 jit_solution(9073510024079122812)
XLA Ops:
  1.3 1.8 %shard_map.86 = (f32[3,8,128]{2,1,0:T(8,128)}, f32[3,8,128]{2,1,0:T(8,128)}, f32[8,128]{1,0:T(8,128)}, f32[8,128]{1,0:T(8,128)}, f32[8,128]{1,0:T(8,128)}, /*ind...) custom-call(s32[1]{0:T(128)} %bitcast.17.total_ref, f32[3,8,128]{2,1,0:T(8,128)} %bitcast.24, ...), custom_call_target="tpu_custom_call" | custom-call | tf_op jit(solution)/shard_map/pallas_call | solution.py:496
  3.6 11.4 %collective-permute-start.2 = (f32[8,128]{1,0:T(8,128)}, f32[8,128]{1,0:T(8,128)S(1)}, u32[]{:S(2)}, u32[]{:S(2)}) collective-permute-start(f32[8,128]{1,0:T(8,128)} %get-tuple-element.29), channel_id=1, source_target_pairs={{4,0},{8,4},{12,8},{16,12},{20,16},{24,20},{28,24},{32,28},{36,32}... | collective-permute-start | bytes 12296 | tf_op jit(solution)/shard_map/ppermute | solution.py:447
  15.0 1.9 %collective-permute-start.3 = (f32[8,128]{1,0:T(8,128)}, f32[8,128]{1,0:T(8,128)S(1)}, u32[]{:S(2)}, u32[]{:S(2)}) collective-permute-start(f32[8,128]{1,0:T(8,128)} %get-tuple-element.30), channel_id=1, source_target_pairs={{60,0},{0,4},{4,8},{8,12},{12,16},{16,20},{20,24},{24,28},{28,32},... | collective-permute-start | bytes 12296 | tf_op jit(solution)/shard_map/ppermute | solution.py:447
  17.6 4.3 %collective-permute-done.3.a3 = f32[8,128]{1,0:T(8,128)S(1)} collective-permute-done((f32[8,128]{1,0:T(8,128)}, f32[8,128]{1,0:T(8,128)S(1)}, u32[]{:S(2)}, u32[]{:S(2)}) %collective-permute-start.3) | collective-permute-done | bytes 4128 | tf_op jit(solution)/shard_map/ppermute | solution.py:447
  22.9 1.9 %collective-permute-start.5 = (f32[3,8,128]{2,1,0:T(8,128)S(1)}, f32[3,8,128]{2,1,0:T(8,128)S(1)}, u32[]{:S(2)}, u32[]{:S(2)}) collective-permute-start(f32[3,8,128]{2,1,0:T(8,128)S(1)} %get-tuple-element.31), channel_id=1, source_target_pairs={{4,0},{8,4},{12,8},{16,12},{20,16},{24,20},{28,24},{32,28},{36,32}... | collective-permute-start | bytes 36872 | tf_op jit(solution)/shard_map/ppermute | solution.py:447
  24.8 3.9 %collective-permute-start.4 = (f32[3,8,128]{2,1,0:T(8,128)S(1)}, f32[3,8,128]{2,1,0:T(8,128)S(1)}, u32[]{:S(2)}, u32[]{:S(2)}) collective-permute-start(f32[3,8,128]{2,1,0:T(8,128)S(1)} %get-tuple-element.31), channel_id=1, source_target_pairs={{60,0},{0,4},{4,8},{8,12},{12,16},{16,20},{20,24},{24,28},{28,32},... | collective-permute-start | bytes 36872 | tf_op jit(solution)/shard_map/ppermute | solution.py:447
  28.7 2.9 %collective-permute-done.4 = f32[3,8,128]{2,1,0:T(8,128)S(1)} collective-permute-done((f32[3,8,128]{2,1,0:T(8,128)S(1)}, f32[3,8,128]{2,1,0:T(8,128)S(1)}, u32[]{:S(2)}, u32[]{:S(2)}) %collective-permute-start.4) | collective-permute-done | bytes 12320 | tf_op jit(solution)/shard_map/ppermute | solution.py:447
  31.6 10.3 %all_to_all.20.middle.c1 = f32[4,3,3,8,128]{4,3,2,1,0:T(8,128)S(1)} all-to-all(f32[4,3,3,8,128]{4,3,2,1,0:T(8,128)S(1)} %broadcast_in_dim.8), channel_id=1, replica_groups=mesh['gx'=8,'gy'=16,'gz'=4] {'gz'}, dimensions={0} | all-to-all | bytes 294912 | tf_op jit(solution)/shard_map/all_to_all | solution.py:462
  42.5 2.2 %collective-permute-done.7.ahead.c2 = f32[4,3,3,8,128]{4,3,2,1,0:T(8,128)S(1)} collective-permute-done((f32[4,3,3,8,128]{4,3,2,1,0:T(8,128)S(1)}, f32[4,3,3,8,128]{4,3,2,1,0:T(8,128)S(1)}, u32[]{:S(2)}, u32[]{:S(2)}) %collective-permute-start.7) | collective-permute-done | bytes 147488 | tf_op jit(solution)/shard_map/ppermute | solution.py:447
  44.6 1.9 %collective-permute-done.6.behind.c0 = f32[4,3,3,8,128]{4,3,2,1,0:T(8,128)S(1)} collective-permute-done((f32[4,3,3,8,128]{4,3,2,1,0:T(8,128)S(1)}, f32[4,3,3,8,128]{4,3,2,1,0:T(8,128)S(1)}, u32[]{:S(2)}, u32[]{:S(2)}) %collective-permute-start.6) | collective-permute-done | bytes 147488 | tf_op jit(solution)/shard_map/ppermute | solution.py:447
  46.5 5.4 %shard_map.88.own_slope = f32[8,128]{1,0:T(8,128)S(1)} custom-call(s32[8,128]{1,0:T(8,128)S(1)} %copy-done, f32[8,128]{1,0:T(8,128)S(1)} %copy-done.2, f32[4,3,3,8,128]{4,3,2,1,0:T(8,128)S(1)} %collective-permute-done.6.behind.c0, f32[4,3,3,8,128]{4,3,2,1,0:T(8,128)S(1)} %all_to_all.20.middle.c1, f32[4,3,3,8,128]{4,3,2,1,0:T(8,128)S(1)} %collective-permute-done.7.ahead.c2), custom_call_target="tpu_custom_call" | custom-call | tf_op jit(solution)/shard_map/pallas_call | solution.py:519
  52.0 11.7 %all_to_all.21.plane_ref = f32[32,8,128]{2,1,0:T(8,128)S(1)} all-to-all(f32[32,8,128]{2,1,0:T(8,128)S(1)} %broadcast_in_dim.9), channel_id=1, replica_groups=mesh['gx'=8,'gy'=16,'gz'=4] {'gx','gz'}, dimensions={0} | all-to-all | bytes 262144 | tf_op jit(solution)/shard_map/all_to_all | solution.py:469
  63.7 1.9 %collective-permute-start.9 = (f32[12,8,128]{2,1,0:T(8,128)S(1)}, f32[12,8,128]{2,1,0:T(8,128)S(1)}, u32[]{:S(2)}, u32[]{:S(2)}) collective-permute-start(f32[12,8,128]{2,1,0:T(8,128)S(1)} %shard_map.89.s1), channel_id=1, source_target_pairs={{4,0},{8,4},{12,8},{16,12},{20,16},{24,20},{28,24},{32,28},{36,32}... | collective-permute-start | bytes 147464 | tf_op jit(solution)/shard_map/ppermute | solution.py:447
  65.6 3.9 %collective-permute-start.8 = (f32[12,8,128]{2,1,0:T(8,128)S(1)}, f32[12,8,128]{2,1,0:T(8,128)S(1)}, u32[]{:S(2)}, u32[]{:S(2)}) collective-permute-start(f32[12,8,128]{2,1,0:T(8,128)S(1)} %shard_map.89.s1), channel_id=1, source_target_pairs={{60,0},{0,4},{4,8},{8,12},{12,16},{16,20},{20,24},{24,28},{28,32},... | collective-permute-start | bytes 147464 | tf_op jit(solution)/shard_map/ppermute | solution.py:447
  69.7 3.1 %collective-permute-done.8.s0 = f32[12,8,128]{2,1,0:T(8,128)S(1)} collective-permute-done((f32[12,8,128]{2,1,0:T(8,128)S(1)}, f32[12,8,128]{2,1,0:T(8,128)S(1)}, u32[]{:S(2)}, u32[]{:S(2)}) %collective-permute-start.8) | collective-permute-done | bytes 49184 | tf_op jit(solution)/shard_map/ppermute | solution.py:447
  72.8 8.5 %shard_map.90 = (f32[3,8,128]{2,1,0:T(8,128)S(1)}, f32[3,8,128]{2,1,0:T(8,128)S(1)}, f32[8,128]{1,0:T(8,128)S(1)}, f32[8,128]{1,0:T(8,128)S(1)}, f32[8,128]{1,0:T(8,128)S(1)}, /*index=5*/f32[8,128]{1,0:T(8,128)S(1)}) custom-call(s32[8,128]{1,0:T(8,128)S(1)} %copy-done, f32[4,3,3,8,128]{4,3,2,1,0:T(8,128)S(1)} %collective-permute-done.6.behind.c0, ...), custom_call_target="tpu_custom_call" | custom-call | tf_op jit(solution)/shard_map/pallas_call | solution.py:528
  81.9 1.9 %collective-permute-start.12 = (f32[8,128]{1,0:T(8,128)S(1)}, f32[8,128]{1,0:T(8,128)S(1)}, u32[]{:S(2)}, u32[]{:S(2)}) collective-permute-start(f32[8,128]{1,0:T(8,128)S(1)} %get-tuple-element.39), channel_id=1, source_target_pairs={{4,0},{8,4},{12,8},{16,12},{20,16},{24,20},{28,24},{32,28},{36,32}... | collective-permute-start | bytes 12296 | tf_op jit(solution)/shard_map/ppermute | solution.py:447
  83.8 3.9 %collective-permute-start.13 = (f32[8,128]{1,0:T(8,128)S(1)}, f32[8,128]{1,0:T(8,128)S(1)}, u32[]{:S(2)}, u32[]{:S(2)}) collective-permute-start(f32[8,128]{1,0:T(8,128)S(1)} %get-tuple-element.40), channel_id=1, source_target_pairs={{60,0},{0,4},{4,8},{8,12},{12,16},{16,20},{20,24},{24,28},{28,32},... | collective-permute-start | bytes 12296 | tf_op jit(solution)/shard_map/ppermute | solution.py:447
  87.7 2.8 %collective-permute-done.13.a3 = f32[8,128]{1,0:T(8,128)S(1)} collective-permute-done((f32[8,128]{1,0:T(8,128)S(1)}, f32[8,128]{1,0:T(8,128)S(1)}, u32[]{:S(2)}, u32[]{:S(2)}) %collective-permute-start.13) | collective-permute-done | bytes 4128 | tf_op jit(solution)/shard_map/ppermute | solution.py:447
  90.5 0.8 shard_map.91
  91.3 2.6 %collective-permute-start.15 = (f32[3,8,128]{2,1,0:T(8,128)S(1)}, f32[3,8,128]{2,1,0:T(8,128)S(1)}, u32[]{:S(2)}, u32[]{:S(2)}) collective-permute-start(f32[3,8,128]{2,1,0:T(8,128)S(1)} %get-tuple-element.42), channel_id=1, source_target_pairs={{4,0},{8,4},{12,8},{16,12},{20,16},{24,20},{28,24},{32,28},{36,32}... | collective-permute-start | bytes 36872 | tf_op jit(solution)/shard_map/ppermute | solution.py:447
  93.9 3.2 %collective-permute-start.14 = (f32[3,8,128]{2,1,0:T(8,128)S(1)}, f32[3,8,128]{2,1,0:T(8,128)S(1)}, u32[]{:S(2)}, u32[]{:S(2)}) collective-permute-start(f32[3,8,128]{2,1,0:T(8,128)S(1)} %get-tuple-element.42), channel_id=1, source_target_pairs={{60,0},{0,4},{4,8},{8,12},{12,16},{16,20},{20,24},{24,28},{28,32},... | collective-permute-start | bytes 36872 | tf_op jit(solution)/shard_map/ppermute | solution.py:447
  97.2 3.6 %collective-permute-done.14 = f32[3,8,128]{2,1,0:T(8,128)S(1)} collective-permute-done((f32[3,8,128]{2,1,0:T(8,128)S(1)}, f32[3,8,128]{2,1,0:T(8,128)S(1)}, u32[]{:S(2)}, u32[]{:S(2)}) %collective-permute-start.14) | collective-permute-done | bytes 12320 | tf_op jit(solution)/shard_map/ppermute | solution.py:447
  100.8 8.9 %all_to_all.22.middle.c1 = f32[4,3,3,8,128]{4,3,2,1,0:T(8,128)S(1)} all-to-all(f32[4,3,3,8,128]{4,3,2,1,0:T(8,128)S(1)} %broadcast_in_dim.10), channel_id=1, replica_groups=mesh['gx'=8,'gy'=16,'gz'=4] {'gz'}, dimensions={0} | all-to-all | bytes 294912 | tf_op jit(solution)/shard_map/all_to_all | solution.py:462
  110.1 2.2 %collective-permute-done.17.ahead.c2 = f32[4,3,3,8,128]{4,3,2,1,0:T(8,128)S(1)} collective-permute-done((f32[4,3,3,8,128]{4,3,2,1,0:T(8,128)S(1)}, f32[4,3,3,8,128]{4,3,2,1,0:T(8,128)S(1)}, u32[]{:S(2)}, u32[]{:S(2)}) %collective-permute-start.17) | collective-permute-done | bytes 147488 | tf_op jit(solution)/shard_map/ppermute | solution.py:447
  112.3 1.9 %collective-permute-done.16.behind.c0 = f32[4,3,3,8,128]{4,3,2,1,0:T(8,128)S(1)} collective-permute-done((f32[4,3,3,8,128]{4,3,2,1,0:T(8,128)S(1)}, f32[4,3,3,8,128]{4,3,2,1,0:T(8,128)S(1)}, u32[]{:S(2)}, u32[]{:S(2)}) %collective-permute-start.16) | collective-permute-done | bytes 147488 | tf_op jit(solution)/shard_map/ppermute | solution.py:447
  114.2 5.4 %shard_map.92.own_slope = f32[8,128]{1,0:T(8,128)S(1)} custom-call(s32[8,128]{1,0:T(8,128)S(1)} %copy-done, f32[8,128]{1,0:T(8,128)S(1)} %copy-done.2, f32[4,3,3,8,128]{4,3,2,1,0:T(8,128)S(1)} %collective-permute-done.16.behind.c0, f32[4,3,3,8,128]{4,3,2,1,0:T(8,128)S(1)} %all_to_all.22.middle.c1, f32[4,3,3,8,128]{4,3,2,1,0:T(8,128)S(1)} %collective-permute-done.17.ahead.c2), custom_call_target="tpu_custom_call" | custom-call | tf_op jit(solution)/shard_map/pallas_call | solution.py:519
  119.6 11.7 %all_to_all.23.plane_ref = f32[32,8,128]{2,1,0:T(8,128)S(1)} all-to-all(f32[32,8,128]{2,1,0:T(8,128)S(1)} %broadcast_in_dim.11), channel_id=1, replica_groups=mesh['gx'=8,'gy'=16,'gz'=4] {'gx','gz'}, dimensions={0} | all-to-all | bytes 262144 | tf_op jit(solution)/shard_map/all_to_all | solution.py:469
  131.3 1.9 %collective-permute-start.19 = (f32[12,8,128]{2,1,0:T(8,128)S(1)}, f32[12,8,128]{2,1,0:T(8,128)S(1)}, u32[]{:S(2)}, u32[]{:S(2)}) collective-permute-start(f32[12,8,128]{2,1,0:T(8,128)S(1)} %shard_map.93.s1), channel_id=1, source_target_pairs={{4,0},{8,4},{12,8},{16,12},{20,16},{24,20},{28,24},{32,28},{36,32}... | collective-permute-start | bytes 147464 | tf_op jit(solution)/shard_map/ppermute | solution.py:447
  133.2 3.9 %collective-permute-start.18 = (f32[12,8,128]{2,1,0:T(8,128)S(1)}, f32[12,8,128]{2,1,0:T(8,128)S(1)}, u32[]{:S(2)}, u32[]{:S(2)}) collective-permute-start(f32[12,8,128]{2,1,0:T(8,128)S(1)} %shard_map.93.s1), channel_id=1, source_target_pairs={{60,0},{0,4},{4,8},{8,12},{12,16},{16,20},{20,24},{24,28},{28,32},... | collective-permute-start | bytes 147464 | tf_op jit(solution)/shard_map/ppermute | solution.py:447
  137.3 3.1 %collective-permute-done.18.s0 = f32[12,8,128]{2,1,0:T(8,128)S(1)} collective-permute-done((f32[12,8,128]{2,1,0:T(8,128)S(1)}, f32[12,8,128]{2,1,0:T(8,128)S(1)}, u32[]{:S(2)}, u32[]{:S(2)}) %collective-permute-start.18) | collective-permute-done | bytes 49184 | tf_op jit(solution)/shard_map/ppermute | solution.py:447
  140.4 8.9 %shard_map.94 = f32[3,8,128]{2,1,0:T(8,128)} custom-call(s32[8,128]{1,0:T(8,128)S(1)} %copy-done, f32[4,3,3,8,128]{4,3,2,1,0:T(8,128)S(1)} %collective-permute-done.16.behind.c0, f32[4,3,3,8,128]{4,3,2,1,0:T(8,128)S(1)} %all_to_all.22.middle.c1, f32[4,3,3,8,128]{4,3,2,1,0:T(8,128)S(1)} %collective-permute-done.17.ahead.c2, ...), custom_call_target="tpu_custom_call" | custom-call | tf_op jit(solution)/shard_map/pallas_call | solution.py:535
  (37 shorter events, 3.3 us)
Async XLA Ops:
  3.1 18.9 %copy-start.3 = (f32[3,8,128]{2,1,0:T(8,128)S(1)}, f32[3,8,128]{2,1,0:T(8,128)}, u32[]{:S(2)}) copy-start(f32[3,8,128]{2,1,0:T(8,128)} %get-tuple-element.24.place_in) | copy-start | bytes 36868
  3.1 14.5 %collective-permute-start = (f32[8,128]{1,0:T(8,128)}, f32[8,128]{1,0:T(8,128)S(1)}, u32[]{:S(2)}, u32[]{:S(2)}) collective-permute-start(f32[8,128]{1,0:T(8,128)} %get-tuple-element.27), channel_id=1, source_target_pairs={{64,0},{128,64},{192,128},{256,192},{320,256},{384,320},{448,384},... | collective-permute-start | bytes 12296 | tf_op jit(solution)/shard_map/ppermute | solution.py:447
  3.1 14.5 %collective-permute-start.1 = (f32[8,128]{1,0:T(8,128)}, f32[8,128]{1,0:T(8,128)S(1)}, u32[]{:S(2)}, u32[]{:S(2)}) collective-permute-start(f32[8,128]{1,0:T(8,128)} %get-tuple-element.28), channel_id=1, source_target_pairs={{448,0},{0,64},{64,128},{128,192},{192,256},{256,320},{320,384},{3... | collective-permute-start | bytes 12296 | tf_op jit(solution)/shard_map/ppermute | solution.py:447
  3.6 14.0 %collective-permute-start.2 = (f32[8,128]{1,0:T(8,128)}, f32[8,128]{1,0:T(8,128)S(1)}, u32[]{:S(2)}, u32[]{:S(2)}) collective-permute-start(f32[8,128]{1,0:T(8,128)} %get-tuple-element.29), channel_id=1, source_target_pairs={{4,0},{8,4},{12,8},{16,12},{20,16},{24,20},{28,24},{32,28},{36,32}... | collective-permute-start | bytes 12296 | tf_op jit(solution)/shard_map/ppermute | solution.py:447
  15.0 6.9 %collective-permute-start.3 = (f32[8,128]{1,0:T(8,128)}, f32[8,128]{1,0:T(8,128)S(1)}, u32[]{:S(2)}, u32[]{:S(2)}) collective-permute-start(f32[8,128]{1,0:T(8,128)} %get-tuple-element.30), channel_id=1, source_target_pairs={{60,0},{0,4},{4,8},{8,12},{12,16},{16,20},{20,24},{24,28},{28,32},... | collective-permute-start | bytes 12296 | tf_op jit(solution)/shard_map/ppermute | solution.py:447
  17.6 4.4 %copy-start.1 = (s32[2,4,128]{2,1,0:T(4,128)S(1)}, s32[2,4,128]{2,1,0:T(4,128)}, u32[]{:S(2)}) copy-start(s32[2,4,128]{2,1,0:T(4,128)} %get-tuple-element.26.slots_in.slots_ref) | copy-start | bytes 12292
  21.9 0.7 copy-start.4
  22.9 5.9 %collective-permute-start.5 = (f32[3,8,128]{2,1,0:T(8,128)S(1)}, f32[3,8,128]{2,1,0:T(8,128)S(1)}, u32[]{:S(2)}, u32[]{:S(2)}) collective-permute-start(f32[3,8,128]{2,1,0:T(8,128)S(1)} %get-tuple-element.31), channel_id=1, source_target_pairs={{4,0},{8,4},{12,8},{16,12},{20,16},{24,20},{28,24},{32,28},{36,32}... | collective-permute-start | bytes 36872 | tf_op jit(solution)/shard_map/ppermute | solution.py:447
  24.8 6.8 %collective-permute-start.4 = (f32[3,8,128]{2,1,0:T(8,128)S(1)}, f32[3,8,128]{2,1,0:T(8,128)S(1)}, u32[]{:S(2)}, u32[]{:S(2)}) collective-permute-start(f32[3,8,128]{2,1,0:T(8,128)S(1)} %get-tuple-element.31), channel_id=1, source_target_pairs={{60,0},{0,4},{4,8},{8,12},{12,16},{16,20},{20,24},{24,28},{28,32},... | collective-permute-start | bytes 36872 | tf_op jit(solution)/shard_map/ppermute | solution.py:447
  31.6 14.9 %copy-start = (s32[8,128]{1,0:T(8,128)S(1)}, s32[8,128]{1,0:T(8,128)}, u32[]{:S(2)}) copy-start(s32[8,128]{1,0:T(8,128)} %get-tuple-element.23.plan_in) | copy-start | bytes 12292
  31.6 14.9 %copy-start.2 = (f32[8,128]{1,0:T(8,128)S(1)}, f32[8,128]{1,0:T(8,128)}, u32[]{:S(2)}) copy-start(f32[8,128]{1,0:T(8,128)} %get-tuple-element.32.selves_ref) | copy-start | bytes 12292
  42.0 2.7 %collective-permute-start.7 = (f32[4,3,3,8,128]{4,3,2,1,0:T(8,128)S(1)}, f32[4,3,3,8,128]{4,3,2,1,0:T(8,128)S(1)}, u32[]{:S(2)}, u32[]{:S(2)}) collective-permute-start(f32[4,3,3,8,128]{4,3,2,1,0:T(8,128)S(1)} %all_to_all.20.middle.c1), channel_id=1, source_target_pairs={{64,0},{128,64},{192,128},{256,192},{320,256},{384,320},{448,384},... | collective-permute-start | bytes 442376 | tf_op jit(solution)/shard_map/ppermute | solution.py:447
  42.0 4.6 %collective-permute-start.6 = (f32[4,3,3,8,128]{4,3,2,1,0:T(8,128)S(1)}, f32[4,3,3,8,128]{4,3,2,1,0:T(8,128)S(1)}, u32[]{:S(2)}, u32[]{:S(2)}) collective-permute-start(f32[4,3,3,8,128]{4,3,2,1,0:T(8,128)S(1)} %all_to_all.20.middle.c1), channel_id=1, source_target_pairs={{448,0},{0,64},{64,128},{128,192},{192,256},{256,320},{320,384},{3... | collective-permute-start | bytes 442376 | tf_op jit(solution)/shard_map/ppermute | solution.py:447
  63.7 6.0 %collective-permute-start.9 = (f32[12,8,128]{2,1,0:T(8,128)S(1)}, f32[12,8,128]{2,1,0:T(8,128)S(1)}, u32[]{:S(2)}, u32[]{:S(2)}) collective-permute-start(f32[12,8,128]{2,1,0:T(8,128)S(1)} %shard_map.89.s1), channel_id=1, source_target_pairs={{4,0},{8,4},{12,8},{16,12},{20,16},{24,20},{28,24},{32,28},{36,32}... | collective-permute-start | bytes 147464 | tf_op jit(solution)/shard_map/ppermute | solution.py:447
  65.6 7.2 %collective-permute-start.8 = (f32[12,8,128]{2,1,0:T(8,128)S(1)}, f32[12,8,128]{2,1,0:T(8,128)S(1)}, u32[]{:S(2)}, u32[]{:S(2)}) collective-permute-start(f32[12,8,128]{2,1,0:T(8,128)S(1)} %shard_map.89.s1), channel_id=1, source_target_pairs={{60,0},{0,4},{4,8},{8,12},{12,16},{16,20},{20,24},{24,28},{28,32},... | collective-permute-start | bytes 147464 | tf_op jit(solution)/shard_map/ppermute | solution.py:447
  81.3 6.4 %collective-permute-start.10 = (f32[8,128]{1,0:T(8,128)S(1)}, f32[8,128]{1,0:T(8,128)S(1)}, u32[]{:S(2)}, u32[]{:S(2)}) collective-permute-start(f32[8,128]{1,0:T(8,128)S(1)} %get-tuple-element.37), channel_id=1, source_target_pairs={{64,0},{128,64},{192,128},{256,192},{320,256},{384,320},{448,384},... | collective-permute-start | bytes 12296 | tf_op jit(solution)/shard_map/ppermute | solution.py:447
  81.4 6.4 %collective-permute-start.11 = (f32[8,128]{1,0:T(8,128)S(1)}, f32[8,128]{1,0:T(8,128)S(1)}, u32[]{:S(2)}, u32[]{:S(2)}) collective-permute-start(f32[8,128]{1,0:T(8,128)S(1)} %get-tuple-element.38), channel_id=1, source_target_pairs={{448,0},{0,64},{64,128},{128,192},{192,256},{256,320},{320,384},{3... | collective-permute-start | bytes 12296 | tf_op jit(solution)/shard_map/ppermute | solution.py:447
  81.9 5.9 %collective-permute-start.12 = (f32[8,128]{1,0:T(8,128)S(1)}, f32[8,128]{1,0:T(8,128)S(1)}, u32[]{:S(2)}, u32[]{:S(2)}) collective-permute-start(f32[8,128]{1,0:T(8,128)S(1)} %get-tuple-element.39), channel_id=1, source_target_pairs={{4,0},{8,4},{12,8},{16,12},{20,16},{24,20},{28,24},{32,28},{36,32}... | collective-permute-start | bytes 12296 | tf_op jit(solution)/shard_map/ppermute | solution.py:447
  83.8 6.7 %collective-permute-start.13 = (f32[8,128]{1,0:T(8,128)S(1)}, f32[8,128]{1,0:T(8,128)S(1)}, u32[]{:S(2)}, u32[]{:S(2)}) collective-permute-start(f32[8,128]{1,0:T(8,128)S(1)} %get-tuple-element.40), channel_id=1, source_target_pairs={{60,0},{0,4},{4,8},{8,12},{12,16},{16,20},{20,24},{24,28},{28,32},... | collective-permute-start | bytes 12296 | tf_op jit(solution)/shard_map/ppermute | solution.py:447
  91.3 5.8 %collective-permute-start.15 = (f32[3,8,128]{2,1,0:T(8,128)S(1)}, f32[3,8,128]{2,1,0:T(8,128)S(1)}, u32[]{:S(2)}, u32[]{:S(2)}) collective-permute-start(f32[3,8,128]{2,1,0:T(8,128)S(1)} %get-tuple-element.42), channel_id=1, source_target_pairs={{4,0},{8,4},{12,8},{16,12},{20,16},{24,20},{28,24},{32,28},{36,32}... | collective-permute-start | bytes 36872 | tf_op jit(solution)/shard_map/ppermute | solution.py:447
  93.9 6.8 %collective-permute-start.14 = (f32[3,8,128]{2,1,0:T(8,128)S(1)}, f32[3,8,128]{2,1,0:T(8,128)S(1)}, u32[]{:S(2)}, u32[]{:S(2)}) collective-permute-start(f32[3,8,128]{2,1,0:T(8,128)S(1)} %get-tuple-element.42), channel_id=1, source_target_pairs={{60,0},{0,4},{4,8},{8,12},{12,16},{16,20},{20,24},{24,28},{28,32},... | collective-permute-start | bytes 36872 | tf_op jit(solution)/shard_map/ppermute | solution.py:447
  109.6 2.7 %collective-permute-start.17 = (f32[4,3,3,8,128]{4,3,2,1,0:T(8,128)S(1)}, f32[4,3,3,8,128]{4,3,2,1,0:T(8,128)S(1)}, u32[]{:S(2)}, u32[]{:S(2)}) collective-permute-start(f32[4,3,3,8,128]{4,3,2,1,0:T(8,128)S(1)} %all_to_all.22.middle.c1), channel_id=1, source_target_pairs={{64,0},{128,64},{192,128},{256,192},{320,256},{384,320},{448,384},... | collective-permute-start | bytes 442376 | tf_op jit(solution)/shard_map/ppermute | solution.py:447
  109.6 4.6 %collective-permute-start.16 = (f32[4,3,3,8,128]{4,3,2,1,0:T(8,128)S(1)}, f32[4,3,3,8,128]{4,3,2,1,0:T(8,128)S(1)}, u32[]{:S(2)}, u32[]{:S(2)}) collective-permute-start(f32[4,3,3,8,128]{4,3,2,1,0:T(8,128)S(1)} %all_to_all.22.middle.c1), channel_id=1, source_target_pairs={{448,0},{0,64},{64,128},{128,192},{192,256},{256,320},{320,384},{3... | collective-permute-start | bytes 442376 | tf_op jit(solution)/shard_map/ppermute | solution.py:447
  131.3 6.0 %collective-permute-start.19 = (f32[12,8,128]{2,1,0:T(8,128)S(1)}, f32[12,8,128]{2,1,0:T(8,128)S(1)}, u32[]{:S(2)}, u32[]{:S(2)}) collective-permute-start(f32[12,8,128]{2,1,0:T(8,128)S(1)} %shard_map.93.s1), channel_id=1, source_target_pairs={{4,0},{8,4},{12,8},{16,12},{20,16},{24,20},{28,24},{32,28},{36,32}... | collective-permute-start | bytes 147464 | tf_op jit(solution)/shard_map/ppermute | solution.py:447
  133.2 7.2 %collective-permute-start.18 = (f32[12,8,128]{2,1,0:T(8,128)S(1)}, f32[12,8,128]{2,1,0:T(8,128)S(1)}, u32[]{:S(2)}, u32[]{:S(2)}) collective-permute-start(f32[12,8,128]{2,1,0:T(8,128)S(1)} %shard_map.93.s1), channel_id=1, source_target_pairs={{60,0},{0,4},{4,8},{8,12},{12,16},{16,20},{20,24},{24,28},{28,32},... | collective-permute-start | bytes 147464 | tf_op jit(solution)/shard_map/ppermute | solution.py:447

commit v3 on v2

v3 whole, which is shorter than its diff:
```python
import functools

import jax
import jax.numpy as jnp
from jax import lax
from jax.experimental import pallas as pl
from jax.experimental.pallas import tpu as pltpu
from jax.sharding import PartitionSpec as P

cutoff_sq = 0.81
cutoff = 0.9
height_ratio = 0.25
density_scale = 1.0 / 256.0
repulsion = 1.0 / 512.0
time_step = 0.25
kick = 0.5 * time_step
flat_scale = 1.0 / cutoff
tall_scale = height_ratio / cutoff
cube_factor = -8.0 * repulsion / cutoff_sq
slope_factor = -6.0 * density_scale / cutoff_sq
far_away = 1e15

VMEM = pl.BlockSpec(memory_space=pltpu.VMEM)
ANY = pl.BlockSpec(memory_space=pl.ANY)
SMEM = pl.BlockSpec(memory_space=pltpu.SMEM)
unrolled = 4
nt_dims = (((1,), (1,)), ((), ()))
nn_dims = (((1,), (0,)), ((), ()))


def dot(left, right, dims):
    return lax.dot_general(left, right, dims, preferred_element_type=jnp.float32)


def pieces(values, count):
    out = []
    for _ in range(count):
        part = values.astype(jnp.bfloat16)
        out.append(part)
        values = values - part.astype(jnp.float32)
    return out


def slot_masks(slots_ref, direction):
    slots = slots_ref[direction : direction + 1, :]
    lane_hit = lax.broadcasted_iota(jnp.int32, (128, 128), 0) == (slots & 127)
    tile_hit = lax.broadcasted_iota(jnp.int32, (8, 128), 0) == (slots >> 7)
    return jnp.where(lane_hit, 1.0, 0.0).astype(jnp.bfloat16), tile_hit


def drift_and_pack(place, speed, push, slots_ref, place_ref, speed_ref, packed_refs):
    speed = [speed[c] + kick * push[c] for c in range(3)]
    rates = (time_step, time_step, time_step / height_ratio)
    place = [place[c] + rates[c] * speed[c] for c in range(3)]
    for c in range(3):
        place_ref[c] = place[c]
        speed_ref[c] = speed[c]
    rows = jnp.concatenate(place + speed, axis=0)
    split = jnp.concatenate(pieces(rows, 3), axis=0)
    for direction in range(4):
        lane_hit, tile_hit = slot_masks(slots_ref, direction)
        found = dot(split, lane_hit, nn_dims)
        found = found[0:48] + found[48:96] + found[96:144]
        for c in range(6):
            chosen = jnp.where(tile_hit, found[8 * c : 8 * c + 8], 0.0)
            packed_refs[direction][c : c + 1, :] = jnp.sum(chosen, axis=0, keepdims=True)
        packed_refs[direction][6:8, :] = jnp.zeros((2, 128), jnp.float32)


def put_plan(listed, near, far, late, plan_ref):
    lanes = lax.broadcasted_iota(jnp.int32, (1, 128), 1)
    part = jnp.where(listed, jnp.where(late, near + 8, near), -1)
    rows = lax.broadcasted_iota(jnp.int32, (16, 128), 0)
    mine = jnp.where(rows == part, 1.0, 0.0).astype(jnp.bfloat16)
    before = lax.broadcasted_iota(jnp.int32, (128, 128), 0) < lax.broadcasted_iota(
        jnp.int32, (128, 128), 1
    )
    rank = dot(mine, jnp.where(before, 1.0, 0.0).astype(jnp.bfloat16), nn_dims)
    count = dot(mine, jnp.ones((128, 128), jnp.bfloat16), nn_dims)
    groups = (count.astype(jnp.int32) + (unrolled - 1)) // unrolled
    place = jnp.full((1, 128), -1, jnp.int32)
    start = jnp.zeros((1, 128), jnp.int32)
    starts = jnp.zeros((1, 128), jnp.int32)
    for t in range(16):
        at = start * unrolled + rank[t : t + 1].astype(jnp.int32)
        place = jnp.where(part == t, at, place)
        starts = jnp.where(lanes == t, start, starts)
        start = start + groups[t : t + 1]
    starts = jnp.where(lanes == 16, start, starts)
    values = jnp.where(
        rows == 0,
        (far >> 3).astype(jnp.float32),
        jnp.where(rows == 1, (far & 7).astype(jnp.float32), 1.0),
    ).astype(jnp.bfloat16)
    for half in range(2):
        spot = lax.broadcasted_iota(jnp.int32, (128, 128), 0) + 128 * half
        sent = jnp.where(spot == place, 1.0, 0.0).astype(jnp.bfloat16)
        sorted_rows = dot(values, sent, nt_dims).astype(jnp.int32)
        brick = jnp.where(sorted_rows[2:3] > 0, sorted_rows[0:1], 36)
        plan_ref[half : half + 1, :] = brick * 8 + sorted_rows[1:2]
    plan_ref[2:3, :] = starts
    plan_ref[3:8, :] = jnp.zeros((5, 128), jnp.int32)


def plan_kernel(total_ref, count_ref, tiles_ref, density_plan, force_plan, selves_ref):
    zbrick = lax.axis_index("gz")
    near = tiles_ref[0:1, :]
    far = tiles_ref[1:2, :]
    listed = lax.broadcasted_iota(jnp.int32, (1, 128), 1) < total_ref[0]
    listed = jnp.logical_and(listed, near * 128 < count_ref[0])
    brick = far >> 3
    put_plan(listed, near, far, jnp.logical_or(brick < 12, brick >= 24), density_plan)
    put_plan(listed, near, far, ((brick >> 2) + 2) % 3 != 0, force_plan)
    rows = lax.broadcasted_iota(jnp.int32, (16, 128), 0)
    itself = jnp.logical_and(listed, far == (16 + zbrick) * 8 + near)
    itself = jnp.where(jnp.logical_and(itself, rows == near), 1.0, 0.0).astype(jnp.bfloat16)
    selves_ref[...] = dot(itself, jnp.ones((128, 128), jnp.bfloat16), nn_dims)[0:8]


def pack_kernel(rows_in, slots_in, place_ref, speed_ref, slots_out, *packed_refs):
    slots_out[...] = slots_in[...]
    drift_and_pack(
        [rows_in[c] for c in range(3)],
        [rows_in[c + 3] for c in range(3)],
        [rows_in[c + 6] for c in range(3)],
        slots_in.at[0],
        place_ref,
        speed_ref,
        packed_refs,
    )


def unpack_kernel(
    step, count_ref, place_in, speed_in, slots_in, a0, a1, a2, a3, place_ref, speed_ref, sent_ref
):
    slots_ref = slots_in.at[step]
    total = jnp.zeros((160, 128), jnp.float32)
    plan = ((a0, 0, 1.0), (a1, 0, -1.0), (a2, 1, 1.0), (a3, 1, -1.0))
    for direction, (arrived, component, shift) in enumerate(plan):
        lane_hit, tile_hit = slot_masks(slots_ref, direction)
        rows = []
        for c in range(6):
            row = arrived[c : c + 1, :]
            if c == component:
                row = row + shift
            rows.append(jnp.where(tile_hit, row, 0.0))
        marks = jnp.where(tile_hit, 1.0, 0.0)
        split = pieces(jnp.concatenate(rows, axis=0), 3)
        split.append(jnp.concatenate([marks, jnp.zeros_like(marks)], axis=0).astype(jnp.bfloat16))
        total = total + dot(jnp.concatenate(split, axis=0), lane_hit, nt_dims)
    put = total[0:48] + total[48:96] + total[96:144]
    taken = total[144:152] > 0.5
    slot_ids = lax.broadcasted_iota(jnp.int32, (8, 128), 0) * 128 + lax.broadcasted_iota(
        jnp.int32, (8, 128), 1
    )
    live = slot_ids < count_ref[0]
    scales = (flat_scale, flat_scale, tall_scale)
    for c in range(3):
        place = jnp.where(taken, put[8 * c : 8 * c + 8], place_in[c])
        place_ref[c] = place
        speed_ref[c] = jnp.where(taken, put[24 + 8 * c : 32 + 8 * c], speed_in[c])
        sent_ref[c] = jnp.where(live, place * scales[c], far_away)


def put_ghosts(cells, ghost_ref, wanted):
    zbrick = lax.axis_index("gz")
    for level in range(4):
        rise = ((level - zbrick).astype(jnp.float32) - 0.5) * tall_scale
        for dx, cell in enumerate(cells):
            for dy in range(3):
                if not wanted(dx, dy):
                    continue
                brick = dx * 12 + dy * 4 + level
                ghost_ref[brick, 0] = cell[level, dy, 0] + (dx - 1.5) * flat_scale
                ghost_ref[brick, 1] = cell[level, dy, 1] + (dy - 1.5) * flat_scale
                ghost_ref[brick, 2] = cell[level, dy, 2] + rise
    ghost_ref[36] = jnp.full(ghost_ref.shape[1:], far_away, jnp.float32)


def own_places(middle):
    zbrick = lax.axis_index("gz")
    own = [middle[zbrick, 1, c] for c in range(3)]
    live = own[0] < 0.5 * far_away
    shifts = (0.5 * flat_scale, 0.5 * flat_scale, 0.5 * tall_scale)
    return [jnp.where(live, row - shift, -far_away) for row, shift in zip(own, shifts)], live


def put_columns(rows, column_ref):
    turned = jnp.concatenate(rows, axis=0).T
    for at in range(8 * len(rows)):
        column_ref[at] = jnp.broadcast_to(turned[:, at : at + 1], (128, 128))


def row_sums(block):
    first = block.astype(jnp.bfloat16)
    second = (block - first.astype(jnp.float32)).astype(jnp.bfloat16)
    split = jnp.concatenate([first, second], axis=1)
    sums = dot(split, jnp.ones((256, 128), jnp.bfloat16), nn_dims)
    on_line = lax.broadcasted_iota(jnp.int32, (128, 128), 0) == lax.broadcasted_iota(
        jnp.int32, (128, 128), 1
    )
    return jnp.sum(jnp.where(on_line, sums, 0.0), axis=0, keepdims=True)


def over_entries(plan_in, plan_ref, sem, late, prepare, body):
    copy = pltpu.make_async_copy(plan_in, plan_ref, sem)
    copy.start()
    prepare()
    copy.wait()

    def over_tile(near, carry):
        def over_group(group, carry):
            first = group * unrolled
            codes = [plan_ref[(first + i) >> 7, (first + i) & 127] for i in range(unrolled)]
            body(near, [(code >> 3, code & 7) for code in codes])
            return carry

        segment = near + 8 * late
        return lax.fori_loop(plan_ref[2, segment], plan_ref[2, segment + 1], over_group, carry)

    lax.fori_loop(0, 8, over_tile, 0)


def density_sums(plan_in, cells, column_ref, late, plan_ref, ghost_ref, sum_ref, sem):
    def prepare():
        put_ghosts(cells, ghost_ref, lambda dx, dy: (dx != 1) == late)
        sum_ref[...] = jnp.zeros_like(sum_ref)

    def add(near, ghosts):
        far = []
        for brick, tile in ghosts:
            x, y, z = (ghost_ref[brick, c, pl.ds(tile, 1), :] for c in range(3))
            rows = (2.0 * x, 2.0 * y, 2.0 * z, 0.5 - (x * x + y * y + z * z))
            far.append([jnp.broadcast_to(row, (8, 128)) for row in rows])
        for r in range(16):
            part = pl.ds(8 * r, 8)
            ax, ay, az, rest = (column_ref[8 * c + near, part, :] for c in range(4))
            total = sum_ref[near, part, :]
            for cx, cy, cz, cn in far:
                shrink = jnp.maximum((ax * cx + ay * cy) + (az * cz + (rest + cn)), 0.0)
                total = total + shrink * shrink * shrink
            sum_ref[near, part, :] = total

    over_entries(plan_in, plan_ref, sem, late, prepare, add)


def early_density_kernel(
    plan_in, middle, column_ref, early_ref, plan_ref, ghost_ref, sum_ref, sem
):
    own, _ = own_places(middle)
    rest = 0.5 - (own[0] * own[0] + own[1] * own[1] + own[2] * own[2])
    put_columns(own + [rest], column_ref)
    cells = (None, middle, None)
    density_sums(plan_in, cells, column_ref, False, plan_ref, ghost_ref, sum_ref, sem)
    for t in range(8):
        early_ref[t : t + 1, :] = row_sums(sum_ref[t])


def late_density_kernel(
    plan_in,
    selves_ref,
    early_ref,
    column_ref,
    behind,
    middle,
    ahead,
    slope_ref,
    plan_ref,
    ghost_ref,
    sum_ref,
    row_ref,
    sem,
):
    cells = (behind, middle, ahead)
    density_sums(plan_in, cells, column_ref, True, plan_ref, ghost_ref, sum_ref, sem)
    for t in range(8):
        row_ref[t : t + 1, :] = row_sums(sum_ref[t])
    _, live = own_places(middle)
    itself = jnp.where(live, selves_ref[...], 0.0)
    density = (row_ref[...] + early_ref[...] - itself) * density_scale
    slope_ref[...] = (-0.5 * slope_factor / cube_factor) / jnp.sqrt(1.0 + density)


def force_sums(
    plan_in, cells, slope_cells, column_ref, slopes_ref, late, plan_ref, ghost_ref, sum_ref, sem
):
    def prepare():
        put_ghosts(cells, ghost_ref, lambda dx, dy: (dy != 1) == late)
        for dy, cell in enumerate(slope_cells):
            if (dy != 1) == late:
                for dx in range(3):
                    for level in range(4):
                        ghost_ref[dx * 12 + dy * 4 + level, 3] = cell[dx * 4 + level]
        sum_ref[...] = jnp.zeros_like(sum_ref)

    def add(near, ghosts):
        far = []
        for brick, tile in ghosts:
            rows = [ghost_ref[brick, c, pl.ds(tile, 1), :] for c in range(4)]
            far.append([jnp.broadcast_to(row, (8, 128)) for row in rows])
        for r in range(16):
            part = pl.ds(8 * r, 8)
            ax, ay, az = (column_ref[8 * c + near, part, :] for c in range(3))
            slope = slopes_ref[near, part, :]
            sums = [sum_ref[8 * c + near, part, :] for c in range(3)]
            for cx, cy, cz, far_slope in far:
                dx = ax - cx
                dy = ay - cy
                dz = az - cz
                shrink = jnp.maximum(1.0 - (dx * dx + dy * dy + dz * dz), 0.0)
                weight = shrink * shrink * (shrink + (slope + far_slope))
                sums = [sums[0] + weight * dx, sums[1] + weight * dy, sums[2] + weight * dz]
            for c in range(3):
                sum_ref[8 * c + near, part, :] = sums[c]

    over_entries(plan_in, plan_ref, sem, late, prepare, add)


def early_force_kernel(
    plan_in,
    c0,
    c1,
    c2,
    column_ref,
    own_slope,
    s1,
    slopes_ref,
    early_ref,
    plan_ref,
    ghost_ref,
    sum_ref,
    sem,
):
    put_columns([own_slope[...]], slopes_ref)
    force_sums(
        plan_in,
        (c0, c1, c2),
        (None, s1, None),
        column_ref,
        slopes_ref,
        False,
        plan_ref,
        ghost_ref,
        sum_ref,
        sem,
    )
    for c in range(3):
        for t in range(8):
            early_ref[c, t : t + 1, :] = row_sums(sum_ref[8 * c + t])


def late_force_kernel(
    step,
    plan_in,
    c0,
    c1,
    c2,
    column_ref,
    s0,
    s2,
    slopes_ref,
    early_ref,
    place_in,
    speed_in,
    *rest,
):
    *outs, plan_ref, ghost_ref, sum_ref, push_ref, sem = rest
    force_sums(
        plan_in,
        (c0, c1, c2),
        (s0, None, s2),
        column_ref,
        slopes_ref,
        True,
        plan_ref,
        ghost_ref,
        sum_ref,
        sem,
    )
    for c in range(3):
        for t in range(8):
            push_ref[c, t : t + 1, :] = row_sums(sum_ref[8 * c + t])
    push = [(-cutoff * cube_factor) * (push_ref[c] + early_ref[c]) for c in range(3)]
    place = [place_in[c] for c in range(3)]
    speed = [speed_in[c] + kick * push[c] for c in range(3)]
    if step is None:
        place_ref, speed_ref = outs
        for c in range(3):
            place_ref[c] = place[c]
            speed_ref[c] = speed[c]
    else:
        slots_ref, place_ref, speed_ref, *packed = outs
        drift_and_pack(place, speed, push, slots_ref.at[step], place_ref, speed_ref, packed)


def pick_kernel(plane_ref, column_ref):
    count = lax.axis_size("gx")
    xbrick = lax.axis_index("gx")
    for dx in range(3):
        at = lax.rem(xbrick + (dx - 1 + count), count)
        for level in range(4):
            column_ref[dx * 4 + level] = plane_ref[at * 4 + level]


def shaped(*extent):
    return jax.ShapeDtypeStruct(extent, jnp.float32)


def call(kernel, outs, specs, scratch=(), mega_ops=1):
    return pl.pallas_call(
        kernel,
        out_shape=outs,
        in_specs=specs,
        out_specs=[VMEM] * len(outs),
        scratch_shapes=list(scratch),
        compiler_params=pltpu.CompilerParams(vmem_limit_bytes=24 * 2**20),
        cost_estimate=pl.CostEstimate(
            flops=mega_ops * 10**6, bytes_accessed=mega_ops * 10**5, transcendentals=0
        ),
    )


def moved(values, axis, shift):
    count = lax.axis_size(axis)
    return lax.ppermute(values, axis, [((i + shift) % count, i) for i in range(count)])


def migrants(packed):
    return (
        moved(packed[1], "gx", 1),
        moved(packed[0], "gx", -1),
        moved(packed[3], "gy", 1),
        moved(packed[2], "gy", -1),
    )


def around(values, beside):
    ends, beside = lax.optimization_barrier(
        ((moved(values, "gy", -1), moved(values, "gy", 1)), beside)
    )
    rows = jnp.stack([ends[0], values, ends[1]])
    copies = jnp.broadcast_to(rows[None], (4,) + rows.shape)
    tower = lax.all_to_all(copies, "gz", 0, 0, tiled=True)
    return (moved(tower, "gx", -1), tower, moved(tower, "gx", 1)), beside


def slope_column(values):
    count = lax.axis_size("gx") * lax.axis_size("gz")
    copies = jnp.broadcast_to(values[None], (count,) + values.shape)
    plane = lax.all_to_all(copies, ("gx", "gz"), 0, 0, tiled=True)
    (column,) = call(pick_kernel, [shaped(12, 8, 128)], [VMEM])(plane)
    return column


def per_device(positions, velocities, forces, counts, pair_tiles, pair_count, mig_slots):
    live_count = counts.reshape(1)
    total = pair_count.reshape(1)
    steps = mig_slots.shape[0]
    slots = mig_slots.reshape(steps, 4, 128)
    atoms = shaped(3, 8, 128)
    block = shaped(8, 128)
    columns = shaped(32, 128, 128)
    slope_columns = shaped(8, 128, 128)
    atoms_scratch = pltpu.VMEM((3, 8, 128), jnp.float32)
    plan_shape = jax.ShapeDtypeStruct((8, 128), jnp.int32)

    def pair_scratch(comps, sums, *found):
        return (
            pltpu.SMEM((8, 128), jnp.int32),
            pltpu.VMEM((37, comps, 8, 128), jnp.float32),
            pltpu.VMEM((8 * sums, 128, 128), jnp.float32),
            *found,
            pltpu.SemaphoreType.DMA,
        )

    rows = jnp.concatenate([a.reshape(3, 8, 128) for a in (positions, velocities, forces)], axis=0)
    place, speed, slots, *packed = call(
        pack_kernel,
        [atoms, atoms, jax.ShapeDtypeStruct(slots.shape, jnp.int32)] + [block] * 4,
        [VMEM] * 2,
    )(rows, slots)
    plans = call(
        plan_kernel, [plan_shape, plan_shape, block], [SMEM, SMEM, VMEM]
    )(total, live_count, pair_tiles.reshape(2, 128))
    for n in range(steps):
        place, speed, sent = call(
            functools.partial(unpack_kernel, n), [atoms, atoms, atoms], [SMEM] + [VMEM] * 7
        )(live_count, place, speed, slots, *migrants(packed))
        cells, plans = around(sent, plans)
        density_plan, force_plan, selves = plans
        column, early = call(
            early_density_kernel,
            [columns, block],
            [ANY, VMEM],
            pair_scratch(3, 1),
            mega_ops=60,
        )(density_plan, cells[1])
        (slope,) = call(
            late_density_kernel,
            [block],
            [ANY] + [VMEM] * 6,
            pair_scratch(3, 1, pltpu.VMEM((8, 128), jnp.float32)),
        )(density_plan, selves, early, column, *cells)
        here = slope_column(slope)
        below, above = moved(here, "gy", -1), moved(here, "gy", 1)
        slopes, early = call(
            early_force_kernel,
            [slope_columns, atoms],
            [ANY] + [VMEM] * 6,
            pair_scratch(4, 3),
            mega_ops=60,
        )(force_plan, *cells, column, slope, here)
        last = n + 1 == steps
        place, speed, *packed = call(
            functools.partial(late_force_kernel, None if last else n + 1),
            [atoms, atoms] + [block] * (0 if last else 4),
            [ANY] + [VMEM] * (10 if last else 11),
            pair_scratch(4, 3, atoms_scratch),
        )(
            force_plan,
            *cells,
            column,
            below,
            above,
            slopes,
            early,
            place,
            speed,
            *(() if last else (slots,)),
        )
    return (place.reshape(positions.shape), speed.reshape(velocities.shape))


def solution(mesh):
    placed = (
        P(None, "gx", "gy", "gz", None),
        P(None, "gx", "gy", "gz", None),
        P(None, "gx", "gy", "gz", None),
        P("gx", "gy", "gz"),
        P(None, "gx", "gy", "gz", None),
        P("gx", "gy", "gz"),
        P(None, None, "gx", "gy", "gz", None),
    )
    return jax.shard_map(
        per_device,
        mesh=mesh,
        in_specs=placed,
        out_specs=(P(None, "gx", "gy", "gz", None), P(None, "gx", "gy", "gz", None)),
        check_vma=False,
    )
```

time: 150 us -> 140 us (0.933)
  the two profiles are of different devices: /device:TPU:4 before, /device:TPU:1 now
where the time goes in v3:
time: 140 us; the launch traced here: 139 us
  starting transfers between devices  56.4 us (40%)
  blocking collectives  44.3 us (32%)
  Pallas kernels  25 us (18%)
  waiting for transfers between devices  8.51 us (6%)
  between operations  2.23 us (2%)
  local copies, waits for them, and re-layouts  1.41 us (1%)
    ppermute x20, starting transfers between devices, moved(): lax.ppermute(values, axis, [((i + shift) % count, i) for i in range(count)])  56.4 us
    all_to_all x2, blocking collectives, slope_column(): plane = lax.all_to_all(copies, ('gx', 'gz'), 0, 0, tiled=True)  27.7 us
    all_to_all x2, blocking collectives, around(): tower = lax.all_to_all(copies, 'gz', 0, 0, tiled=True)  16.6 us
    ppermute x20, waiting for transfers between devices, moved(): lax.ppermute(values, axis, [((i + shift) % count, i) for i in range(count)])  8.51 us
    pallas_call x2, Pallas kernels, per_device(): call(functools.partial(late_force_kernel, None if last else n + 1), [atom...  7.95 us
    pallas_call x2, Pallas kernels, per_device(): call(early_force_kernel, [slope_columns, atoms], [ANY] + [VMEM] * 6, pair...  6.36 us
    pallas_call x2, Pallas kernels, per_device(): call(late_density_kernel, [block], [ANY] + [VMEM] * 6, pair_scratch(3, 1,...  5.18 us
    pallas_call x2, Pallas kernels, per_device(): call(early_density_kernel, [columns, block], [ANY, VMEM], pair_scratch(3,...  4.31 us
  transfers between devices with their start and end apart: 20, of which 7 were waited for; matrix products, arithmetic and copies ran while one was open for 0% of the time, Pallas kernels for 8%

profile of v3, /device:TPU:1, one launch (start us, length us, event | category | flops | bytes accessed | tf_op | source)
XLA Modules:
  0.0 138.6 jit_solution(15439200891152804301)
XLA Ops:
  0.6 0.7 pad_maximum_fusion.rows_in
  2.3 6.9 %collective-permute-start = (f32[8,128]{1,0:T(8,128)S(1)}, f32[8,128]{1,0:T(8,128)S(1)}, u32[]{:S(2)}, u32[]{:S(2)}) collective-permute-start(f32[8,128]{1,0:T(8,128)S(1)} %get-tuple-element.47), channel_id=1, source_target_pairs={{64,0},{128,64},{192,128},{256,192},{320,256},{384,320},{448,384},... | collective-permute-start | bytes 12296 | tf_op jit(solution)/shard_map/ppermute | solution.py:425
  9.2 6.9 %collective-permute-start.2 = (f32[8,128]{1,0:T(8,128)S(1)}, f32[8,128]{1,0:T(8,128)S(1)}, u32[]{:S(2)}, u32[]{:S(2)}) collective-permute-start(f32[8,128]{1,0:T(8,128)S(1)} %get-tuple-element.49), channel_id=1, source_target_pairs={{4,0},{8,4},{12,8},{16,12},{20,16},{24,20},{28,24},{32,28},{36,32}... | collective-permute-start | bytes 12296 | tf_op jit(solution)/shard_map/ppermute | solution.py:425
  16.1 1.9 %collective-permute-start.3 = (f32[8,128]{1,0:T(8,128)S(1)}, f32[8,128]{1,0:T(8,128)S(1)}, u32[]{:S(2)}, u32[]{:S(2)}) collective-permute-start(f32[8,128]{1,0:T(8,128)S(1)} %get-tuple-element.50), channel_id=1, source_target_pairs={{60,0},{0,4},{4,8},{8,12},{12,16},{16,20},{20,24},{24,28},{28,32},... | collective-permute-start | bytes 12296 | tf_op jit(solution)/shard_map/ppermute | solution.py:425
  18.7 3.0 %collective-permute-done.3.a3 = f32[8,128]{1,0:T(8,128)S(1)} collective-permute-done((f32[8,128]{1,0:T(8,128)S(1)}, f32[8,128]{1,0:T(8,128)S(1)}, u32[]{:S(2)}, u32[]{:S(2)}) %collective-permute-start.3) | collective-permute-done | bytes 4128 | tf_op jit(solution)/shard_map/ppermute | solution.py:425
  21.8 1.9 %collective-permute-start.5 = (f32[3,8,128]{2,1,0:T(8,128)S(1)}, f32[3,8,128]{2,1,0:T(8,128)S(1)}, u32[]{:S(2)}, u32[]{:S(2)}) collective-permute-start(f32[3,8,128]{2,1,0:T(8,128)S(1)} %get-tuple-element.51), channel_id=1, source_target_pairs={{4,0},{8,4},{12,8},{16,12},{20,16},{24,20},{28,24},{32,28},{36,32}... | collective-permute-start | bytes 36872 | tf_op jit(solution)/shard_map/ppermute | solution.py:425
  23.8 3.4 %collective-permute-start.4 = (f32[3,8,128]{2,1,0:T(8,128)S(1)}, f32[3,8,128]{2,1,0:T(8,128)S(1)}, u32[]{:S(2)}, u32[]{:S(2)}) collective-permute-start(f32[3,8,128]{2,1,0:T(8,128)S(1)} %get-tuple-element.51), channel_id=1, source_target_pairs={{60,0},{0,4},{4,8},{8,12},{12,16},{16,20},{20,24},{24,28},{28,32},... | collective-permute-start | bytes 36872 | tf_op jit(solution)/shard_map/ppermute | solution.py:425
  29.4 8.9 %all_to_all.20.middle.c1 = f32[4,3,3,8,128]{4,3,2,1,0:T(8,128)S(1)} all-to-all(f32[4,3,3,8,128]{4,3,2,1,0:T(8,128)S(1)} %broadcast_in_dim.8), channel_id=1, replica_groups=mesh['gx'=8,'gy'=16,'gz'=4] {'gz'}, dimensions={0} | all-to-all | bytes 294912 | tf_op jit(solution)/shard_map/all_to_all | solution.py:443
  38.3 5.1 %collective-permute-start.7 = (f32[4,3,3,8,128]{4,3,2,1,0:T(8,128)S(1)}, f32[4,3,3,8,128]{4,3,2,1,0:T(8,128)S(1)}, u32[]{:S(2)}, u32[]{:S(2)}) collective-permute-start(f32[4,3,3,8,128]{4,3,2,1,0:T(8,128)S(1)} %all_to_all.20.middle.c1), channel_id=1, source_target_pairs={{64,0},{128,64},{192,128},{256,192},{320,256},{384,320},{448,384},... | collective-permute-start | bytes 442376 | tf_op jit(solution)/shard_map/ppermute | solution.py:425
  43.4 2.1 %shard_map.89 = (f32[32,128,128]{2,1,0:T(8,128)S(1)}, f32[8,128]{1,0:T(8,128)S(1)}) custom-call(s32[8,128]{1,0:T(8,128)S(1)} %get-tuple-element.76.plan_in, f32[4,3,3,8,128]{4,3,2,1,0:T(8,128)S(1)} %all_to_all.20.middle.c1), custom_call_target="tpu_custom_call" | custom-call | flops 60000000 | bytes 6000000 | tf_op jit(solution)/shard_map/pallas_call | solution.py:491
  45.7 2.6 %shard_map.90.own_slope = f32[8,128]{1,0:T(8,128)S(1)} custom-call(s32[8,128]{1,0:T(8,128)S(1)} %get-tuple-element.76.plan_in, f32[8,128]{1,0:T(8,128)S(1)} %get-tuple-element.78.selves_ref, f32[8,128]{1,0:T(8,128)S(1)} %get-tuple-element.61.early_ref, f32[32,128,128]{2,1,0:T(8,128)S(1)} %get-tuple-element.59.column_ref, ...), custom_call_target="tpu_custom_call" | custom-call | flops 1000000 | bytes 100000 | tf_op jit(solution)/shard_map/pallas_call | solution.py:498
  48.3 14.0 %all_to_all.21.plane_ref = f32[32,8,128]{2,1,0:T(8,128)S(1)} all-to-all(f32[32,8,128]{2,1,0:T(8,128)S(1)} %broadcast_in_dim.9), channel_id=1, replica_groups=mesh['gx'=8,'gy'=16,'gz'=4] {'gx','gz'}, dimensions={0} | all-to-all | bytes 262144 | tf_op jit(solution)/shard_map/all_to_all | solution.py:450
  62.3 2.4 %collective-permute-start.9 = (f32[12,8,128]{2,1,0:T(8,128)S(1)}, f32[12,8,128]{2,1,0:T(8,128)S(1)}, u32[]{:S(2)}, u32[]{:S(2)}) collective-permute-start(f32[12,8,128]{2,1,0:T(8,128)S(1)} %shard_map.91.s1), channel_id=1, source_target_pairs={{4,0},{8,4},{12,8},{16,12},{20,16},{24,20},{28,24},{32,28},{36,32}... | collective-permute-start | bytes 147464 | tf_op jit(solution)/shard_map/ppermute | solution.py:425
  64.7 2.8 %collective-permute-start.8 = (f32[12,8,128]{2,1,0:T(8,128)S(1)}, f32[12,8,128]{2,1,0:T(8,128)S(1)}, u32[]{:S(2)}, u32[]{:S(2)}) collective-permute-start(f32[12,8,128]{2,1,0:T(8,128)S(1)} %shard_map.91.s1), channel_id=1, source_target_pairs={{60,0},{0,4},{4,8},{8,12},{12,16},{16,20},{20,24},{24,28},{28,32},... | collective-permute-start | bytes 147464 | tf_op jit(solution)/shard_map/ppermute | solution.py:425
  67.6 3.2 %shard_map.92 = (f32[8,128,128]{2,1,0:T(8,128)S(1)}, f32[3,8,128]{2,1,0:T(8,128)S(1)}) custom-call(s32[8,128]{1,0:T(8,128)S(1)} %get-tuple-element.73.plan_in, f32[4,3,3,8,128]{4,3,2,1,0:T(8,128)S(1)} %collective-permute-done.6.behind.c0, f32[4,3,3,8,128]{4,3,2,1,0:T(8,128)S(1)} %all_to_all.20.middle.c1, ...), custom_call_target="tpu_custom_call" | custom-call | flops 60000000 | bytes 6000000 | tf_op jit(solution)/shard_map/pallas_call | solution.py:506
  70.8 3.8 %shard_map.93 = (f32[3,8,128]{2,1,0:T(8,128)S(1)}, f32[3,8,128]{2,1,0:T(8,128)S(1)}, f32[8,128]{1,0:T(8,128)S(1)}, f32[8,128]{1,0:T(8,128)S(1)}, f32[8,128]{1,0:T(8,128)S(1)}, /*index=5*/f32[8,128]{1,0:T(8,128)S(1)}) custom-call(s32[8,128]{1,0:T(8,128)S(1)} %get-tuple-element.73.plan_in, f32[4,3,3,8,128]{4,3,2,1,0:T(8,128)S(1)} %collective-permute-done.6.behind.c0, ...), custom_call_target="tpu_custom_call" | custom-call | flops 1000000 | bytes 100000 | tf_op jit(solution)/shard_map/pallas_call | solution.py:514
  75.2 4.0 %collective-permute-start.11 = (f32[8,128]{1,0:T(8,128)S(1)}, f32[8,128]{1,0:T(8,128)S(1)}, u32[]{:S(2)}, u32[]{:S(2)}) collective-permute-start(f32[8,128]{1,0:T(8,128)S(1)} %get-tuple-element.69), channel_id=1, source_target_pairs={{448,0},{0,64},{64,128},{128,192},{192,256},{256,320},{320,384},{3... | collective-permute-start | bytes 12296 | tf_op jit(solution)/shard_map/ppermute | solution.py:425
  79.2 1.9 %collective-permute-start.12 = (f32[8,128]{1,0:T(8,128)S(1)}, f32[8,128]{1,0:T(8,128)S(1)}, u32[]{:S(2)}, u32[]{:S(2)}) collective-permute-start(f32[8,128]{1,0:T(8,128)S(1)} %get-tuple-element.70), channel_id=1, source_target_pairs={{4,0},{8,4},{12,8},{16,12},{20,16},{24,20},{28,24},{32,28},{36,32}... | collective-permute-start | bytes 12296 | tf_op jit(solution)/shard_map/ppermute | solution.py:425
  81.1 3.4 %collective-permute-start.13 = (f32[8,128]{1,0:T(8,128)S(1)}, f32[8,128]{1,0:T(8,128)S(1)}, u32[]{:S(2)}, u32[]{:S(2)}) collective-permute-start(f32[8,128]{1,0:T(8,128)S(1)} %get-tuple-element.71), channel_id=1, source_target_pairs={{60,0},{0,4},{4,8},{8,12},{12,16},{16,20},{20,24},{24,28},{28,32},... | collective-permute-start | bytes 12296 | tf_op jit(solution)/shard_map/ppermute | solution.py:425
  84.5 2.2 %collective-permute-done.13.a3 = f32[8,128]{1,0:T(8,128)S(1)} collective-permute-done((f32[8,128]{1,0:T(8,128)S(1)}, f32[8,128]{1,0:T(8,128)S(1)}, u32[]{:S(2)}, u32[]{:S(2)}) %collective-permute-start.13) | collective-permute-done | bytes 4128 | tf_op jit(solution)/shard_map/ppermute | solution.py:425
  86.9 1.9 %collective-permute-start.15 = (f32[3,8,128]{2,1,0:T(8,128)S(1)}, f32[3,8,128]{2,1,0:T(8,128)S(1)}, u32[]{:S(2)}, u32[]{:S(2)}) collective-permute-start(f32[3,8,128]{2,1,0:T(8,128)S(1)} %get-tuple-element.72), channel_id=1, source_target_pairs={{4,0},{8,4},{12,8},{16,12},{20,16},{24,20},{28,24},{32,28},{36,32}... | collective-permute-start | bytes 36872 | tf_op jit(solution)/shard_map/ppermute | solution.py:425
  88.8 3.4 %collective-permute-start.14 = (f32[3,8,128]{2,1,0:T(8,128)S(1)}, f32[3,8,128]{2,1,0:T(8,128)S(1)}, u32[]{:S(2)}, u32[]{:S(2)}) collective-permute-start(f32[3,8,128]{2,1,0:T(8,128)S(1)} %get-tuple-element.72), channel_id=1, source_target_pairs={{60,0},{0,4},{4,8},{8,12},{12,16},{16,20},{20,24},{24,28},{28,32},... | collective-permute-start | bytes 36872 | tf_op jit(solution)/shard_map/ppermute | solution.py:425
  92.2 2.3 %collective-permute-done.14 = f32[3,8,128]{2,1,0:T(8,128)S(1)} collective-permute-done((f32[3,8,128]{2,1,0:T(8,128)S(1)}, f32[3,8,128]{2,1,0:T(8,128)S(1)}, u32[]{:S(2)}, u32[]{:S(2)}) %collective-permute-start.14) | collective-permute-done | bytes 12320 | tf_op jit(solution)/shard_map/ppermute | solution.py:425
  94.5 7.7 %all_to_all.22.middle.c1 = f32[4,3,3,8,128]{4,3,2,1,0:T(8,128)S(1)} all-to-all(f32[4,3,3,8,128]{4,3,2,1,0:T(8,128)S(1)} %broadcast_in_dim.10), channel_id=1, replica_groups=mesh['gx'=8,'gy'=16,'gz'=4] {'gz'}, dimensions={0} | all-to-all | bytes 294912 | tf_op jit(solution)/shard_map/all_to_all | solution.py:443
  102.2 4.7 %collective-permute-start.17 = (f32[4,3,3,8,128]{4,3,2,1,0:T(8,128)S(1)}, f32[4,3,3,8,128]{4,3,2,1,0:T(8,128)S(1)}, u32[]{:S(2)}, u32[]{:S(2)}) collective-permute-start(f32[4,3,3,8,128]{4,3,2,1,0:T(8,128)S(1)} %all_to_all.22.middle.c1), channel_id=1, source_target_pairs={{64,0},{128,64},{192,128},{256,192},{320,256},{384,320},{448,384},... | collective-permute-start | bytes 442376 | tf_op jit(solution)/shard_map/ppermute | solution.py:425
  106.8 2.2 %shard_map.95 = (f32[32,128,128]{2,1,0:T(8,128)S(1)}, f32[8,128]{1,0:T(8,128)S(1)}) custom-call(s32[8,128]{1,0:T(8,128)S(1)} %get-tuple-element.76.plan_in, f32[4,3,3,8,128]{4,3,2,1,0:T(8,128)S(1)} %all_to_all.22.middle.c1), custom_call_target="tpu_custom_call" | custom-call | flops 60000000 | bytes 6000000 | tf_op jit(solution)/shard_map/pallas_call | solution.py:491
  109.5 2.6 %shard_map.96.own_slope = f32[8,128]{1,0:T(8,128)S(1)} custom-call(s32[8,128]{1,0:T(8,128)S(1)} %get-tuple-element.76.plan_in, f32[8,128]{1,0:T(8,128)S(1)} %get-tuple-element.78.selves_ref, f32[8,128]{1,0:T(8,128)S(1)} %get-tuple-element.79.early_ref, f32[32,128,128]{2,1,0:T(8,128)S(1)} %get-tuple-element.77.column_ref, ...), custom_call_target="tpu_custom_call" | custom-call | flops 1000000 | bytes 100000 | tf_op jit(solution)/shard_map/pallas_call | solution.py:498
  112.1 13.7 %all_to_all.23.plane_ref = f32[32,8,128]{2,1,0:T(8,128)S(1)} all-to-all(f32[32,8,128]{2,1,0:T(8,128)S(1)} %broadcast_in_dim.11), channel_id=1, replica_groups=mesh['gx'=8,'gy'=16,'gz'=4] {'gx','gz'}, dimensions={0} | all-to-all | bytes 262144 | tf_op jit(solution)/shard_map/all_to_all | solution.py:450
  125.8 2.5 %collective-permute-start.19 = (f32[12,8,128]{2,1,0:T(8,128)S(1)}, f32[12,8,128]{2,1,0:T(8,128)S(1)}, u32[]{:S(2)}, u32[]{:S(2)}) collective-permute-start(f32[12,8,128]{2,1,0:T(8,128)S(1)} %shard_map.97.s1), channel_id=1, source_target_pairs={{4,0},{8,4},{12,8},{16,12},{20,16},{24,20},{28,24},{32,28},{36,32}... | collective-permute-start | bytes 147464 | tf_op jit(solution)/shard_map/ppermute | solution.py:425
  128.3 2.7 %collective-permute-start.18 = (f32[12,8,128]{2,1,0:T(8,128)S(1)}, f32[12,8,128]{2,1,0:T(8,128)S(1)}, u32[]{:S(2)}, u32[]{:S(2)}) collective-permute-start(f32[12,8,128]{2,1,0:T(8,128)S(1)} %shard_map.97.s1), channel_id=1, source_target_pairs={{60,0},{0,4},{4,8},{8,12},{12,16},{16,20},{20,24},{24,28},{28,32},... | collective-permute-start | bytes 147464 | tf_op jit(solution)/shard_map/ppermute | solution.py:425
  131.1 3.2 %shard_map.98 = (f32[8,128,128]{2,1,0:T(8,128)S(1)}, f32[3,8,128]{2,1,0:T(8,128)S(1)}) custom-call(s32[8,128]{1,0:T(8,128)S(1)} %get-tuple-element.73.plan_in, f32[4,3,3,8,128]{4,3,2,1,0:T(8,128)S(1)} %collective-permute-done.16.behind.c0, f32[4,3,3,8,128]{4,3,2,1,0:T(8,128)S(1)} %all_to_all.22.middle.c1, ...), custom_call_target="tpu_custom_call" | custom-call | flops 60000000 | bytes 6000000 | tf_op jit(solution)/shard_map/pallas_call | solution.py:506
  134.4 4.2 %shard_map.99 = (f32[3,8,128]{2,1,0:T(8,128)}, f32[3,8,128]{2,1,0:T(8,128)}) custom-call(s32[8,128]{1,0:T(8,128)S(1)} %get-tuple-element.73.plan_in, f32[4,3,3,8,128]{4,3,2,1,0:T(8,128)S(1)} %collective-permute-done.16.behind.c0, f32[4,3,3,8,128]{4,3,2,1,0:T(8,128)S(1)} %all_to_all.22.middle.c1, f32[4,3,3,8,128]{4,3,2,1,0:T(8,128)S(1)} %collective-permute-done.17.ahead.c2, ...), custom_call_target="tpu_custom_call" | custom-call | flops 1000000 | bytes 100000 | tf_op jit(solution)/shard_map/pallas_call | solution.py:514
  (37 shorter events, 4.4 us)
Async XLA Ops:
  1.4 0.7 copy-start
  2.3 16.3 %collective-permute-start = (f32[8,128]{1,0:T(8,128)S(1)}, f32[8,128]{1,0:T(8,128)S(1)}, u32[]{:S(2)}, u32[]{:S(2)}) collective-permute-start(f32[8,128]{1,0:T(8,128)S(1)} %get-tuple-element.47), channel_id=1, source_target_pairs={{64,0},{128,64},{192,128},{256,192},{320,256},{384,320},{448,384},... | collective-permute-start | bytes 12296 | tf_op jit(solution)/shard_map/ppermute | solution.py:425
  9.2 9.5 %collective-permute-start.1 = (f32[8,128]{1,0:T(8,128)S(1)}, f32[8,128]{1,0:T(8,128)S(1)}, u32[]{:S(2)}, u32[]{:S(2)}) collective-permute-start(f32[8,128]{1,0:T(8,128)S(1)} %get-tuple-element.48), channel_id=1, source_target_pairs={{448,0},{0,64},{64,128},{128,192},{192,256},{256,320},{320,384},{3... | collective-permute-start | bytes 12296 | tf_op jit(solution)/shard_map/ppermute | solution.py:425
  9.2 9.5 %collective-permute-start.2 = (f32[8,128]{1,0:T(8,128)S(1)}, f32[8,128]{1,0:T(8,128)S(1)}, u32[]{:S(2)}, u32[]{:S(2)}) collective-permute-start(f32[8,128]{1,0:T(8,128)S(1)} %get-tuple-element.49), channel_id=1, source_target_pairs={{4,0},{8,4},{12,8},{16,12},{20,16},{24,20},{28,24},{32,28},{36,32}... | collective-permute-start | bytes 12296 | tf_op jit(solution)/shard_map/ppermute | solution.py:425
  16.1 5.6 %collective-permute-start.3 = (f32[8,128]{1,0:T(8,128)S(1)}, f32[8,128]{1,0:T(8,128)S(1)}, u32[]{:S(2)}, u32[]{:S(2)}) collective-permute-start(f32[8,128]{1,0:T(8,128)S(1)} %get-tuple-element.50), channel_id=1, source_target_pairs={{60,0},{0,4},{4,8},{8,12},{12,16},{16,20},{20,24},{24,28},{28,32},... | collective-permute-start | bytes 12296 | tf_op jit(solution)/shard_map/ppermute | solution.py:425
  21.8 7.1 %collective-permute-start.5 = (f32[3,8,128]{2,1,0:T(8,128)S(1)}, f32[3,8,128]{2,1,0:T(8,128)S(1)}, u32[]{:S(2)}, u32[]{:S(2)}) collective-permute-start(f32[3,8,128]{2,1,0:T(8,128)S(1)} %get-tuple-element.51), channel_id=1, source_target_pairs={{4,0},{8,4},{12,8},{16,12},{20,16},{24,20},{28,24},{32,28},{36,32}... | collective-permute-start | bytes 36872 | tf_op jit(solution)/shard_map/ppermute | solution.py:425
  23.8 5.7 %collective-permute-start.4 = (f32[3,8,128]{2,1,0:T(8,128)S(1)}, f32[3,8,128]{2,1,0:T(8,128)S(1)}, u32[]{:S(2)}, u32[]{:S(2)}) collective-permute-start(f32[3,8,128]{2,1,0:T(8,128)S(1)} %get-tuple-element.51), channel_id=1, source_target_pairs={{60,0},{0,4},{4,8},{8,12},{12,16},{16,20},{20,24},{24,28},{28,32},... | collective-permute-start | bytes 36872 | tf_op jit(solution)/shard_map/ppermute | solution.py:425
  27.8 0.7 copy-start.1
  38.3 7.3 %collective-permute-start.7 = (f32[4,3,3,8,128]{4,3,2,1,0:T(8,128)S(1)}, f32[4,3,3,8,128]{4,3,2,1,0:T(8,128)S(1)}, u32[]{:S(2)}, u32[]{:S(2)}) collective-permute-start(f32[4,3,3,8,128]{4,3,2,1,0:T(8,128)S(1)} %all_to_all.20.middle.c1), channel_id=1, source_target_pairs={{64,0},{128,64},{192,128},{256,192},{320,256},{384,320},{448,384},... | collective-permute-start | bytes 442376 | tf_op jit(solution)/shard_map/ppermute | solution.py:425
  43.4 2.2 %collective-permute-start.6 = (f32[4,3,3,8,128]{4,3,2,1,0:T(8,128)S(1)}, f32[4,3,3,8,128]{4,3,2,1,0:T(8,128)S(1)}, u32[]{:S(2)}, u32[]{:S(2)}) collective-permute-start(f32[4,3,3,8,128]{4,3,2,1,0:T(8,128)S(1)} %all_to_all.20.middle.c1), channel_id=1, source_target_pairs={{448,0},{0,64},{64,128},{128,192},{192,256},{256,320},{320,384},{3... | collective-permute-start | bytes 442376 | tf_op jit(solution)/shard_map/ppermute | solution.py:425
  62.3 8.5 %collective-permute-start.9 = (f32[12,8,128]{2,1,0:T(8,128)S(1)}, f32[12,8,128]{2,1,0:T(8,128)S(1)}, u32[]{:S(2)}, u32[]{:S(2)}) collective-permute-start(f32[12,8,128]{2,1,0:T(8,128)S(1)} %shard_map.91.s1), channel_id=1, source_target_pairs={{4,0},{8,4},{12,8},{16,12},{20,16},{24,20},{28,24},{32,28},{36,32}... | collective-permute-start | bytes 147464 | tf_op jit(solution)/shard_map/ppermute | solution.py:425
  64.7 6.0 %collective-permute-start.8 = (f32[12,8,128]{2,1,0:T(8,128)S(1)}, f32[12,8,128]{2,1,0:T(8,128)S(1)}, u32[]{:S(2)}, u32[]{:S(2)}) collective-permute-start(f32[12,8,128]{2,1,0:T(8,128)S(1)} %shard_map.91.s1), channel_id=1, source_target_pairs={{60,0},{0,4},{4,8},{8,12},{12,16},{16,20},{20,24},{24,28},{28,32},... | collective-permute-start | bytes 147464 | tf_op jit(solution)/shard_map/ppermute | solution.py:425
  74.6 9.9 %collective-permute-start.10 = (f32[8,128]{1,0:T(8,128)S(1)}, f32[8,128]{1,0:T(8,128)S(1)}, u32[]{:S(2)}, u32[]{:S(2)}) collective-permute-start(f32[8,128]{1,0:T(8,128)S(1)} %get-tuple-element.68), channel_id=1, source_target_pairs={{64,0},{128,64},{192,128},{256,192},{320,256},{384,320},{448,384},... | collective-permute-start | bytes 12296 | tf_op jit(solution)/shard_map/ppermute | solution.py:425
  75.2 9.3 %collective-permute-start.11 = (f32[8,128]{1,0:T(8,128)S(1)}, f32[8,128]{1,0:T(8,128)S(1)}, u32[]{:S(2)}, u32[]{:S(2)}) collective-permute-start(f32[8,128]{1,0:T(8,128)S(1)} %get-tuple-element.69), channel_id=1, source_target_pairs={{448,0},{0,64},{64,128},{128,192},{192,256},{256,320},{320,384},{3... | collective-permute-start | bytes 12296 | tf_op jit(solution)/shard_map/ppermute | solution.py:425
  79.2 5.3 %collective-permute-start.12 = (f32[8,128]{1,0:T(8,128)S(1)}, f32[8,128]{1,0:T(8,128)S(1)}, u32[]{:S(2)}, u32[]{:S(2)}) collective-permute-start(f32[8,128]{1,0:T(8,128)S(1)} %get-tuple-element.70), channel_id=1, source_target_pairs={{4,0},{8,4},{12,8},{16,12},{20,16},{24,20},{28,24},{32,28},{36,32}... | collective-permute-start | bytes 12296 | tf_op jit(solution)/shard_map/ppermute | solution.py:425
  81.1 5.6 %collective-permute-start.13 = (f32[8,128]{1,0:T(8,128)S(1)}, f32[8,128]{1,0:T(8,128)S(1)}, u32[]{:S(2)}, u32[]{:S(2)}) collective-permute-start(f32[8,128]{1,0:T(8,128)S(1)} %get-tuple-element.71), channel_id=1, source_target_pairs={{60,0},{0,4},{4,8},{8,12},{12,16},{16,20},{20,24},{24,28},{28,32},... | collective-permute-start | bytes 12296 | tf_op jit(solution)/shard_map/ppermute | solution.py:425
  86.9 5.3 %collective-permute-start.15 = (f32[3,8,128]{2,1,0:T(8,128)S(1)}, f32[3,8,128]{2,1,0:T(8,128)S(1)}, u32[]{:S(2)}, u32[]{:S(2)}) collective-permute-start(f32[3,8,128]{2,1,0:T(8,128)S(1)} %get-tuple-element.72), channel_id=1, source_target_pairs={{4,0},{8,4},{12,8},{16,12},{20,16},{24,20},{28,24},{32,28},{36,32}... | collective-permute-start | bytes 36872 | tf_op jit(solution)/shard_map/ppermute | solution.py:425
  88.8 5.7 %collective-permute-start.14 = (f32[3,8,128]{2,1,0:T(8,128)S(1)}, f32[3,8,128]{2,1,0:T(8,128)S(1)}, u32[]{:S(2)}, u32[]{:S(2)}) collective-permute-start(f32[3,8,128]{2,1,0:T(8,128)S(1)} %get-tuple-element.72), channel_id=1, source_target_pairs={{60,0},{0,4},{4,8},{8,12},{12,16},{16,20},{20,24},{24,28},{28,32},... | collective-permute-start | bytes 36872 | tf_op jit(solution)/shard_map/ppermute | solution.py:425
  102.2 7.3 %collective-permute-start.17 = (f32[4,3,3,8,128]{4,3,2,1,0:T(8,128)S(1)}, f32[4,3,3,8,128]{4,3,2,1,0:T(8,128)S(1)}, u32[]{:S(2)}, u32[]{:S(2)}) collective-permute-start(f32[4,3,3,8,128]{4,3,2,1,0:T(8,128)S(1)} %all_to_all.22.middle.c1), channel_id=1, source_target_pairs={{64,0},{128,64},{192,128},{256,192},{320,256},{384,320},{448,384},... | collective-permute-start | bytes 442376 | tf_op jit(solution)/shard_map/ppermute | solution.py:425
  106.8 2.7 %collective-permute-start.16 = (f32[4,3,3,8,128]{4,3,2,1,0:T(8,128)S(1)}, f32[4,3,3,8,128]{4,3,2,1,0:T(8,128)S(1)}, u32[]{:S(2)}, u32[]{:S(2)}) collective-permute-start(f32[4,3,3,8,128]{4,3,2,1,0:T(8,128)S(1)} %all_to_all.22.middle.c1), channel_id=1, source_target_pairs={{448,0},{0,64},{64,128},{128,192},{192,256},{256,320},{320,384},{3... | collective-permute-start | bytes 442376 | tf_op jit(solution)/shard_map/ppermute | solution.py:425
  125.8 8.5 %collective-permute-start.19 = (f32[12,8,128]{2,1,0:T(8,128)S(1)}, f32[12,8,128]{2,1,0:T(8,128)S(1)}, u32[]{:S(2)}, u32[]{:S(2)}) collective-permute-start(f32[12,8,128]{2,1,0:T(8,128)S(1)} %shard_map.97.s1), channel_id=1, source_target_pairs={{4,0},{8,4},{12,8},{16,12},{20,16},{24,20},{28,24},{32,28},{36,32}... | collective-permute-start | bytes 147464 | tf_op jit(solution)/shard_map/ppermute | solution.py:425
  128.3 6.0 %collective-permute-start.18 = (f32[12,8,128]{2,1,0:T(8,128)S(1)}, f32[12,8,128]{2,1,0:T(8,128)S(1)}, u32[]{:S(2)}, u32[]{:S(2)}) collective-permute-start(f32[12,8,128]{2,1,0:T(8,128)S(1)} %shard_map.97.s1), channel_id=1, source_target_pairs={{60,0},{0,4},{4,8},{8,12},{12,16},{16,20},{20,24},{24,28},{28,32},... | collective-permute-start | bytes 147464 | tf_op jit(solution)/shard_map/ppermute | solution.py:425

commit v4 on v3

--- a/solution.py
+++ b/solution.py
@@ -41,8 +41,20 @@
     return out
 
 
-def slot_masks(slots_ref, direction):
-    slots = slots_ref[direction : direction + 1, :]
+def parity(axis):
+    return lax.axis_index(axis) & 1
+
+
+def away(kind, axis):
+    return (2 - 2 * parity(axis), 1, 2 * parity(axis))[kind]
+
+
+swaps = (("gy", 2), ("gx", 2), ("gy", 0), ("gx", 0))
+
+
+def slot_masks(slots_ref, axis, kind):
+    row = (0 if axis == "gx" else 2) + 1 - away(kind, axis) // 2
+    slots = slots_ref[pl.ds(row, 1), :]
     lane_hit = lax.broadcasted_iota(jnp.int32, (128, 128), 0) == (slots & 127)
     tile_hit = lax.broadcasted_iota(jnp.int32, (8, 128), 0) == (slots >> 7)
     return jnp.where(lane_hit, 1.0, 0.0).astype(jnp.bfloat16), tile_hit
@@ -57,14 +69,14 @@
         speed_ref[c] = speed[c]
     rows = jnp.concatenate(place + speed, axis=0)
     split = jnp.concatenate(pieces(rows, 3), axis=0)
-    for direction in range(4):
-        lane_hit, tile_hit = slot_masks(slots_ref, direction)
+    for (axis, kind), packed_ref in zip(swaps, packed_refs):
+        lane_hit, tile_hit = slot_masks(slots_ref, axis, kind)
         found = dot(split, lane_hit, nn_dims)
         found = found[0:48] + found[48:96] + found[96:144]
         for c in range(6):
             chosen = jnp.where(tile_hit, found[8 * c : 8 * c + 8], 0.0)
-            packed_refs[direction][c : c + 1, :] = jnp.sum(chosen, axis=0, keepdims=True)
-        packed_refs[direction][6:8, :] = jnp.zeros((2, 128), jnp.float32)
+            packed_ref[c : c + 1, :] = jnp.sum(chosen, axis=0, keepdims=True)
+        packed_ref[6:8, :] = jnp.zeros((2, 128), jnp.float32)
 
 
 def put_plan(listed, near, far, late, plan_ref):
@@ -117,13 +129,15 @@
     selves_ref[...] = dot(itself, jnp.ones((128, 128), jnp.bfloat16), nn_dims)[0:8]
 
 
-def pack_kernel(rows_in, slots_in, place_ref, speed_ref, slots_out, *packed_refs):
-    slots_out[...] = slots_in[...]
+def pack_kernel(rows_in, place_ref, speed_ref, slots_out, *packed_refs):
+    steps = slots_out.shape[0]
+    for n in range(steps):
+        slots_out[n] = rows_in[9, 4 * n : 4 * n + 4].astype(jnp.int32)
     drift_and_pack(
         [rows_in[c] for c in range(3)],
         [rows_in[c + 3] for c in range(3)],
         [rows_in[c + 6] for c in range(3)],
-        slots_in.at[0],
+        slots_out.at[0],
         place_ref,
         speed_ref,
         packed_refs,
@@ -135,9 +149,10 @@
 ):
     slots_ref = slots_in.at[step]
     total = jnp.zeros((160, 128), jnp.float32)
-    plan = ((a0, 0, 1.0), (a1, 0, -1.0), (a2, 1, 1.0), (a3, 1, -1.0))
-    for direction, (arrived, component, shift) in enumerate(plan):
-        lane_hit, tile_hit = slot_masks(slots_ref, direction)
+    for (axis, kind), arrived in zip(swaps, (a0, a1, a2, a3)):
+        lane_hit, tile_hit = slot_masks(slots_ref, axis, kind)
+        component = 0 if axis == "gx" else 1
+        shift = (away(kind, axis) - 1).astype(jnp.float32)
         rows = []
         for c in range(6):
             row = arrived[c : c + 1, :]
@@ -164,16 +179,21 @@
 
 def put_ghosts(cells, ghost_ref, wanted):
     zbrick = lax.axis_index("gz")
-    for level in range(4):
-        rise = ((level - zbrick).astype(jnp.float32) - 0.5) * tall_scale
-        for dx, cell in enumerate(cells):
-            for dy in range(3):
-                if not wanted(dx, dy):
-                    continue
+    for kind_x, cell in enumerate(cells):
+        dx = away(kind_x, "gx")
+        for kind_y in range(3):
+            if not wanted(kind_x, kind_y):
+                continue
+            dy = away(kind_y, "gy")
+            for level in range(4):
                 brick = dx * 12 + dy * 4 + level
-                ghost_ref[brick, 0] = cell[level, dy, 0] + (dx - 1.5) * flat_scale
-                ghost_ref[brick, 1] = cell[level, dy, 1] + (dy - 1.5) * flat_scale
-                ghost_ref[brick, 2] = cell[level, dy, 2] + rise
+                shifts = (
+                    (jnp.float32(dx) - 1.5) * flat_scale,
+                    (jnp.float32(dy) - 1.5) * flat_scale,
+                    ((level - zbrick).astype(jnp.float32) - 0.5) * tall_scale,
+                )
+                for c in range(3):
+                    ghost_ref[brick, c] = cell[level, kind_y, c] + shifts[c]
     ghost_ref[36] = jnp.full(ghost_ref.shape[1:], far_away, jnp.float32)
 
 
@@ -223,7 +243,7 @@
 
 def density_sums(plan_in, cells, column_ref, late, plan_ref, ghost_ref, sum_ref, sem):
     def prepare():
-        put_ghosts(cells, ghost_ref, lambda dx, dy: (dx != 1) == late)
+        put_ghosts(cells, ghost_ref, lambda kind_x, kind_y: (kind_x != 1) == late)
         sum_ref[...] = jnp.zeros_like(sum_ref)
 
     def add(near, ghosts):
@@ -261,9 +281,9 @@
     selves_ref,
     early_ref,
     column_ref,
-    behind,
+    beside,
     middle,
-    ahead,
+    beyond,
     slope_ref,
     plan_ref,
     ghost_ref,
@@ -271,7 +291,7 @@
     row_ref,
     sem,
 ):
-    cells = (behind, middle, ahead)
+    cells = (beside, middle, beyond)
     density_sums(plan_in, cells, column_ref, True, plan_ref, ghost_ref, sum_ref, sem)
     for t in range(8):
         row_ref[t : t + 1, :] = row_sums(sum_ref[t])
@@ -285,9 +305,10 @@
     plan_in, cells, slope_cells, column_ref, slopes_ref, late, plan_ref, ghost_ref, sum_ref, sem
 ):
     def prepare():
-        put_ghosts(cells, ghost_ref, lambda dx, dy: (dy != 1) == late)
-        for dy, cell in enumerate(slope_cells):
-            if (dy != 1) == late:
+        put_ghosts(cells, ghost_ref, lambda kind_x, kind_y: (kind_y != 1) == late)
+        for kind, cell in enumerate(slope_cells):
+            if (kind != 1) == late:
+                dy = away(kind, "gy")
                 for dx in range(3):
                     for level in range(4):
                         ghost_ref[dx * 12 + dy * 4 + level, 3] = cell[dx * 4 + level]
@@ -420,28 +441,21 @@
     )
 
 
-def moved(values, axis, shift):
+def swapped(values, axis, kind):
     count = lax.axis_size(axis)
-    return lax.ppermute(values, axis, [((i + shift) % count, i) for i in range(count)])
-
-
-def migrants(packed):
-    return (
-        moved(packed[1], "gx", 1),
-        moved(packed[0], "gx", -1),
-        moved(packed[3], "gy", 1),
-        moved(packed[2], "gy", -1),
-    )
+    shift = 0 if kind == 0 else 1
+    other = [((i + shift) % count ^ 1) - shift for i in range(count)]
+    return lax.ppermute(values, axis, [(i, other[i] % count) for i in range(count)])
 
 
 def around(values, beside):
     ends, beside = lax.optimization_barrier(
-        ((moved(values, "gy", -1), moved(values, "gy", 1)), beside)
+        ((swapped(values, "gy", 0), swapped(values, "gy", 2)), beside)
     )
     rows = jnp.stack([ends[0], values, ends[1]])
     copies = jnp.broadcast_to(rows[None], (4,) + rows.shape)
     tower = lax.all_to_all(copies, "gz", 0, 0, tiled=True)
-    return (moved(tower, "gx", -1), tower, moved(tower, "gx", 1)), beside
+    return (swapped(tower, "gx", 0), tower, swapped(tower, "gx", 2)), beside
 
 
 def slope_column(values):
@@ -456,7 +470,6 @@
     live_count = counts.reshape(1)
     total = pair_count.reshape(1)
     steps = mig_slots.shape[0]
-    slots = mig_slots.reshape(steps, 4, 128)
     atoms = shaped(3, 8, 128)
     block = shaped(8, 128)
     columns = shaped(32, 128, 128)
@@ -473,19 +486,22 @@
             pltpu.SemaphoreType.DMA,
         )
 
-    rows = jnp.concatenate([a.reshape(3, 8, 128) for a in (positions, velocities, forces)], axis=0)
+    slots = mig_slots.reshape(1, 4 * steps, 128).astype(jnp.float32)
+    slots = jnp.pad(slots, ((0, 0), (0, 8 - 4 * steps), (0, 0)))
+    rows = [a.reshape(3, 8, 128) for a in (positions, velocities, forces)]
     place, speed, slots, *packed = call(
         pack_kernel,
-        [atoms, atoms, jax.ShapeDtypeStruct(slots.shape, jnp.int32)] + [block] * 4,
-        [VMEM] * 2,
-    )(rows, slots)
+        [atoms, atoms, jax.ShapeDtypeStruct((steps, 4, 128), jnp.int32)] + [block] * 4,
+        [VMEM],
+    )(jnp.concatenate(rows + [slots], axis=0))
     plans = call(
         plan_kernel, [plan_shape, plan_shape, block], [SMEM, SMEM, VMEM]
     )(total, live_count, pair_tiles.reshape(2, 128))
     for n in range(steps):
+        arrived = [swapped(sent, *swap) for sent, swap in zip(packed, swaps)]
         place, speed, sent = call(
             functools.partial(unpack_kernel, n), [atoms, atoms, atoms], [SMEM] + [VMEM] * 7
-        )(live_count, place, speed, slots, *migrants(packed))
+        )(live_count, place, speed, slots, *arrived)
         cells, plans = around(sent, plans)
         density_plan, force_plan, selves = plans
         column, early = call(
@@ -502,7 +518,7 @@
             pair_scratch(3, 1, pltpu.VMEM((8, 128), jnp.float32)),
         )(density_plan, selves, early, column, *cells)
         here = slope_column(slope)
-        below, above = moved(here, "gy", -1), moved(here, "gy", 1)
+        ends = swapped(here, "gy", 0), swapped(here, "gy", 2)
         slopes, early = call(
             early_force_kernel,
             [slope_columns, atoms],
@@ -520,8 +536,7 @@
             force_plan,
             *cells,
             column,
-            below,
-            above,
+            *ends,
             slopes,
             early,
             place,

time: 140 us -> 149 us (1.064); the launches traced: 139 us -> 146 us
  starting transfers between devices: 56.4 us -> 74.8 us
  Pallas kernels: 25 us -> 20 us
  waiting for transfers between devices: 8.51 us -> 4.09 us
  blocking collectives: 44.3 us -> 42.6 us
    ppermute x20, starting transfers between devices: 56.4 us -> 74.8 us  [swapped(): lax.ppermute(values, axis, [(i, other[i] % count) for i in range(count)])]
    ppermute x20, waiting for transfers between devices: 8.51 us -> 4.09 us  [swapped(): lax.ppermute(values, axis, [(i, other[i] % count) for i in range(count)])]
    all_to_all x2, blocking collectives: 27.7 us -> 25.5 us  [slope_column(): plane = lax.all_to_all(copies, ('gx', 'gz'), 0, 0, tiled=True)]
    pallas_call x2, Pallas kernels: 6.36 us -> 4.48 us  [per_device(): call(early_force_kernel, [slope_columns, atoms], [ANY] + [VMEM] * 6, pair...]
  transfers between devices with their start and end apart: 20 -> 20, of which waited for: 7 -> 7; matrix products, arithmetic and copies ran while one was open for 0% -> 0% of each run, Pallas kernels for 8% -> 6%
where the time goes in v4:
time: 149 us; the launch traced here: 146 us
  starting transfers between devices  74.8 us (50%)
  blocking collectives  42.6 us (29%)
  Pallas kernels  20 us (13%)
  waiting for transfers between devices  4.09 us (3%)
  between operations  2.3 us (2%)
    ppermute x20, starting transfers between devices, swapped(): lax.ppermute(values, axis, [(i, other[i] % count) for i in range(count)])  74.8 us
    all_to_all x2, blocking collectives, slope_column(): plane = lax.all_to_all(copies, ('gx', 'gz'), 0, 0, tiled=True)  25.5 us
    all_to_all x2, blocking collectives, around(): tower = lax.all_to_all(copies, 'gz', 0, 0, tiled=True)  17.1 us
    pallas_call x2, Pallas kernels, per_device(): call(functools.partial(late_force_kernel, None if last else n + 1), [atom...  6.46 us
    pallas_call x2, Pallas kernels, per_device(): call(early_force_kernel, [slope_columns, atoms], [ANY] + [VMEM] * 6, pair...  4.48 us
    ppermute x20, waiting for transfers between devices, swapped(): lax.ppermute(values, axis, [(i, other[i] % count) for i in range(count)])  4.09 us
    pallas_call x2, Pallas kernels, per_device(): call(late_density_kernel, [block], [ANY] + [VMEM] * 6, pair_scratch(3, 1,...  4.01 us
    pallas_call x2, Pallas kernels, per_device(): call(early_density_kernel, [columns, block], [ANY, VMEM], pair_scratch(3,...  3.84 us
  transfers between devices with their start and end apart: 20, of which 7 were waited for; matrix products, arithmetic and copies ran while one was open for 0% of the time, Pallas kernels for 6%

profile of v4, /device:TPU:1, one launch (start us, length us, event | category | flops | bytes accessed | tf_op | source)
XLA Modules:
  0.0 146.0 jit_solution(10471514939857016987)
XLA Ops:
  2.3 12.0 %collective-permute-start = (f32[8,128]{1,0:T(8,128)S(1)}, f32[8,128]{1,0:T(8,128)S(1)}, u32[]{:S(2)}, u32[]{:S(2)}) collective-permute-start(f32[8,128]{1,0:T(8,128)S(1)} %get-tuple-element.47), channel_id=1, source_target_pairs={{0,60},{4,8},{8,4},{12,16},{16,12},{20,24},{24,20},{28,32},{32,28}... | collective-permute-start | bytes 12296 | tf_op jit(solution)/shard_map/ppermute | solution.py:448
  14.3 4.0 %collective-permute-start.1 = (f32[8,128]{1,0:T(8,128)S(1)}, f32[8,128]{1,0:T(8,128)S(1)}, u32[]{:S(2)}, u32[]{:S(2)}) collective-permute-start(f32[8,128]{1,0:T(8,128)S(1)} %get-tuple-element.48), channel_id=1, source_target_pairs={{0,448},{64,128},{128,64},{192,256},{256,192},{320,384},{384,320},... | collective-permute-start | bytes 12296 | tf_op jit(solution)/shard_map/ppermute | solution.py:448
  18.2 1.9 %collective-permute-start.2 = (f32[8,128]{1,0:T(8,128)S(1)}, f32[8,128]{1,0:T(8,128)S(1)}, u32[]{:S(2)}, u32[]{:S(2)}) collective-permute-start(f32[8,128]{1,0:T(8,128)S(1)} %get-tuple-element.49), channel_id=1, source_target_pairs={{0,4},{4,0},{8,12},{12,8},{16,20},{20,16},{24,28},{28,24},{32,36},... | collective-permute-start | bytes 12296 | tf_op jit(solution)/shard_map/ppermute | solution.py:448
  20.2 2.7 %collective-permute-start.3 = (f32[8,128]{1,0:T(8,128)S(1)}, f32[8,128]{1,0:T(8,128)S(1)}, u32[]{:S(2)}, u32[]{:S(2)}) collective-permute-start(f32[8,128]{1,0:T(8,128)S(1)} %get-tuple-element.50), channel_id=1, source_target_pairs={{0,64},{64,0},{128,192},{192,128},{256,320},{320,256},{384,448},{4... | collective-permute-start | bytes 12296 | tf_op jit(solution)/shard_map/ppermute | solution.py:448
  24.0 3.6 %collective-permute-start.5 = (f32[3,8,128]{2,1,0:T(8,128)S(1)}, f32[3,8,128]{2,1,0:T(8,128)S(1)}, u32[]{:S(2)}, u32[]{:S(2)}) collective-permute-start(f32[3,8,128]{2,1,0:T(8,128)S(1)} %get-tuple-element.51), channel_id=1, source_target_pairs={{0,60},{4,8},{8,4},{12,16},{16,12},{20,24},{24,20},{28,32},{32,28}... | collective-permute-start | bytes 36872 | tf_op jit(solution)/shard_map/ppermute | solution.py:448
  27.6 1.9 %collective-permute-start.4 = (f32[3,8,128]{2,1,0:T(8,128)S(1)}, f32[3,8,128]{2,1,0:T(8,128)S(1)}, u32[]{:S(2)}, u32[]{:S(2)}) collective-permute-start(f32[3,8,128]{2,1,0:T(8,128)S(1)} %get-tuple-element.51), channel_id=1, source_target_pairs={{0,4},{4,0},{8,12},{12,8},{16,20},{20,16},{24,28},{28,24},{32,36},... | collective-permute-start | bytes 36872 | tf_op jit(solution)/shard_map/ppermute | solution.py:448
  32.1 8.9 %all_to_all.20.middle.c1 = f32[4,3,3,8,128]{4,3,2,1,0:T(8,128)S(1)} all-to-all(f32[4,3,3,8,128]{4,3,2,1,0:T(8,128)S(1)} %broadcast_in_dim.8), channel_id=1, replica_groups=mesh['gx'=8,'gy'=16,'gz'=4] {'gz'}, dimensions={0} | all-to-all | bytes 294912 | tf_op jit(solution)/shard_map/all_to_all | solution.py:457
  41.0 5.3 %collective-permute-start.7 = (f32[4,3,3,8,128]{4,3,2,1,0:T(8,128)S(1)}, f32[4,3,3,8,128]{4,3,2,1,0:T(8,128)S(1)}, u32[]{:S(2)}, u32[]{:S(2)}) collective-permute-start(f32[4,3,3,8,128]{4,3,2,1,0:T(8,128)S(1)} %all_to_all.20.middle.c1), channel_id=1, source_target_pairs={{0,448},{64,128},{128,64},{192,256},{256,192},{320,384},{384,320},... | collective-permute-start | bytes 442376 | tf_op jit(solution)/shard_map/ppermute | solution.py:448
  46.2 1.9 %collective-permute-start.6 = (f32[4,3,3,8,128]{4,3,2,1,0:T(8,128)S(1)}, f32[4,3,3,8,128]{4,3,2,1,0:T(8,128)S(1)}, u32[]{:S(2)}, u32[]{:S(2)}) collective-permute-start(f32[4,3,3,8,128]{4,3,2,1,0:T(8,128)S(1)} %all_to_all.20.middle.c1), channel_id=1, source_target_pairs={{0,64},{64,0},{128,192},{192,128},{256,320},{320,256},{384,448},{4... | collective-permute-start | bytes 442376 | tf_op jit(solution)/shard_map/ppermute | solution.py:448
  48.2 1.9 %shard_map.89 = (f32[32,128,128]{2,1,0:T(8,128)S(1)}, f32[8,128]{1,0:T(8,128)S(1)}) custom-call(s32[8,128]{1,0:T(8,128)S(1)} %get-tuple-element.76.plan_in, f32[4,3,3,8,128]{4,3,2,1,0:T(8,128)S(1)} %all_to_all.20.middle.c1), custom_call_target="tpu_custom_call" | custom-call | flops 60000000 | bytes 6000000 | tf_op jit(solution)/shard_map/pallas_call | solution.py:507
  50.1 2.0 %shard_map.90.own_slope = f32[8,128]{1,0:T(8,128)S(1)} custom-call(s32[8,128]{1,0:T(8,128)S(1)} %get-tuple-element.76.plan_in, f32[8,128]{1,0:T(8,128)S(1)} %get-tuple-element.78.selves_ref, f32[8,128]{1,0:T(8,128)S(1)} %get-tuple-element.61.early_ref, f32[32,128,128]{2,1,0:T(8,128)S(1)} %get-tuple-element.59.column_ref, ...), custom_call_target="tpu_custom_call" | custom-call | flops 1000000 | bytes 100000 | tf_op jit(solution)/shard_map/pallas_call | solution.py:514
  52.1 13.1 %all_to_all.21.plane_ref = f32[32,8,128]{2,1,0:T(8,128)S(1)} all-to-all(f32[32,8,128]{2,1,0:T(8,128)S(1)} %broadcast_in_dim.9), channel_id=1, replica_groups=mesh['gx'=8,'gy'=16,'gz'=4] {'gx','gz'}, dimensions={0} | all-to-all | bytes 262144 | tf_op jit(solution)/shard_map/all_to_all | solution.py:464
  65.2 5.0 %collective-permute-start.9 = (f32[12,8,128]{2,1,0:T(8,128)S(1)}, f32[12,8,128]{2,1,0:T(8,128)S(1)}, u32[]{:S(2)}, u32[]{:S(2)}) collective-permute-start(f32[12,8,128]{2,1,0:T(8,128)S(1)} %shard_map.91.s1), channel_id=1, source_target_pairs={{0,60},{4,8},{8,4},{12,16},{16,12},{20,24},{24,20},{28,32},{32,28}... | collective-permute-start | bytes 147464 | tf_op jit(solution)/shard_map/ppermute | solution.py:448
  70.2 1.9 %collective-permute-start.8 = (f32[12,8,128]{2,1,0:T(8,128)S(1)}, f32[12,8,128]{2,1,0:T(8,128)S(1)}, u32[]{:S(2)}, u32[]{:S(2)}) collective-permute-start(f32[12,8,128]{2,1,0:T(8,128)S(1)} %shard_map.91.s1), channel_id=1, source_target_pairs={{0,4},{4,0},{8,12},{12,8},{16,20},{20,16},{24,28},{28,24},{32,36},... | collective-permute-start | bytes 147464 | tf_op jit(solution)/shard_map/ppermute | solution.py:448
  72.2 2.2 %shard_map.92 = (f32[8,128,128]{2,1,0:T(8,128)S(1)}, f32[3,8,128]{2,1,0:T(8,128)S(1)}) custom-call(s32[8,128]{1,0:T(8,128)S(1)} %get-tuple-element.73.plan_in, f32[4,3,3,8,128]{4,3,2,1,0:T(8,128)S(1)} %collective-permute-done.6.beside.c0, f32[4,3,3,8,128]{4,3,2,1,0:T(8,128)S(1)} %all_to_all.20.middle.c1, ...), custom_call_target="tpu_custom_call" | custom-call | flops 60000000 | bytes 6000000 | tf_op jit(solution)/shard_map/pallas_call | solution.py:522
  75.1 3.0 %shard_map.93 = (f32[3,8,128]{2,1,0:T(8,128)S(1)}, f32[3,8,128]{2,1,0:T(8,128)S(1)}, f32[8,128]{1,0:T(8,128)S(1)}, f32[8,128]{1,0:T(8,128)S(1)}, f32[8,128]{1,0:T(8,128)S(1)}, /*index=5*/f32[8,128]{1,0:T(8,128)S(1)}) custom-call(s32[8,128]{1,0:T(8,128)S(1)} %get-tuple-element.73.plan_in, f32[4,3,3,8,128]{4,3,2,1,0:T(8,128)S(1)} %collective-permute-done.6.beside.c0, ...), custom_call_target="tpu_custom_call" | custom-call | flops 1000000 | bytes 100000 | tf_op jit(solution)/shard_map/pallas_call | solution.py:530
  78.1 2.6 %collective-permute-start.10 = (f32[8,128]{1,0:T(8,128)S(1)}, f32[8,128]{1,0:T(8,128)S(1)}, u32[]{:S(2)}, u32[]{:S(2)}) collective-permute-start(f32[8,128]{1,0:T(8,128)S(1)} %get-tuple-element.68), channel_id=1, source_target_pairs={{0,60},{4,8},{8,4},{12,16},{16,12},{20,24},{24,20},{28,32},{32,28}... | collective-permute-start | bytes 12296 | tf_op jit(solution)/shard_map/ppermute | solution.py:448
  80.8 3.5 %collective-permute-start.11 = (f32[8,128]{1,0:T(8,128)S(1)}, f32[8,128]{1,0:T(8,128)S(1)}, u32[]{:S(2)}, u32[]{:S(2)}) collective-permute-start(f32[8,128]{1,0:T(8,128)S(1)} %get-tuple-element.69), channel_id=1, source_target_pairs={{0,448},{64,128},{128,64},{192,256},{256,192},{320,384},{384,320},... | collective-permute-start | bytes 12296 | tf_op jit(solution)/shard_map/ppermute | solution.py:448
  84.3 2.7 %collective-permute-start.12 = (f32[8,128]{1,0:T(8,128)S(1)}, f32[8,128]{1,0:T(8,128)S(1)}, u32[]{:S(2)}, u32[]{:S(2)}) collective-permute-start(f32[8,128]{1,0:T(8,128)S(1)} %get-tuple-element.70), channel_id=1, source_target_pairs={{0,4},{4,0},{8,12},{12,8},{16,20},{20,16},{24,28},{28,24},{32,36},... | collective-permute-start | bytes 12296 | tf_op jit(solution)/shard_map/ppermute | solution.py:448
  86.9 5.8 %collective-permute-start.13 = (f32[8,128]{1,0:T(8,128)S(1)}, f32[8,128]{1,0:T(8,128)S(1)}, u32[]{:S(2)}, u32[]{:S(2)}) collective-permute-start(f32[8,128]{1,0:T(8,128)S(1)} %get-tuple-element.71), channel_id=1, source_target_pairs={{0,64},{64,0},{128,192},{192,128},{256,320},{320,256},{384,448},{4... | collective-permute-start | bytes 12296 | tf_op jit(solution)/shard_map/ppermute | solution.py:448
  93.7 2.1 %collective-permute-start.15 = (f32[3,8,128]{2,1,0:T(8,128)S(1)}, f32[3,8,128]{2,1,0:T(8,128)S(1)}, u32[]{:S(2)}, u32[]{:S(2)}) collective-permute-start(f32[3,8,128]{2,1,0:T(8,128)S(1)} %get-tuple-element.72), channel_id=1, source_target_pairs={{0,60},{4,8},{8,4},{12,16},{16,12},{20,24},{24,20},{28,32},{32,28}... | collective-permute-start | bytes 36872 | tf_op jit(solution)/shard_map/ppermute | solution.py:448
  95.9 3.4 %collective-permute-start.14 = (f32[3,8,128]{2,1,0:T(8,128)S(1)}, f32[3,8,128]{2,1,0:T(8,128)S(1)}, u32[]{:S(2)}, u32[]{:S(2)}) collective-permute-start(f32[3,8,128]{2,1,0:T(8,128)S(1)} %get-tuple-element.72), channel_id=1, source_target_pairs={{0,4},{4,0},{8,12},{12,8},{16,20},{20,16},{24,28},{28,24},{32,36},... | collective-permute-start | bytes 36872 | tf_op jit(solution)/shard_map/ppermute | solution.py:448
  100.5 8.2 %all_to_all.22.middle.c1 = f32[4,3,3,8,128]{4,3,2,1,0:T(8,128)S(1)} all-to-all(f32[4,3,3,8,128]{4,3,2,1,0:T(8,128)S(1)} %broadcast_in_dim.10), channel_id=1, replica_groups=mesh['gx'=8,'gy'=16,'gz'=4] {'gz'}, dimensions={0} | all-to-all | bytes 294912 | tf_op jit(solution)/shard_map/all_to_all | solution.py:457
  108.7 6.4 %collective-permute-start.17 = (f32[4,3,3,8,128]{4,3,2,1,0:T(8,128)S(1)}, f32[4,3,3,8,128]{4,3,2,1,0:T(8,128)S(1)}, u32[]{:S(2)}, u32[]{:S(2)}) collective-permute-start(f32[4,3,3,8,128]{4,3,2,1,0:T(8,128)S(1)} %all_to_all.22.middle.c1), channel_id=1, source_target_pairs={{0,448},{64,128},{128,64},{192,256},{256,192},{320,384},{384,320},... | collective-permute-start | bytes 442376 | tf_op jit(solution)/shard_map/ppermute | solution.py:448
  115.2 1.9 %collective-permute-start.16 = (f32[4,3,3,8,128]{4,3,2,1,0:T(8,128)S(1)}, f32[4,3,3,8,128]{4,3,2,1,0:T(8,128)S(1)}, u32[]{:S(2)}, u32[]{:S(2)}) collective-permute-start(f32[4,3,3,8,128]{4,3,2,1,0:T(8,128)S(1)} %all_to_all.22.middle.c1), channel_id=1, source_target_pairs={{0,64},{64,0},{128,192},{192,128},{256,320},{320,256},{384,448},{4... | collective-permute-start | bytes 442376 | tf_op jit(solution)/shard_map/ppermute | solution.py:448
  117.1 1.9 %shard_map.95 = (f32[32,128,128]{2,1,0:T(8,128)S(1)}, f32[8,128]{1,0:T(8,128)S(1)}) custom-call(s32[8,128]{1,0:T(8,128)S(1)} %get-tuple-element.76.plan_in, f32[4,3,3,8,128]{4,3,2,1,0:T(8,128)S(1)} %all_to_all.22.middle.c1), custom_call_target="tpu_custom_call" | custom-call | flops 60000000 | bytes 6000000 | tf_op jit(solution)/shard_map/pallas_call | solution.py:507
  119.0 2.0 %shard_map.96.own_slope = f32[8,128]{1,0:T(8,128)S(1)} custom-call(s32[8,128]{1,0:T(8,128)S(1)} %get-tuple-element.76.plan_in, f32[8,128]{1,0:T(8,128)S(1)} %get-tuple-element.78.selves_ref, f32[8,128]{1,0:T(8,128)S(1)} %get-tuple-element.79.early_ref, f32[32,128,128]{2,1,0:T(8,128)S(1)} %get-tuple-element.77.column_ref, ...), custom_call_target="tpu_custom_call" | custom-call | flops 1000000 | bytes 100000 | tf_op jit(solution)/shard_map/pallas_call | solution.py:514
  121.1 12.5 %all_to_all.23.plane_ref = f32[32,8,128]{2,1,0:T(8,128)S(1)} all-to-all(f32[32,8,128]{2,1,0:T(8,128)S(1)} %broadcast_in_dim.11), channel_id=1, replica_groups=mesh['gx'=8,'gy'=16,'gz'=4] {'gx','gz'}, dimensions={0} | all-to-all | bytes 262144 | tf_op jit(solution)/shard_map/all_to_all | solution.py:464
  133.6 4.2 %collective-permute-start.19 = (f32[12,8,128]{2,1,0:T(8,128)S(1)}, f32[12,8,128]{2,1,0:T(8,128)S(1)}, u32[]{:S(2)}, u32[]{:S(2)}) collective-permute-start(f32[12,8,128]{2,1,0:T(8,128)S(1)} %shard_map.97.s1), channel_id=1, source_target_pairs={{0,60},{4,8},{8,4},{12,16},{16,12},{20,24},{24,20},{28,32},{32,28}... | collective-permute-start | bytes 147464 | tf_op jit(solution)/shard_map/ppermute | solution.py:448
  137.8 1.9 %collective-permute-start.18 = (f32[12,8,128]{2,1,0:T(8,128)S(1)}, f32[12,8,128]{2,1,0:T(8,128)S(1)}, u32[]{:S(2)}, u32[]{:S(2)}) collective-permute-start(f32[12,8,128]{2,1,0:T(8,128)S(1)} %shard_map.97.s1), channel_id=1, source_target_pairs={{0,4},{4,0},{8,12},{12,8},{16,20},{20,16},{24,28},{28,24},{32,36},... | collective-permute-start | bytes 147464 | tf_op jit(solution)/shard_map/ppermute | solution.py:448
  139.7 2.2 %shard_map.98 = (f32[8,128,128]{2,1,0:T(8,128)S(1)}, f32[3,8,128]{2,1,0:T(8,128)S(1)}) custom-call(s32[8,128]{1,0:T(8,128)S(1)} %get-tuple-element.73.plan_in, f32[4,3,3,8,128]{4,3,2,1,0:T(8,128)S(1)} %collective-permute-done.16.beside.c0, f32[4,3,3,8,128]{4,3,2,1,0:T(8,128)S(1)} %all_to_all.22.middle.c1, ...), custom_call_target="tpu_custom_call" | custom-call | flops 60000000 | bytes 6000000 | tf_op jit(solution)/shard_map/pallas_call | solution.py:522
  142.6 3.4 %shard_map.99 = (f32[3,8,128]{2,1,0:T(8,128)}, f32[3,8,128]{2,1,0:T(8,128)}) custom-call(s32[8,128]{1,0:T(8,128)S(1)} %get-tuple-element.73.plan_in, f32[4,3,3,8,128]{4,3,2,1,0:T(8,128)S(1)} %collective-permute-done.16.beside.c0, f32[4,3,3,8,128]{4,3,2,1,0:T(8,128)S(1)} %all_to_all.22.middle.c1, f32[4,3,3,8,128]{4,3,2,1,0:T(8,128)S(1)} %collective-permute-done.17.beyond.c2, ...), custom_call_target="tpu_custom_call" | custom-call | flops 1000000 | bytes 100000 | tf_op jit(solution)/shard_map/pallas_call | solution.py:530
  (36 shorter events, 7.5 us)
Async XLA Ops:
  2.3 21.2 %collective-permute-start = (f32[8,128]{1,0:T(8,128)S(1)}, f32[8,128]{1,0:T(8,128)S(1)}, u32[]{:S(2)}, u32[]{:S(2)}) collective-permute-start(f32[8,128]{1,0:T(8,128)S(1)} %get-tuple-element.47), channel_id=1, source_target_pairs={{0,60},{4,8},{8,4},{12,16},{16,12},{20,24},{24,20},{28,32},{32,28}... | collective-permute-start | bytes 12296 | tf_op jit(solution)/shard_map/ppermute | solution.py:448
  14.3 9.3 %collective-permute-start.1 = (f32[8,128]{1,0:T(8,128)S(1)}, f32[8,128]{1,0:T(8,128)S(1)}, u32[]{:S(2)}, u32[]{:S(2)}) collective-permute-start(f32[8,128]{1,0:T(8,128)S(1)} %get-tuple-element.48), channel_id=1, source_target_pairs={{0,448},{64,128},{128,64},{192,256},{256,192},{320,384},{384,320},... | collective-permute-start | bytes 12296 | tf_op jit(solution)/shard_map/ppermute | solution.py:448
  18.2 5.3 %collective-permute-start.2 = (f32[8,128]{1,0:T(8,128)S(1)}, f32[8,128]{1,0:T(8,128)S(1)}, u32[]{:S(2)}, u32[]{:S(2)}) collective-permute-start(f32[8,128]{1,0:T(8,128)S(1)} %get-tuple-element.49), channel_id=1, source_target_pairs={{0,4},{4,0},{8,12},{12,8},{16,20},{20,16},{24,28},{28,24},{32,36},... | collective-permute-start | bytes 12296 | tf_op jit(solution)/shard_map/ppermute | solution.py:448
  20.2 3.5 %collective-permute-start.3 = (f32[8,128]{1,0:T(8,128)S(1)}, f32[8,128]{1,0:T(8,128)S(1)}, u32[]{:S(2)}, u32[]{:S(2)}) collective-permute-start(f32[8,128]{1,0:T(8,128)S(1)} %get-tuple-element.50), channel_id=1, source_target_pairs={{0,64},{64,0},{128,192},{192,128},{256,320},{320,256},{384,448},{4... | collective-permute-start | bytes 12296 | tf_op jit(solution)/shard_map/ppermute | solution.py:448
  24.0 7.4 %collective-permute-start.5 = (f32[3,8,128]{2,1,0:T(8,128)S(1)}, f32[3,8,128]{2,1,0:T(8,128)S(1)}, u32[]{:S(2)}, u32[]{:S(2)}) collective-permute-start(f32[3,8,128]{2,1,0:T(8,128)S(1)} %get-tuple-element.51), channel_id=1, source_target_pairs={{0,60},{4,8},{8,4},{12,16},{16,12},{20,24},{24,20},{28,32},{32,28}... | collective-permute-start | bytes 36872 | tf_op jit(solution)/shard_map/ppermute | solution.py:448
  27.6 4.4 %collective-permute-start.4 = (f32[3,8,128]{2,1,0:T(8,128)S(1)}, f32[3,8,128]{2,1,0:T(8,128)S(1)}, u32[]{:S(2)}, u32[]{:S(2)}) collective-permute-start(f32[3,8,128]{2,1,0:T(8,128)S(1)} %get-tuple-element.51), channel_id=1, source_target_pairs={{0,4},{4,0},{8,12},{12,8},{16,20},{20,16},{24,28},{28,24},{32,36},... | collective-permute-start | bytes 36872 | tf_op jit(solution)/shard_map/ppermute | solution.py:448
  30.2 0.7 copy-start
  41.0 9.1 %collective-permute-start.7 = (f32[4,3,3,8,128]{4,3,2,1,0:T(8,128)S(1)}, f32[4,3,3,8,128]{4,3,2,1,0:T(8,128)S(1)}, u32[]{:S(2)}, u32[]{:S(2)}) collective-permute-start(f32[4,3,3,8,128]{4,3,2,1,0:T(8,128)S(1)} %all_to_all.20.middle.c1), channel_id=1, source_target_pairs={{0,448},{64,128},{128,64},{192,256},{256,192},{320,384},{384,320},... | collective-permute-start | bytes 442376 | tf_op jit(solution)/shard_map/ppermute | solution.py:448
  46.2 3.9 %collective-permute-start.6 = (f32[4,3,3,8,128]{4,3,2,1,0:T(8,128)S(1)}, f32[4,3,3,8,128]{4,3,2,1,0:T(8,128)S(1)}, u32[]{:S(2)}, u32[]{:S(2)}) collective-permute-start(f32[4,3,3,8,128]{4,3,2,1,0:T(8,128)S(1)} %all_to_all.20.middle.c1), channel_id=1, source_target_pairs={{0,64},{64,0},{128,192},{192,128},{256,320},{320,256},{384,448},{4... | collective-permute-start | bytes 442376 | tf_op jit(solution)/shard_map/ppermute | solution.py:448
  65.2 9.2 %collective-permute-start.9 = (f32[12,8,128]{2,1,0:T(8,128)S(1)}, f32[12,8,128]{2,1,0:T(8,128)S(1)}, u32[]{:S(2)}, u32[]{:S(2)}) collective-permute-start(f32[12,8,128]{2,1,0:T(8,128)S(1)} %shard_map.91.s1), channel_id=1, source_target_pairs={{0,60},{4,8},{8,4},{12,16},{16,12},{20,24},{24,20},{28,32},{32,28}... | collective-permute-start | bytes 147464 | tf_op jit(solution)/shard_map/ppermute | solution.py:448
  70.2 4.8 %collective-permute-start.8 = (f32[12,8,128]{2,1,0:T(8,128)S(1)}, f32[12,8,128]{2,1,0:T(8,128)S(1)}, u32[]{:S(2)}, u32[]{:S(2)}) collective-permute-start(f32[12,8,128]{2,1,0:T(8,128)S(1)} %shard_map.91.s1), channel_id=1, source_target_pairs={{0,4},{4,0},{8,12},{12,8},{16,20},{20,16},{24,28},{28,24},{32,36},... | collective-permute-start | bytes 147464 | tf_op jit(solution)/shard_map/ppermute | solution.py:448
  78.1 14.6 %collective-permute-start.10 = (f32[8,128]{1,0:T(8,128)S(1)}, f32[8,128]{1,0:T(8,128)S(1)}, u32[]{:S(2)}, u32[]{:S(2)}) collective-permute-start(f32[8,128]{1,0:T(8,128)S(1)} %get-tuple-element.68), channel_id=1, source_target_pairs={{0,60},{4,8},{8,4},{12,16},{16,12},{20,24},{24,20},{28,32},{32,28}... | collective-permute-start | bytes 12296 | tf_op jit(solution)/shard_map/ppermute | solution.py:448
  80.8 12.0 %collective-permute-start.11 = (f32[8,128]{1,0:T(8,128)S(1)}, f32[8,128]{1,0:T(8,128)S(1)}, u32[]{:S(2)}, u32[]{:S(2)}) collective-permute-start(f32[8,128]{1,0:T(8,128)S(1)} %get-tuple-element.69), channel_id=1, source_target_pairs={{0,448},{64,128},{128,64},{192,256},{256,192},{320,384},{384,320},... | collective-permute-start | bytes 12296 | tf_op jit(solution)/shard_map/ppermute | solution.py:448
  84.3 8.5 %collective-permute-start.12 = (f32[8,128]{1,0:T(8,128)S(1)}, f32[8,128]{1,0:T(8,128)S(1)}, u32[]{:S(2)}, u32[]{:S(2)}) collective-permute-start(f32[8,128]{1,0:T(8,128)S(1)} %get-tuple-element.70), channel_id=1, source_target_pairs={{0,4},{4,0},{8,12},{12,8},{16,20},{20,16},{24,28},{28,24},{32,36},... | collective-permute-start | bytes 12296 | tf_op jit(solution)/shard_map/ppermute | solution.py:448
  86.9 6.6 %collective-permute-start.13 = (f32[8,128]{1,0:T(8,128)S(1)}, f32[8,128]{1,0:T(8,128)S(1)}, u32[]{:S(2)}, u32[]{:S(2)}) collective-permute-start(f32[8,128]{1,0:T(8,128)S(1)} %get-tuple-element.71), channel_id=1, source_target_pairs={{0,64},{64,0},{128,192},{192,128},{256,320},{320,256},{384,448},{4... | collective-permute-start | bytes 12296 | tf_op jit(solution)/shard_map/ppermute | solution.py:448
  93.7 5.7 %collective-permute-start.15 = (f32[3,8,128]{2,1,0:T(8,128)S(1)}, f32[3,8,128]{2,1,0:T(8,128)S(1)}, u32[]{:S(2)}, u32[]{:S(2)}) collective-permute-start(f32[3,8,128]{2,1,0:T(8,128)S(1)} %get-tuple-element.72), channel_id=1, source_target_pairs={{0,60},{4,8},{8,4},{12,16},{16,12},{20,24},{24,20},{28,32},{32,28}... | collective-permute-start | bytes 36872 | tf_op jit(solution)/shard_map/ppermute | solution.py:448
  95.9 4.6 %collective-permute-start.14 = (f32[3,8,128]{2,1,0:T(8,128)S(1)}, f32[3,8,128]{2,1,0:T(8,128)S(1)}, u32[]{:S(2)}, u32[]{:S(2)}) collective-permute-start(f32[3,8,128]{2,1,0:T(8,128)S(1)} %get-tuple-element.72), channel_id=1, source_target_pairs={{0,4},{4,0},{8,12},{12,8},{16,20},{20,16},{24,28},{28,24},{32,36},... | collective-permute-start | bytes 36872 | tf_op jit(solution)/shard_map/ppermute | solution.py:448
  108.7 10.3 %collective-permute-start.17 = (f32[4,3,3,8,128]{4,3,2,1,0:T(8,128)S(1)}, f32[4,3,3,8,128]{4,3,2,1,0:T(8,128)S(1)}, u32[]{:S(2)}, u32[]{:S(2)}) collective-permute-start(f32[4,3,3,8,128]{4,3,2,1,0:T(8,128)S(1)} %all_to_all.22.middle.c1), channel_id=1, source_target_pairs={{0,448},{64,128},{128,64},{192,256},{256,192},{320,384},{384,320},... | collective-permute-start | bytes 442376 | tf_op jit(solution)/shard_map/ppermute | solution.py:448
  115.2 3.9 %collective-permute-start.16 = (f32[4,3,3,8,128]{4,3,2,1,0:T(8,128)S(1)}, f32[4,3,3,8,128]{4,3,2,1,0:T(8,128)S(1)}, u32[]{:S(2)}, u32[]{:S(2)}) collective-permute-start(f32[4,3,3,8,128]{4,3,2,1,0:T(8,128)S(1)} %all_to_all.22.middle.c1), channel_id=1, source_target_pairs={{0,64},{64,0},{128,192},{192,128},{256,320},{320,256},{384,448},{4... | collective-permute-start | bytes 442376 | tf_op jit(solution)/shard_map/ppermute | solution.py:448
  133.6 8.4 %collective-permute-start.19 = (f32[12,8,128]{2,1,0:T(8,128)S(1)}, f32[12,8,128]{2,1,0:T(8,128)S(1)}, u32[]{:S(2)}, u32[]{:S(2)}) collective-permute-start(f32[12,8,128]{2,1,0:T(8,128)S(1)} %shard_map.97.s1), channel_id=1, source_target_pairs={{0,60},{4,8},{8,4},{12,16},{16,12},{20,24},{24,20},{28,32},{32,28}... | collective-permute-start | bytes 147464 | tf_op jit(solution)/shard_map/ppermute | solution.py:448
  137.8 4.8 %collective-permute-start.18 = (f32[12,8,128]{2,1,0:T(8,128)S(1)}, f32[12,8,128]{2,1,0:T(8,128)S(1)}, u32[]{:S(2)}, u32[]{:S(2)}) collective-permute-start(f32[12,8,128]{2,1,0:T(8,128)S(1)} %shard_map.97.s1), channel_id=1, source_target_pairs={{0,4},{4,0},{8,12},{12,8},{16,20},{20,16},{24,28},{28,24},{32,36},... | collective-permute-start | bytes 147464 | tf_op jit(solution)/shard_map/ppermute | solution.py:448

commit v5 on v3

--- a/solution.py
+++ b/solution.py
@@ -102,15 +102,13 @@
     plan_ref[3:8, :] = jnp.zeros((5, 128), jnp.int32)
 
 
-def plan_kernel(total_ref, count_ref, tiles_ref, density_plan, force_plan, selves_ref):
+def plan_kernel(total_ref, count_ref, tiles_ref, plan_ref, selves_ref):
     zbrick = lax.axis_index("gz")
     near = tiles_ref[0:1, :]
     far = tiles_ref[1:2, :]
     listed = lax.broadcasted_iota(jnp.int32, (1, 128), 1) < total_ref[0]
     listed = jnp.logical_and(listed, near * 128 < count_ref[0])
-    brick = far >> 3
-    put_plan(listed, near, far, jnp.logical_or(brick < 12, brick >= 24), density_plan)
-    put_plan(listed, near, far, ((brick >> 2) + 2) % 3 != 0, force_plan)
+    put_plan(listed, near, far, ((far >> 5) + 2) % 3 != 0, plan_ref)
     rows = lax.broadcasted_iota(jnp.int32, (16, 128), 0)
     itself = jnp.logical_and(listed, far == (16 + zbrick) * 8 + near)
     itself = jnp.where(jnp.logical_and(itself, rows == near), 1.0, 0.0).astype(jnp.bfloat16)
@@ -162,24 +160,24 @@
         sent_ref[c] = jnp.where(live, place * scales[c], far_away)
 
 
-def put_ghosts(cells, ghost_ref, wanted):
+def put_ghosts(cells, ghost_ref, late):
     zbrick = lax.axis_index("gz")
-    for level in range(4):
-        rise = ((level - zbrick).astype(jnp.float32) - 0.5) * tall_scale
-        for dx, cell in enumerate(cells):
-            for dy in range(3):
-                if not wanted(dx, dy):
-                    continue
+    for dy, cell in enumerate(cells):
+        if (dy != 1) != late:
+            continue
+        for dx in range(3):
+            for level in range(4):
+                rise = ((level - zbrick).astype(jnp.float32) - 0.5) * tall_scale
                 brick = dx * 12 + dy * 4 + level
-                ghost_ref[brick, 0] = cell[level, dy, 0] + (dx - 1.5) * flat_scale
-                ghost_ref[brick, 1] = cell[level, dy, 1] + (dy - 1.5) * flat_scale
-                ghost_ref[brick, 2] = cell[level, dy, 2] + rise
+                ghost_ref[brick, 0] = cell[dx * 4 + level, 0] + (dx - 1.5) * flat_scale
+                ghost_ref[brick, 1] = cell[dx * 4 + level, 1] + (dy - 1.5) * flat_scale
+                ghost_ref[brick, 2] = cell[dx * 4 + level, 2] + rise
     ghost_ref[36] = jnp.full(ghost_ref.shape[1:], far_away, jnp.float32)
 
 
-def own_places(middle):
-    zbrick = lax.axis_index("gz")
-    own = [middle[zbrick, 1, c] for c in range(3)]
+def own_places(here):
+    at = lax.axis_index("gz") + 4
+    own = [here[at, c] for c in range(3)]
     live = own[0] < 0.5 * far_away
     shifts = (0.5 * flat_scale, 0.5 * flat_scale, 0.5 * tall_scale)
     return [jnp.where(live, row - shift, -far_away) for row, shift in zip(own, shifts)], live
@@ -207,12 +205,14 @@
     copy.start()
     prepare()
     copy.wait()
+    begin = plan_ref[2, 8] if late else 0
 
     def over_tile(near, carry):
         def over_group(group, carry):
             first = group * unrolled
             codes = [plan_ref[(first + i) >> 7, (first + i) & 127] for i in range(unrolled)]
-            body(near, [(code >> 3, code & 7) for code in codes])
+            spots = [(group - begin) * unrolled + i for i in range(unrolled)]
+            body(near, [(code >> 3, code & 7) for code in codes], spots)
             return carry
 
         segment = near + 8 * late
@@ -221,12 +221,12 @@
     lax.fori_loop(0, 8, over_tile, 0)
 
 
-def density_sums(plan_in, cells, column_ref, late, plan_ref, ghost_ref, sum_ref, sem):
+def density_sums(plan_in, cells, column_ref, late, shrink_ref, plan_ref, ghost_ref, sum_ref, sem):
     def prepare():
-        put_ghosts(cells, ghost_ref, lambda dx, dy: (dx != 1) == late)
+        put_ghosts(cells, ghost_ref, late)
         sum_ref[...] = jnp.zeros_like(sum_ref)
 
-    def add(near, ghosts):
+    def add(near, ghosts, spots):
         far = []
         for brick, tile in ghosts:
             x, y, z = (ghost_ref[brick, c, pl.ds(tile, 1), :] for c in range(3))
@@ -236,8 +236,9 @@
             part = pl.ds(8 * r, 8)
             ax, ay, az, rest = (column_ref[8 * c + near, part, :] for c in range(4))
             total = sum_ref[near, part, :]
-            for cx, cy, cz, cn in far:
+            for (cx, cy, cz, cn), spot in zip(far, spots):
                 shrink = jnp.maximum((ax * cx + ay * cy) + (az * cz + (rest + cn)), 0.0)
+                shrink_ref[spot, part, :] = shrink
                 total = total + shrink * shrink * shrink
             sum_ref[near, part, :] = total
 
@@ -245,13 +246,13 @@
 
 
 def early_density_kernel(
-    plan_in, middle, column_ref, early_ref, plan_ref, ghost_ref, sum_ref, sem
+    plan_in, here, column_ref, early_ref, shrink_ref, plan_ref, ghost_ref, sum_ref, sem
 ):
-    own, _ = own_places(middle)
+    own, _ = own_places(here)
     rest = 0.5 - (own[0] * own[0] + own[1] * own[1] + own[2] * own[2])
     put_columns(own + [rest], column_ref)
-    cells = (None, middle, None)
-    density_sums(plan_in, cells, column_ref, False, plan_ref, ghost_ref, sum_ref, sem)
+    cells = (None, here, None)
+    density_sums(plan_in, cells, column_ref, False, shrink_ref, plan_ref, ghost_ref, sum_ref, sem)
     for t in range(8):
         early_ref[t : t + 1, :] = row_sums(sum_ref[t])
 
@@ -261,55 +262,63 @@
     selves_ref,
     early_ref,
     column_ref,
-    behind,
-    middle,
-    ahead,
+    below,
+    here,
+    above,
     slope_ref,
+    shrink_ref,
     plan_ref,
     ghost_ref,
     sum_ref,
     row_ref,
     sem,
 ):
-    cells = (behind, middle, ahead)
-    density_sums(plan_in, cells, column_ref, True, plan_ref, ghost_ref, sum_ref, sem)
+    cells = (below, here, above)
+    density_sums(plan_in, cells, column_ref, True, shrink_ref, plan_ref, ghost_ref, sum_ref, sem)
     for t in range(8):
         row_ref[t : t + 1, :] = row_sums(sum_ref[t])
-    _, live = own_places(middle)
+    _, live = own_places(here)
     itself = jnp.where(live, selves_ref[...], 0.0)
     density = (row_ref[...] + early_ref[...] - itself) * density_scale
-    slope_ref[...] = (-0.5 * slope_factor / cube_factor) / jnp.sqrt(1.0 + density)
+    slope_ref[0] = (-0.5 * slope_factor / cube_factor) / jnp.sqrt(1.0 + density)
 
 
 def force_sums(
-    plan_in, cells, slope_cells, column_ref, slopes_ref, late, plan_ref, ghost_ref, sum_ref, sem
+    plan_in,
+    cells,
+    slope_cells,
+    column_ref,
+    slopes_ref,
+    shrink_ref,
+    late,
+    plan_ref,
+    ghost_ref,
+    sum_ref,
+    sem,
 ):
     def prepare():
-        put_ghosts(cells, ghost_ref, lambda dx, dy: (dy != 1) == late)
+        put_ghosts(cells, ghost_ref, late)
         for dy, cell in enumerate(slope_cells):
             if (dy != 1) == late:
                 for dx in range(3):
                     for level in range(4):
-                        ghost_ref[dx * 12 + dy * 4 + level, 3] = cell[dx * 4 + level]
+                        ghost_ref[dx * 12 + dy * 4 + level, 3] = cell[dx * 4 + level, 0]
         sum_ref[...] = jnp.zeros_like(sum_ref)
 
-    def add(near, ghosts):
+    def add(near, ghosts, spots):
         far = []
         for brick, tile in ghosts:
             rows = [ghost_ref[brick, c, pl.ds(tile, 1), :] for c in range(4)]
             far.append([jnp.broadcast_to(row, (8, 128)) for row in rows])
         for r in range(16):
             part = pl.ds(8 * r, 8)
-            ax, ay, az = (column_ref[8 * c + near, part, :] for c in range(3))
+            place = [column_ref[8 * c + near, part, :] for c in range(3)]
             slope = slopes_ref[near, part, :]
             sums = [sum_ref[8 * c + near, part, :] for c in range(3)]
-            for cx, cy, cz, far_slope in far:
-                dx = ax - cx
-                dy = ay - cy
-                dz = az - cz
-                shrink = jnp.maximum(1.0 - (dx * dx + dy * dy + dz * dz), 0.0)
-                weight = shrink * shrink * (shrink + (slope + far_slope))
-                sums = [sums[0] + weight * dx, sums[1] + weight * dy, sums[2] + weight * dz]
+            for rows, spot in zip(far, spots):
+                shrink = shrink_ref[spot, part, :]
+                weight = shrink * shrink * (shrink + (slope + rows[3]))
+                sums = [sums[c] + weight * (place[c] - rows[c]) for c in range(3)]
             for c in range(3):
                 sum_ref[8 * c + near, part, :] = sums[c]
 
@@ -318,12 +327,11 @@
 
 def early_force_kernel(
     plan_in,
-    c0,
-    c1,
-    c2,
+    here,
     column_ref,
     own_slope,
-    s1,
+    slope_here,
+    shrink_ref,
     slopes_ref,
     early_ref,
     plan_ref,
@@ -331,13 +339,14 @@
     sum_ref,
     sem,
 ):
-    put_columns([own_slope[...]], slopes_ref)
+    put_columns([own_slope[0]], slopes_ref)
     force_sums(
         plan_in,
-        (c0, c1, c2),
-        (None, s1, None),
+        (None, here, None),
+        (None, slope_here, None),
         column_ref,
         slopes_ref,
+        shrink_ref,
         False,
         plan_ref,
         ghost_ref,
@@ -352,12 +361,12 @@
 def late_force_kernel(
     step,
     plan_in,
-    c0,
-    c1,
-    c2,
+    below,
+    above,
     column_ref,
-    s0,
-    s2,
+    slope_below,
+    slope_above,
+    shrink_ref,
     slopes_ref,
     early_ref,
     place_in,
@@ -367,10 +376,11 @@
     *outs, plan_ref, ghost_ref, sum_ref, push_ref, sem = rest
     force_sums(
         plan_in,
-        (c0, c1, c2),
-        (s0, None, s2),
+        (below, None, above),
+        (slope_below, None, slope_above),
         column_ref,
         slopes_ref,
+        shrink_ref,
         True,
         plan_ref,
         ghost_ref,
@@ -434,22 +444,16 @@
     )
 
 
-def around(values, beside):
-    ends, beside = lax.optimization_barrier(
-        ((moved(values, "gy", -1), moved(values, "gy", 1)), beside)
-    )
-    rows = jnp.stack([ends[0], values, ends[1]])
-    copies = jnp.broadcast_to(rows[None], (4,) + rows.shape)
-    tower = lax.all_to_all(copies, "gz", 0, 0, tiled=True)
-    return (moved(tower, "gx", -1), tower, moved(tower, "gx", 1)), beside
-
-
-def slope_column(values):
+def row_around(values):
     count = lax.axis_size("gx") * lax.axis_size("gz")
     copies = jnp.broadcast_to(values[None], (count,) + values.shape)
     plane = lax.all_to_all(copies, ("gx", "gz"), 0, 0, tiled=True)
-    (column,) = call(pick_kernel, [shaped(12, 8, 128)], [VMEM])(plane)
-    return column
+    (row,) = call(pick_kernel, [shaped(12, *values.shape)], [VMEM])(plane)
+    return row
+
+
+def beside(row):
+    return moved(row, "gy", -1), moved(row, "gy", 1)
 
 
 def per_device(positions, velocities, forces, counts, pair_tiles, pair_count, mig_slots):
@@ -459,7 +463,9 @@
     slots = mig_slots.reshape(steps, 4, 128)
     atoms = shaped(3, 8, 128)
     block = shaped(8, 128)
+    slope_block = shaped(1, 8, 128)
     columns = shaped(32, 128, 128)
+    shrinks = shaped(128 + 8 * (unrolled - 1), 128, 128)
     slope_columns = shaped(8, 128, 128)
     atoms_scratch = pltpu.VMEM((3, 8, 128), jnp.float32)
     plan_shape = jax.ShapeDtypeStruct((8, 128), jnp.int32)
@@ -479,37 +485,38 @@
         [atoms, atoms, jax.ShapeDtypeStruct(slots.shape, jnp.int32)] + [block] * 4,
         [VMEM] * 2,
     )(rows, slots)
-    plans = call(
-        plan_kernel, [plan_shape, plan_shape, block], [SMEM, SMEM, VMEM]
-    )(total, live_count, pair_tiles.reshape(2, 128))
+    plan, selves = call(plan_kernel, [plan_shape, block], [SMEM, SMEM, VMEM])(
+        total, live_count, pair_tiles.reshape(2, 128)
+    )
     for n in range(steps):
+        arrived, (plan, selves) = lax.optimization_barrier((migrants(packed), (plan, selves)))
         place, speed, sent = call(
             functools.partial(unpack_kernel, n), [atoms, atoms, atoms], [SMEM] + [VMEM] * 7
-        )(live_count, place, speed, slots, *migrants(packed))
-        cells, plans = around(sent, plans)
-        density_plan, force_plan, selves = plans
-        column, early = call(
+        )(live_count, place, speed, slots, *arrived)
+        here = row_around(sent)
+        below, above = beside(here)
+        column, early, early_shrinks = call(
             early_density_kernel,
-            [columns, block],
+            [columns, block, shrinks],
             [ANY, VMEM],
             pair_scratch(3, 1),
             mega_ops=60,
-        )(density_plan, cells[1])
-        (slope,) = call(
+        )(plan, here)
+        slope, late_shrinks = call(
             late_density_kernel,
-            [block],
+            [slope_block, shrinks],
             [ANY] + [VMEM] * 6,
             pair_scratch(3, 1, pltpu.VMEM((8, 128), jnp.float32)),
-        )(density_plan, selves, early, column, *cells)
-        here = slope_column(slope)
-        below, above = moved(here, "gy", -1), moved(here, "gy", 1)
+        )(plan, selves, early, column, below, here, above)
+        slope_here = row_around(slope)
+        slope_below, slope_above = beside(slope_here)
         slopes, early = call(
             early_force_kernel,
             [slope_columns, atoms],
-            [ANY] + [VMEM] * 6,
+            [ANY] + [VMEM] * 5,
             pair_scratch(4, 3),
             mega_ops=60,
-        )(force_plan, *cells, column, slope, here)
+        )(plan, here, column, slope, slope_here, early_shrinks)
         last = n + 1 == steps
         place, speed, *packed = call(
             functools.partial(late_force_kernel, None if last else n + 1),
@@ -517,11 +524,13 @@
             [ANY] + [VMEM] * (10 if last else 11),
             pair_scratch(4, 3, atoms_scratch),
         )(
-            force_plan,
-            *cells,
-            column,
+            plan,
             below,
             above,
+            column,
+            slope_below,
+            slope_above,
+            late_shrinks,
             slopes,
             early,
             place,

time: 140 us -> 143 us (1.021)
  blocking collectives: 44.3 us -> 62.2 us
  starting transfers between devices: 56.4 us -> 43.8 us
  Pallas kernels: 25 us -> 20.3 us
  waiting for transfers between devices: 8.51 us -> 10.7 us
    all_to_all x4, blocking collectives: 44.3 us -> 62.2 us  [row_around(): plane = lax.all_to_all(copies, ('gx', 'gz'), 0, 0, tiled=True)]
    ppermute x20 -> x16, starting transfers between devices: 56.4 us -> 43.8 us  [moved(): lax.ppermute(values, axis, [((i + shift) % count, i) for i in range(count)])]
    pallas_call x9 -> x11, Pallas kernels: 16.4 us -> 13.6 us  [the longest x2 4.76 us: per_device(): call(early_force_kernel, [slope_columns, atoms], [ANY] + [VMEM] * 5, pair...]
    ppermute x20 -> x16, waiting for transfers between devices: 8.51 us -> 10.7 us  [moved(): lax.ppermute(values, axis, [((i + shift) % count, i) for i in range(count)])]
    pallas_call x2, Pallas kernels: 7.95 us -> 6.06 us  [per_device(): call(functools.partial(late_force_kernel, None if last else n + 1), [atom...]
  transfers between devices with their start and end apart: 20 -> 16, of which waited for: 7 -> 6; matrix products, arithmetic and copies ran while one was open for 0% -> 0% of each run, Pallas kernels for 8% -> 6%
where the time goes in v5:
time: 143 us; the launch traced here: 141 us
  blocking collectives  62.2 us (43%)
  starting transfers between devices  43.8 us (31%)
  Pallas kernels  20.3 us (14%)
  waiting for transfers between devices  10.7 us (7%)
  between operations  2.23 us (2%)
  local copies, waits for them, and re-layouts  1.44 us (1%)
    all_to_all x4, blocking collectives, row_around(): plane = lax.all_to_all(copies, ('gx', 'gz'), 0, 0, tiled=True)  62.2 us
    ppermute x16, starting transfers between devices, moved(): lax.ppermute(values, axis, [((i + shift) % count, i) for i in range(count)])  43.8 us
    ppermute x16, waiting for transfers between devices, moved(): lax.ppermute(values, axis, [((i + shift) % count, i) for i in range(count)])  10.7 us
    pallas_call x2, Pallas kernels, per_device(): call(functools.partial(late_force_kernel, None if last else n + 1), [atom...  6.06 us
    pallas_call x2, Pallas kernels, per_device(): call(early_force_kernel, [slope_columns, atoms], [ANY] + [VMEM] * 5, pair...  4.76 us
    pallas_call x2, Pallas kernels, per_device(): call(late_density_kernel, [slope_block, shrinks], [ANY] + [VMEM] * 6, pai...  4.41 us
    pallas_call x2, Pallas kernels, per_device(): call(early_density_kernel, [columns, block, shrinks], [ANY, VMEM], pair_s...  4.04 us
  transfers between devices with their start and end apart: 16, of which 6 were waited for; matrix products, arithmetic and copies ran while one was open for 0% of the time, Pallas kernels for 6%

profile of v5, /device:TPU:1, one launch (start us, length us, event | category | flops | bytes accessed | tf_op | source)
XLA Modules:
  0.0 141.4 jit_solution(1441267833145300798)
XLA Ops:
  0.6 0.7 pad_maximum_fusion.rows_in
  2.3 6.9 %collective-permute-start = (f32[8,128]{1,0:T(8,128)S(1)}, f32[8,128]{1,0:T(8,128)S(1)}, u32[]{:S(2)}, u32[]{:S(2)}) collective-permute-start(f32[8,128]{1,0:T(8,128)S(1)} %get-tuple-element.51), channel_id=1, source_target_pairs={{64,0},{128,64},{192,128},{256,192},{320,256},{384,320},{448,384},... | collective-permute-start | bytes 12296 | tf_op jit(solution)/shard_map/ppermute | solution.py:435
  9.2 6.9 %collective-permute-start.2 = (f32[8,128]{1,0:T(8,128)S(1)}, f32[8,128]{1,0:T(8,128)S(1)}, u32[]{:S(2)}, u32[]{:S(2)}) collective-permute-start(f32[8,128]{1,0:T(8,128)S(1)} %get-tuple-element.53), channel_id=1, source_target_pairs={{4,0},{8,4},{12,8},{16,12},{20,16},{24,20},{28,24},{32,28},{36,32}... | collective-permute-start | bytes 12296 | tf_op jit(solution)/shard_map/ppermute | solution.py:435
  16.1 1.9 %collective-permute-start.3 = (f32[8,128]{1,0:T(8,128)S(1)}, f32[8,128]{1,0:T(8,128)S(1)}, u32[]{:S(2)}, u32[]{:S(2)}) collective-permute-start(f32[8,128]{1,0:T(8,128)S(1)} %get-tuple-element.54), channel_id=1, source_target_pairs={{60,0},{0,4},{4,8},{8,12},{12,16},{16,20},{20,24},{24,28},{28,32},... | collective-permute-start | bytes 12296 | tf_op jit(solution)/shard_map/ppermute | solution.py:435
  20.3 1.3 collective-permute-done.3.a3
  21.9 17.9 %all_to_all.20.plane_ref = f32[32,3,8,128]{3,2,1,0:T(8,128)S(1)} all-to-all(f32[32,3,8,128]{3,2,1,0:T(8,128)S(1)} %broadcast_in_dim.12), channel_id=1, replica_groups=mesh['gx'=8,'gy'=16,'gz'=4] {'gx','gz'}, dimensions={0} | all-to-all | bytes 786432 | tf_op jit(solution)/shard_map/all_to_all | solution.py:450
  39.8 3.3 %collective-permute-start.5 = (f32[12,3,8,128]{3,2,1,0:T(8,128)S(1)}, f32[12,3,8,128]{3,2,1,0:T(8,128)S(1)}, u32[]{:S(2)}, u32[]{:S(2)}) collective-permute-start(f32[12,3,8,128]{3,2,1,0:T(8,128)S(1)} %shard_map.89.here), channel_id=1, source_target_pairs={{4,0},{8,4},{12,8},{16,12},{20,16},{24,20},{28,24},{32,28},{36,32}... | collective-permute-start | bytes 442376 | tf_op jit(solution)/shard_map/ppermute | solution.py:435
  43.1 2.0 %collective-permute-start.4 = (f32[12,3,8,128]{3,2,1,0:T(8,128)S(1)}, f32[12,3,8,128]{3,2,1,0:T(8,128)S(1)}, u32[]{:S(2)}, u32[]{:S(2)}) collective-permute-start(f32[12,3,8,128]{3,2,1,0:T(8,128)S(1)} %shard_map.89.here), channel_id=1, source_target_pairs={{60,0},{0,4},{4,8},{8,12},{12,16},{16,20},{20,24},{24,28},{28,32},... | collective-permute-start | bytes 442376 | tf_op jit(solution)/shard_map/ppermute | solution.py:435
  45.1 2.0 %shard_map.90 = (f32[32,128,128]{2,1,0:T(8,128)S(1)}, f32[8,128]{1,0:T(8,128)S(1)}, f32[152,128,128]{2,1,0:T(8,128)S(1)}) custom-call(s32[8,128]{1,0:T(8,128)S(1)} %get-tuple-element.80.plan_in, f32[12,3,8,128]{3,2,1,0:T(8,128)S(1)} %shard_map.89.here), custom_call_target="tpu_custom_call" | custom-call | flops 60000000 | bytes 6000000 | tf_op jit(solution)/shard_map/pallas_call | solution.py:498
  47.2 3.4 %collective-permute-done.4.below = f32[12,3,8,128]{3,2,1,0:T(8,128)S(1)} collective-permute-done((f32[12,3,8,128]{3,2,1,0:T(8,128)S(1)}, f32[12,3,8,128]{3,2,1,0:T(8,128)S(1)}, u32[]{:S(2)}, u32[]{:S(2)}) %collective-permute-start.4) | collective-permute-done | bytes 147488 | tf_op jit(solution)/shard_map/ppermute | solution.py:435
  50.6 2.2 %shard_map.91 = (f32[1,8,128]{2,1,0:T(8,128)S(1)}, f32[152,128,128]{2,1,0:T(8,128)S(1)}) custom-call(s32[8,128]{1,0:T(8,128)S(1)} %get-tuple-element.80.plan_in, f32[8,128]{1,0:T(8,128)S(1)} %get-tuple-element.89.selves_ref, f32[8,128]{1,0:T(8,128)S(1)} %get-tuple-element.68.early_ref, f32[32,128,128]{2,1,0:T(8,128)S(1)} %get-tuple-element.66.column_ref, ...), custom_call_target="tpu_custom_call" | custom-call | flops 1000000 | bytes 100000 | tf_op jit(solution)/shard_map/pallas_call | solution.py:505
  52.8 14.3 %all_to_all.21.plane_ref = f32[32,1,8,128]{3,2,1,0:T(8,128)S(1)} all-to-all(f32[32,1,8,128]{3,2,1,0:T(8,128)S(1)} %broadcast_in_dim.14), channel_id=1, replica_groups=mesh['gx'=8,'gy'=16,'gz'=4] {'gx','gz'}, dimensions={0} | all-to-all | bytes 262144 | tf_op jit(solution)/shard_map/all_to_all | solution.py:450
  67.1 1.9 %collective-permute-start.7 = (f32[12,1,8,128]{3,2,1,0:T(8,128)S(1)}, f32[12,1,8,128]{3,2,1,0:T(8,128)S(1)}, u32[]{:S(2)}, u32[]{:S(2)}) collective-permute-start(f32[12,1,8,128]{3,2,1,0:T(8,128)S(1)} %shard_map.92.slope_here), channel_id=1, source_target_pairs={{4,0},{8,4},{12,8},{16,12},{20,16},{24,20},{28,24},{32,28},{36,32}... | collective-permute-start | bytes 147464 | tf_op jit(solution)/shard_map/ppermute | solution.py:435
  69.0 3.4 %collective-permute-start.6 = (f32[12,1,8,128]{3,2,1,0:T(8,128)S(1)}, f32[12,1,8,128]{3,2,1,0:T(8,128)S(1)}, u32[]{:S(2)}, u32[]{:S(2)}) collective-permute-start(f32[12,1,8,128]{3,2,1,0:T(8,128)S(1)} %shard_map.92.slope_here), channel_id=1, source_target_pairs={{60,0},{0,4},{4,8},{8,12},{12,16},{16,20},{20,24},{24,28},{28,32},... | collective-permute-start | bytes 147464 | tf_op jit(solution)/shard_map/ppermute | solution.py:435
  72.3 2.4 %shard_map.93 = (f32[8,128,128]{2,1,0:T(8,128)S(1)}, f32[3,8,128]{2,1,0:T(8,128)S(1)}) custom-call(s32[8,128]{1,0:T(8,128)S(1)} %get-tuple-element.80.plan_in, f32[12,3,8,128]{3,2,1,0:T(8,128)S(1)} %shard_map.89.here, f32[32,128,128]{2,1,0:T(8,128)S(1)} %get-tuple-element.66.column_ref, f32[1,8,128]{2,1,0:T(8,128)S(1)} %get-tuple-element.69.own_slope, ...), custom_call_target="tpu_custom_call" | custom-call | flops 60000000 | bytes 6000000 | tf_op jit(solution)/shard_map/pallas_call | solution.py:513
  75.0 2.8 %shard_map.94 = (f32[3,8,128]{2,1,0:T(8,128)S(1)}, f32[3,8,128]{2,1,0:T(8,128)S(1)}, f32[8,128]{1,0:T(8,128)S(1)}, f32[8,128]{1,0:T(8,128)S(1)}, f32[8,128]{1,0:T(8,128)S(1)}, /*index=5*/f32[8,128]{1,0:T(8,128)S(1)}) custom-call(s32[8,128]{1,0:T(8,128)S(1)} %get-tuple-element.80.plan_in, f32[12,3,8,128]{3,2,1,0:T(8,128)S(1)} %collective-permute-done.4.below, ...), custom_call_target="tpu_custom_call" | custom-call | flops 1000000 | bytes 100000 | tf_op jit(solution)/shard_map/pallas_call | solution.py:521
  77.9 1.0 collective-permute-start.8
  78.9 0.8 collective-permute-start.9
  79.6 2.9 %collective-permute-start.10 = (f32[8,128]{1,0:T(8,128)S(1)}, f32[8,128]{1,0:T(8,128)S(1)}, u32[]{:S(2)}, u32[]{:S(2)}) collective-permute-start(f32[8,128]{1,0:T(8,128)S(1)} %get-tuple-element.78), channel_id=1, source_target_pairs={{4,0},{8,4},{12,8},{16,12},{20,16},{24,20},{28,24},{32,28},{36,32}... | collective-permute-start | bytes 12296 | tf_op jit(solution)/shard_map/ppermute | solution.py:435
  82.5 2.4 %collective-permute-start.11 = (f32[8,128]{1,0:T(8,128)S(1)}, f32[8,128]{1,0:T(8,128)S(1)}, u32[]{:S(2)}, u32[]{:S(2)}) collective-permute-start(f32[8,128]{1,0:T(8,128)S(1)} %get-tuple-element.79), channel_id=1, source_target_pairs={{60,0},{0,4},{4,8},{8,12},{12,16},{16,20},{20,24},{24,28},{28,32},... | collective-permute-start | bytes 12296 | tf_op jit(solution)/shard_map/ppermute | solution.py:435
  84.9 3.1 %collective-permute-done.11.a3 = f32[8,128]{1,0:T(8,128)S(1)} collective-permute-done((f32[8,128]{1,0:T(8,128)S(1)}, f32[8,128]{1,0:T(8,128)S(1)}, u32[]{:S(2)}, u32[]{:S(2)}) %collective-permute-start.11) | collective-permute-done | bytes 4128 | tf_op jit(solution)/shard_map/ppermute | solution.py:435
  88.3 16.3 %all_to_all.22.plane_ref = f32[32,3,8,128]{3,2,1,0:T(8,128)S(1)} all-to-all(f32[32,3,8,128]{3,2,1,0:T(8,128)S(1)} %broadcast_in_dim.15), channel_id=1, replica_groups=mesh['gx'=8,'gy'=16,'gz'=4] {'gx','gz'}, dimensions={0} | all-to-all | bytes 786432 | tf_op jit(solution)/shard_map/all_to_all | solution.py:450
  104.6 1.9 %collective-permute-start.13 = (f32[12,3,8,128]{3,2,1,0:T(8,128)S(1)}, f32[12,3,8,128]{3,2,1,0:T(8,128)S(1)}, u32[]{:S(2)}, u32[]{:S(2)}) collective-permute-start(f32[12,3,8,128]{3,2,1,0:T(8,128)S(1)} %shard_map.96.here), channel_id=1, source_target_pairs={{4,0},{8,4},{12,8},{16,12},{20,16},{24,20},{28,24},{32,28},{36,32}... | collective-permute-start | bytes 442376 | tf_op jit(solution)/shard_map/ppermute | solution.py:435
  106.5 3.4 %collective-permute-start.12 = (f32[12,3,8,128]{3,2,1,0:T(8,128)S(1)}, f32[12,3,8,128]{3,2,1,0:T(8,128)S(1)}, u32[]{:S(2)}, u32[]{:S(2)}) collective-permute-start(f32[12,3,8,128]{3,2,1,0:T(8,128)S(1)} %shard_map.96.here), channel_id=1, source_target_pairs={{60,0},{0,4},{4,8},{8,12},{12,16},{16,20},{20,24},{24,28},{28,32},... | collective-permute-start | bytes 442376 | tf_op jit(solution)/shard_map/ppermute | solution.py:435
  109.9 2.0 %shard_map.97 = (f32[32,128,128]{2,1,0:T(8,128)S(1)}, f32[8,128]{1,0:T(8,128)S(1)}, f32[152,128,128]{2,1,0:T(8,128)S(1)}) custom-call(s32[8,128]{1,0:T(8,128)S(1)} %get-tuple-element.80.plan_in, f32[12,3,8,128]{3,2,1,0:T(8,128)S(1)} %shard_map.96.here), custom_call_target="tpu_custom_call" | custom-call | flops 60000000 | bytes 6000000 | tf_op jit(solution)/shard_map/pallas_call | solution.py:498
  111.9 2.3 %collective-permute-done.12.below = f32[12,3,8,128]{3,2,1,0:T(8,128)S(1)} collective-permute-done((f32[12,3,8,128]{3,2,1,0:T(8,128)S(1)}, f32[12,3,8,128]{3,2,1,0:T(8,128)S(1)}, u32[]{:S(2)}, u32[]{:S(2)}) %collective-permute-start.12) | collective-permute-done | bytes 147488 | tf_op jit(solution)/shard_map/ppermute | solution.py:435
  114.3 2.2 %shard_map.98 = (f32[1,8,128]{2,1,0:T(8,128)S(1)}, f32[152,128,128]{2,1,0:T(8,128)S(1)}) custom-call(s32[8,128]{1,0:T(8,128)S(1)} %get-tuple-element.80.plan_in, f32[8,128]{1,0:T(8,128)S(1)} %get-tuple-element.89.selves_ref, f32[8,128]{1,0:T(8,128)S(1)} %get-tuple-element.90.early_ref, f32[32,128,128]{2,1,0:T(8,128)S(1)} %get-tuple-element.88.column_ref, ...), custom_call_target="tpu_custom_call" | custom-call | flops 1000000 | bytes 100000 | tf_op jit(solution)/shard_map/pallas_call | solution.py:505
  116.5 13.7 %all_to_all.23.plane_ref = f32[32,1,8,128]{3,2,1,0:T(8,128)S(1)} all-to-all(f32[32,1,8,128]{3,2,1,0:T(8,128)S(1)} %broadcast_in_dim.33), channel_id=1, replica_groups=mesh['gx'=8,'gy'=16,'gz'=4] {'gx','gz'}, dimensions={0} | all-to-all | bytes 262144 | tf_op jit(solution)/shard_map/all_to_all | solution.py:450
  130.2 1.9 %collective-permute-start.15 = (f32[12,1,8,128]{3,2,1,0:T(8,128)S(1)}, f32[12,1,8,128]{3,2,1,0:T(8,128)S(1)}, u32[]{:S(2)}, u32[]{:S(2)}) collective-permute-start(f32[12,1,8,128]{3,2,1,0:T(8,128)S(1)} %shard_map.99.slope_here), channel_id=1, source_target_pairs={{4,0},{8,4},{12,8},{16,12},{20,16},{24,20},{28,24},{32,28},{36,32}... | collective-permute-start | bytes 147464 | tf_op jit(solution)/shard_map/ppermute | solution.py:435
  132.1 3.4 %collective-permute-start.14 = (f32[12,1,8,128]{3,2,1,0:T(8,128)S(1)}, f32[12,1,8,128]{3,2,1,0:T(8,128)S(1)}, u32[]{:S(2)}, u32[]{:S(2)}) collective-permute-start(f32[12,1,8,128]{3,2,1,0:T(8,128)S(1)} %shard_map.99.slope_here), channel_id=1, source_target_pairs={{60,0},{0,4},{4,8},{8,12},{12,16},{16,20},{20,24},{24,28},{28,32},... | collective-permute-start | bytes 147464 | tf_op jit(solution)/shard_map/ppermute | solution.py:435
  135.5 2.4 %shard_map.100 = (f32[8,128,128]{2,1,0:T(8,128)S(1)}, f32[3,8,128]{2,1,0:T(8,128)S(1)}) custom-call(s32[8,128]{1,0:T(8,128)S(1)} %get-tuple-element.80.plan_in, f32[12,3,8,128]{3,2,1,0:T(8,128)S(1)} %shard_map.96.here, f32[32,128,128]{2,1,0:T(8,128)S(1)} %get-tuple-element.88.column_ref, f32[1,8,128]{2,1,0:T(8,128)S(1)} %get-tuple-element.91.own_slope, ...), custom_call_target="tpu_custom_call" | custom-call | flops 60000000 | bytes 6000000 | tf_op jit(solution)/shard_map/pallas_call | solution.py:513
  138.2 3.2 %shard_map.101 = (f32[3,8,128]{2,1,0:T(8,128)}, f32[3,8,128]{2,1,0:T(8,128)}) custom-call(s32[8,128]{1,0:T(8,128)S(1)} %get-tuple-element.80.plan_in, f32[12,3,8,128]{3,2,1,0:T(8,128)S(1)} %collective-permute-done.12.below, f32[12,3,8,128]{3,2,1,0:T(8,128)S(1)} %collective-permute-done.13.above, f32[32,128,128]{2,1,0:T(8,128)S(1)} %get-tuple-element.88.column_ref, ...), custom_call_target="tpu_custom_call" | custom-call | flops 1000000 | bytes 100000 | tf_op jit(solution)/shard_map/pallas_call | solution.py:521
  (29 shorter events, 3.0 us)
Async XLA Ops:
  1.4 0.7 copy-start
  2.3 18.0 %collective-permute-start = (f32[8,128]{1,0:T(8,128)S(1)}, f32[8,128]{1,0:T(8,128)S(1)}, u32[]{:S(2)}, u32[]{:S(2)}) collective-permute-start(f32[8,128]{1,0:T(8,128)S(1)} %get-tuple-element.51), channel_id=1, source_target_pairs={{64,0},{128,64},{192,128},{256,192},{320,256},{384,320},{448,384},... | collective-permute-start | bytes 12296 | tf_op jit(solution)/shard_map/ppermute | solution.py:435
  9.2 11.1 %collective-permute-start.1 = (f32[8,128]{1,0:T(8,128)S(1)}, f32[8,128]{1,0:T(8,128)S(1)}, u32[]{:S(2)}, u32[]{:S(2)}) collective-permute-start(f32[8,128]{1,0:T(8,128)S(1)} %get-tuple-element.52), channel_id=1, source_target_pairs={{448,0},{0,64},{64,128},{128,192},{192,256},{256,320},{320,384},{3... | collective-permute-start | bytes 12296 | tf_op jit(solution)/shard_map/ppermute | solution.py:435
  9.2 11.1 %collective-permute-start.2 = (f32[8,128]{1,0:T(8,128)S(1)}, f32[8,128]{1,0:T(8,128)S(1)}, u32[]{:S(2)}, u32[]{:S(2)}) collective-permute-start(f32[8,128]{1,0:T(8,128)S(1)} %get-tuple-element.53), channel_id=1, source_target_pairs={{4,0},{8,4},{12,8},{16,12},{20,16},{24,20},{28,24},{32,28},{36,32}... | collective-permute-start | bytes 12296 | tf_op jit(solution)/shard_map/ppermute | solution.py:435
  16.1 5.6 %collective-permute-start.3 = (f32[8,128]{1,0:T(8,128)S(1)}, f32[8,128]{1,0:T(8,128)S(1)}, u32[]{:S(2)}, u32[]{:S(2)}) collective-permute-start(f32[8,128]{1,0:T(8,128)S(1)} %get-tuple-element.54), channel_id=1, source_target_pairs={{60,0},{0,4},{4,8},{8,12},{12,16},{16,20},{20,24},{24,28},{28,32},... | collective-permute-start | bytes 12296 | tf_op jit(solution)/shard_map/ppermute | solution.py:435
  19.3 0.7 copy-start.1
  39.8 7.3 %collective-permute-start.5 = (f32[12,3,8,128]{3,2,1,0:T(8,128)S(1)}, f32[12,3,8,128]{3,2,1,0:T(8,128)S(1)}, u32[]{:S(2)}, u32[]{:S(2)}) collective-permute-start(f32[12,3,8,128]{3,2,1,0:T(8,128)S(1)} %shard_map.89.here), channel_id=1, source_target_pairs={{4,0},{8,4},{12,8},{16,12},{20,16},{24,20},{28,24},{32,28},{36,32}... | collective-permute-start | bytes 442376 | tf_op jit(solution)/shard_map/ppermute | solution.py:435
  43.1 7.5 %collective-permute-start.4 = (f32[12,3,8,128]{3,2,1,0:T(8,128)S(1)}, f32[12,3,8,128]{3,2,1,0:T(8,128)S(1)}, u32[]{:S(2)}, u32[]{:S(2)}) collective-permute-start(f32[12,3,8,128]{3,2,1,0:T(8,128)S(1)} %shard_map.89.here), channel_id=1, source_target_pairs={{60,0},{0,4},{4,8},{8,12},{12,16},{16,20},{20,24},{24,28},{28,32},... | collective-permute-start | bytes 442376 | tf_op jit(solution)/shard_map/ppermute | solution.py:435
  67.1 7.7 %collective-permute-start.7 = (f32[12,1,8,128]{3,2,1,0:T(8,128)S(1)}, f32[12,1,8,128]{3,2,1,0:T(8,128)S(1)}, u32[]{:S(2)}, u32[]{:S(2)}) collective-permute-start(f32[12,1,8,128]{3,2,1,0:T(8,128)S(1)} %shard_map.92.slope_here), channel_id=1, source_target_pairs={{4,0},{8,4},{12,8},{16,12},{20,16},{24,20},{28,24},{32,28},{36,32}... | collective-permute-start | bytes 147464 | tf_op jit(solution)/shard_map/ppermute | solution.py:435
  69.0 6.0 %collective-permute-start.6 = (f32[12,1,8,128]{3,2,1,0:T(8,128)S(1)}, f32[12,1,8,128]{3,2,1,0:T(8,128)S(1)}, u32[]{:S(2)}, u32[]{:S(2)}) collective-permute-start(f32[12,1,8,128]{3,2,1,0:T(8,128)S(1)} %shard_map.92.slope_here), channel_id=1, source_target_pairs={{60,0},{0,4},{4,8},{8,12},{12,16},{16,20},{20,24},{24,28},{28,32},... | collective-permute-start | bytes 147464 | tf_op jit(solution)/shard_map/ppermute | solution.py:435
  77.9 7.0 %collective-permute-start.8 = (f32[8,128]{1,0:T(8,128)S(1)}, f32[8,128]{1,0:T(8,128)S(1)}, u32[]{:S(2)}, u32[]{:S(2)}) collective-permute-start(f32[8,128]{1,0:T(8,128)S(1)} %get-tuple-element.76), channel_id=1, source_target_pairs={{64,0},{128,64},{192,128},{256,192},{320,256},{384,320},{448,384},... | collective-permute-start | bytes 12296 | tf_op jit(solution)/shard_map/ppermute | solution.py:435
  78.9 6.1 %collective-permute-start.9 = (f32[8,128]{1,0:T(8,128)S(1)}, f32[8,128]{1,0:T(8,128)S(1)}, u32[]{:S(2)}, u32[]{:S(2)}) collective-permute-start(f32[8,128]{1,0:T(8,128)S(1)} %get-tuple-element.77), channel_id=1, source_target_pairs={{448,0},{0,64},{64,128},{128,192},{192,256},{256,320},{320,384},{3... | collective-permute-start | bytes 12296 | tf_op jit(solution)/shard_map/ppermute | solution.py:435
  79.6 5.3 %collective-permute-start.10 = (f32[8,128]{1,0:T(8,128)S(1)}, f32[8,128]{1,0:T(8,128)S(1)}, u32[]{:S(2)}, u32[]{:S(2)}) collective-permute-start(f32[8,128]{1,0:T(8,128)S(1)} %get-tuple-element.78), channel_id=1, source_target_pairs={{4,0},{8,4},{12,8},{16,12},{20,16},{24,20},{28,24},{32,28},{36,32}... | collective-permute-start | bytes 12296 | tf_op jit(solution)/shard_map/ppermute | solution.py:435
  82.5 5.6 %collective-permute-start.11 = (f32[8,128]{1,0:T(8,128)S(1)}, f32[8,128]{1,0:T(8,128)S(1)}, u32[]{:S(2)}, u32[]{:S(2)}) collective-permute-start(f32[8,128]{1,0:T(8,128)S(1)} %get-tuple-element.79), channel_id=1, source_target_pairs={{60,0},{0,4},{4,8},{8,12},{12,16},{16,20},{20,24},{24,28},{28,32},... | collective-permute-start | bytes 12296 | tf_op jit(solution)/shard_map/ppermute | solution.py:435
  104.6 7.3 %collective-permute-start.13 = (f32[12,3,8,128]{3,2,1,0:T(8,128)S(1)}, f32[12,3,8,128]{3,2,1,0:T(8,128)S(1)}, u32[]{:S(2)}, u32[]{:S(2)}) collective-permute-start(f32[12,3,8,128]{3,2,1,0:T(8,128)S(1)} %shard_map.96.here), channel_id=1, source_target_pairs={{4,0},{8,4},{12,8},{16,12},{20,16},{24,20},{28,24},{32,28},{36,32}... | collective-permute-start | bytes 442376 | tf_op jit(solution)/shard_map/ppermute | solution.py:435
  106.5 7.7 %collective-permute-start.12 = (f32[12,3,8,128]{3,2,1,0:T(8,128)S(1)}, f32[12,3,8,128]{3,2,1,0:T(8,128)S(1)}, u32[]{:S(2)}, u32[]{:S(2)}) collective-permute-start(f32[12,3,8,128]{3,2,1,0:T(8,128)S(1)} %shard_map.96.here), channel_id=1, source_target_pairs={{60,0},{0,4},{4,8},{8,12},{12,16},{16,20},{20,24},{24,28},{28,32},... | collective-permute-start | bytes 442376 | tf_op jit(solution)/shard_map/ppermute | solution.py:435
  130.2 7.7 %collective-permute-start.15 = (f32[12,1,8,128]{3,2,1,0:T(8,128)S(1)}, f32[12,1,8,128]{3,2,1,0:T(8,128)S(1)}, u32[]{:S(2)}, u32[]{:S(2)}) collective-permute-start(f32[12,1,8,128]{3,2,1,0:T(8,128)S(1)} %shard_map.99.slope_here), channel_id=1, source_target_pairs={{4,0},{8,4},{12,8},{16,12},{20,16},{24,20},{28,24},{32,28},{36,32}... | collective-permute-start | bytes 147464 | tf_op jit(solution)/shard_map/ppermute | solution.py:435
  132.1 6.0 %collective-permute-start.14 = (f32[12,1,8,128]{3,2,1,0:T(8,128)S(1)}, f32[12,1,8,128]{3,2,1,0:T(8,128)S(1)}, u32[]{:S(2)}, u32[]{:S(2)}) collective-permute-start(f32[12,1,8,128]{3,2,1,0:T(8,128)S(1)} %shard_map.99.slope_here), channel_id=1, source_target_pairs={{60,0},{0,4},{4,8},{8,12},{12,16},{16,20},{20,24},{24,28},{28,32},... | collective-permute-start | bytes 147464 | tf_op jit(solution)/shard_map/ppermute | solution.py:435

commit v6 on v3

--- a/solution.py
+++ b/solution.py
@@ -24,6 +24,8 @@
 ANY = pl.BlockSpec(memory_space=pl.ANY)
 SMEM = pl.BlockSpec(memory_space=pltpu.SMEM)
 unrolled = 4
+nothing = 128
+unused = 129
 nt_dims = (((1,), (1,)), ((), ()))
 nn_dims = (((1,), (0,)), ((), ()))
 
@@ -67,7 +69,7 @@
         packed_refs[direction][6:8, :] = jnp.zeros((2, 128), jnp.float32)
 
 
-def put_plan(listed, near, far, late, plan_ref):
+def put_plan(listed, near, far, late, spots, empty, plan_ref):
     lanes = lax.broadcasted_iota(jnp.int32, (1, 128), 1)
     part = jnp.where(listed, jnp.where(late, near + 8, near), -1)
     rows = lax.broadcasted_iota(jnp.int32, (16, 128), 0)
@@ -87,19 +89,22 @@
         starts = jnp.where(lanes == t, start, starts)
         start = start + groups[t : t + 1]
     starts = jnp.where(lanes == 16, start, starts)
-    values = jnp.where(
-        rows == 0,
-        (far >> 3).astype(jnp.float32),
-        jnp.where(rows == 1, (far & 7).astype(jnp.float32), 1.0),
-    ).astype(jnp.bfloat16)
+    values = jnp.where(rows == 2, 1.0, 0.0)
+    for at, row in enumerate((far >> 3, far & 7, None, *spots)):
+        if row is not None:
+            values = jnp.where(rows == at, row.astype(jnp.float32), values)
+    values = values.astype(jnp.bfloat16)
+    plan_ref[7:8, :] = jnp.zeros((1, 128), jnp.int32)
     for half in range(2):
         spot = lax.broadcasted_iota(jnp.int32, (128, 128), 0) + 128 * half
         sent = jnp.where(spot == place, 1.0, 0.0).astype(jnp.bfloat16)
         sorted_rows = dot(values, sent, nt_dims).astype(jnp.int32)
-        brick = jnp.where(sorted_rows[2:3] > 0, sorted_rows[0:1], 36)
+        found = sorted_rows[2:3] > 0
+        brick = jnp.where(found, sorted_rows[0:1], 36)
         plan_ref[half : half + 1, :] = brick * 8 + sorted_rows[1:2]
+        plan_ref[3 + half : 4 + half, :] = jnp.where(found, sorted_rows[3:4], empty)
+        plan_ref[5 + half : 6 + half, :] = jnp.where(found, sorted_rows[4:5], empty)
     plan_ref[2:3, :] = starts
-    plan_ref[3:8, :] = jnp.zeros((5, 128), jnp.int32)
 
 
 def plan_kernel(total_ref, count_ref, tiles_ref, density_plan, force_plan, selves_ref):
@@ -109,8 +114,11 @@
     listed = lax.broadcasted_iota(jnp.int32, (1, 128), 1) < total_ref[0]
     listed = jnp.logical_and(listed, near * 128 < count_ref[0])
     brick = far >> 3
-    put_plan(listed, near, far, jnp.logical_or(brick < 12, brick >= 24), density_plan)
-    put_plan(listed, near, far, ((brick >> 2) + 2) % 3 != 0, force_plan)
+    late = jnp.logical_or(brick < 12, brick >= 24)
+    spots = lax.broadcasted_iota(jnp.int32, (1, 128), 1)
+    put_plan(listed, near, far, late, (spots, spots), unused, density_plan)
+    spots = jnp.where(late, nothing, spots), jnp.where(late, spots, nothing)
+    put_plan(listed, near, far, ((brick >> 2) + 2) % 3 != 0, spots, nothing, force_plan)
     rows = lax.broadcasted_iota(jnp.int32, (16, 128), 0)
     itself = jnp.logical_and(listed, far == (16 + zbrick) * 8 + near)
     itself = jnp.where(jnp.logical_and(itself, rows == near), 1.0, 0.0).astype(jnp.bfloat16)
@@ -210,9 +218,10 @@
 
     def over_tile(near, carry):
         def over_group(group, carry):
-            first = group * unrolled
-            codes = [plan_ref[(first + i) >> 7, (first + i) & 127] for i in range(unrolled)]
-            body(near, [(code >> 3, code & 7) for code in codes])
+            places = [group * unrolled + i for i in range(unrolled)]
+            places = [(place >> 7, place & 127) for place in places]
+            codes = [plan_ref[row, lane] for row, lane in places]
+            body(near, [(code >> 3, code & 7) for code in codes], places)
             return carry
 
         segment = near + 8 * late
@@ -221,23 +230,26 @@
     lax.fori_loop(0, 8, over_tile, 0)
 
 
-def density_sums(plan_in, cells, column_ref, late, plan_ref, ghost_ref, sum_ref, sem):
+def density_sums(plan_in, cells, column_ref, late, shrink_ref, plan_ref, ghost_ref, sum_ref, sem):
     def prepare():
         put_ghosts(cells, ghost_ref, lambda dx, dy: (dx != 1) == late)
         sum_ref[...] = jnp.zeros_like(sum_ref)
-
-    def add(near, ghosts):
+        shrink_ref[nothing] = jnp.zeros((128, 128), jnp.float32)
+
+    def add(near, ghosts, places):
         far = []
-        for brick, tile in ghosts:
+        for (brick, tile), (row, lane) in zip(ghosts, places):
             x, y, z = (ghost_ref[brick, c, pl.ds(tile, 1), :] for c in range(3))
             rows = (2.0 * x, 2.0 * y, 2.0 * z, 0.5 - (x * x + y * y + z * z))
-            far.append([jnp.broadcast_to(row, (8, 128)) for row in rows])
+            rows = [jnp.broadcast_to(row, (8, 128)) for row in rows]
+            far.append((rows, plan_ref[3 + row, lane]))
         for r in range(16):
             part = pl.ds(8 * r, 8)
             ax, ay, az, rest = (column_ref[8 * c + near, part, :] for c in range(4))
             total = sum_ref[near, part, :]
-            for cx, cy, cz, cn in far:
+            for (cx, cy, cz, cn), spot in far:
                 shrink = jnp.maximum((ax * cx + ay * cy) + (az * cz + (rest + cn)), 0.0)
+                shrink_ref[spot, part, :] = shrink
                 total = total + shrink * shrink * shrink
             sum_ref[near, part, :] = total
 
@@ -245,13 +257,13 @@
 
 
 def early_density_kernel(
-    plan_in, middle, column_ref, early_ref, plan_ref, ghost_ref, sum_ref, sem
+    plan_in, middle, column_ref, early_ref, shrink_ref, plan_ref, ghost_ref, sum_ref, sem
 ):
     own, _ = own_places(middle)
     rest = 0.5 - (own[0] * own[0] + own[1] * own[1] + own[2] * own[2])
     put_columns(own + [rest], column_ref)
     cells = (None, middle, None)
-    density_sums(plan_in, cells, column_ref, False, plan_ref, ghost_ref, sum_ref, sem)
+    density_sums(plan_in, cells, column_ref, False, shrink_ref, plan_ref, ghost_ref, sum_ref, sem)
     for t in range(8):
         early_ref[t : t + 1, :] = row_sums(sum_ref[t])
 
@@ -265,6 +277,7 @@
     middle,
     ahead,
     slope_ref,
+    shrink_ref,
     plan_ref,
     ghost_ref,
     sum_ref,
@@ -272,7 +285,7 @@
     sem,
 ):
     cells = (behind, middle, ahead)
-    density_sums(plan_in, cells, column_ref, True, plan_ref, ghost_ref, sum_ref, sem)
+    density_sums(plan_in, cells, column_ref, True, shrink_ref, plan_ref, ghost_ref, sum_ref, sem)
     for t in range(8):
         row_ref[t : t + 1, :] = row_sums(sum_ref[t])
     _, live = own_places(middle)
@@ -282,8 +295,20 @@
 
 
 def force_sums(
-    plan_in, cells, slope_cells, column_ref, slopes_ref, late, plan_ref, ghost_ref, sum_ref, sem
+    plan_in,
+    cells,
+    slope_cells,
+    column_ref,
+    slopes_ref,
+    shrink_refs,
+    late,
+    plan_ref,
+    ghost_ref,
+    sum_ref,
+    sem,
 ):
+    first_ref, second_ref = shrink_refs
+
     def prepare():
         put_ghosts(cells, ghost_ref, lambda dx, dy: (dy != 1) == late)
         for dy, cell in enumerate(slope_cells):
@@ -293,23 +318,21 @@
                         ghost_ref[dx * 12 + dy * 4 + level, 3] = cell[dx * 4 + level]
         sum_ref[...] = jnp.zeros_like(sum_ref)
 
-    def add(near, ghosts):
+    def add(near, ghosts, places):
         far = []
-        for brick, tile in ghosts:
+        for (brick, tile), (row, lane) in zip(ghosts, places):
             rows = [ghost_ref[brick, c, pl.ds(tile, 1), :] for c in range(4)]
-            far.append([jnp.broadcast_to(row, (8, 128)) for row in rows])
+            rows = [jnp.broadcast_to(row, (8, 128)) for row in rows]
+            far.append((rows, plan_ref[3 + row, lane], plan_ref[5 + row, lane]))
         for r in range(16):
             part = pl.ds(8 * r, 8)
-            ax, ay, az = (column_ref[8 * c + near, part, :] for c in range(3))
+            place = [column_ref[8 * c + near, part, :] for c in range(3)]
             slope = slopes_ref[near, part, :]
             sums = [sum_ref[8 * c + near, part, :] for c in range(3)]
-            for cx, cy, cz, far_slope in far:
-                dx = ax - cx
-                dy = ay - cy
-                dz = az - cz
-                shrink = jnp.maximum(1.0 - (dx * dx + dy * dy + dz * dz), 0.0)
-                weight = shrink * shrink * (shrink + (slope + far_slope))
-                sums = [sums[0] + weight * dx, sums[1] + weight * dy, sums[2] + weight * dz]
+            for rows, first, second in far:
+                shrink = first_ref[first, part, :] + second_ref[second, part, :]
+                weight = shrink * shrink * (shrink + (slope + rows[3]))
+                sums = [sums[c] + weight * (place[c] - rows[c]) for c in range(3)]
             for c in range(3):
                 sum_ref[8 * c + near, part, :] = sums[c]
 
@@ -324,6 +347,8 @@
     column_ref,
     own_slope,
     s1,
+    h0,
+    h1,
     slopes_ref,
     early_ref,
     plan_ref,
@@ -338,6 +363,7 @@
         (None, s1, None),
         column_ref,
         slopes_ref,
+        (h0, h1),
         False,
         plan_ref,
         ghost_ref,
@@ -358,6 +384,8 @@
     column_ref,
     s0,
     s2,
+    h0,
+    h1,
     slopes_ref,
     early_ref,
     place_in,
@@ -371,6 +399,7 @@
         (s0, None, s2),
         column_ref,
         slopes_ref,
+        (h0, h1),
         True,
         plan_ref,
         ghost_ref,
@@ -434,14 +463,11 @@
     )
 
 
-def around(values, beside):
-    ends, beside = lax.optimization_barrier(
-        ((moved(values, "gy", -1), moved(values, "gy", 1)), beside)
-    )
-    rows = jnp.stack([ends[0], values, ends[1]])
+def around(values):
+    rows = jnp.stack([moved(values, "gy", -1), values, moved(values, "gy", 1)])
     copies = jnp.broadcast_to(rows[None], (4,) + rows.shape)
     tower = lax.all_to_all(copies, "gz", 0, 0, tiled=True)
-    return (moved(tower, "gx", -1), tower, moved(tower, "gx", 1)), beside
+    return moved(tower, "gx", -1), tower, moved(tower, "gx", 1)
 
 
 def slope_column(values):
@@ -462,6 +488,7 @@
     columns = shaped(32, 128, 128)
     slope_columns = shaped(8, 128, 128)
     atoms_scratch = pltpu.VMEM((3, 8, 128), jnp.float32)
+    shrinks = shaped(130, 128, 128)
     plan_shape = jax.ShapeDtypeStruct((8, 128), jnp.int32)
 
     def pair_scratch(comps, sums, *found):
@@ -483,21 +510,22 @@
         plan_kernel, [plan_shape, plan_shape, block], [SMEM, SMEM, VMEM]
     )(total, live_count, pair_tiles.reshape(2, 128))
     for n in range(steps):
+        arrived, plans = lax.optimization_barrier((migrants(packed), plans))
+        density_plan, force_plan, selves = plans
         place, speed, sent = call(
             functools.partial(unpack_kernel, n), [atoms, atoms, atoms], [SMEM] + [VMEM] * 7
-        )(live_count, place, speed, slots, *migrants(packed))
-        cells, plans = around(sent, plans)
-        density_plan, force_plan, selves = plans
-        column, early = call(
+        )(live_count, place, speed, slots, *arrived)
+        cells = around(sent)
+        column, early, early_shrinks = call(
             early_density_kernel,
-            [columns, block],
+            [columns, block, shrinks],
             [ANY, VMEM],
             pair_scratch(3, 1),
             mega_ops=60,
         )(density_plan, cells[1])
-        (slope,) = call(
+        slope, late_shrinks = call(
             late_density_kernel,
-            [block],
+            [block, shrinks],
             [ANY] + [VMEM] * 6,
             pair_scratch(3, 1, pltpu.VMEM((8, 128), jnp.float32)),
         )(density_plan, selves, early, column, *cells)
@@ -506,15 +534,15 @@
         slopes, early = call(
             early_force_kernel,
             [slope_columns, atoms],
-            [ANY] + [VMEM] * 6,
+            [ANY] + [VMEM] * 8,
             pair_scratch(4, 3),
             mega_ops=60,
-        )(force_plan, *cells, column, slope, here)
+        )(force_plan, *cells, column, slope, here, early_shrinks, late_shrinks)
         last = n + 1 == steps
         place, speed, *packed = call(
             functools.partial(late_force_kernel, None if last else n + 1),
             [atoms, atoms] + [block] * (0 if last else 4),
-            [ANY] + [VMEM] * (10 if last else 11),
+            [ANY] + [VMEM] * (12 if last else 13),
             pair_scratch(4, 3, atoms_scratch),
         )(
             force_plan,
@@ -522,6 +550,8 @@
             column,
             below,
             above,
+            early_shrinks,
+            late_shrinks,
             slopes,
             early,
             place,

time: 140 us -> 138 us (0.986)
  waiting for transfers between devices: 8.51 us -> 10.6 us
  starting transfers between devices: 56.4 us -> 54.6 us
  Pallas kernels: 25 us -> 23.4 us
    ppermute x20, waiting for transfers between devices: 8.51 us -> 10.6 us  [moved(): lax.ppermute(values, axis, [((i + shift) % count, i) for i in range(count)])]
    ppermute x20, starting transfers between devices: 56.4 us -> 54.6 us  [moved(): lax.ppermute(values, axis, [((i + shift) % count, i) for i in range(count)])]
    all_to_all x2, blocking collectives: 27.7 us -> 26 us  [slope_column(): plane = lax.all_to_all(copies, ('gx', 'gz'), 0, 0, tiled=True)]
  transfers between devices with their start and end apart: 20 -> 20, of which waited for: 7 -> 6; matrix products, arithmetic and copies ran while one was open for 0% -> 0% of each run, Pallas kernels for 8% -> 8%
where the time goes in v6:
time: 138 us; the launch traced here: 136 us
  starting transfers between devices  54.6 us (40%)
  blocking collectives  43.3 us (31%)
  Pallas kernels  23.4 us (17%)
  waiting for transfers between devices  10.6 us (8%)
  between operations  2.25 us (2%)
  local copies, waits for them, and re-layouts  1.41 us (1%)
    ppermute x20, starting transfers between devices, moved(): lax.ppermute(values, axis, [((i + shift) % count, i) for i in range(count)])  54.6 us
    all_to_all x2, blocking collectives, slope_column(): plane = lax.all_to_all(copies, ('gx', 'gz'), 0, 0, tiled=True)  26 us
    all_to_all x2, blocking collectives, around(): tower = lax.all_to_all(copies, 'gz', 0, 0, tiled=True)  17.2 us
    ppermute x20, waiting for transfers between devices, moved(): lax.ppermute(values, axis, [((i + shift) % count, i) for i in range(count)])  10.6 us
    pallas_call x2, Pallas kernels, per_device(): call(functools.partial(late_force_kernel, None if last else n + 1), [atom...  7.06 us
    pallas_call x2, Pallas kernels, per_device(): call(early_force_kernel, [slope_columns, atoms], [ANY] + [VMEM] * 8, pair...  5.34 us
    pallas_call x2, Pallas kernels, per_device(): call(late_density_kernel, [block, shrinks], [ANY] + [VMEM] * 6, pair_scra...  5.11 us
    pallas_call x2, Pallas kernels, per_device(): call(early_density_kernel, [columns, block, shrinks], [ANY, VMEM], pair_s...  4.72 us
  transfers between devices with their start and end apart: 20, of which 6 were waited for; matrix products, arithmetic and copies ran while one was open for 0% of the time, Pallas kernels for 8%

profile of v6, /device:TPU:1, one launch (start us, length us, event | category | flops | bytes accessed | tf_op | source)
XLA Modules:
  0.0 136.2 jit_solution(953385404586933335)
XLA Ops:
  2.3 6.9 %collective-permute-start = (f32[8,128]{1,0:T(8,128)S(1)}, f32[8,128]{1,0:T(8,128)S(1)}, u32[]{:S(2)}, u32[]{:S(2)}) collective-permute-start(f32[8,128]{1,0:T(8,128)S(1)} %get-tuple-element.54), channel_id=1, source_target_pairs={{64,0},{128,64},{192,128},{256,192},{320,256},{384,320},{448,384},... | collective-permute-start | bytes 12296 | tf_op jit(solution)/shard_map/ppermute | solution.py:454
  9.2 6.9 %collective-permute-start.2 = (f32[8,128]{1,0:T(8,128)S(1)}, f32[8,128]{1,0:T(8,128)S(1)}, u32[]{:S(2)}, u32[]{:S(2)}) collective-permute-start(f32[8,128]{1,0:T(8,128)S(1)} %get-tuple-element.56), channel_id=1, source_target_pairs={{4,0},{8,4},{12,8},{16,12},{20,16},{24,20},{28,24},{32,28},{36,32}... | collective-permute-start | bytes 12296 | tf_op jit(solution)/shard_map/ppermute | solution.py:454
  16.1 1.9 %collective-permute-start.3 = (f32[8,128]{1,0:T(8,128)S(1)}, f32[8,128]{1,0:T(8,128)S(1)}, u32[]{:S(2)}, u32[]{:S(2)}) collective-permute-start(f32[8,128]{1,0:T(8,128)S(1)} %get-tuple-element.57), channel_id=1, source_target_pairs={{60,0},{0,4},{4,8},{8,12},{12,16},{16,20},{20,24},{24,28},{28,32},... | collective-permute-start | bytes 12296 | tf_op jit(solution)/shard_map/ppermute | solution.py:454
  21.8 3.5 %collective-permute-start.5 = (f32[3,8,128]{2,1,0:T(8,128)S(1)}, f32[3,8,128]{2,1,0:T(8,128)S(1)}, u32[]{:S(2)}, u32[]{:S(2)}) collective-permute-start(f32[3,8,128]{2,1,0:T(8,128)S(1)} %get-tuple-element.69), channel_id=1, source_target_pairs={{4,0},{8,4},{12,8},{16,12},{20,16},{24,20},{28,24},{32,28},{36,32}... | collective-permute-start | bytes 36872 | tf_op jit(solution)/shard_map/ppermute | solution.py:454
  25.3 1.9 %collective-permute-start.4 = (f32[3,8,128]{2,1,0:T(8,128)S(1)}, f32[3,8,128]{2,1,0:T(8,128)S(1)}, u32[]{:S(2)}, u32[]{:S(2)}) collective-permute-start(f32[3,8,128]{2,1,0:T(8,128)S(1)} %get-tuple-element.69), channel_id=1, source_target_pairs={{60,0},{0,4},{4,8},{8,12},{12,16},{16,20},{20,24},{24,28},{28,32},... | collective-permute-start | bytes 36872 | tf_op jit(solution)/shard_map/ppermute | solution.py:454
  27.3 3.7 %collective-permute-done.4 = f32[3,8,128]{2,1,0:T(8,128)S(1)} collective-permute-done((f32[3,8,128]{2,1,0:T(8,128)S(1)}, f32[3,8,128]{2,1,0:T(8,128)S(1)}, u32[]{:S(2)}, u32[]{:S(2)}) %collective-permute-start.4) | collective-permute-done | bytes 12320 | tf_op jit(solution)/shard_map/ppermute | solution.py:454
  31.0 8.9 %all_to_all.20.middle.c1 = f32[4,3,3,8,128]{4,3,2,1,0:T(8,128)S(1)} all-to-all(f32[4,3,3,8,128]{4,3,2,1,0:T(8,128)S(1)} %broadcast_in_dim.8), channel_id=1, replica_groups=mesh['gx'=8,'gy'=16,'gz'=4] {'gz'}, dimensions={0} | all-to-all | bytes 294912 | tf_op jit(solution)/shard_map/all_to_all | solution.py:469
  39.9 4.5 %collective-permute-start.7 = (f32[4,3,3,8,128]{4,3,2,1,0:T(8,128)S(1)}, f32[4,3,3,8,128]{4,3,2,1,0:T(8,128)S(1)}, u32[]{:S(2)}, u32[]{:S(2)}) collective-permute-start(f32[4,3,3,8,128]{4,3,2,1,0:T(8,128)S(1)} %all_to_all.20.middle.c1), channel_id=1, source_target_pairs={{64,0},{128,64},{192,128},{256,192},{320,256},{384,320},{448,384},... | collective-permute-start | bytes 442376 | tf_op jit(solution)/shard_map/ppermute | solution.py:454
  44.4 2.4 %shard_map.89 = (f32[32,128,128]{2,1,0:T(8,128)S(1)}, f32[8,128]{1,0:T(8,128)S(1)}, f32[130,128,128]{2,1,0:T(8,128)S(1)}) custom-call(s32[8,128]{1,0:T(8,128)S(1)} %get-tuple-element.93.plan_in, f32[4,3,3,8,128]{4,3,2,1,0:T(8,128)S(1)} %all_to_all.20.middle.c1), custom_call_target="tpu_custom_call" | custom-call | flops 60000000 | bytes 6000000 | tf_op jit(solution)/shard_map/pallas_call | solution.py:519
  46.8 2.6 %shard_map.90 = (f32[8,128]{1,0:T(8,128)S(1)}, f32[130,128,128]{2,1,0:T(8,128)S(1)}) custom-call(s32[8,128]{1,0:T(8,128)S(1)} %get-tuple-element.93.plan_in, f32[8,128]{1,0:T(8,128)S(1)} %get-tuple-element.95.selves_ref, f32[8,128]{1,0:T(8,128)S(1)} %get-tuple-element.73.early_ref, f32[32,128,128]{2,1,0:T(8,128)S(1)} %get-tuple-element.71.column_ref, ...), custom_call_target="tpu_custom_call" | custom-call | flops 1000000 | bytes 100000 | tf_op jit(solution)/shard_map/pallas_call | solution.py:526
  49.4 13.8 %all_to_all.21.plane_ref = f32[32,8,128]{2,1,0:T(8,128)S(1)} all-to-all(f32[32,8,128]{2,1,0:T(8,128)S(1)} %broadcast_in_dim.9), channel_id=1, replica_groups=mesh['gx'=8,'gy'=16,'gz'=4] {'gx','gz'}, dimensions={0} | all-to-all | bytes 262144 | tf_op jit(solution)/shard_map/all_to_all | solution.py:476
  63.1 1.9 %collective-permute-start.9 = (f32[12,8,128]{2,1,0:T(8,128)S(1)}, f32[12,8,128]{2,1,0:T(8,128)S(1)}, u32[]{:S(2)}, u32[]{:S(2)}) collective-permute-start(f32[12,8,128]{2,1,0:T(8,128)S(1)} %shard_map.91.s1), channel_id=1, source_target_pairs={{4,0},{8,4},{12,8},{16,12},{20,16},{24,20},{28,24},{32,28},{36,32}... | collective-permute-start | bytes 147464 | tf_op jit(solution)/shard_map/ppermute | solution.py:454
  65.1 3.4 %collective-permute-start.8 = (f32[12,8,128]{2,1,0:T(8,128)S(1)}, f32[12,8,128]{2,1,0:T(8,128)S(1)}, u32[]{:S(2)}, u32[]{:S(2)}) collective-permute-start(f32[12,8,128]{2,1,0:T(8,128)S(1)} %shard_map.91.s1), channel_id=1, source_target_pairs={{60,0},{0,4},{4,8},{8,12},{12,16},{16,20},{20,24},{24,28},{28,32},... | collective-permute-start | bytes 147464 | tf_op jit(solution)/shard_map/ppermute | solution.py:454
  68.4 2.7 %shard_map.92 = (f32[8,128,128]{2,1,0:T(8,128)S(1)}, f32[3,8,128]{2,1,0:T(8,128)S(1)}) custom-call(s32[8,128]{1,0:T(8,128)S(1)} %get-tuple-element.85.plan_in, f32[4,3,3,8,128]{4,3,2,1,0:T(8,128)S(1)} %collective-permute-done.6.behind.c0, f32[4,3,3,8,128]{4,3,2,1,0:T(8,128)S(1)} %all_to_all.20.middle.c1, ...), custom_call_target="tpu_custom_call" | custom-call | flops 60000000 | bytes 6000000 | tf_op jit(solution)/shard_map/pallas_call | solution.py:534
  71.1 3.4 %shard_map.93 = (f32[3,8,128]{2,1,0:T(8,128)S(1)}, f32[3,8,128]{2,1,0:T(8,128)S(1)}, f32[8,128]{1,0:T(8,128)S(1)}, f32[8,128]{1,0:T(8,128)S(1)}, f32[8,128]{1,0:T(8,128)S(1)}, /*index=5*/f32[8,128]{1,0:T(8,128)S(1)}) custom-call(s32[8,128]{1,0:T(8,128)S(1)} %get-tuple-element.85.plan_in, f32[4,3,3,8,128]{4,3,2,1,0:T(8,128)S(1)} %collective-permute-done.6.behind.c0, ...), custom_call_target="tpu_custom_call" | custom-call | flops 1000000 | bytes 100000 | tf_op jit(solution)/shard_map/pallas_call | solution.py:542
  74.5 1.4 collective-permute-start.10
  75.8 2.0 %collective-permute-start.11 = (f32[8,128]{1,0:T(8,128)S(1)}, f32[8,128]{1,0:T(8,128)S(1)}, u32[]{:S(2)}, u32[]{:S(2)}) collective-permute-start(f32[8,128]{1,0:T(8,128)S(1)} %get-tuple-element.82), channel_id=1, source_target_pairs={{448,0},{0,64},{64,128},{128,192},{192,256},{256,320},{320,384},{3... | collective-permute-start | bytes 12296 | tf_op jit(solution)/shard_map/ppermute | solution.py:454
  77.8 1.9 %collective-permute-start.12 = (f32[8,128]{1,0:T(8,128)S(1)}, f32[8,128]{1,0:T(8,128)S(1)}, u32[]{:S(2)}, u32[]{:S(2)}) collective-permute-start(f32[8,128]{1,0:T(8,128)S(1)} %get-tuple-element.83), channel_id=1, source_target_pairs={{4,0},{8,4},{12,8},{16,12},{20,16},{24,20},{28,24},{32,28},{36,32}... | collective-permute-start | bytes 12296 | tf_op jit(solution)/shard_map/ppermute | solution.py:454
  79.8 3.4 %collective-permute-start.13 = (f32[8,128]{1,0:T(8,128)S(1)}, f32[8,128]{1,0:T(8,128)S(1)}, u32[]{:S(2)}, u32[]{:S(2)}) collective-permute-start(f32[8,128]{1,0:T(8,128)S(1)} %get-tuple-element.84), channel_id=1, source_target_pairs={{60,0},{0,4},{4,8},{8,12},{12,16},{16,20},{20,24},{24,28},{28,32},... | collective-permute-start | bytes 12296 | tf_op jit(solution)/shard_map/ppermute | solution.py:454
  83.2 2.2 %collective-permute-done.13.a3 = f32[8,128]{1,0:T(8,128)S(1)} collective-permute-done((f32[8,128]{1,0:T(8,128)S(1)}, f32[8,128]{1,0:T(8,128)S(1)}, u32[]{:S(2)}, u32[]{:S(2)}) %collective-permute-start.13) | collective-permute-done | bytes 4128 | tf_op jit(solution)/shard_map/ppermute | solution.py:454
  85.5 1.9 %collective-permute-start.15 = (f32[3,8,128]{2,1,0:T(8,128)S(1)}, f32[3,8,128]{2,1,0:T(8,128)S(1)}, u32[]{:S(2)}, u32[]{:S(2)}) collective-permute-start(f32[3,8,128]{2,1,0:T(8,128)S(1)} %get-tuple-element.92), channel_id=1, source_target_pairs={{4,0},{8,4},{12,8},{16,12},{20,16},{24,20},{28,24},{32,28},{36,32}... | collective-permute-start | bytes 36872 | tf_op jit(solution)/shard_map/ppermute | solution.py:454
  87.5 3.4 %collective-permute-start.14 = (f32[3,8,128]{2,1,0:T(8,128)S(1)}, f32[3,8,128]{2,1,0:T(8,128)S(1)}, u32[]{:S(2)}, u32[]{:S(2)}) collective-permute-start(f32[3,8,128]{2,1,0:T(8,128)S(1)} %get-tuple-element.92), channel_id=1, source_target_pairs={{60,0},{0,4},{4,8},{8,12},{12,16},{16,20},{20,24},{24,28},{28,32},... | collective-permute-start | bytes 36872 | tf_op jit(solution)/shard_map/ppermute | solution.py:454
  90.9 2.3 %collective-permute-done.14 = f32[3,8,128]{2,1,0:T(8,128)S(1)} collective-permute-done((f32[3,8,128]{2,1,0:T(8,128)S(1)}, f32[3,8,128]{2,1,0:T(8,128)S(1)}, u32[]{:S(2)}, u32[]{:S(2)}) %collective-permute-start.14) | collective-permute-done | bytes 12320 | tf_op jit(solution)/shard_map/ppermute | solution.py:454
  93.1 8.3 %all_to_all.22.middle.c1 = f32[4,3,3,8,128]{4,3,2,1,0:T(8,128)S(1)} all-to-all(f32[4,3,3,8,128]{4,3,2,1,0:T(8,128)S(1)} %broadcast_in_dim.10), channel_id=1, replica_groups=mesh['gx'=8,'gy'=16,'gz'=4] {'gz'}, dimensions={0} | all-to-all | bytes 294912 | tf_op jit(solution)/shard_map/all_to_all | solution.py:469
  101.5 3.3 %collective-permute-start.17 = (f32[4,3,3,8,128]{4,3,2,1,0:T(8,128)S(1)}, f32[4,3,3,8,128]{4,3,2,1,0:T(8,128)S(1)}, u32[]{:S(2)}, u32[]{:S(2)}) collective-permute-start(f32[4,3,3,8,128]{4,3,2,1,0:T(8,128)S(1)} %all_to_all.22.middle.c1), channel_id=1, source_target_pairs={{64,0},{128,64},{192,128},{256,192},{320,256},{384,320},{448,384},... | collective-permute-start | bytes 442376 | tf_op jit(solution)/shard_map/ppermute | solution.py:454
  106.0 2.4 %shard_map.95 = (f32[32,128,128]{2,1,0:T(8,128)S(1)}, f32[8,128]{1,0:T(8,128)S(1)}, f32[130,128,128]{2,1,0:T(8,128)S(1)}) custom-call(s32[8,128]{1,0:T(8,128)S(1)} %get-tuple-element.93.plan_in, f32[4,3,3,8,128]{4,3,2,1,0:T(8,128)S(1)} %all_to_all.22.middle.c1), custom_call_target="tpu_custom_call" | custom-call | flops 60000000 | bytes 6000000 | tf_op jit(solution)/shard_map/pallas_call | solution.py:519
  109.2 2.6 %shard_map.96 = (f32[8,128]{1,0:T(8,128)S(1)}, f32[130,128,128]{2,1,0:T(8,128)S(1)}) custom-call(s32[8,128]{1,0:T(8,128)S(1)} %get-tuple-element.93.plan_in, f32[8,128]{1,0:T(8,128)S(1)} %get-tuple-element.95.selves_ref, f32[8,128]{1,0:T(8,128)S(1)} %get-tuple-element.96.early_ref, f32[32,128,128]{2,1,0:T(8,128)S(1)} %get-tuple-element.94.column_ref, ...), custom_call_target="tpu_custom_call" | custom-call | flops 1000000 | bytes 100000 | tf_op jit(solution)/shard_map/pallas_call | solution.py:526
  111.7 12.3 %all_to_all.23.plane_ref = f32[32,8,128]{2,1,0:T(8,128)S(1)} all-to-all(f32[32,8,128]{2,1,0:T(8,128)S(1)} %broadcast_in_dim.11), channel_id=1, replica_groups=mesh['gx'=8,'gy'=16,'gz'=4] {'gx','gz'}, dimensions={0} | all-to-all | bytes 262144 | tf_op jit(solution)/shard_map/all_to_all | solution.py:476
  124.0 2.5 %collective-permute-start.19 = (f32[12,8,128]{2,1,0:T(8,128)S(1)}, f32[12,8,128]{2,1,0:T(8,128)S(1)}, u32[]{:S(2)}, u32[]{:S(2)}) collective-permute-start(f32[12,8,128]{2,1,0:T(8,128)S(1)} %shard_map.97.s1), channel_id=1, source_target_pairs={{4,0},{8,4},{12,8},{16,12},{20,16},{24,20},{28,24},{32,28},{36,32}... | collective-permute-start | bytes 147464 | tf_op jit(solution)/shard_map/ppermute | solution.py:454
  126.5 2.8 %collective-permute-start.18 = (f32[12,8,128]{2,1,0:T(8,128)S(1)}, f32[12,8,128]{2,1,0:T(8,128)S(1)}, u32[]{:S(2)}, u32[]{:S(2)}) collective-permute-start(f32[12,8,128]{2,1,0:T(8,128)S(1)} %shard_map.97.s1), channel_id=1, source_target_pairs={{60,0},{0,4},{4,8},{8,12},{12,16},{16,20},{20,24},{24,28},{28,32},... | collective-permute-start | bytes 147464 | tf_op jit(solution)/shard_map/ppermute | solution.py:454
  129.3 2.7 %shard_map.98 = (f32[8,128,128]{2,1,0:T(8,128)S(1)}, f32[3,8,128]{2,1,0:T(8,128)S(1)}) custom-call(s32[8,128]{1,0:T(8,128)S(1)} %get-tuple-element.85.plan_in, f32[4,3,3,8,128]{4,3,2,1,0:T(8,128)S(1)} %collective-permute-done.16.behind.c0, f32[4,3,3,8,128]{4,3,2,1,0:T(8,128)S(1)} %all_to_all.22.middle.c1, ...), custom_call_target="tpu_custom_call" | custom-call | flops 60000000 | bytes 6000000 | tf_op jit(solution)/shard_map/pallas_call | solution.py:534
  132.5 3.7 %shard_map.99 = (f32[3,8,128]{2,1,0:T(8,128)}, f32[3,8,128]{2,1,0:T(8,128)}) custom-call(s32[8,128]{1,0:T(8,128)S(1)} %get-tuple-element.85.plan_in, f32[4,3,3,8,128]{4,3,2,1,0:T(8,128)S(1)} %collective-permute-done.16.behind.c0, f32[4,3,3,8,128]{4,3,2,1,0:T(8,128)S(1)} %all_to_all.22.middle.c1, f32[4,3,3,8,128]{4,3,2,1,0:T(8,128)S(1)} %collective-permute-done.17.ahead.c2, ...), custom_call_target="tpu_custom_call" | custom-call | flops 1000000 | bytes 100000 | tf_op jit(solution)/shard_map/pallas_call | solution.py:542
  (37 shorter events, 7.1 us)
Async XLA Ops:
  1.4 0.7 copy-start
  2.3 18.2 %collective-permute-start = (f32[8,128]{1,0:T(8,128)S(1)}, f32[8,128]{1,0:T(8,128)S(1)}, u32[]{:S(2)}, u32[]{:S(2)}) collective-permute-start(f32[8,128]{1,0:T(8,128)S(1)} %get-tuple-element.54), channel_id=1, source_target_pairs={{64,0},{128,64},{192,128},{256,192},{320,256},{384,320},{448,384},... | collective-permute-start | bytes 12296 | tf_op jit(solution)/shard_map/ppermute | solution.py:454
  9.2 11.3 %collective-permute-start.1 = (f32[8,128]{1,0:T(8,128)S(1)}, f32[8,128]{1,0:T(8,128)S(1)}, u32[]{:S(2)}, u32[]{:S(2)}) collective-permute-start(f32[8,128]{1,0:T(8,128)S(1)} %get-tuple-element.55), channel_id=1, source_target_pairs={{448,0},{0,64},{64,128},{128,192},{192,256},{256,320},{320,384},{3... | collective-permute-start | bytes 12296 | tf_op jit(solution)/shard_map/ppermute | solution.py:454
  9.2 11.3 %collective-permute-start.2 = (f32[8,128]{1,0:T(8,128)S(1)}, f32[8,128]{1,0:T(8,128)S(1)}, u32[]{:S(2)}, u32[]{:S(2)}) collective-permute-start(f32[8,128]{1,0:T(8,128)S(1)} %get-tuple-element.56), channel_id=1, source_target_pairs={{4,0},{8,4},{12,8},{16,12},{20,16},{24,20},{28,24},{32,28},{36,32}... | collective-permute-start | bytes 12296 | tf_op jit(solution)/shard_map/ppermute | solution.py:454
  16.1 5.6 %collective-permute-start.3 = (f32[8,128]{1,0:T(8,128)S(1)}, f32[8,128]{1,0:T(8,128)S(1)}, u32[]{:S(2)}, u32[]{:S(2)}) collective-permute-start(f32[8,128]{1,0:T(8,128)S(1)} %get-tuple-element.57), channel_id=1, source_target_pairs={{60,0},{0,4},{4,8},{8,12},{12,16},{16,20},{20,24},{24,28},{28,32},... | collective-permute-start | bytes 12296 | tf_op jit(solution)/shard_map/ppermute | solution.py:454
  19.3 0.7 copy-start.1
  21.8 5.4 %collective-permute-start.5 = (f32[3,8,128]{2,1,0:T(8,128)S(1)}, f32[3,8,128]{2,1,0:T(8,128)S(1)}, u32[]{:S(2)}, u32[]{:S(2)}) collective-permute-start(f32[3,8,128]{2,1,0:T(8,128)S(1)} %get-tuple-element.69), channel_id=1, source_target_pairs={{4,0},{8,4},{12,8},{16,12},{20,16},{24,20},{28,24},{32,28},{36,32}... | collective-permute-start | bytes 36872 | tf_op jit(solution)/shard_map/ppermute | solution.py:454
  25.3 5.7 %collective-permute-start.4 = (f32[3,8,128]{2,1,0:T(8,128)S(1)}, f32[3,8,128]{2,1,0:T(8,128)S(1)}, u32[]{:S(2)}, u32[]{:S(2)}) collective-permute-start(f32[3,8,128]{2,1,0:T(8,128)S(1)} %get-tuple-element.69), channel_id=1, source_target_pairs={{60,0},{0,4},{4,8},{8,12},{12,16},{16,20},{20,24},{24,28},{28,32},... | collective-permute-start | bytes 36872 | tf_op jit(solution)/shard_map/ppermute | solution.py:454
  39.9 6.9 %collective-permute-start.7 = (f32[4,3,3,8,128]{4,3,2,1,0:T(8,128)S(1)}, f32[4,3,3,8,128]{4,3,2,1,0:T(8,128)S(1)}, u32[]{:S(2)}, u32[]{:S(2)}) collective-permute-start(f32[4,3,3,8,128]{4,3,2,1,0:T(8,128)S(1)} %all_to_all.20.middle.c1), channel_id=1, source_target_pairs={{64,0},{128,64},{192,128},{256,192},{320,256},{384,320},{448,384},... | collective-permute-start | bytes 442376 | tf_op jit(solution)/shard_map/ppermute | solution.py:454
  44.4 2.4 %collective-permute-start.6 = (f32[4,3,3,8,128]{4,3,2,1,0:T(8,128)S(1)}, f32[4,3,3,8,128]{4,3,2,1,0:T(8,128)S(1)}, u32[]{:S(2)}, u32[]{:S(2)}) collective-permute-start(f32[4,3,3,8,128]{4,3,2,1,0:T(8,128)S(1)} %all_to_all.20.middle.c1), channel_id=1, source_target_pairs={{448,0},{0,64},{64,128},{128,192},{192,256},{256,320},{320,384},{3... | collective-permute-start | bytes 442376 | tf_op jit(solution)/shard_map/ppermute | solution.py:454
  63.1 8.0 %collective-permute-start.9 = (f32[12,8,128]{2,1,0:T(8,128)S(1)}, f32[12,8,128]{2,1,0:T(8,128)S(1)}, u32[]{:S(2)}, u32[]{:S(2)}) collective-permute-start(f32[12,8,128]{2,1,0:T(8,128)S(1)} %shard_map.91.s1), channel_id=1, source_target_pairs={{4,0},{8,4},{12,8},{16,12},{20,16},{24,20},{28,24},{32,28},{36,32}... | collective-permute-start | bytes 147464 | tf_op jit(solution)/shard_map/ppermute | solution.py:454
  65.1 6.1 %collective-permute-start.8 = (f32[12,8,128]{2,1,0:T(8,128)S(1)}, f32[12,8,128]{2,1,0:T(8,128)S(1)}, u32[]{:S(2)}, u32[]{:S(2)}) collective-permute-start(f32[12,8,128]{2,1,0:T(8,128)S(1)} %shard_map.91.s1), channel_id=1, source_target_pairs={{60,0},{0,4},{4,8},{8,12},{12,16},{16,20},{20,24},{24,28},{28,32},... | collective-permute-start | bytes 147464 | tf_op jit(solution)/shard_map/ppermute | solution.py:454
  74.5 8.6 %collective-permute-start.10 = (f32[8,128]{1,0:T(8,128)S(1)}, f32[8,128]{1,0:T(8,128)S(1)}, u32[]{:S(2)}, u32[]{:S(2)}) collective-permute-start(f32[8,128]{1,0:T(8,128)S(1)} %get-tuple-element.81), channel_id=1, source_target_pairs={{64,0},{128,64},{192,128},{256,192},{320,256},{384,320},{448,384},... | collective-permute-start | bytes 12296 | tf_op jit(solution)/shard_map/ppermute | solution.py:454
  75.8 7.3 %collective-permute-start.11 = (f32[8,128]{1,0:T(8,128)S(1)}, f32[8,128]{1,0:T(8,128)S(1)}, u32[]{:S(2)}, u32[]{:S(2)}) collective-permute-start(f32[8,128]{1,0:T(8,128)S(1)} %get-tuple-element.82), channel_id=1, source_target_pairs={{448,0},{0,64},{64,128},{128,192},{192,256},{256,320},{320,384},{3... | collective-permute-start | bytes 12296 | tf_op jit(solution)/shard_map/ppermute | solution.py:454
  77.8 5.3 %collective-permute-start.12 = (f32[8,128]{1,0:T(8,128)S(1)}, f32[8,128]{1,0:T(8,128)S(1)}, u32[]{:S(2)}, u32[]{:S(2)}) collective-permute-start(f32[8,128]{1,0:T(8,128)S(1)} %get-tuple-element.83), channel_id=1, source_target_pairs={{4,0},{8,4},{12,8},{16,12},{20,16},{24,20},{28,24},{32,28},{36,32}... | collective-permute-start | bytes 12296 | tf_op jit(solution)/shard_map/ppermute | solution.py:454
  79.8 5.6 %collective-permute-start.13 = (f32[8,128]{1,0:T(8,128)S(1)}, f32[8,128]{1,0:T(8,128)S(1)}, u32[]{:S(2)}, u32[]{:S(2)}) collective-permute-start(f32[8,128]{1,0:T(8,128)S(1)} %get-tuple-element.84), channel_id=1, source_target_pairs={{60,0},{0,4},{4,8},{8,12},{12,16},{16,20},{20,24},{24,28},{28,32},... | collective-permute-start | bytes 12296 | tf_op jit(solution)/shard_map/ppermute | solution.py:454
  85.5 5.3 %collective-permute-start.15 = (f32[3,8,128]{2,1,0:T(8,128)S(1)}, f32[3,8,128]{2,1,0:T(8,128)S(1)}, u32[]{:S(2)}, u32[]{:S(2)}) collective-permute-start(f32[3,8,128]{2,1,0:T(8,128)S(1)} %get-tuple-element.92), channel_id=1, source_target_pairs={{4,0},{8,4},{12,8},{16,12},{20,16},{24,20},{28,24},{32,28},{36,32}... | collective-permute-start | bytes 36872 | tf_op jit(solution)/shard_map/ppermute | solution.py:454
  87.5 5.7 %collective-permute-start.14 = (f32[3,8,128]{2,1,0:T(8,128)S(1)}, f32[3,8,128]{2,1,0:T(8,128)S(1)}, u32[]{:S(2)}, u32[]{:S(2)}) collective-permute-start(f32[3,8,128]{2,1,0:T(8,128)S(1)} %get-tuple-element.92), channel_id=1, source_target_pairs={{60,0},{0,4},{4,8},{8,12},{12,16},{16,20},{20,24},{24,28},{28,32},... | collective-permute-start | bytes 36872 | tf_op jit(solution)/shard_map/ppermute | solution.py:454
  101.5 7.7 %collective-permute-start.17 = (f32[4,3,3,8,128]{4,3,2,1,0:T(8,128)S(1)}, f32[4,3,3,8,128]{4,3,2,1,0:T(8,128)S(1)}, u32[]{:S(2)}, u32[]{:S(2)}) collective-permute-start(f32[4,3,3,8,128]{4,3,2,1,0:T(8,128)S(1)} %all_to_all.22.middle.c1), channel_id=1, source_target_pairs={{64,0},{128,64},{192,128},{256,192},{320,256},{384,320},{448,384},... | collective-permute-start | bytes 442376 | tf_op jit(solution)/shard_map/ppermute | solution.py:454
  104.7 4.4 %collective-permute-start.16 = (f32[4,3,3,8,128]{4,3,2,1,0:T(8,128)S(1)}, f32[4,3,3,8,128]{4,3,2,1,0:T(8,128)S(1)}, u32[]{:S(2)}, u32[]{:S(2)}) collective-permute-start(f32[4,3,3,8,128]{4,3,2,1,0:T(8,128)S(1)} %all_to_all.22.middle.c1), channel_id=1, source_target_pairs={{448,0},{0,64},{64,128},{128,192},{192,256},{256,320},{320,384},{3... | collective-permute-start | bytes 442376 | tf_op jit(solution)/shard_map/ppermute | solution.py:454
  124.0 8.0 %collective-permute-start.19 = (f32[12,8,128]{2,1,0:T(8,128)S(1)}, f32[12,8,128]{2,1,0:T(8,128)S(1)}, u32[]{:S(2)}, u32[]{:S(2)}) collective-permute-start(f32[12,8,128]{2,1,0:T(8,128)S(1)} %shard_map.97.s1), channel_id=1, source_target_pairs={{4,0},{8,4},{12,8},{16,12},{20,16},{24,20},{28,24},{32,28},{36,32}... | collective-permute-start | bytes 147464 | tf_op jit(solution)/shard_map/ppermute | solution.py:454
  126.5 6.0 %collective-permute-start.18 = (f32[12,8,128]{2,1,0:T(8,128)S(1)}, f32[12,8,128]{2,1,0:T(8,128)S(1)}, u32[]{:S(2)}, u32[]{:S(2)}) collective-permute-start(f32[12,8,128]{2,1,0:T(8,128)S(1)} %shard_map.97.s1), channel_id=1, source_target_pairs={{60,0},{0,4},{4,8},{8,12},{12,16},{16,20},{20,24},{24,28},{28,32},... | collective-permute-start | bytes 147464 | tf_op jit(solution)/shard_map/ppermute | solution.py:454

commit v7 on v6

--- a/solution.py
+++ b/solution.py
@@ -139,7 +139,7 @@
 
 
 def unpack_kernel(
-    step, count_ref, place_in, speed_in, slots_in, a0, a1, a2, a3, place_ref, speed_ref, sent_ref
+    step, count_ref, place_in, speed_in, slots_in, a2, a3, a0, a1, place_ref, speed_ref, sent_ref
 ):
     slots_ref = slots_in.at[step]
     total = jnp.zeros((160, 128), jnp.float32)
@@ -456,10 +456,10 @@
 
 def migrants(packed):
     return (
+        moved(packed[3], "gy", 1),
+        moved(packed[2], "gy", -1),
         moved(packed[1], "gx", 1),
         moved(packed[0], "gx", -1),
-        moved(packed[3], "gy", 1),
-        moved(packed[2], "gy", -1),
     )
 
 

time: 138 us -> 139 us (level)
  Pallas kernels: 23.4 us -> 17.3 us
  blocking collectives: 43.3 us -> 46.8 us
  starting transfers between devices: 54.6 us -> 57.2 us
    ppermute x20, starting transfers between devices: 54.6 us -> 57.2 us  [moved(): lax.ppermute(values, axis, [((i + shift) % count, i) for i in range(count)])]
    all_to_all x2, blocking collectives: 26 us -> 28 us  [slope_column(): plane = lax.all_to_all(copies, ('gx', 'gz'), 0, 0, tiled=True)]
    pallas_call x2, Pallas kernels: 7.06 us -> 5.3 us  [per_device(): call(functools.partial(late_force_kernel, None if last else n + 1), [atom...]
    pallas_call x2, Pallas kernels: 5.11 us -> 3.5 us  [per_device(): call(late_density_kernel, [block, shrinks], [ANY] + [VMEM] * 6, pair_scra...]
    pallas_call x2, Pallas kernels: 4.72 us -> 3.12 us  [per_device(): call(early_density_kernel, [columns, block, shrinks], [ANY, VMEM], pair_s...]
    all_to_all x2, blocking collectives: 17.2 us -> 18.8 us  [around(): tower = lax.all_to_all(copies, 'gz', 0, 0, tiled=True)]
  transfers between devices with their start and end apart: 20 -> 20, of which waited for: 6 -> 9; matrix products, arithmetic and copies ran while one was open for 0% -> 0% of each run, Pallas kernels for 8% -> 6%
where the time goes in v7:
time: 139 us; the launch traced here: 137 us
  starting transfers between devices  57.2 us (41%)
  blocking collectives  46.8 us (34%)
  Pallas kernels  17.3 us (12%)
  waiting for transfers between devices  11.5 us (8%)
  between operations  2.22 us (2%)
  local copies, waits for them, and re-layouts  1.41 us (1%)
    ppermute x20, starting transfers between devices, moved(): lax.ppermute(values, axis, [((i + shift) % count, i) for i in range(count)])  57.2 us
    all_to_all x2, blocking collectives, slope_column(): plane = lax.all_to_all(copies, ('gx', 'gz'), 0, 0, tiled=True)  28 us
    all_to_all x2, blocking collectives, around(): tower = lax.all_to_all(copies, 'gz', 0, 0, tiled=True)  18.8 us
    ppermute x20, waiting for transfers between devices, moved(): lax.ppermute(values, axis, [((i + shift) % count, i) for i in range(count)])  11.5 us
    pallas_call x2, Pallas kernels, per_device(): call(functools.partial(late_force_kernel, None if last else n + 1), [atom...  5.3 us
    pallas_call x2, Pallas kernels, per_device(): call(early_force_kernel, [slope_columns, atoms], [ANY] + [VMEM] * 8, pair...  4.17 us
    pallas_call x2, Pallas kernels, per_device(): call(late_density_kernel, [block, shrinks], [ANY] + [VMEM] * 6, pair_scra...  3.5 us
    pallas_call x2, Pallas kernels, per_device(): call(early_density_kernel, [columns, block, shrinks], [ANY, VMEM], pair_s...  3.12 us
  transfers between devices with their start and end apart: 20, of which 9 were waited for; matrix products, arithmetic and copies ran while one was open for 0% of the time, Pallas kernels for 6%

profile of v7, /device:TPU:1, one launch (start us, length us, event | category | flops | bytes accessed | tf_op | source)
XLA Modules:
  0.0 137.1 jit_solution(5874516682436707092)
XLA Ops:
  2.3 12.0 %collective-permute-start = (f32[8,128]{1,0:T(8,128)S(1)}, f32[8,128]{1,0:T(8,128)S(1)}, u32[]{:S(2)}, u32[]{:S(2)}) collective-permute-start(f32[8,128]{1,0:T(8,128)S(1)} %get-tuple-element.54), channel_id=1, source_target_pairs={{4,0},{8,4},{12,8},{16,12},{20,16},{24,20},{28,24},{32,28},{36,32}... | collective-permute-start | bytes 12296 | tf_op jit(solution)/shard_map/ppermute | solution.py:454
  14.3 1.9 %collective-permute-start.1 = (f32[8,128]{1,0:T(8,128)S(1)}, f32[8,128]{1,0:T(8,128)S(1)}, u32[]{:S(2)}, u32[]{:S(2)}) collective-permute-start(f32[8,128]{1,0:T(8,128)S(1)} %get-tuple-element.55), channel_id=1, source_target_pairs={{60,0},{0,4},{4,8},{8,12},{12,16},{16,20},{20,24},{24,28},{28,32},... | collective-permute-start | bytes 12296 | tf_op jit(solution)/shard_map/ppermute | solution.py:454
  17.2 1.1 collective-permute-start.3
  21.0 4.9 %collective-permute-start.5 = (f32[3,8,128]{2,1,0:T(8,128)S(1)}, f32[3,8,128]{2,1,0:T(8,128)S(1)}, u32[]{:S(2)}, u32[]{:S(2)}) collective-permute-start(f32[3,8,128]{2,1,0:T(8,128)S(1)} %get-tuple-element.69), channel_id=1, source_target_pairs={{4,0},{8,4},{12,8},{16,12},{20,16},{24,20},{28,24},{32,28},{36,32}... | collective-permute-start | bytes 36872 | tf_op jit(solution)/shard_map/ppermute | solution.py:454
  25.9 1.9 %collective-permute-start.4 = (f32[3,8,128]{2,1,0:T(8,128)S(1)}, f32[3,8,128]{2,1,0:T(8,128)S(1)}, u32[]{:S(2)}, u32[]{:S(2)}) collective-permute-start(f32[3,8,128]{2,1,0:T(8,128)S(1)} %get-tuple-element.69), channel_id=1, source_target_pairs={{60,0},{0,4},{4,8},{8,12},{12,16},{16,20},{20,24},{24,28},{28,32},... | collective-permute-start | bytes 36872 | tf_op jit(solution)/shard_map/ppermute | solution.py:454
  27.8 3.7 %collective-permute-done.4 = f32[3,8,128]{2,1,0:T(8,128)S(1)} collective-permute-done((f32[3,8,128]{2,1,0:T(8,128)S(1)}, f32[3,8,128]{2,1,0:T(8,128)S(1)}, u32[]{:S(2)}, u32[]{:S(2)}) %collective-permute-start.4) | collective-permute-done | bytes 12320 | tf_op jit(solution)/shard_map/ppermute | solution.py:454
  31.6 8.9 %all_to_all.20.middle.c1 = f32[4,3,3,8,128]{4,3,2,1,0:T(8,128)S(1)} all-to-all(f32[4,3,3,8,128]{4,3,2,1,0:T(8,128)S(1)} %broadcast_in_dim.8), channel_id=1, replica_groups=mesh['gx'=8,'gy'=16,'gz'=4] {'gz'}, dimensions={0} | all-to-all | bytes 294912 | tf_op jit(solution)/shard_map/all_to_all | solution.py:469
  40.5 5.1 %collective-permute-start.7 = (f32[4,3,3,8,128]{4,3,2,1,0:T(8,128)S(1)}, f32[4,3,3,8,128]{4,3,2,1,0:T(8,128)S(1)}, u32[]{:S(2)}, u32[]{:S(2)}) collective-permute-start(f32[4,3,3,8,128]{4,3,2,1,0:T(8,128)S(1)} %all_to_all.20.middle.c1), channel_id=1, source_target_pairs={{64,0},{128,64},{192,128},{256,192},{320,256},{384,320},{448,384},... | collective-permute-start | bytes 442376 | tf_op jit(solution)/shard_map/ppermute | solution.py:454
  45.6 1.6 %shard_map.89 = (f32[32,128,128]{2,1,0:T(8,128)S(1)}, f32[8,128]{1,0:T(8,128)S(1)}, f32[130,128,128]{2,1,0:T(8,128)S(1)}) custom-call(s32[8,128]{1,0:T(8,128)S(1)} %get-tuple-element.93.plan_in, f32[4,3,3,8,128]{4,3,2,1,0:T(8,128)S(1)} %all_to_all.20.middle.c1), custom_call_target="tpu_custom_call" | custom-call | flops 60000000 | bytes 6000000 | tf_op jit(solution)/shard_map/pallas_call | solution.py:519
  47.7 1.8 %shard_map.90 = (f32[8,128]{1,0:T(8,128)S(1)}, f32[130,128,128]{2,1,0:T(8,128)S(1)}) custom-call(s32[8,128]{1,0:T(8,128)S(1)} %get-tuple-element.93.plan_in, f32[8,128]{1,0:T(8,128)S(1)} %get-tuple-element.95.selves_ref, f32[8,128]{1,0:T(8,128)S(1)} %get-tuple-element.73.early_ref, f32[32,128,128]{2,1,0:T(8,128)S(1)} %get-tuple-element.71.column_ref, ...), custom_call_target="tpu_custom_call" | custom-call | flops 1000000 | bytes 100000 | tf_op jit(solution)/shard_map/pallas_call | solution.py:526
  49.4 15.0 %all_to_all.21.plane_ref = f32[32,8,128]{2,1,0:T(8,128)S(1)} all-to-all(f32[32,8,128]{2,1,0:T(8,128)S(1)} %broadcast_in_dim.9), channel_id=1, replica_groups=mesh['gx'=8,'gy'=16,'gz'=4] {'gx','gz'}, dimensions={0} | all-to-all | bytes 262144 | tf_op jit(solution)/shard_map/all_to_all | solution.py:476
  64.5 1.9 %collective-permute-start.9 = (f32[12,8,128]{2,1,0:T(8,128)S(1)}, f32[12,8,128]{2,1,0:T(8,128)S(1)}, u32[]{:S(2)}, u32[]{:S(2)}) collective-permute-start(f32[12,8,128]{2,1,0:T(8,128)S(1)} %shard_map.91.s1), channel_id=1, source_target_pairs={{4,0},{8,4},{12,8},{16,12},{20,16},{24,20},{28,24},{32,28},{36,32}... | collective-permute-start | bytes 147464 | tf_op jit(solution)/shard_map/ppermute | solution.py:454
  66.4 3.4 %collective-permute-start.8 = (f32[12,8,128]{2,1,0:T(8,128)S(1)}, f32[12,8,128]{2,1,0:T(8,128)S(1)}, u32[]{:S(2)}, u32[]{:S(2)}) collective-permute-start(f32[12,8,128]{2,1,0:T(8,128)S(1)} %shard_map.91.s1), channel_id=1, source_target_pairs={{60,0},{0,4},{4,8},{8,12},{12,16},{16,20},{20,24},{24,28},{28,32},... | collective-permute-start | bytes 147464 | tf_op jit(solution)/shard_map/ppermute | solution.py:454
  69.8 2.1 %shard_map.92 = (f32[8,128,128]{2,1,0:T(8,128)S(1)}, f32[3,8,128]{2,1,0:T(8,128)S(1)}) custom-call(s32[8,128]{1,0:T(8,128)S(1)} %get-tuple-element.85.plan_in, f32[4,3,3,8,128]{4,3,2,1,0:T(8,128)S(1)} %collective-permute-done.6.behind.c0, f32[4,3,3,8,128]{4,3,2,1,0:T(8,128)S(1)} %all_to_all.20.middle.c1, ...), custom_call_target="tpu_custom_call" | custom-call | flops 60000000 | bytes 6000000 | tf_op jit(solution)/shard_map/pallas_call | solution.py:534
  72.4 2.5 %shard_map.93 = (f32[3,8,128]{2,1,0:T(8,128)S(1)}, f32[3,8,128]{2,1,0:T(8,128)S(1)}, f32[8,128]{1,0:T(8,128)S(1)}, f32[8,128]{1,0:T(8,128)S(1)}, f32[8,128]{1,0:T(8,128)S(1)}, /*index=5*/f32[8,128]{1,0:T(8,128)S(1)}) custom-call(s32[8,128]{1,0:T(8,128)S(1)} %get-tuple-element.85.plan_in, f32[4,3,3,8,128]{4,3,2,1,0:T(8,128)S(1)} %collective-permute-done.6.behind.c0, ...), custom_call_target="tpu_custom_call" | custom-call | flops 1000000 | bytes 100000 | tf_op jit(solution)/shard_map/pallas_call | solution.py:542
  74.9 3.6 %collective-permute-start.10 = (f32[8,128]{1,0:T(8,128)S(1)}, f32[8,128]{1,0:T(8,128)S(1)}, u32[]{:S(2)}, u32[]{:S(2)}) collective-permute-start(f32[8,128]{1,0:T(8,128)S(1)} %get-tuple-element.81), channel_id=1, source_target_pairs={{4,0},{8,4},{12,8},{16,12},{20,16},{24,20},{28,24},{32,28},{36,32}... | collective-permute-start | bytes 12296 | tf_op jit(solution)/shard_map/ppermute | solution.py:454
  78.5 1.9 %collective-permute-start.11 = (f32[8,128]{1,0:T(8,128)S(1)}, f32[8,128]{1,0:T(8,128)S(1)}, u32[]{:S(2)}, u32[]{:S(2)}) collective-permute-start(f32[8,128]{1,0:T(8,128)S(1)} %get-tuple-element.82), channel_id=1, source_target_pairs={{60,0},{0,4},{4,8},{8,12},{12,16},{16,20},{20,24},{24,28},{28,32},... | collective-permute-start | bytes 12296 | tf_op jit(solution)/shard_map/ppermute | solution.py:454
  80.5 3.4 %collective-permute-start.12 = (f32[8,128]{1,0:T(8,128)S(1)}, f32[8,128]{1,0:T(8,128)S(1)}, u32[]{:S(2)}, u32[]{:S(2)}) collective-permute-start(f32[8,128]{1,0:T(8,128)S(1)} %get-tuple-element.83), channel_id=1, source_target_pairs={{64,0},{128,64},{192,128},{256,192},{320,256},{384,320},{448,384},... | collective-permute-start | bytes 12296 | tf_op jit(solution)/shard_map/ppermute | solution.py:454
  85.3 3.0 %collective-permute-start.15 = (f32[3,8,128]{2,1,0:T(8,128)S(1)}, f32[3,8,128]{2,1,0:T(8,128)S(1)}, u32[]{:S(2)}, u32[]{:S(2)}) collective-permute-start(f32[3,8,128]{2,1,0:T(8,128)S(1)} %get-tuple-element.92), channel_id=1, source_target_pairs={{4,0},{8,4},{12,8},{16,12},{20,16},{24,20},{28,24},{32,28},{36,32}... | collective-permute-start | bytes 36872 | tf_op jit(solution)/shard_map/ppermute | solution.py:454
  88.3 2.3 %collective-permute-start.14 = (f32[3,8,128]{2,1,0:T(8,128)S(1)}, f32[3,8,128]{2,1,0:T(8,128)S(1)}, u32[]{:S(2)}, u32[]{:S(2)}) collective-permute-start(f32[3,8,128]{2,1,0:T(8,128)S(1)} %get-tuple-element.92), channel_id=1, source_target_pairs={{60,0},{0,4},{4,8},{8,12},{12,16},{16,20},{20,24},{24,28},{28,32},... | collective-permute-start | bytes 36872 | tf_op jit(solution)/shard_map/ppermute | solution.py:454
  90.6 3.4 %collective-permute-done.14 = f32[3,8,128]{2,1,0:T(8,128)S(1)} collective-permute-done((f32[3,8,128]{2,1,0:T(8,128)S(1)}, f32[3,8,128]{2,1,0:T(8,128)S(1)}, u32[]{:S(2)}, u32[]{:S(2)}) %collective-permute-start.14) | collective-permute-done | bytes 12320 | tf_op jit(solution)/shard_map/ppermute | solution.py:454
  94.0 9.9 %all_to_all.22.middle.c1 = f32[4,3,3,8,128]{4,3,2,1,0:T(8,128)S(1)} all-to-all(f32[4,3,3,8,128]{4,3,2,1,0:T(8,128)S(1)} %broadcast_in_dim.10), channel_id=1, replica_groups=mesh['gx'=8,'gy'=16,'gz'=4] {'gz'}, dimensions={0} | all-to-all | bytes 294912 | tf_op jit(solution)/shard_map/all_to_all | solution.py:469
  103.9 3.3 %collective-permute-start.17 = (f32[4,3,3,8,128]{4,3,2,1,0:T(8,128)S(1)}, f32[4,3,3,8,128]{4,3,2,1,0:T(8,128)S(1)}, u32[]{:S(2)}, u32[]{:S(2)}) collective-permute-start(f32[4,3,3,8,128]{4,3,2,1,0:T(8,128)S(1)} %all_to_all.22.middle.c1), channel_id=1, source_target_pairs={{64,0},{128,64},{192,128},{256,192},{320,256},{384,320},{448,384},... | collective-permute-start | bytes 442376 | tf_op jit(solution)/shard_map/ppermute | solution.py:454
  107.1 1.3 collective-permute-start.16
  108.4 1.6 %shard_map.95 = (f32[32,128,128]{2,1,0:T(8,128)S(1)}, f32[8,128]{1,0:T(8,128)S(1)}, f32[130,128,128]{2,1,0:T(8,128)S(1)}) custom-call(s32[8,128]{1,0:T(8,128)S(1)} %get-tuple-element.93.plan_in, f32[4,3,3,8,128]{4,3,2,1,0:T(8,128)S(1)} %all_to_all.22.middle.c1), custom_call_target="tpu_custom_call" | custom-call | flops 60000000 | bytes 6000000 | tf_op jit(solution)/shard_map/pallas_call | solution.py:519
  110.0 1.5 %collective-permute-done.17.ahead.c2 = f32[4,3,3,8,128]{4,3,2,1,0:T(8,128)S(1)} collective-permute-done((f32[4,3,3,8,128]{4,3,2,1,0:T(8,128)S(1)}, f32[4,3,3,8,128]{4,3,2,1,0:T(8,128)S(1)}, u32[]{:S(2)}, u32[]{:S(2)}) %collective-permute-start.17) | collective-permute-done | bytes 147488 | tf_op jit(solution)/shard_map/ppermute | solution.py:454
  111.5 1.7 %shard_map.96 = (f32[8,128]{1,0:T(8,128)S(1)}, f32[130,128,128]{2,1,0:T(8,128)S(1)}) custom-call(s32[8,128]{1,0:T(8,128)S(1)} %get-tuple-element.93.plan_in, f32[8,128]{1,0:T(8,128)S(1)} %get-tuple-element.95.selves_ref, f32[8,128]{1,0:T(8,128)S(1)} %get-tuple-element.96.early_ref, f32[32,128,128]{2,1,0:T(8,128)S(1)} %get-tuple-element.94.column_ref, ...), custom_call_target="tpu_custom_call" | custom-call | flops 1000000 | bytes 100000 | tf_op jit(solution)/shard_map/pallas_call | solution.py:526
  113.3 13.0 %all_to_all.23.plane_ref = f32[32,8,128]{2,1,0:T(8,128)S(1)} all-to-all(f32[32,8,128]{2,1,0:T(8,128)S(1)} %broadcast_in_dim.11), channel_id=1, replica_groups=mesh['gx'=8,'gy'=16,'gz'=4] {'gx','gz'}, dimensions={0} | all-to-all | bytes 262144 | tf_op jit(solution)/shard_map/all_to_all | solution.py:476
  126.3 1.9 %collective-permute-start.19 = (f32[12,8,128]{2,1,0:T(8,128)S(1)}, f32[12,8,128]{2,1,0:T(8,128)S(1)}, u32[]{:S(2)}, u32[]{:S(2)}) collective-permute-start(f32[12,8,128]{2,1,0:T(8,128)S(1)} %shard_map.97.s1), channel_id=1, source_target_pairs={{4,0},{8,4},{12,8},{16,12},{20,16},{24,20},{28,24},{32,28},{36,32}... | collective-permute-start | bytes 147464 | tf_op jit(solution)/shard_map/ppermute | solution.py:454
  128.2 3.4 %collective-permute-start.18 = (f32[12,8,128]{2,1,0:T(8,128)S(1)}, f32[12,8,128]{2,1,0:T(8,128)S(1)}, u32[]{:S(2)}, u32[]{:S(2)}) collective-permute-start(f32[12,8,128]{2,1,0:T(8,128)S(1)} %shard_map.97.s1), channel_id=1, source_target_pairs={{60,0},{0,4},{4,8},{8,12},{12,16},{16,20},{20,24},{24,28},{28,32},... | collective-permute-start | bytes 147464 | tf_op jit(solution)/shard_map/ppermute | solution.py:454
  131.6 2.1 %shard_map.98 = (f32[8,128,128]{2,1,0:T(8,128)S(1)}, f32[3,8,128]{2,1,0:T(8,128)S(1)}) custom-call(s32[8,128]{1,0:T(8,128)S(1)} %get-tuple-element.85.plan_in, f32[4,3,3,8,128]{4,3,2,1,0:T(8,128)S(1)} %collective-permute-done.16.behind.c0, f32[4,3,3,8,128]{4,3,2,1,0:T(8,128)S(1)} %all_to_all.22.middle.c1, ...), custom_call_target="tpu_custom_call" | custom-call | flops 60000000 | bytes 6000000 | tf_op jit(solution)/shard_map/pallas_call | solution.py:534
  134.3 2.8 %shard_map.99 = (f32[3,8,128]{2,1,0:T(8,128)}, f32[3,8,128]{2,1,0:T(8,128)}) custom-call(s32[8,128]{1,0:T(8,128)S(1)} %get-tuple-element.85.plan_in, f32[4,3,3,8,128]{4,3,2,1,0:T(8,128)S(1)} %collective-permute-done.16.behind.c0, f32[4,3,3,8,128]{4,3,2,1,0:T(8,128)S(1)} %all_to_all.22.middle.c1, f32[4,3,3,8,128]{4,3,2,1,0:T(8,128)S(1)} %collective-permute-done.17.ahead.c2, ...), custom_call_target="tpu_custom_call" | custom-call | flops 1000000 | bytes 100000 | tf_op jit(solution)/shard_map/pallas_call | solution.py:542
  (37 shorter events, 7.2 us)
Async XLA Ops:
  1.4 0.7 copy-start
  2.3 18.5 %collective-permute-start = (f32[8,128]{1,0:T(8,128)S(1)}, f32[8,128]{1,0:T(8,128)S(1)}, u32[]{:S(2)}, u32[]{:S(2)}) collective-permute-start(f32[8,128]{1,0:T(8,128)S(1)} %get-tuple-element.54), channel_id=1, source_target_pairs={{4,0},{8,4},{12,8},{16,12},{20,16},{24,20},{28,24},{32,28},{36,32}... | collective-permute-start | bytes 12296 | tf_op jit(solution)/shard_map/ppermute | solution.py:454
  14.3 6.5 %collective-permute-start.1 = (f32[8,128]{1,0:T(8,128)S(1)}, f32[8,128]{1,0:T(8,128)S(1)}, u32[]{:S(2)}, u32[]{:S(2)}) collective-permute-start(f32[8,128]{1,0:T(8,128)S(1)} %get-tuple-element.55), channel_id=1, source_target_pairs={{60,0},{0,4},{4,8},{8,12},{12,16},{16,20},{20,24},{24,28},{28,32},... | collective-permute-start | bytes 12296 | tf_op jit(solution)/shard_map/ppermute | solution.py:454
  16.2 4.6 %collective-permute-start.2 = (f32[8,128]{1,0:T(8,128)S(1)}, f32[8,128]{1,0:T(8,128)S(1)}, u32[]{:S(2)}, u32[]{:S(2)}) collective-permute-start(f32[8,128]{1,0:T(8,128)S(1)} %get-tuple-element.56), channel_id=1, source_target_pairs={{64,0},{128,64},{192,128},{256,192},{320,256},{384,320},{448,384},... | collective-permute-start | bytes 12296 | tf_op jit(solution)/shard_map/ppermute | solution.py:454
  17.2 3.6 %collective-permute-start.3 = (f32[8,128]{1,0:T(8,128)S(1)}, f32[8,128]{1,0:T(8,128)S(1)}, u32[]{:S(2)}, u32[]{:S(2)}) collective-permute-start(f32[8,128]{1,0:T(8,128)S(1)} %get-tuple-element.57), channel_id=1, source_target_pairs={{448,0},{0,64},{64,128},{128,192},{192,256},{256,320},{320,384},{3... | collective-permute-start | bytes 12296 | tf_op jit(solution)/shard_map/ppermute | solution.py:454
  19.6 0.7 copy-start.1
  21.0 6.8 %collective-permute-start.5 = (f32[3,8,128]{2,1,0:T(8,128)S(1)}, f32[3,8,128]{2,1,0:T(8,128)S(1)}, u32[]{:S(2)}, u32[]{:S(2)}) collective-permute-start(f32[3,8,128]{2,1,0:T(8,128)S(1)} %get-tuple-element.69), channel_id=1, source_target_pairs={{4,0},{8,4},{12,8},{16,12},{20,16},{24,20},{28,24},{32,28},{36,32}... | collective-permute-start | bytes 36872 | tf_op jit(solution)/shard_map/ppermute | solution.py:454
  25.9 5.7 %collective-permute-start.4 = (f32[3,8,128]{2,1,0:T(8,128)S(1)}, f32[3,8,128]{2,1,0:T(8,128)S(1)}, u32[]{:S(2)}, u32[]{:S(2)}) collective-permute-start(f32[3,8,128]{2,1,0:T(8,128)S(1)} %get-tuple-element.69), channel_id=1, source_target_pairs={{60,0},{0,4},{4,8},{8,12},{12,16},{16,20},{20,24},{24,28},{28,32},... | collective-permute-start | bytes 36872 | tf_op jit(solution)/shard_map/ppermute | solution.py:454
  40.5 6.7 %collective-permute-start.7 = (f32[4,3,3,8,128]{4,3,2,1,0:T(8,128)S(1)}, f32[4,3,3,8,128]{4,3,2,1,0:T(8,128)S(1)}, u32[]{:S(2)}, u32[]{:S(2)}) collective-permute-start(f32[4,3,3,8,128]{4,3,2,1,0:T(8,128)S(1)} %all_to_all.20.middle.c1), channel_id=1, source_target_pairs={{64,0},{128,64},{192,128},{256,192},{320,256},{384,320},{448,384},... | collective-permute-start | bytes 442376 | tf_op jit(solution)/shard_map/ppermute | solution.py:454
  45.6 2.1 %collective-permute-start.6 = (f32[4,3,3,8,128]{4,3,2,1,0:T(8,128)S(1)}, f32[4,3,3,8,128]{4,3,2,1,0:T(8,128)S(1)}, u32[]{:S(2)}, u32[]{:S(2)}) collective-permute-start(f32[4,3,3,8,128]{4,3,2,1,0:T(8,128)S(1)} %all_to_all.20.middle.c1), channel_id=1, source_target_pairs={{448,0},{0,64},{64,128},{128,192},{192,256},{256,320},{320,384},{3... | collective-permute-start | bytes 442376 | tf_op jit(solution)/shard_map/ppermute | solution.py:454
  64.5 7.4 %collective-permute-start.9 = (f32[12,8,128]{2,1,0:T(8,128)S(1)}, f32[12,8,128]{2,1,0:T(8,128)S(1)}, u32[]{:S(2)}, u32[]{:S(2)}) collective-permute-start(f32[12,8,128]{2,1,0:T(8,128)S(1)} %shard_map.91.s1), channel_id=1, source_target_pairs={{4,0},{8,4},{12,8},{16,12},{20,16},{24,20},{28,24},{32,28},{36,32}... | collective-permute-start | bytes 147464 | tf_op jit(solution)/shard_map/ppermute | solution.py:454
  66.4 6.0 %collective-permute-start.8 = (f32[12,8,128]{2,1,0:T(8,128)S(1)}, f32[12,8,128]{2,1,0:T(8,128)S(1)}, u32[]{:S(2)}, u32[]{:S(2)}) collective-permute-start(f32[12,8,128]{2,1,0:T(8,128)S(1)} %shard_map.91.s1), channel_id=1, source_target_pairs={{60,0},{0,4},{4,8},{8,12},{12,16},{16,20},{20,24},{24,28},{28,32},... | collective-permute-start | bytes 147464 | tf_op jit(solution)/shard_map/ppermute | solution.py:454
  74.9 9.0 %collective-permute-start.10 = (f32[8,128]{1,0:T(8,128)S(1)}, f32[8,128]{1,0:T(8,128)S(1)}, u32[]{:S(2)}, u32[]{:S(2)}) collective-permute-start(f32[8,128]{1,0:T(8,128)S(1)} %get-tuple-element.81), channel_id=1, source_target_pairs={{4,0},{8,4},{12,8},{16,12},{20,16},{24,20},{28,24},{32,28},{36,32}... | collective-permute-start | bytes 12296 | tf_op jit(solution)/shard_map/ppermute | solution.py:454
  78.5 5.6 %collective-permute-start.11 = (f32[8,128]{1,0:T(8,128)S(1)}, f32[8,128]{1,0:T(8,128)S(1)}, u32[]{:S(2)}, u32[]{:S(2)}) collective-permute-start(f32[8,128]{1,0:T(8,128)S(1)} %get-tuple-element.82), channel_id=1, source_target_pairs={{60,0},{0,4},{4,8},{8,12},{12,16},{16,20},{20,24},{24,28},{28,32},... | collective-permute-start | bytes 12296 | tf_op jit(solution)/shard_map/ppermute | solution.py:454
  80.5 4.3 %collective-permute-start.12 = (f32[8,128]{1,0:T(8,128)S(1)}, f32[8,128]{1,0:T(8,128)S(1)}, u32[]{:S(2)}, u32[]{:S(2)}) collective-permute-start(f32[8,128]{1,0:T(8,128)S(1)} %get-tuple-element.83), channel_id=1, source_target_pairs={{64,0},{128,64},{192,128},{256,192},{320,256},{384,320},{448,384},... | collective-permute-start | bytes 12296 | tf_op jit(solution)/shard_map/ppermute | solution.py:454
  83.9 1.2 collective-permute-start.13
  85.3 5.3 %collective-permute-start.15 = (f32[3,8,128]{2,1,0:T(8,128)S(1)}, f32[3,8,128]{2,1,0:T(8,128)S(1)}, u32[]{:S(2)}, u32[]{:S(2)}) collective-permute-start(f32[3,8,128]{2,1,0:T(8,128)S(1)} %get-tuple-element.92), channel_id=1, source_target_pairs={{4,0},{8,4},{12,8},{16,12},{20,16},{24,20},{28,24},{32,28},{36,32}... | collective-permute-start | bytes 36872 | tf_op jit(solution)/shard_map/ppermute | solution.py:454
  88.3 5.7 %collective-permute-start.14 = (f32[3,8,128]{2,1,0:T(8,128)S(1)}, f32[3,8,128]{2,1,0:T(8,128)S(1)}, u32[]{:S(2)}, u32[]{:S(2)}) collective-permute-start(f32[3,8,128]{2,1,0:T(8,128)S(1)} %get-tuple-element.92), channel_id=1, source_target_pairs={{60,0},{0,4},{4,8},{8,12},{12,16},{16,20},{20,24},{24,28},{28,32},... | collective-permute-start | bytes 36872 | tf_op jit(solution)/shard_map/ppermute | solution.py:454
  103.9 7.7 %collective-permute-start.17 = (f32[4,3,3,8,128]{4,3,2,1,0:T(8,128)S(1)}, f32[4,3,3,8,128]{4,3,2,1,0:T(8,128)S(1)}, u32[]{:S(2)}, u32[]{:S(2)}) collective-permute-start(f32[4,3,3,8,128]{4,3,2,1,0:T(8,128)S(1)} %all_to_all.22.middle.c1), channel_id=1, source_target_pairs={{64,0},{128,64},{192,128},{256,192},{320,256},{384,320},{448,384},... | collective-permute-start | bytes 442376 | tf_op jit(solution)/shard_map/ppermute | solution.py:454
  107.1 4.4 %collective-permute-start.16 = (f32[4,3,3,8,128]{4,3,2,1,0:T(8,128)S(1)}, f32[4,3,3,8,128]{4,3,2,1,0:T(8,128)S(1)}, u32[]{:S(2)}, u32[]{:S(2)}) collective-permute-start(f32[4,3,3,8,128]{4,3,2,1,0:T(8,128)S(1)} %all_to_all.22.middle.c1), channel_id=1, source_target_pairs={{448,0},{0,64},{64,128},{128,192},{192,256},{256,320},{320,384},{3... | collective-permute-start | bytes 442376 | tf_op jit(solution)/shard_map/ppermute | solution.py:454
  126.3 7.4 %collective-permute-start.19 = (f32[12,8,128]{2,1,0:T(8,128)S(1)}, f32[12,8,128]{2,1,0:T(8,128)S(1)}, u32[]{:S(2)}, u32[]{:S(2)}) collective-permute-start(f32[12,8,128]{2,1,0:T(8,128)S(1)} %shard_map.97.s1), channel_id=1, source_target_pairs={{4,0},{8,4},{12,8},{16,12},{20,16},{24,20},{28,24},{32,28},{36,32}... | collective-permute-start | bytes 147464 | tf_op jit(solution)/shard_map/ppermute | solution.py:454
  128.2 6.0 %collective-permute-start.18 = (f32[12,8,128]{2,1,0:T(8,128)S(1)}, f32[12,8,128]{2,1,0:T(8,128)S(1)}, u32[]{:S(2)}, u32[]{:S(2)}) collective-permute-start(f32[12,8,128]{2,1,0:T(8,128)S(1)} %shard_map.97.s1), channel_id=1, source_target_pairs={{60,0},{0,4},{4,8},{8,12},{12,16},{16,20},{20,24},{24,28},{28,32},... | collective-permute-start | bytes 147464 | tf_op jit(solution)/shard_map/ppermute | solution.py:454

commit v8 on v3

--- a/solution.py
+++ b/solution.py
@@ -102,12 +102,31 @@
     plan_ref[3:8, :] = jnp.zeros((5, 128), jnp.int32)
 
 
-def plan_kernel(total_ref, count_ref, tiles_ref, density_plan, force_plan, selves_ref):
+def live_ghosts(cells, far):
+    lanes = lax.broadcasted_iota(jnp.int32, (8, 128), 1)
+    rows = lax.broadcasted_iota(jnp.int32, (8, 128), 0)
+    first = jnp.zeros((8, 128), jnp.float32)
+    for dx, cell in enumerate(cells):
+        for dy in range(3):
+            for level in range(4):
+                column = jnp.broadcast_to(cell[level, dy, 0][:, 0:1], (8, 128))
+                first = jnp.where(lanes == dx * 12 + dy * 4 + level, column, first)
+    live = jnp.where(first < 0.5 * far_away, 1.0, 0.0)
+    live = jnp.concatenate([live, jnp.zeros_like(live)], axis=0).astype(jnp.bfloat16)
+    bricks = lax.broadcasted_iota(jnp.int32, (128, 128), 0) == (far >> 3)
+    found = dot(live, jnp.where(bricks, 1.0, 0.0).astype(jnp.bfloat16), nn_dims)[0:8]
+    return jnp.sum(jnp.where(rows == (far & 7), found, 0.0), axis=0, keepdims=True) > 0.5
+
+
+def plan_kernel(total_ref, count_ref, tiles_ref, *rest):
+    *cells, density_plan, force_plan, selves_ref = rest
     zbrick = lax.axis_index("gz")
     near = tiles_ref[0:1, :]
     far = tiles_ref[1:2, :]
     listed = lax.broadcasted_iota(jnp.int32, (1, 128), 1) < total_ref[0]
     listed = jnp.logical_and(listed, near * 128 < count_ref[0])
+    if cells:
+        listed = jnp.logical_and(listed, live_ghosts(cells, far))
     brick = far >> 3
     put_plan(listed, near, far, jnp.logical_or(brick < 12, brick >= 24), density_plan)
     put_plan(listed, near, far, ((brick >> 2) + 2) % 3 != 0, force_plan)
@@ -479,15 +498,17 @@
         [atoms, atoms, jax.ShapeDtypeStruct(slots.shape, jnp.int32)] + [block] * 4,
         [VMEM] * 2,
     )(rows, slots)
-    plans = call(
-        plan_kernel, [plan_shape, plan_shape, block], [SMEM, SMEM, VMEM]
-    )(total, live_count, pair_tiles.reshape(2, 128))
+    plan_ins = total, live_count, pair_tiles.reshape(2, 128)
+    plan_outs = [plan_shape, plan_shape, block]
+    plans = call(plan_kernel, plan_outs, [SMEM, SMEM, VMEM])(*plan_ins)
     for n in range(steps):
         place, speed, sent = call(
             functools.partial(unpack_kernel, n), [atoms, atoms, atoms], [SMEM] + [VMEM] * 7
         )(live_count, place, speed, slots, *migrants(packed))
         cells, plans = around(sent, plans)
         density_plan, force_plan, selves = plans
+        if n == 0:
+            plans = call(plan_kernel, plan_outs, [SMEM, SMEM] + [VMEM] * 4)(*plan_ins, *cells)
         column, early = call(
             early_density_kernel,
             [columns, block],

time: 140 us -> 146 us (1.043)
  starting transfers between devices: 56.4 us -> 66.7 us
  Pallas kernels: 25 us -> 16.5 us
  waiting for transfers between devices: 8.51 us -> 12.3 us
    ppermute x20, starting transfers between devices: 56.4 us -> 66.7 us  [moved(): lax.ppermute(values, axis, [((i + shift) % count, i) for i in range(count)])]
    ppermute x20, waiting for transfers between devices: 8.51 us -> 12.3 us  [moved(): lax.ppermute(values, axis, [((i + shift) % count, i) for i in range(count)])]
    pallas_call x2, Pallas kernels: 7.95 us -> 4.96 us  [per_device(): call(functools.partial(late_force_kernel, None if last else n + 1), [atom...]
    pallas_call x2, Pallas kernels: 6.36 us -> 3.38 us  [per_device(): call(early_force_kernel, [slope_columns, atoms], [ANY] + [VMEM] * 6, pair...]
    pallas_call x2, Pallas kernels: 5.18 us -> 3.07 us  [per_device(): call(late_density_kernel, [block], [ANY] + [VMEM] * 6, pair_scratch(3, 1,...]
  transfers between devices with their start and end apart: 20 -> 20, of which waited for: 7 -> 6; matrix products, arithmetic and copies ran while one was open for 0% -> 0% of each run, Pallas kernels for 8% -> 5%
where the time goes in v8:
time: 146 us; the launch traced here: 144 us
  starting transfers between devices  66.7 us (46%)
  blocking collectives  43.8 us (30%)
  Pallas kernels  16.5 us (11%)
  waiting for transfers between devices  12.3 us (8%)
  between operations  2.28 us (2%)
    ppermute x20, starting transfers between devices, moved(): lax.ppermute(values, axis, [((i + shift) % count, i) for i in range(count)])  66.7 us
    all_to_all x2, blocking collectives, slope_column(): plane = lax.all_to_all(copies, ('gx', 'gz'), 0, 0, tiled=True)  27.7 us
    all_to_all x2, blocking collectives, around(): tower = lax.all_to_all(copies, 'gz', 0, 0, tiled=True)  16.2 us
    ppermute x20, waiting for transfers between devices, moved(): lax.ppermute(values, axis, [((i + shift) % count, i) for i in range(count)])  12.3 us
    pallas_call x2, Pallas kernels, per_device(): call(functools.partial(late_force_kernel, None if last else n + 1), [atom...  4.96 us
    pallas_call x2, Pallas kernels, per_device(): call(early_force_kernel, [slope_columns, atoms], [ANY] + [VMEM] * 6, pair...  3.38 us
    pallas_call x2, Pallas kernels, per_device(): call(early_density_kernel, [columns, block], [ANY, VMEM], pair_scratch(3,...  3.14 us
    pallas_call x2, Pallas kernels, per_device(): call(late_density_kernel, [block], [ANY] + [VMEM] * 6, pair_scratch(3, 1,...  3.07 us
  transfers between devices with their start and end apart: 20, of which 6 were waited for; matrix products, arithmetic and copies ran while one was open for 0% of the time, Pallas kernels for 5%

profile of v8, /device:TPU:1, one launch (start us, length us, event | category | flops | bytes accessed | tf_op | source)
XLA Modules:
  0.0 143.8 jit_solution(2991561409466770487)
XLA Ops:
  2.3 6.9 %collective-permute-start = (f32[8,128]{1,0:T(8,128)S(1)}, f32[8,128]{1,0:T(8,128)S(1)}, u32[]{:S(2)}, u32[]{:S(2)}) collective-permute-start(f32[8,128]{1,0:T(8,128)S(1)} %get-tuple-element.50), channel_id=1, source_target_pairs={{64,0},{128,64},{192,128},{256,192},{320,256},{384,320},{448,384},... | collective-permute-start | bytes 12296 | tf_op jit(solution)/shard_map/ppermute | solution.py:444
  9.2 6.9 %collective-permute-start.2 = (f32[8,128]{1,0:T(8,128)S(1)}, f32[8,128]{1,0:T(8,128)S(1)}, u32[]{:S(2)}, u32[]{:S(2)}) collective-permute-start(f32[8,128]{1,0:T(8,128)S(1)} %get-tuple-element.52), channel_id=1, source_target_pairs={{4,0},{8,4},{12,8},{16,12},{20,16},{24,20},{28,24},{32,28},{36,32}... | collective-permute-start | bytes 12296 | tf_op jit(solution)/shard_map/ppermute | solution.py:444
  16.1 1.9 %collective-permute-start.3 = (f32[8,128]{1,0:T(8,128)S(1)}, f32[8,128]{1,0:T(8,128)S(1)}, u32[]{:S(2)}, u32[]{:S(2)}) collective-permute-start(f32[8,128]{1,0:T(8,128)S(1)} %get-tuple-element.53), channel_id=1, source_target_pairs={{60,0},{0,4},{4,8},{8,12},{12,16},{16,20},{20,24},{24,28},{28,32},... | collective-permute-start | bytes 12296 | tf_op jit(solution)/shard_map/ppermute | solution.py:444
  18.7 3.0 %collective-permute-done.3.a3 = f32[8,128]{1,0:T(8,128)S(1)} collective-permute-done((f32[8,128]{1,0:T(8,128)S(1)}, f32[8,128]{1,0:T(8,128)S(1)}, u32[]{:S(2)}, u32[]{:S(2)}) %collective-permute-start.3) | collective-permute-done | bytes 4128 | tf_op jit(solution)/shard_map/ppermute | solution.py:444
  21.8 1.9 %collective-permute-start.4 = (f32[3,8,128]{2,1,0:T(8,128)S(1)}, f32[3,8,128]{2,1,0:T(8,128)S(1)}, u32[]{:S(2)}, u32[]{:S(2)}) collective-permute-start(f32[3,8,128]{2,1,0:T(8,128)S(1)} %get-tuple-element.54), channel_id=1, source_target_pairs={{60,0},{0,4},{4,8},{8,12},{12,16},{16,20},{20,24},{24,28},{28,32},... | collective-permute-start | bytes 36872 | tf_op jit(solution)/shard_map/ppermute | solution.py:444
  23.8 4.6 %collective-permute-start.5 = (f32[3,8,128]{2,1,0:T(8,128)S(1)}, f32[3,8,128]{2,1,0:T(8,128)S(1)}, u32[]{:S(2)}, u32[]{:S(2)}) collective-permute-start(f32[3,8,128]{2,1,0:T(8,128)S(1)} %get-tuple-element.54), channel_id=1, source_target_pairs={{4,0},{8,4},{12,8},{16,12},{20,16},{24,20},{28,24},{32,28},{36,32}... | collective-permute-start | bytes 36872 | tf_op jit(solution)/shard_map/ppermute | solution.py:444
  30.2 8.9 %all_to_all.20.middle.c1.rest_1_ = f32[4,3,3,8,128]{4,3,2,1,0:T(8,128)S(1)} all-to-all(f32[4,3,3,8,128]{4,3,2,1,0:T(8,128)S(1)} %broadcast_in_dim.8), channel_id=1, replica_groups=mesh['gx'=8,'gy'=16,'gz'=4] {'gz'}, dimensions={0} | all-to-all | bytes 294912 | tf_op jit(solution)/shard_map/all_to_all | solution.py:462
  39.1 3.9 %collective-permute-start.6 = (f32[4,3,3,8,128]{4,3,2,1,0:T(8,128)S(1)}, f32[4,3,3,8,128]{4,3,2,1,0:T(8,128)S(1)}, u32[]{:S(2)}, u32[]{:S(2)}) collective-permute-start(f32[4,3,3,8,128]{4,3,2,1,0:T(8,128)S(1)} %all_to_all.20.middle.c1.rest_1_), channel_id=1, source_target_pairs={{448,0},{0,64},{64,128},{128,192},{192,256},{256,320},{320,384},{3... | collective-permute-start | bytes 442376 | tf_op jit(solution)/shard_map/ppermute | solution.py:444
  43.6 1.6 %shard_map.89 = (f32[32,128,128]{2,1,0:T(8,128)S(1)}, f32[8,128]{1,0:T(8,128)S(1)}) custom-call(s32[8,128]{1,0:T(8,128)S(1)} %get-tuple-element.61.plan_in, f32[4,3,3,8,128]{4,3,2,1,0:T(8,128)S(1)} %all_to_all.20.middle.c1.rest_1_), custom_call_target="tpu_custom_call" | custom-call | flops 60000000 | bytes 6000000 | tf_op jit(solution)/shard_map/pallas_call | solution.py:512
  45.2 2.7 %collective-permute-done.7.ahead.c2.rest_2_ = f32[4,3,3,8,128]{4,3,2,1,0:T(8,128)S(1)} collective-permute-done((f32[4,3,3,8,128]{4,3,2,1,0:T(8,128)S(1)}, f32[4,3,3,8,128]{4,3,2,1,0:T(8,128)S(1)}, u32[]{:S(2)}, u32[]{:S(2)}) %collective-permute-start.7) | collective-permute-done | bytes 147488 | tf_op jit(solution)/shard_map/ppermute | solution.py:444
  47.9 1.5 %shard_map.90.own_slope = f32[8,128]{1,0:T(8,128)S(1)} custom-call(s32[8,128]{1,0:T(8,128)S(1)} %get-tuple-element.61.plan_in, f32[8,128]{1,0:T(8,128)S(1)} %get-tuple-element.63.selves_ref, f32[8,128]{1,0:T(8,128)S(1)} %get-tuple-element.64.early_ref, f32[32,128,128]{2,1,0:T(8,128)S(1)} %get-tuple-element.62.column_ref, ...), custom_call_target="tpu_custom_call" | custom-call | flops 1000000 | bytes 100000 | tf_op jit(solution)/shard_map/pallas_call | solution.py:519
  49.5 14.5 %all_to_all.21.plane_ref = f32[32,8,128]{2,1,0:T(8,128)S(1)} all-to-all(f32[32,8,128]{2,1,0:T(8,128)S(1)} %broadcast_in_dim.9), channel_id=1, replica_groups=mesh['gx'=8,'gy'=16,'gz'=4] {'gx','gz'}, dimensions={0} | all-to-all | bytes 262144 | tf_op jit(solution)/shard_map/all_to_all | solution.py:469
  63.9 1.9 %collective-permute-start.8 = (f32[12,8,128]{2,1,0:T(8,128)S(1)}, f32[12,8,128]{2,1,0:T(8,128)S(1)}, u32[]{:S(2)}, u32[]{:S(2)}) collective-permute-start(f32[12,8,128]{2,1,0:T(8,128)S(1)} %shard_map.91.s1), channel_id=1, source_target_pairs={{60,0},{0,4},{4,8},{8,12},{12,16},{16,20},{20,24},{24,28},{28,32},... | collective-permute-start | bytes 147464 | tf_op jit(solution)/shard_map/ppermute | solution.py:444
  65.8 6.2 %collective-permute-start.9 = (f32[12,8,128]{2,1,0:T(8,128)S(1)}, f32[12,8,128]{2,1,0:T(8,128)S(1)}, u32[]{:S(2)}, u32[]{:S(2)}) collective-permute-start(f32[12,8,128]{2,1,0:T(8,128)S(1)} %shard_map.91.s1), channel_id=1, source_target_pairs={{4,0},{8,4},{12,8},{16,12},{20,16},{24,20},{28,24},{32,28},{36,32}... | collective-permute-start | bytes 147464 | tf_op jit(solution)/shard_map/ppermute | solution.py:444
  72.0 1.7 %shard_map.92 = (f32[8,128,128]{2,1,0:T(8,128)S(1)}, f32[3,8,128]{2,1,0:T(8,128)S(1)}) custom-call(s32[8,128]{1,0:T(8,128)S(1)} %get-tuple-element.58.plan_in, f32[4,3,3,8,128]{4,3,2,1,0:T(8,128)S(1)} %collective-permute-done.6.behind.c0.rest_0_, f32[4,3,3,8,128]{4,3,2,1,0:T(8,128)S(1)} %all_to_all.20.middle.c1.rest_1_, ...), custom_call_target="tpu_custom_call" | custom-call | flops 60000000 | bytes 6000000 | tf_op jit(solution)/shard_map/pallas_call | solution.py:527
  73.7 2.3 %shard_map.93 = (f32[3,8,128]{2,1,0:T(8,128)S(1)}, f32[3,8,128]{2,1,0:T(8,128)S(1)}, f32[8,128]{1,0:T(8,128)S(1)}, f32[8,128]{1,0:T(8,128)S(1)}, f32[8,128]{1,0:T(8,128)S(1)}, /*index=5*/f32[8,128]{1,0:T(8,128)S(1)}) custom-call(s32[8,128]{1,0:T(8,128)S(1)} %get-tuple-element.58.plan_in, f32[4,3,3,8,128]{4,3,2,1,0:T(8,128)S(1)} %collective-permute-done.6.behind.c0.rest_0_, ...), custom_call_target="tpu_custom_call" | custom-call | flops 1000000 | bytes 100000 | tf_op jit(solution)/shard_map/pallas_call | solution.py:535
  76.0 3.0 %collective-permute-start.10 = (f32[8,128]{1,0:T(8,128)S(1)}, f32[8,128]{1,0:T(8,128)S(1)}, u32[]{:S(2)}, u32[]{:S(2)}) collective-permute-start(f32[8,128]{1,0:T(8,128)S(1)} %get-tuple-element.71), channel_id=1, source_target_pairs={{64,0},{128,64},{192,128},{256,192},{320,256},{384,320},{448,384},... | collective-permute-start | bytes 12296 | tf_op jit(solution)/shard_map/ppermute | solution.py:444
  79.1 8.3 %collective-permute-start.12 = (f32[8,128]{1,0:T(8,128)S(1)}, f32[8,128]{1,0:T(8,128)S(1)}, u32[]{:S(2)}, u32[]{:S(2)}) collective-permute-start(f32[8,128]{1,0:T(8,128)S(1)} %get-tuple-element.73), channel_id=1, source_target_pairs={{4,0},{8,4},{12,8},{16,12},{20,16},{24,20},{28,24},{32,28},{36,32}... | collective-permute-start | bytes 12296 | tf_op jit(solution)/shard_map/ppermute | solution.py:444
  87.4 1.9 %collective-permute-start.13 = (f32[8,128]{1,0:T(8,128)S(1)}, f32[8,128]{1,0:T(8,128)S(1)}, u32[]{:S(2)}, u32[]{:S(2)}) collective-permute-start(f32[8,128]{1,0:T(8,128)S(1)} %get-tuple-element.74), channel_id=1, source_target_pairs={{60,0},{0,4},{4,8},{8,12},{12,16},{16,20},{20,24},{24,28},{28,32},... | collective-permute-start | bytes 12296 | tf_op jit(solution)/shard_map/ppermute | solution.py:444
  89.4 3.6 %collective-permute-done.13.a3 = f32[8,128]{1,0:T(8,128)S(1)} collective-permute-done((f32[8,128]{1,0:T(8,128)S(1)}, f32[8,128]{1,0:T(8,128)S(1)}, u32[]{:S(2)}, u32[]{:S(2)}) %collective-permute-start.13) | collective-permute-done | bytes 4128 | tf_op jit(solution)/shard_map/ppermute | solution.py:444
  93.2 1.9 %collective-permute-start.14 = (f32[3,8,128]{2,1,0:T(8,128)S(1)}, f32[3,8,128]{2,1,0:T(8,128)S(1)}, u32[]{:S(2)}, u32[]{:S(2)}) collective-permute-start(f32[3,8,128]{2,1,0:T(8,128)S(1)} %get-tuple-element.75), channel_id=1, source_target_pairs={{60,0},{0,4},{4,8},{8,12},{12,16},{16,20},{20,24},{24,28},{28,32},... | collective-permute-start | bytes 36872 | tf_op jit(solution)/shard_map/ppermute | solution.py:444
  95.1 4.6 %collective-permute-start.15 = (f32[3,8,128]{2,1,0:T(8,128)S(1)}, f32[3,8,128]{2,1,0:T(8,128)S(1)}, u32[]{:S(2)}, u32[]{:S(2)}) collective-permute-start(f32[3,8,128]{2,1,0:T(8,128)S(1)} %get-tuple-element.75), channel_id=1, source_target_pairs={{4,0},{8,4},{12,8},{16,12},{20,16},{24,20},{28,24},{32,28},{36,32}... | collective-permute-start | bytes 36872 | tf_op jit(solution)/shard_map/ppermute | solution.py:444
  100.5 7.3 %all_to_all.22.middle.c1 = f32[4,3,3,8,128]{4,3,2,1,0:T(8,128)S(1)} all-to-all(f32[4,3,3,8,128]{4,3,2,1,0:T(8,128)S(1)} %broadcast_in_dim.10), channel_id=1, replica_groups=mesh['gx'=8,'gy'=16,'gz'=4] {'gz'}, dimensions={0} | all-to-all | bytes 294912 | tf_op jit(solution)/shard_map/all_to_all | solution.py:462
  107.8 4.2 %collective-permute-start.16 = (f32[4,3,3,8,128]{4,3,2,1,0:T(8,128)S(1)}, f32[4,3,3,8,128]{4,3,2,1,0:T(8,128)S(1)}, u32[]{:S(2)}, u32[]{:S(2)}) collective-permute-start(f32[4,3,3,8,128]{4,3,2,1,0:T(8,128)S(1)} %all_to_all.22.middle.c1), channel_id=1, source_target_pairs={{448,0},{0,64},{64,128},{128,192},{192,256},{256,320},{320,384},{3... | collective-permute-start | bytes 442376 | tf_op jit(solution)/shard_map/ppermute | solution.py:444
  112.0 1.6 %shard_map.96 = (f32[32,128,128]{2,1,0:T(8,128)S(1)}, f32[8,128]{1,0:T(8,128)S(1)}) custom-call(s32[8,128]{1,0:T(8,128)S(1)} %get-tuple-element.82.plan_in, f32[4,3,3,8,128]{4,3,2,1,0:T(8,128)S(1)} %all_to_all.22.middle.c1), custom_call_target="tpu_custom_call" | custom-call | flops 60000000 | bytes 6000000 | tf_op jit(solution)/shard_map/pallas_call | solution.py:512
  114.1 2.5 %collective-permute-done.17.ahead.c2 = f32[4,3,3,8,128]{4,3,2,1,0:T(8,128)S(1)} collective-permute-done((f32[4,3,3,8,128]{4,3,2,1,0:T(8,128)S(1)}, f32[4,3,3,8,128]{4,3,2,1,0:T(8,128)S(1)}, u32[]{:S(2)}, u32[]{:S(2)}) %collective-permute-start.17) | collective-permute-done | bytes 147488 | tf_op jit(solution)/shard_map/ppermute | solution.py:444
  116.6 1.5 %shard_map.97.own_slope = f32[8,128]{1,0:T(8,128)S(1)} custom-call(s32[8,128]{1,0:T(8,128)S(1)} %get-tuple-element.82.plan_in, f32[8,128]{1,0:T(8,128)S(1)} %get-tuple-element.84.selves_ref, f32[8,128]{1,0:T(8,128)S(1)} %get-tuple-element.85.early_ref, f32[32,128,128]{2,1,0:T(8,128)S(1)} %get-tuple-element.83.column_ref, ...), custom_call_target="tpu_custom_call" | custom-call | flops 1000000 | bytes 100000 | tf_op jit(solution)/shard_map/pallas_call | solution.py:519
  118.1 13.2 %all_to_all.23.plane_ref = f32[32,8,128]{2,1,0:T(8,128)S(1)} all-to-all(f32[32,8,128]{2,1,0:T(8,128)S(1)} %broadcast_in_dim.11), channel_id=1, replica_groups=mesh['gx'=8,'gy'=16,'gz'=4] {'gx','gz'}, dimensions={0} | all-to-all | bytes 262144 | tf_op jit(solution)/shard_map/all_to_all | solution.py:469
  131.3 1.9 %collective-permute-start.18 = (f32[12,8,128]{2,1,0:T(8,128)S(1)}, f32[12,8,128]{2,1,0:T(8,128)S(1)}, u32[]{:S(2)}, u32[]{:S(2)}) collective-permute-start(f32[12,8,128]{2,1,0:T(8,128)S(1)} %shard_map.98.s1), channel_id=1, source_target_pairs={{60,0},{0,4},{4,8},{8,12},{12,16},{16,20},{20,24},{24,28},{28,32},... | collective-permute-start | bytes 147464 | tf_op jit(solution)/shard_map/ppermute | solution.py:444
  133.3 6.1 %collective-permute-start.19 = (f32[12,8,128]{2,1,0:T(8,128)S(1)}, f32[12,8,128]{2,1,0:T(8,128)S(1)}, u32[]{:S(2)}, u32[]{:S(2)}) collective-permute-start(f32[12,8,128]{2,1,0:T(8,128)S(1)} %shard_map.98.s1), channel_id=1, source_target_pairs={{4,0},{8,4},{12,8},{16,12},{20,16},{24,20},{28,24},{32,28},{36,32}... | collective-permute-start | bytes 147464 | tf_op jit(solution)/shard_map/ppermute | solution.py:444
  139.4 1.7 %shard_map.99 = (f32[8,128,128]{2,1,0:T(8,128)S(1)}, f32[3,8,128]{2,1,0:T(8,128)S(1)}) custom-call(s32[8,128]{1,0:T(8,128)S(1)} %get-tuple-element.79.plan_in, f32[4,3,3,8,128]{4,3,2,1,0:T(8,128)S(1)} %collective-permute-done.16.behind.c0, f32[4,3,3,8,128]{4,3,2,1,0:T(8,128)S(1)} %all_to_all.22.middle.c1, ...), custom_call_target="tpu_custom_call" | custom-call | flops 60000000 | bytes 6000000 | tf_op jit(solution)/shard_map/pallas_call | solution.py:527
  141.1 2.7 %shard_map.100 = (f32[3,8,128]{2,1,0:T(8,128)}, f32[3,8,128]{2,1,0:T(8,128)}) custom-call(s32[8,128]{1,0:T(8,128)S(1)} %get-tuple-element.79.plan_in, f32[4,3,3,8,128]{4,3,2,1,0:T(8,128)S(1)} %collective-permute-done.16.behind.c0, f32[4,3,3,8,128]{4,3,2,1,0:T(8,128)S(1)} %all_to_all.22.middle.c1, f32[4,3,3,8,128]{4,3,2,1,0:T(8,128)S(1)} %collective-permute-done.17.ahead.c2, ...), custom_call_target="tpu_custom_call" | custom-call | flops 1000000 | bytes 100000 | tf_op jit(solution)/shard_map/pallas_call | solution.py:535
  (40 shorter events, 5.3 us)
Async XLA Ops:
  1.4 0.7 copy-start
  2.3 16.3 %collective-permute-start = (f32[8,128]{1,0:T(8,128)S(1)}, f32[8,128]{1,0:T(8,128)S(1)}, u32[]{:S(2)}, u32[]{:S(2)}) collective-permute-start(f32[8,128]{1,0:T(8,128)S(1)} %get-tuple-element.50), channel_id=1, source_target_pairs={{64,0},{128,64},{192,128},{256,192},{320,256},{384,320},{448,384},... | collective-permute-start | bytes 12296 | tf_op jit(solution)/shard_map/ppermute | solution.py:444
  9.2 9.5 %collective-permute-start.1 = (f32[8,128]{1,0:T(8,128)S(1)}, f32[8,128]{1,0:T(8,128)S(1)}, u32[]{:S(2)}, u32[]{:S(2)}) collective-permute-start(f32[8,128]{1,0:T(8,128)S(1)} %get-tuple-element.51), channel_id=1, source_target_pairs={{448,0},{0,64},{64,128},{128,192},{192,256},{256,320},{320,384},{3... | collective-permute-start | bytes 12296 | tf_op jit(solution)/shard_map/ppermute | solution.py:444
  9.2 9.5 %collective-permute-start.2 = (f32[8,128]{1,0:T(8,128)S(1)}, f32[8,128]{1,0:T(8,128)S(1)}, u32[]{:S(2)}, u32[]{:S(2)}) collective-permute-start(f32[8,128]{1,0:T(8,128)S(1)} %get-tuple-element.52), channel_id=1, source_target_pairs={{4,0},{8,4},{12,8},{16,12},{20,16},{24,20},{28,24},{32,28},{36,32}... | collective-permute-start | bytes 12296 | tf_op jit(solution)/shard_map/ppermute | solution.py:444
  16.1 5.6 %collective-permute-start.3 = (f32[8,128]{1,0:T(8,128)S(1)}, f32[8,128]{1,0:T(8,128)S(1)}, u32[]{:S(2)}, u32[]{:S(2)}) collective-permute-start(f32[8,128]{1,0:T(8,128)S(1)} %get-tuple-element.53), channel_id=1, source_target_pairs={{60,0},{0,4},{4,8},{8,12},{12,16},{16,20},{20,24},{24,28},{28,32},... | collective-permute-start | bytes 12296 | tf_op jit(solution)/shard_map/ppermute | solution.py:444
  21.8 8.3 %collective-permute-start.4 = (f32[3,8,128]{2,1,0:T(8,128)S(1)}, f32[3,8,128]{2,1,0:T(8,128)S(1)}, u32[]{:S(2)}, u32[]{:S(2)}) collective-permute-start(f32[3,8,128]{2,1,0:T(8,128)S(1)} %get-tuple-element.54), channel_id=1, source_target_pairs={{60,0},{0,4},{4,8},{8,12},{12,16},{16,20},{20,24},{24,28},{28,32},... | collective-permute-start | bytes 36872 | tf_op jit(solution)/shard_map/ppermute | solution.py:444
  23.8 6.4 %collective-permute-start.5 = (f32[3,8,128]{2,1,0:T(8,128)S(1)}, f32[3,8,128]{2,1,0:T(8,128)S(1)}, u32[]{:S(2)}, u32[]{:S(2)}) collective-permute-start(f32[3,8,128]{2,1,0:T(8,128)S(1)} %get-tuple-element.54), channel_id=1, source_target_pairs={{4,0},{8,4},{12,8},{16,12},{20,16},{24,20},{28,24},{32,28},{36,32}... | collective-permute-start | bytes 36872 | tf_op jit(solution)/shard_map/ppermute | solution.py:444
  29.0 0.7 copy-start.1
  39.1 6.1 %collective-permute-start.6 = (f32[4,3,3,8,128]{4,3,2,1,0:T(8,128)S(1)}, f32[4,3,3,8,128]{4,3,2,1,0:T(8,128)S(1)}, u32[]{:S(2)}, u32[]{:S(2)}) collective-permute-start(f32[4,3,3,8,128]{4,3,2,1,0:T(8,128)S(1)} %all_to_all.20.middle.c1.rest_1_), channel_id=1, source_target_pairs={{448,0},{0,64},{64,128},{128,192},{192,256},{256,320},{320,384},{3... | collective-permute-start | bytes 442376 | tf_op jit(solution)/shard_map/ppermute | solution.py:444
  43.0 4.9 %collective-permute-start.7 = (f32[4,3,3,8,128]{4,3,2,1,0:T(8,128)S(1)}, f32[4,3,3,8,128]{4,3,2,1,0:T(8,128)S(1)}, u32[]{:S(2)}, u32[]{:S(2)}) collective-permute-start(f32[4,3,3,8,128]{4,3,2,1,0:T(8,128)S(1)} %all_to_all.20.middle.c1.rest_1_), channel_id=1, source_target_pairs={{64,0},{128,64},{192,128},{256,192},{320,256},{384,320},{448,384},... | collective-permute-start | bytes 442376 | tf_op jit(solution)/shard_map/ppermute | solution.py:444
  63.9 9.8 %collective-permute-start.8 = (f32[12,8,128]{2,1,0:T(8,128)S(1)}, f32[12,8,128]{2,1,0:T(8,128)S(1)}, u32[]{:S(2)}, u32[]{:S(2)}) collective-permute-start(f32[12,8,128]{2,1,0:T(8,128)S(1)} %shard_map.91.s1), channel_id=1, source_target_pairs={{60,0},{0,4},{4,8},{8,12},{12,16},{16,20},{20,24},{24,28},{28,32},... | collective-permute-start | bytes 147464 | tf_op jit(solution)/shard_map/ppermute | solution.py:444
  65.8 7.9 %collective-permute-start.9 = (f32[12,8,128]{2,1,0:T(8,128)S(1)}, f32[12,8,128]{2,1,0:T(8,128)S(1)}, u32[]{:S(2)}, u32[]{:S(2)}) collective-permute-start(f32[12,8,128]{2,1,0:T(8,128)S(1)} %shard_map.91.s1), channel_id=1, source_target_pairs={{4,0},{8,4},{12,8},{16,12},{20,16},{24,20},{28,24},{32,28},{36,32}... | collective-permute-start | bytes 147464 | tf_op jit(solution)/shard_map/ppermute | solution.py:444
  73.7 26.0 %copy-start.2 = (s32[2,1,1,1,128]{4,3,2,1,0:T(1,128)S(1)}, s32[2,1,1,1,128]{4,3,2,1,0:T(1,128)}, u32[]{:S(2)}) copy-start(s32[2,1,1,1,128]{4,3,2,1,0:T(1,128)} %param.11) | copy-start | bytes 3076
  76.0 13.3 %collective-permute-start.10 = (f32[8,128]{1,0:T(8,128)S(1)}, f32[8,128]{1,0:T(8,128)S(1)}, u32[]{:S(2)}, u32[]{:S(2)}) collective-permute-start(f32[8,128]{1,0:T(8,128)S(1)} %get-tuple-element.71), channel_id=1, source_target_pairs={{64,0},{128,64},{192,128},{256,192},{320,256},{384,320},{448,384},... | collective-permute-start | bytes 12296 | tf_op jit(solution)/shard_map/ppermute | solution.py:444
  79.1 10.3 %collective-permute-start.11 = (f32[8,128]{1,0:T(8,128)S(1)}, f32[8,128]{1,0:T(8,128)S(1)}, u32[]{:S(2)}, u32[]{:S(2)}) collective-permute-start(f32[8,128]{1,0:T(8,128)S(1)} %get-tuple-element.72), channel_id=1, source_target_pairs={{448,0},{0,64},{64,128},{128,192},{192,256},{256,320},{320,384},{3... | collective-permute-start | bytes 12296 | tf_op jit(solution)/shard_map/ppermute | solution.py:444
  79.1 10.3 %collective-permute-start.12 = (f32[8,128]{1,0:T(8,128)S(1)}, f32[8,128]{1,0:T(8,128)S(1)}, u32[]{:S(2)}, u32[]{:S(2)}) collective-permute-start(f32[8,128]{1,0:T(8,128)S(1)} %get-tuple-element.73), channel_id=1, source_target_pairs={{4,0},{8,4},{12,8},{16,12},{20,16},{24,20},{28,24},{32,28},{36,32}... | collective-permute-start | bytes 12296 | tf_op jit(solution)/shard_map/ppermute | solution.py:444
  87.4 5.6 %collective-permute-start.13 = (f32[8,128]{1,0:T(8,128)S(1)}, f32[8,128]{1,0:T(8,128)S(1)}, u32[]{:S(2)}, u32[]{:S(2)}) collective-permute-start(f32[8,128]{1,0:T(8,128)S(1)} %get-tuple-element.74), channel_id=1, source_target_pairs={{60,0},{0,4},{4,8},{8,12},{12,16},{16,20},{20,24},{24,28},{28,32},... | collective-permute-start | bytes 12296 | tf_op jit(solution)/shard_map/ppermute | solution.py:444
  93.2 7.2 %collective-permute-start.14 = (f32[3,8,128]{2,1,0:T(8,128)S(1)}, f32[3,8,128]{2,1,0:T(8,128)S(1)}, u32[]{:S(2)}, u32[]{:S(2)}) collective-permute-start(f32[3,8,128]{2,1,0:T(8,128)S(1)} %get-tuple-element.75), channel_id=1, source_target_pairs={{60,0},{0,4},{4,8},{8,12},{12,16},{16,20},{20,24},{24,28},{28,32},... | collective-permute-start | bytes 36872 | tf_op jit(solution)/shard_map/ppermute | solution.py:444
  95.1 5.4 %collective-permute-start.15 = (f32[3,8,128]{2,1,0:T(8,128)S(1)}, f32[3,8,128]{2,1,0:T(8,128)S(1)}, u32[]{:S(2)}, u32[]{:S(2)}) collective-permute-start(f32[3,8,128]{2,1,0:T(8,128)S(1)} %get-tuple-element.75), channel_id=1, source_target_pairs={{4,0},{8,4},{12,8},{16,12},{20,16},{24,20},{28,24},{32,28},{36,32}... | collective-permute-start | bytes 36872 | tf_op jit(solution)/shard_map/ppermute | solution.py:444
  107.8 6.3 %collective-permute-start.16 = (f32[4,3,3,8,128]{4,3,2,1,0:T(8,128)S(1)}, f32[4,3,3,8,128]{4,3,2,1,0:T(8,128)S(1)}, u32[]{:S(2)}, u32[]{:S(2)}) collective-permute-start(f32[4,3,3,8,128]{4,3,2,1,0:T(8,128)S(1)} %all_to_all.22.middle.c1), channel_id=1, source_target_pairs={{448,0},{0,64},{64,128},{128,192},{192,256},{256,320},{320,384},{3... | collective-permute-start | bytes 442376 | tf_op jit(solution)/shard_map/ppermute | solution.py:444
  112.0 4.6 %collective-permute-start.17 = (f32[4,3,3,8,128]{4,3,2,1,0:T(8,128)S(1)}, f32[4,3,3,8,128]{4,3,2,1,0:T(8,128)S(1)}, u32[]{:S(2)}, u32[]{:S(2)}) collective-permute-start(f32[4,3,3,8,128]{4,3,2,1,0:T(8,128)S(1)} %all_to_all.22.middle.c1), channel_id=1, source_target_pairs={{64,0},{128,64},{192,128},{256,192},{320,256},{384,320},{448,384},... | collective-permute-start | bytes 442376 | tf_op jit(solution)/shard_map/ppermute | solution.py:444
  131.3 9.7 %collective-permute-start.18 = (f32[12,8,128]{2,1,0:T(8,128)S(1)}, f32[12,8,128]{2,1,0:T(8,128)S(1)}, u32[]{:S(2)}, u32[]{:S(2)}) collective-permute-start(f32[12,8,128]{2,1,0:T(8,128)S(1)} %shard_map.98.s1), channel_id=1, source_target_pairs={{60,0},{0,4},{4,8},{8,12},{12,16},{16,20},{20,24},{24,28},{28,32},... | collective-permute-start | bytes 147464 | tf_op jit(solution)/shard_map/ppermute | solution.py:444
  133.3 7.8 %collective-permute-start.19 = (f32[12,8,128]{2,1,0:T(8,128)S(1)}, f32[12,8,128]{2,1,0:T(8,128)S(1)}, u32[]{:S(2)}, u32[]{:S(2)}) collective-permute-start(f32[12,8,128]{2,1,0:T(8,128)S(1)} %shard_map.98.s1), channel_id=1, source_target_pairs={{4,0},{8,4},{12,8},{16,12},{20,16},{24,20},{28,24},{32,28},{36,32}... | collective-permute-start | bytes 147464 | tf_op jit(solution)/shard_map/ppermute | solution.py:444
